TPU v7x, 32 devices: a whole 2x2x4 slice. The times are simulated.
32 devices in a mesh: gx: 4 (over z), gy: 4 (over x, core), pa: 2 (over y).
Axes of the slice: x: 2, y: 2, z: 4, core: 2. Of those that a mesh axis runs over, the one named last changes fastest.
Arguments:
- conductivity: float32 [32, 512, 256], P('gx', 'gy', 'pa'), may hold values from 0.5 to 1
- stored_state: bfloat16 [32, 512, 256], P('gx', 'gy', 'pa'), may hold values from -4 to 5
- row_scales: float32 [32, 512], P('gx', 'gy'), may hold values from 0.5 to 4
- cotangent: float32 [32, 512, 256], P('gx', 'gy', 'pa'), may hold values from -5 to 6
- upper_bound: float32 [1], replicated, may hold values from 97 to 145
Outputs:
- grad_conductivity: float32 [32, 512, 256], P('gx', 'gy', 'pa')
- adjoint: float32 [32, 512, 256], P('gx', 'gy', 'pa')
- state_new: float32 [32, 512, 256], P('gx', 'gy', 'pa')
- residuals: float32 [2, 32, 512, 256], P(None, 'gx', 'gy', 'pa')
All inputs are finite; a program needn't handle non-finite values.
Results may differ from a plain program's by a relative error of at most 0.0003.
Values may be sent and summed in bfloat16 or wider, within the bound.
No kernel may reach another device: no remote copies, remote signals or barrier semaphores. Data moves between devices by JAX's collectives and lax.ppermute only.
A program may use at most 128 MiB of HBM per device.

v0:
```python
import jax
import jax.numpy as jnp
from jax import lax
from jax.sharding import PartitionSpec as P

CHEB = 16


time_step = 8.0


def with_halo(cells, sides, width):
    for axis, dim in sides:
        count = lax.axis_size(axis)
        head = lax.slice_in_dim(cells, 0, width, axis=dim)
        tail = lax.slice_in_dim(cells, cells.shape[dim] - width, cells.shape[dim], axis=dim)
        cells = jnp.concatenate(
            [
                lax.ppermute(tail, axis, [(i, (i + 1) % count) for i in range(count)]),
                cells,
                lax.ppermute(head, axis, [((i + 1) % count, i) for i in range(count)]),
            ],
            axis=dim,
        )
    return cells


def swapped(x, axis, bit):
    return lax.ppermute(x, axis, [(i, i ^ 1 << bit) for i in range(lax.axis_size(axis))])


def region(arr, spatial, offset):
    extent = arr.shape[-3:]
    window = [slice(1, length - 1) for length in extent]
    window[spatial] = slice(offset, extent[spatial] - 2 + offset)
    leading = [slice(None)] * (arr.ndim - 3)
    return arr[tuple(leading + window)]


def apply_operator(padded, kpad):
    centre = region(padded, 0, 1)
    kcentre = region(kpad, 0, 1)
    summed = jnp.zeros_like(centre)
    for spatial in range(3):
        for offset in (0, 2):
            summed = summed + 0.5 * (kcentre + region(kpad, spatial, offset)) * (
                centre - region(padded, spatial, offset)
            )
    return centre + time_step * summed


def chebyshev(rhs, kpad, upper):
    theta = 0.5 * (upper + 1.0)
    delta = 0.5 * (upper - 1.0)
    sigma = theta / delta
    rho = 1.0 / sigma
    start = (jnp.zeros_like(rhs), rhs, rhs / theta, rho)

    def sweep(step, carry):
        solution, residual, direction, rho_now = carry
        padded = with_halo(direction, (("gx", 1), ("gy", 2), ("pa", 3)), 1)
        solution = solution + direction
        residual = residual - apply_operator(padded, kpad)
        rho_next = 1.0 / (2.0 * sigma - rho_now)
        direction = rho_next * rho_now * direction + 2.0 * rho_next / delta * residual
        return (solution, residual, direction, rho_next)

    final = lax.fori_loop(0, CHEB, sweep, start)
    return (final[0], final[1])


def body(conductivity, stored_state, row_scales, cotangent, upper_bound):
    upper = upper_bound[0]
    rim_width = 1
    kpad = with_halo(conductivity, (("gx", 0), ("gy", 1), ("pa", 2)), rim_width)
    partner = swapped(stored_state, "pa", 0)
    previous = partner.astype(jnp.float32) * row_scales[:, :, None]
    forward_sol, forward_res = chebyshev(previous[None], kpad, upper)
    adjoint_sol, adjoint_res = chebyshev(cotangent[None], kpad, upper)
    state_new = forward_sol[0]
    adjoint = adjoint_sol[0]
    residuals = jnp.concatenate((forward_res, adjoint_res), axis=0)
    pair = with_halo(jnp.stack((state_new, adjoint)), (("gx", 1), ("gy", 2), ("pa", 3)), 1)
    centre = region(pair, 0, 1)
    summed = jnp.zeros_like(state_new)
    for spatial in range(3):
        for offset in (0, 2):
            differ = centre - region(pair, spatial, offset)
            summed = summed + differ[0] * differ[1]
    grad_conductivity = -0.5 * time_step * summed
    return (grad_conductivity, adjoint, state_new, residuals)


def solution(mesh):
    return jax.shard_map(
        body,
        mesh=mesh,
        in_specs=(
            P("gx", "gy", "pa"),
            P("gx", "gy", "pa"),
            P("gx", "gy"),
            P("gx", "gy", "pa"),
            P(),
        ),
        out_specs=(
            P("gx", "gy", "pa"),
            P("gx", "gy", "pa"),
            P("gx", "gy", "pa"),
            P(None, "gx", "gy", "pa"),
        ),
        check_vma=False,
    )
```

profile of v0, /device:TPU:8, one launch (start us, length us, event | category | flops | bytes accessed | tf_op | source)
XLA Modules:
  0.0 750.2 jit_solution(3895316732864309329)
XLA Ops:
  23.3 350.4 %while.39 = (s32[]{:T(128)}, f32[1,8,128,128]{3,2,1,0:T(8,128)}, f32[1,8,128,128]{3,2,1,0:T(8,128)}, f32[1,8,128,128]{3,2,1,0:T(8,128)}, f32[]{:T(128)}, /*index...) while((s32[]{:T(128)}, f32[1,8,128,128]{3,2,1,0:T(8,128)}, ...), condition=%wide.region_3.0_spmd.clone, body=%wide.region_2.0_spmd.clone.sunk | while | flops 5706760 | bytes 11741379 | solution.py:68
  41.3 3.6 multiply_add_fusion.5
  61.3 3.6 multiply_add_fusion.5
  82.9 3.6 multiply_add_fusion.5
  105.1 3.6 multiply_add_fusion.5
  127.1 3.6 multiply_add_fusion.5
  149.2 3.6 multiply_add_fusion.5
  171.3 3.6 multiply_add_fusion.5
  193.4 3.6 multiply_add_fusion.5
  215.5 3.6 multiply_add_fusion.5
  237.6 3.6 multiply_add_fusion.5
  259.6 3.6 multiply_add_fusion.5
  281.8 3.6 multiply_add_fusion.5
  303.8 3.6 multiply_add_fusion.5
  326.0 3.6 multiply_add_fusion.5
  348.0 3.6 multiply_add_fusion.5
  370.1 3.6 multiply_add_fusion.5
  373.8 330.0 %while.38 = (s32[]{:T(128)}, f32[1,8,128,128]{3,2,1,0:T(8,128)}, f32[1,8,128,128]{3,2,1,0:T(8,128)}, f32[1,8,128,128]{3,2,1,0:T(8,128)}, f32[]{:T(128)}, /*index...) while((s32[]{:T(128)}, f32[1,8,128,128]{3,2,1,0:T(8,128)}, ...), condition=%wide.region_1.0_spmd.clone, body=%wide.region_0.0_spmd.clone.sunk | while | flops 5706760 | bytes 15935739 | solution.py:68
  391.3 3.6 multiply_add_fusion.4
  454.4 3.6 multiply_add_fusion.4
  710.1 3.9 collective-permute-done.19
  726.7 6.8 fusion.43
  735.7 10.4 %fusion.41 = (f32[2,8,128,128]{3,0,2,1:T(2,128)S(1)}, f32[2,8,128,128]{3,0,2,1:T(2,128)S(1)}) fusion(f32[2,10,130,1]{3,0,2,1:T(2,128)S(1)} %copy.45, f32[2,10,1,128]{3,0,2,1:T(2,128)S(1)} %collective-permute-done.22, f32[2,10,1,128]{3,0,2,1:T(2,128)S(1)} %collective-permute-done.21, f32[2,1,128,128]{3,0,2,1:T(2,128)S(1)} %collective-permute-done.20, ...), kind=kLoop, calls=%fused_computation.86 | loop fusion | flops 3932160 | bytes 3449152 | tf_op jit(solution)/shard_map/sub | solution.py:88
  746.2 4.0 fusion.58
  (914 shorter events, 653.8 us)
Async XLA Ops:
  10.2 12.0 %collective-permute-start.12 = (bf16[8,128,128]{2,1,0:T(8,128)(2,1)}, bf16[8,128,128]{2,1,0:T(8,128)(2,1)S(1)}, u32[]{:S(2)}, u32[]{:S(2)}) collective-permute-start(bf16[8,128,128]{2,1,0:T(8,128)(2,1)} %param.10), channel_id=1, source_target_pairs={{0,1},{1,0},{2,3},{3,2},{4,5},{5,4},{6,7},{7,6},{8,9},{9,8},{10,11... | collective-permute-start | bytes 786440 | tf_op jit(solution)/shard_map/ppermute | solution.py:29
  46.7 6.2 collective-permute-start.7
  67.0 6.6 collective-permute-start.7
  87.6 6.1 collective-permute-start.6
  89.3 6.3 collective-permute-start.7
  109.7 6.1 collective-permute-start.6
  111.1 6.7 collective-permute-start.7
  131.8 6.1 collective-permute-start.6
  133.5 6.3 collective-permute-start.7
  155.2 6.7 collective-permute-start.7
  176.0 6.1 collective-permute-start.6
  177.7 6.3 collective-permute-start.7
  198.1 6.1 collective-permute-start.6
  199.4 6.7 collective-permute-start.7
  221.9 6.3 collective-permute-start.7
  243.6 6.7 collective-permute-start.7
  266.1 6.3 collective-permute-start.7
  287.8 6.7 collective-permute-start.7
  310.2 6.3 collective-permute-start.7
  332.0 6.7 collective-permute-start.7
  354.4 6.3 collective-permute-start.7
  706.1 7.9 %collective-permute-start.19 = (f32[2,1,128,128]{3,0,2,1:T(2,128)S(1)}, f32[2,1,128,128]{3,0,2,1:T(2,128)S(1)}, u32[]{:S(2)}, u32[]{:S(2)}) collective-permute-start(f32[2,1,128,128]{3,0,2,1:T(2,128)S(1)} %get-tuple-element.473), channel_id=1, source_target_pairs={{0,8},{8,16},{16,24},{24,0},{1,9},{9,17},{17,25},{25,1},{2,10},{10... | collective-permute-start | bytes 393224 | tf_op jit(solution)/shard_map/ppermute | solution.py:19
  723.7 9.9 %collective-permute-start.23 = (f32[2,10,130,1]{2,0,3,1:T(2,128)S(1)}, f32[2,10,130,1]{2,0,3,1:T(2,128)S(1)}, u32[]{:S(2)}, u32[]{:S(2)}) collective-permute-start(f32[2,10,130,1]{2,0,3,1:T(2,128)S(1)} %copy.44), channel_id=1, source_target_pairs={{0,1},{1,0},{2,3},{3,2},{4,5},{5,4},{6,7},{7,6},{8,9},{9,8},{10,11... | collective-permute-start | bytes 31208 | tf_op jit(solution)/shard_map/ppermute | solution.py:19
  726.2 8.4 %collective-permute-start.24 = (f32[2,10,130,1]{2,0,3,1:T(2,128)S(1)}, f32[2,10,130,1]{2,0,3,1:T(2,128)S(1)}, u32[]{:S(2)}, u32[]{:S(2)}) collective-permute-start(f32[2,10,130,1]{2,0,3,1:T(2,128)S(1)} %copy.46), channel_id=1, source_target_pairs={{1,0},{0,1},{3,2},{2,3},{5,4},{4,5},{7,6},{6,7},{9,8},{8,9},{11,10... | collective-permute-start | bytes 31208 | tf_op jit(solution)/shard_map/ppermute | solution.py:21
  (221 other events, 876.3 us)
where the time goes:
time: 756 us; the launch traced here: 750 us
  waiting for transfers between devices  272 us (36%)
  starting transfers between devices  188 us (25%)
  other arithmetic  187 us (25%)
  local copies, waits for them, and re-layouts  97.9 us (13%)
    ppermute x102, waiting for transfers between devices, with_halo(): lax.ppermute(tail, axis, [(i, (i + 1) % count) for i in range(count)])  180 us
    add x32, other arithmetic, sweep(): rho_next * rho_now * direction + 2.0 * rho_next / delta * residual  116 us
    ppermute x102, starting transfers between devices, with_halo(): lax.ppermute(tail, axis, [(i, (i + 1) % count) for i in range(count)])  106 us
    ppermute x102, waiting for transfers between devices, with_halo(): lax.ppermute(head, axis, [((i + 1) % count, i) for i in range(count)])  92.4 us
    ppermute x102, starting transfers between devices, with_halo(): lax.ppermute(head, axis, [((i + 1) % count, i) for i in range(count)])  80.2 us
    while x128, local copies, waits for them, and re-layouts  34.6 us
    while x32, other arithmetic  32.5 us
    slice x99, local copies, waits for them, and re-layouts, with_halo(): lax.slice_in_dim(cells, cells.shape[dim] - width, cells.shape[dim], axis=...  23.8 us
  transfers between devices with their start and end apart: 205, of which 183 were waited for; matrix products, arithmetic and copies ran while one was open for 10% of the time, Pallas kernels for 0%

commit v1 on v0

v1 whole, which is shorter than its diff:
```python
import functools

import jax
import jax.numpy as jnp
from jax import lax
from jax.experimental import pallas as pl
from jax.experimental.pallas import tpu as pltpu
from jax.sharding import PartitionSpec as P

CHEB = 16
LANES = 128
HALO = CHEB
TIME_STEP = 8.0
F32 = jnp.float32


def with_halo(cells, sides, width):
    for axis, dim in sides:
        count = lax.axis_size(axis)
        head = lax.slice_in_dim(cells, 0, width, axis=dim)
        tail = lax.slice_in_dim(cells, cells.shape[dim] - width, cells.shape[dim], axis=dim)
        cells = jnp.concatenate(
            [
                lax.ppermute(tail, axis, [(i, (i + 1) % count) for i in range(count)]),
                cells,
                lax.ppermute(head, axis, [((i + 1) % count, i) for i in range(count)]),
            ],
            axis=dim,
        )
    return cells


def region(arr, spatial, offset):
    extent = arr.shape[-3:]
    window = [slice(1, length - 1) for length in extent]
    window[spatial] = slice(offset, extent[spatial] - 2 + offset)
    leading = [slice(None)] * (arr.ndim - 3)
    return arr[tuple(leading + window)]


def apply_operator(padded, kpad):
    centre = region(padded, 0, 1)
    kcentre = region(kpad, 0, 1)
    summed = jnp.zeros_like(centre)
    for spatial in range(3):
        for offset in (0, 2):
            summed = summed + 0.5 * (kcentre + region(kpad, spatial, offset)) * (
                centre - region(padded, spatial, offset)
            )
    return centre + TIME_STEP * summed


def stepwise(conductivity, stored_state, row_scales, cotangent, upper_bound):
    upper = upper_bound[0]
    kpad = with_halo(conductivity, (("gx", 0), ("gy", 1), ("pa", 2)), 1)
    count = lax.axis_size("pa")
    partner = lax.ppermute(stored_state, "pa", [(i, (i + count // 2) % count) for i in range(count)])
    previous = partner.astype(F32) * row_scales[:, :, None]
    rhs = jnp.stack((previous, cotangent))
    theta = 0.5 * (upper + 1.0)
    delta = 0.5 * (upper - 1.0)
    sigma = theta / delta
    sides = (("gx", 1), ("gy", 2), ("pa", 3))

    def sweep(step, carry):
        solved, residual, direction, rho = carry
        padded = with_halo(direction, sides, 1)
        solved = solved + direction
        residual = residual - apply_operator(padded, kpad)
        rho_next = 1.0 / (2.0 * sigma - rho)
        direction = rho_next * rho * direction + 2.0 * rho_next / delta * residual
        return (solved, residual, direction, rho_next)

    start = (jnp.zeros_like(rhs), rhs, rhs / theta, 1.0 / sigma)
    solved, residual, _, _ = lax.fori_loop(0, CHEB, sweep, start)
    pair = with_halo(solved, sides, 1)
    centre = region(pair, 0, 1)
    summed = jnp.zeros_like(solved[0])
    for spatial in range(3):
        for offset in (0, 2):
            differ = centre - region(pair, spatial, offset)
            summed = summed + differ[0] * differ[1]
    return (-0.5 * TIME_STEP * summed, solved[1], solved[0], residual)


G = 4
BX = 8
BY = 128
BZ = 128
STRIP = BZ // G
NXL = G * BX // 2
TOP = 8 + HALO
ROWS = BY + 2 * TOP
MROWS = BY + 8


def lane_ids(rows):
    return lax.broadcasted_iota(jnp.int32, (rows, LANES), 1)


def turn(x, shift):
    return pltpu.roll(x, lax.rem(shift + 4 * LANES, LANES), 1)


def pack_kernel(strips, cond, stored, scales, cot, *outs):
    group = lane_ids(BY) // STRIP
    for a in range(2):
        planes = []
        for b in range(4):
            c = 4 * a + b
            planes.append(
                (cond[c], stored[c].astype(F32) * scales[c], cot[c])
            )
        for d in range(G):
            s = strips[d]
            for n in range(3):
                acc = turn(planes[0][n], -STRIP * s)
                for b in range(1, 4):
                    acc = jnp.where(group == b, turn(planes[b][n], STRIP * b - STRIP * s), acc)
                outs[d][n, a] = acc


def edge_kernel(sources, *refs):
    msgs, (left, right) = refs[:G], refs[G:]
    low = lax.rem(lane_ids(BY), STRIP) < STRIP // 2
    for n in range(3):
        for d in range(G):
            source = sources[d]
            first, second = msgs[d][n, 0], msgs[d][n, 1]
            left[n, source] = jnp.where(low, first, pltpu.roll(second, STRIP // 2, 1))
            right[n, source] = jnp.where(low, pltpu.roll(first, LANES - STRIP // 2, 1), second)


def build_kernel(sources, *refs):
    msgs, (from_left, from_right), (whole, head, tail) = refs[:G], refs[G : G + 2], refs[G + 2 :]
    lane = lane_ids(BY)
    for d in range(G):
        source = sources[d]
        half = 64 * (source // 2)
        first = BX * lax.rem(source, 2)
        place = lane - half
        for n in range(3):
            for a in range(2):
                own = msgs[d][n, a]
                lo = from_left[n, source]
                hi = from_right[n, source]
                for b in range(4):
                    val = jnp.where(
                        place < HALO,
                        turn(lo, half - 32 * b - 16 * a),
                        jnp.where(
                            place < HALO + STRIP,
                            turn(own, half + HALO - 32 * b),
                            turn(hi, half + HALO + STRIP - 32 * b - 16 * a),
                        ),
                    )
                    at = first + 4 * a + b
                    keep = (place >= 0) & (place < 64)
                    whole[n, at] = jnp.where(keep, val, whole[n, at])
    for n in range(3):
        for i in range(NXL):
            head[n, i] = whole[n, i, :HALO]
            tail[n, i] = whole[n, i, BY - HALO :]


def solve_kernel(homes, scalars, whole, above, below, *refs):
    outs = refs[:G]
    xs, rhs, kap, kx, ky, kz, diag = refs[G:]
    nf = 2
    zero8 = jnp.zeros((8, LANES), F32)
    for i in range(NXL):
        for n, dst in ((0, kap), (1, rhs.at[0]), (2, rhs.at[1])):
            dst[i, 0:8] = zero8
            dst[i, ROWS - 8 : ROWS] = zero8
            dst[i, 8:TOP] = above[n, i]
            dst[i, TOP : TOP + BY] = whole[n, i]
            dst[i, TOP + BY : ROWS - 8] = below[n, i]

    @pl.loop(0, ROWS // 8 - 2)
    def _(t):
        r = pl.multiple_of(8 + 8 * t, 8)
        now = kap[0, pl.ds(r, 8)]
        wrapped = pltpu.roll(now, 64, 1)
        for i in range(NXL):
            after = kap[i + 1, pl.ds(r, 8)] if i + 1 < NXL else wrapped
            kx[i, pl.ds(r, 8)] = 4.0 * (now + after)
            ky[i, pl.ds(r, 8)] = 4.0 * (now + kap[i, pl.ds(r + 1, 8)])
            kz[i, pl.ds(r, 8)] = 4.0 * (now + pltpu.roll(now, LANES - 1, 1))
            now = after

    for i in range(NXL):
        ky[i, 0:8] = zero8
    theta_inv = scalars[0, 0]

    @pl.loop(0, ROWS // 8 - 2)
    def _(t):
        r = pl.multiple_of(8 + 8 * t, 8)
        before = pltpu.roll(kx[NXL - 1, pl.ds(r, 8)], 64, 1)
        for i in range(NXL):
            fx = kx[i, pl.ds(r, 8)]
            fz = kz[i, pl.ds(r, 8)]
            total = fx + before + ky[i, pl.ds(r, 8)] + ky[i, pl.ds(r - 1, 8)]
            diag[i, pl.ds(r, 8)] = 1.0 + (total + (fz + pltpu.roll(fz, 1, 1)))
            before = fx
            for f in range(nf):
                xs[0, f, i, pl.ds(r, 8)] = rhs[f, i, pl.ds(r, 8)] * theta_inv
                xs[1, f, i, pl.ds(r, 8)] = zero8

    for i in range(NXL):
        for f in range(nf):
            for slot in range(2):
                xs[slot, f, i, 0:8] = zero8
                xs[slot, f, i, ROWS - 8 : ROWS] = zero8

    def sweep(k, first, count):
        alpha, beta = scalars[k, 0], scalars[k, 1]
        cur = lax.rem(k + 1, 2)
        new = lax.rem(k, 2)

        @pl.loop(0, count)
        def _(t):
            r = pl.multiple_of(first + 8 * t, 8)
            now = [xs[cur, f, 0, pl.ds(r, 8)] for f in range(nf)]
            wrapped = [pltpu.roll(x, 64, 1) for x in now]
            before = [pltpu.roll(xs[cur, f, NXL - 1, pl.ds(r, 8)], 64, 1) for f in range(nf)]
            fbefore = pltpu.roll(kx[NXL - 1, pl.ds(r, 8)], 64, 1)
            for i in range(NXL):
                fx = kx[i, pl.ds(r, 8)]
                fy = ky[i, pl.ds(r, 8)]
                fym = ky[i, pl.ds(r - 1, 8)]
                fz = kz[i, pl.ds(r, 8)]
                centre = (1.0 + alpha) - beta * diag[i, pl.ds(r, 8)]
                for f in range(nf):
                    x = now[f]
                    after = xs[cur, f, i + 1, pl.ds(r, 8)] if i + 1 < NXL else wrapped[f]
                    near = fx * after + fbefore * before[f]
                    near = near + (fy * xs[cur, f, i, pl.ds(r + 1, 8)] + fym * xs[cur, f, i, pl.ds(r - 1, 8)])
                    near = near + (fz * pltpu.roll(x, LANES - 1, 1) + pltpu.roll(fz * x, 1, 1))
                    near = near + rhs[f, i, pl.ds(r, 8)]
                    xs[new, f, i, pl.ds(r, 8)] = (
                        centre * x - alpha * xs[new, f, i, pl.ds(r, 8)] + beta * near
                    )
                    before[f] = x
                    now[f] = after
                fbefore = fx

    @pl.loop(1, CHEB // 2)
    def _(k):
        sweep(k, 8, ROWS // 8 - 2)

    @pl.loop(CHEB // 2, CHEB)
    def _(k):
        sweep(k, 16, ROWS // 8 - 4)

    last = (CHEB - 1) % 2
    lane = lane_ids(8)
    group = lane // STRIP
    sub = lax.broadcasted_iota(jnp.int32, (8, LANES), 0)

    for d in range(G):
        home = homes[d]
        half = 64 * (home // 2)
        i0 = BX * lax.rem(home, 2)
        down = lax.rem(BX * home + 31, 32)
        up = lax.rem(BX * home + 8, 32)

        def gather(f, a, row):
            if a < 2:
                acc = None
                for b in range(4):
                    val = turn(xs[last, f, i0 + 4 * a + b, pl.ds(row, 8)], 32 * b - half - HALO)
                    acc = val if b == 0 else jnp.where(group == b, val, acc)
                return acc
            acc = turn(xs[last, f, lax.rem(down, NXL), pl.ds(row, 8)], -64 * (down // NXL) - HALO)
            val = turn(xs[last, f, lax.rem(up, NXL), pl.ds(row, 8)], 32 - 64 * (up // NXL) - HALO)
            acc = jnp.where(group == 1, val, acc)
            for c in range(BX):
                plane = xs[last, f, i0 + c, pl.ds(row, 8)]
                acc = jnp.where(lane == 64 + c, turn(plane, 64 + c - half - HALO + 1), acc)
                acc = jnp.where(lane == 72 + c, turn(plane, 72 + c - half - HALO - STRIP), acc)
            return acc

        for f in range(nf):

            @pl.loop(0, BY // 8)
            def _(t):
                for a in range(3):
                    outs[d][f, a, pl.ds(pl.multiple_of(8 * t, 8), 8)] = gather(
                        f, a, pl.multiple_of(TOP + 8 * t, 8)
                    )

            for a in range(2):
                over = pltpu.roll(gather(f, a, TOP - 8), 1, 0)
                under = pltpu.roll(gather(f, a, TOP + BY), 1, 0)
                outs[d][f, a, BY : BY + 8] = jnp.where(sub == 0, over, under)
            outs[d][f, 2, BY : BY + 8] = zero8


def final_kernel(strips, m0, m1, m2, m3, cond, kdown, kup, kover, kunder, kzl, kzr, stored, scales, cot, grad, adjoint, state, residuals, xs, ends, kap):
    msgs = (m0, m1, m2, m3)
    lane = lane_ids(BY)
    group = lane // STRIP
    for f in range(2):
        for d in range(G):
            s = strips[d]
            mine = group == s
            ends[f, s] = msgs[d][f, 2, :BY]
            for a in range(2):
                for b in range(4):
                    at = 1 + 4 * a + b
                    val = turn(msgs[d][f, a, :BY], STRIP * s - STRIP * b)
                    xs[f, at, 8 : 8 + BY] = jnp.where(mine, val, xs[f, at, 8 : 8 + BY])
                    val = pltpu.roll(turn(msgs[d][f, a, BY : BY + 8], STRIP * s - STRIP * b), 7, 0)
                    xs[f, at, 0:8] = jnp.where(mine[:8], val, xs[f, at, 0:8])
                    xs[f, at, 8 + BY : 16 + BY] = jnp.where(mine[:8], val, xs[f, at, 8 + BY : 16 + BY])
            for at, b in ((0, 0), (1 + BX, 1)):
                val = turn(msgs[d][f, 2, :BY], STRIP * s - STRIP * b)
                xs[f, at, 8 : 8 + BY] = jnp.where(mine, val, xs[f, at, 8 : 8 + BY])
    zero8 = jnp.zeros((8, LANES), F32)
    sub = lax.broadcasted_iota(jnp.int32, (8, LANES), 0)
    kap[0, 8 : 8 + BY] = kdown[...]
    kap[1 + BX, 8 : 8 + BY] = kup[...]
    for c in range(BX):
        kap[1 + c, 8 : 8 + BY] = cond[c]
        kap[1 + c, 0:8] = jnp.broadcast_to(kover[c : c + 1], (8, LANES))
        kap[1 + c, 8 + BY : 16 + BY] = jnp.broadcast_to(kunder[c : c + 1], (8, LANES))
    lane = lane[:8]

    @pl.loop(0, BY // 8)
    def _(t):
        r = pl.multiple_of(8 * t, 8)
        r8 = pl.multiple_of(8 * t + 8, 8)
        for c in range(BX):
            k = kap[1 + c, pl.ds(r8, 8)]
            x = [xs[f, 1 + c, pl.ds(r8, 8)] for f in range(2)]
            total = [0.0, 0.0]
            product = 0.0

            def sides():
                for at in (c, c + 2):
                    yield kap[at, pl.ds(r8, 8)], [xs[f, at, pl.ds(r8, 8)] for f in range(2)]
                for off in (-1, 1):
                    yield kap[1 + c, pl.ds(r8 + off, 8)], [xs[f, 1 + c, pl.ds(r8 + off, 8)] for f in range(2)]
                yield (
                    jnp.where(lane == 0, kzl[c, pl.ds(r, 8)], pltpu.roll(k, 1, 1)),
                    [
                        jnp.where(
                            lane == 0,
                            pltpu.roll(ends[f, 0, pl.ds(r, 8)], 64 - c, 1),
                            pltpu.roll(x[f], 1, 1),
                        )
                        for f in range(2)
                    ],
                )
                yield (
                    jnp.where(lane == LANES - 1, kzr[c, pl.ds(r, 8)], pltpu.roll(k, LANES - 1, 1)),
                    [
                        jnp.where(
                            lane == LANES - 1,
                            pltpu.roll(ends[f, G - 1, pl.ds(r, 8)], LANES - 1 - 72 - c, 1),
                            pltpu.roll(x[f], LANES - 1, 1),
                        )
                        for f in range(2)
                    ],
                )

            for kn, xn in sides():
                face = k + kn
                differ = [x[f] - xn[f] for f in range(2)]
                product = product + differ[0] * differ[1]
                for f in range(2):
                    total[f] = total[f] + face * differ[f]
            grad[c, pl.ds(r, 8)] = (-0.5 * TIME_STEP) * product
            state[c, pl.ds(r, 8)] = x[0]
            adjoint[c, pl.ds(r, 8)] = x[1]
            previous = stored[c, pl.ds(r, 8)].astype(F32) * scales[c, pl.ds(r, 8)]
            residuals[0, c, pl.ds(r, 8)] = previous - (x[0] + (0.5 * TIME_STEP) * total[0])
            residuals[1, c, pl.ds(r, 8)] = cot[c, pl.ds(r, 8)] - (x[1] + (0.5 * TIME_STEP) * total[1])


def call(kernel, outs, smem, vmem, scratch=()):
    vm = pl.BlockSpec(memory_space=pltpu.VMEM)
    sm = pl.BlockSpec(memory_space=pltpu.SMEM)
    return pl.pallas_call(
        kernel,
        out_shape=[jax.ShapeDtypeStruct(shape, F32) for shape in outs],
        in_specs=[sm] * len(smem) + [vm] * len(vmem),
        out_specs=[vm] * len(outs),
        scratch_shapes=[pltpu.VMEM(shape, F32) for shape in scratch],
        compiler_params=pltpu.CompilerParams(vmem_limit_bytes=48 * 1024 * 1024),
    )(*smem, *vmem)


def shifted(x, axis, by):
    count = lax.axis_size(axis)
    return lax.ppermute(x, axis, [(i, (i + by) % count) for i in range(count)])


def around(x, by):
    order = [2 * g for g in range(G)] + [2 * g + 1 for g in reversed(range(G))]
    pairs = [(order[i], order[(i + by) % len(order)]) for i in range(len(order))]
    return lax.ppermute(x, ("gx", "pa"), pairs)


def chebyshev_scalars(upper):
    theta = 0.5 * (upper + 1.0)
    delta = 0.5 * (upper - 1.0)
    sigma = theta / delta
    rho = 1.0 / sigma
    rows = [(1.0 / theta, 0.0 * theta)]
    for _ in range(1, CHEB):
        rho_next = 1.0 / (2.0 * sigma - rho)
        rows.append((rho_next * rho, 2.0 * rho_next / delta))
        rho = rho_next
    return jnp.stack([jnp.stack(row) for row in rows])


def redistributed(conductivity, stored_state, row_scales, cotangent, upper_bound):
    g = lax.axis_index("gx")
    pa = lax.axis_index("pa")

    def strip_of(device):
        return jnp.where(pa == 0, device, G - 1 - device)

    steps = jnp.arange(G, dtype=jnp.int32)
    ahead = lax.rem(g + steps, G)
    behind = lax.rem(g - steps + G, G)
    scalars = chebyshev_scalars(upper_bound[0])
    stored = shifted(stored_state, "pa", 1)
    scales = row_scales[:, :, None]

    kdown = shifted(conductivity[BX - 1], "gx", 1)
    kup = shifted(conductivity[0], "gx", -1)
    kover = shifted(conductivity[:, BY - 1], "gy", 1)
    kunder = shifted(conductivity[:, 0], "gy", -1)
    kends = shifted(jnp.stack((conductivity[:, :, BZ - 1], conductivity[:, :, 0])), "pa", 1)

    brick = (3, 2, BY, LANES)
    parts = call(pack_kernel, [brick] * G, [strip_of(ahead)], [conductivity, stored, scales, cotangent])
    parts = [parts[0]] + [shifted(parts[d], "gx", d) for d in range(1, G)]
    edge = (3, G, BY, LANES)
    left, right = call(edge_kernel, [edge] * 2, [behind], parts)
    from_right, from_left = around(left, -1), around(right, 1)
    whole, head, tail = call(
        build_kernel,
        [(3, NXL, BY, LANES), (3, NXL, HALO, LANES), (3, NXL, HALO, LANES)],
        [behind],
        [*parts, from_left, from_right],
    )
    below, above = shifted(head, "gy", -1), shifted(tail, "gy", 1)
    field = (NXL, ROWS, LANES)
    solved = call(
        solve_kernel,
        [(2, 3, MROWS, LANES)] * G,
        [ahead, scalars],
        [whole, above, below],
        [(2, 2) + field, (2,) + field] + [field] * 5,
    )
    solved = [solved[0]] + [shifted(solved[d], "gx", d) for d in range(1, G)]
    out = (BX, BY, LANES)
    padded = (BX + 2, BY + 16, LANES)
    return call(
        final_kernel,
        [out, out, out, (2,) + out],
        [strip_of(behind)],
        [*solved, conductivity, kdown, kup, kover, kunder, kends[0][:, :, None], kends[1][:, :, None], stored, scales, cotangent],
        [(2,) + padded, (2, G, BY, LANES), padded],
    )


def body(conductivity, stored_state, row_scales, cotangent, upper_bound):
    strips_fit = (
        lax.axis_size("gx") == G
        and lax.axis_size("pa") == 2
        and conductivity.shape == (BX, BY, BZ)
    )
    run = redistributed if strips_fit else stepwise
    return tuple(run(conductivity, stored_state, row_scales, cotangent, upper_bound))


def solution(mesh):
    return jax.shard_map(
        body,
        mesh=mesh,
        in_specs=(
            P("gx", "gy", "pa"),
            P("gx", "gy", "pa"),
            P("gx", "gy"),
            P("gx", "gy", "pa"),
            P(),
        ),
        out_specs=(
            P("gx", "gy", "pa"),
            P("gx", "gy", "pa"),
            P("gx", "gy", "pa"),
            P(None, "gx", "gy", "pa"),
        ),
        check_vma=False,
    )
```

time: 756 us -> 405 us (0.54)
  Pallas kernels: 0 us -> 278 us
  other arithmetic: 187 us -> 0.65 us
  waiting for transfers between devices: 272 us -> 90.5 us
  starting transfers between devices: 188 us -> 18.5 us
  local copies, waits for them, and re-layouts: 97.9 us -> 12.6 us
    pallas_call x0 -> x5, Pallas kernels: none -> 278 us  [call(): pl.pallas_call(kernel, out_shape=[jax.ShapeDtypeStruct(shape, F32) for sh...]
    ppermute x205 -> x16, waiting for transfers between devices: 272 us -> 90.5 us  [the longest x14 75.2 us: shifted(): return lax.ppermute(x, axis, [(i, (i + by) % count) for i in range(count)])]
    ppermute x205 -> x16, starting transfers between devices: 188 us -> 18.5 us  [the longest x14 16.4 us: shifted(): return lax.ppermute(x, axis, [(i, (i + by) % count) for i in range(count)])]
    add x33 -> x0, other arithmetic: 118 us -> none  [the longest x32 116 us: sweep(): rho_next * rho_now * direction + 2.0 * rho_next / delta * residual]
    slice x168 -> x2, local copies, waits for them, and re-layouts: 39.5 us -> 1.12 us  [the longest x1 1.11 us: redistributed(): conductivity[:, :, BZ - 1]]
    while x128 -> x0, local copies, waits for them, and re-layouts: 34.6 us -> none
    while x32 -> x0, other arithmetic: 32.5 us -> none
    ppermute x68 -> x0, local copies, waits for them, and re-layouts: 21.7 us -> none  [the longest x34 10.8 us: with_halo(): lax.ppermute(head, axis, [((i + 1) % count, i) for i in range(count)])]
  transfers between devices with their start and end apart: 205 -> 16, of which waited for: 183 -> 10; matrix products, arithmetic and copies ran while one was open for 10% -> 2% of each run, Pallas kernels for 0% -> 67%
where the time goes in v1:
time: 405 us; the launch traced here: 403 us
  Pallas kernels  278 us (69%)
  waiting for transfers between devices  90.5 us (22%)
  starting transfers between devices  18.5 us (5%)
  local copies, waits for them, and re-layouts  12.6 us (3%)
    pallas_call x5, Pallas kernels, call(): pl.pallas_call(kernel, out_shape=[jax.ShapeDtypeStruct(shape, F32) for sh...  278 us
    ppermute x14, waiting for transfers between devices, shifted(): return lax.ppermute(x, axis, [(i, (i + by) % count) for i in range(count)])  75.2 us
    ppermute x14, starting transfers between devices, shifted(): return lax.ppermute(x, axis, [(i, (i + by) % count) for i in range(count)])  16.4 us
    ppermute x2, waiting for transfers between devices, around(): return lax.ppermute(x, ('gx', 'pa'), pairs)  15.3 us
    unnamed x20, local copies, waits for them, and re-layouts  9.41 us
  transfers between devices with their start and end apart: 16, of which 10 were waited for; matrix products, arithmetic and copies ran while one was open for 2% of the time, Pallas kernels for 67%

profile of v1, /device:TPU:8, one launch (start us, length us, event | category | flops | bytes accessed | tf_op | source)
XLA Modules:
  0.0 403.1 jit_solution(7781793565552631067)
XLA Ops:
  0.6 1.6 collective-permute-start
  3.1 5.8 %collective-permute-done.stored = bf16[8,128,128]{2,1,0:T(8,128)(2,1)S(1)} collective-permute-done((bf16[8,128,128]{2,1,0:T(8,128)(2,1)}, bf16[8,128,128]{2,1,0:T(8,128)(2,1)S(1)}, u32[]{:S(2)}, u32[]{:S(2)}) %collective-permute-start) | collective-permute-done | bytes 262176 | tf_op jit(solution)/shard_map/ppermute | solution.py:396
  11.0 2.8 shard_map.84
  13.9 1.6 collective-permute-start.1
  16.5 2.0 collective-permute-start.3
  20.8 1.2 copy.65
  22.1 1.6 collective-permute-start.15
  23.6 18.6 %collective-permute-done.1.refs_1_ = f32[3,2,128,128]{3,2,1,0:T(8,128)S(1)} collective-permute-done((f32[3,2,128,128]{3,2,1,0:T(8,128)}, f32[3,2,128,128]{3,2,1,0:T(8,128)S(1)}, u32[]{:S(2)}, u32[]{:S(2)}) %collective-permute-start.1) | collective-permute-done | bytes 393248 | tf_op jit(solution)/shard_map/ppermute | solution.py:396
  42.2 6.3 %collective-permute-done.2.refs_2_ = f32[3,2,128,128]{3,2,1,0:T(8,128)S(1)} collective-permute-done((f32[3,2,128,128]{3,2,1,0:T(8,128)S(1)}, f32[3,2,128,128]{3,2,1,0:T(8,128)S(1)}, u32[]{:S(2)}, u32[]{:S(2)}) %collective-permute-start.2) | collective-permute-done | bytes 393248 | tf_op jit(solution)/shard_map/ppermute | solution.py:396
  48.4 1.8 collective-permute-done.3.refs_3_
  50.3 2.1 shard_map.85
  52.4 2.0 collective-permute-start.5
  56.8 15.3 %collective-permute-done.4.refs_4_ = f32[3,4,128,128]{3,2,1,0:T(8,128)S(1)} collective-permute-done((f32[3,4,128,128]{3,2,1,0:T(8,128)}, f32[3,4,128,128]{3,2,1,0:T(8,128)S(1)}, u32[]{:S(2)}, u32[]{:S(2)}) %collective-permute-start.4) | collective-permute-done | bytes 786464 | tf_op jit(solution)/shard_map/ppermute | solution.py:402
  74.1 8.1 %shard_map.86 = (f32[3,16,128,128]{3,2,1,0:T(8,128)}, f32[3,16,16,128]{3,2,1,0:T(8,128)}, f32[3,16,16,128]{3,2,1,0:T(8,128)}) custom-call(s32[4]{0:T(128)S(1)} %compare_select_fusion.2.sources, f32[3,2,128,128]{3,2,1,0:T(8,128)S(1)} %get-tuple-element.17.refs_0_, f32[3,2,128,128]{3,2,1,0:T(8,128)S(1)} %collective-permute-done.1.refs_1_, ...), custom_call_target="tpu_custom_call" | custom-call | tf_op jit(solution)/shard_map/pallas_call | solution.py:384
  82.2 1.7 collective-permute-start.7
  84.4 7.6 %collective-permute-done.6.above = f32[3,16,16,128]{3,2,1,0:T(8,128)S(1)} collective-permute-done((f32[3,16,16,128]{3,2,1,0:T(8,128)}, f32[3,16,16,128]{3,2,1,0:T(8,128)S(1)}, u32[]{:S(2)}, u32[]{:S(2)}) %collective-permute-start.6) | collective-permute-done | bytes 393248 | tf_op jit(solution)/shard_map/ppermute | solution.py:396
  92.9 1.9 copy-done.2
  94.8 258.0 %shard_map.87 = (f32[2,3,136,128]{3,2,1,0:T(8,128)S(1)}, f32[2,3,136,128]{3,2,1,0:T(8,128)}, f32[2,3,136,128]{3,2,1,0:T(8,128)}, f32[2,3,136,128]{3,2,1,0:T(8,128)}) custom-call(s32[4]{0:T(128)S(1)} %compare_select_fusion.homes, f32[16,2]{1,0:T(8,128)S(1)} %stack.259.scalars, f32[3,16,128,128]{3,2,1,0:T(8,128)S(1)} %copy-done.2, ...), custom_call_target="tpu_custom_call" | custom-call | tf_op jit(solution)/shard_map/pallas_call | solution.py:384
  354.8 1.9 collective-permute-start.9
  358.3 1.3 collective-permute-done.14.kunder
  360.1 1.5 collective-permute-start.12
  362.1 31.4 %collective-permute-done.11.kdown = f32[128,128]{1,0:T(8,128)S(1)} collective-permute-done((f32[128,128]{1,0:T(8,128)}, f32[128,128]{1,0:T(8,128)S(1)}, u32[]{:S(2)}, u32[]{:S(2)}) %collective-permute-start.11) | collective-permute-done | bytes 65568 | tf_op jit(solution)/shard_map/ppermute | solution.py:396
  393.5 1.6 collective-permute-done.12.kup
  396.0 7.1 %shard_map.88 = (f32[8,128,128]{2,1,0:T(8,128)}, f32[8,128,128]{2,1,0:T(8,128)}, f32[8,128,128]{2,1,0:T(8,128)}, f32[2,8,128,128]{3,2,1,0:T(8,128)}) custom-call(s32[4]{0:T(128)S(1)} %broadcast_select_fusion.1.strips, f32[2,3,136,128]{3,2,1,0:T(8,128)S(1)} %get-tuple-element.26.m0, f32[2,3,136,128]{3,2,1,0:T(8,128)} %collective-permute-done.8.m1, ...), custom_call_target="tpu_custom_call" | custom-call | tf_op jit(solution)/shard_map/pallas_call | solution.py:384
  (54 shorter events, 15.6 us)
Async XLA Ops:
  0.6 8.3 %collective-permute-start = (bf16[8,128,128]{2,1,0:T(8,128)(2,1)}, bf16[8,128,128]{2,1,0:T(8,128)(2,1)S(1)}, u32[]{:S(2)}, u32[]{:S(2)}) collective-permute-start(bf16[8,128,128]{2,1,0:T(8,128)(2,1)} %param.6), channel_id=1, source_target_pairs={{0,1},{1,0},{2,3},{3,2},{4,5},{5,4},{6,7},{7,6},{8,9},{9,8},{10,11... | collective-permute-start | bytes 786440 | tf_op jit(solution)/shard_map/ppermute | solution.py:396
  9.0 1.0 copy-start
  10.0 1.0 copy-start.3
  11.0 2.8 copy-start.5
  11.0 43.4 %copy-start.1 = (f32[8,128,128]{2,1,0:T(8,128)S(1)}, f32[8,128,128]{2,1,0:T(8,128)}, u32[]{:S(2)}) copy-start(f32[8,128,128]{2,1,0:T(8,128)} %cond.3) | copy-start | bytes 1572868
  13.9 28.3 %collective-permute-start.1 = (f32[3,2,128,128]{3,2,1,0:T(8,128)}, f32[3,2,128,128]{3,2,1,0:T(8,128)S(1)}, u32[]{:S(2)}, u32[]{:S(2)}) collective-permute-start(f32[3,2,128,128]{3,2,1,0:T(8,128)} %get-tuple-element.18), channel_id=1, source_target_pairs={{0,8},{8,16},{16,24},{24,0},{1,9},{9,17},{17,25},{25,1},{2,10},{10... | collective-permute-start | bytes 1179656 | tf_op jit(solution)/shard_map/ppermute | solution.py:396
  15.5 33.0 %collective-permute-start.2 = (f32[3,2,128,128]{3,2,1,0:T(8,128)S(1)}, f32[3,2,128,128]{3,2,1,0:T(8,128)S(1)}, u32[]{:S(2)}, u32[]{:S(2)}) collective-permute-start(f32[3,2,128,128]{3,2,1,0:T(8,128)S(1)} %get-tuple-element.19), channel_id=1, source_target_pairs={{0,16},{8,24},{16,0},{24,8},{1,17},{9,25},{17,1},{25,9},{2,18},{10... | collective-permute-start | bytes 1179656 | tf_op jit(solution)/shard_map/ppermute | solution.py:396
  16.5 33.8 %collective-permute-start.3 = (f32[3,2,128,128]{3,2,1,0:T(8,128)S(1)}, f32[3,2,128,128]{3,2,1,0:T(8,128)S(1)}, u32[]{:S(2)}, u32[]{:S(2)}) collective-permute-start(f32[3,2,128,128]{3,2,1,0:T(8,128)S(1)} %get-tuple-element.20), channel_id=1, source_target_pairs={{0,24},{8,0},{16,8},{24,16},{1,25},{9,1},{17,9},{25,17},{2,26},{10... | collective-permute-start | bytes 1179656 | tf_op jit(solution)/shard_map/ppermute | solution.py:396
  22.1 338.1 %collective-permute-start.15 = (f32[2,8,128]{2,1,0:T(8,128)S(1)}, f32[2,8,128]{2,1,0:T(8,128)S(1)}, u32[]{:S(2)}, u32[]{:S(2)}) collective-permute-start(f32[2,8,128]{2,1,0:T(8,128)S(1)} %pad_maximum_fusion), channel_id=1, source_target_pairs={{0,1},{1,0},{2,3},{3,2},{4,5},{5,4},{6,7},{7,6},{8,9},{9,8},{10,11... | collective-permute-start | bytes 24584 | tf_op jit(solution)/shard_map/ppermute | solution.py:396
  52.4 19.7 %collective-permute-start.4 = (f32[3,4,128,128]{3,2,1,0:T(8,128)}, f32[3,4,128,128]{3,2,1,0:T(8,128)S(1)}, u32[]{:S(2)}, u32[]{:S(2)}) collective-permute-start(f32[3,4,128,128]{3,2,1,0:T(8,128)} %get-tuple-element.21), channel_id=1, source_target_pairs={{0,8},{8,16},{16,24},{24,25},{25,17},{17,9},{9,1},{1,0},{2,10},{10... | collective-permute-start | bytes 2359304 | tf_op jit(solution)/shard_map/ppermute | solution.py:402
  52.4 20.6 %collective-permute-start.5 = (f32[3,4,128,128]{3,2,1,0:T(8,128)}, f32[3,4,128,128]{3,2,1,0:T(8,128)}, u32[]{:S(2)}, u32[]{:S(2)}) collective-permute-start(f32[3,4,128,128]{3,2,1,0:T(8,128)} %get-tuple-element.22), channel_id=1, source_target_pairs={{0,1},{8,0},{16,8},{24,16},{25,24},{17,25},{9,17},{1,9},{2,3},{10,... | collective-permute-start | bytes 2359304 | tf_op jit(solution)/shard_map/ppermute | solution.py:402
  54.5 302.8 %collective-permute-start.13 = (f32[8,128]{1,0:T(8,128)S(1)}, f32[8,128]{1,0:T(8,128)S(1)}, u32[]{:S(2)}, u32[]{:S(2)}) collective-permute-start(f32[8,128]{1,0:T(8,128)S(1)} %bitcast.86), channel_id=1, source_target_pairs={{0,2},{2,4},{4,6},{6,0},{1,3},{3,5},{5,7},{7,1},{8,10},{10,12},{12... | collective-permute-start | bytes 12296 | tf_op jit(solution)/shard_map/ppermute | solution.py:396
  73.0 1.1 copy-start.8
  74.1 320.9 %copy-start.4 = (f32[8,128,128]{2,1,0:T(8,128)S(1)}, f32[8,128,128]{2,1,0:T(8,128)}, u32[]{:S(2)}) copy-start(f32[8,128,128]{2,1,0:T(8,128)} %cot.3) | copy-start | bytes 1572868
  82.2 9.8 %collective-permute-start.6 = (f32[3,16,16,128]{3,2,1,0:T(8,128)}, f32[3,16,16,128]{3,2,1,0:T(8,128)S(1)}, u32[]{:S(2)}, u32[]{:S(2)}) collective-permute-start(f32[3,16,16,128]{3,2,1,0:T(8,128)} %get-tuple-element.24), channel_id=1, source_target_pairs={{0,2},{2,4},{4,6},{6,0},{1,3},{3,5},{5,7},{7,1},{8,10},{10,12},{12... | collective-permute-start | bytes 1179656 | tf_op jit(solution)/shard_map/ppermute | solution.py:396
  82.2 10.7 %collective-permute-start.7 = (f32[3,16,16,128]{3,2,1,0:T(8,128)}, f32[3,16,16,128]{3,2,1,0:T(8,128)S(1)}, u32[]{:S(2)}, u32[]{:S(2)}) collective-permute-start(f32[3,16,16,128]{3,2,1,0:T(8,128)} %get-tuple-element.25), channel_id=1, source_target_pairs={{0,6},{2,0},{4,2},{6,4},{1,7},{3,1},{5,3},{7,5},{8,14},{10,8},{12,... | collective-permute-start | bytes 1179656 | tf_op jit(solution)/shard_map/ppermute | solution.py:396
  92.9 1.9 copy-start.2
  352.8 42.3 %collective-permute-start.10 = (f32[2,3,136,128]{3,2,1,0:T(8,128)}, f32[2,3,136,128]{3,2,1,0:T(8,128)S(1)}, u32[]{:S(2)}, u32[]{:S(2)}) collective-permute-start(f32[2,3,136,128]{3,2,1,0:T(8,128)} %get-tuple-element.29), channel_id=1, source_target_pairs={{0,24},{8,0},{16,8},{24,16},{1,25},{9,1},{17,9},{25,17},{2,26},{10... | collective-permute-start | bytes 1253384 | tf_op jit(solution)/shard_map/ppermute | solution.py:396
  353.7 41.3 %collective-permute-start.8 = (f32[2,3,136,128]{3,2,1,0:T(8,128)}, f32[2,3,136,128]{3,2,1,0:T(8,128)}, u32[]{:S(2)}, u32[]{:S(2)}) collective-permute-start(f32[2,3,136,128]{3,2,1,0:T(8,128)} %get-tuple-element.27), channel_id=1, source_target_pairs={{0,8},{8,16},{16,24},{24,0},{1,9},{9,17},{17,25},{25,1},{2,10},{10... | collective-permute-start | bytes 1253384 | tf_op jit(solution)/shard_map/ppermute | solution.py:396
  354.8 40.3 %collective-permute-start.9 = (f32[2,3,136,128]{3,2,1,0:T(8,128)}, f32[2,3,136,128]{3,2,1,0:T(8,128)}, u32[]{:S(2)}, u32[]{:S(2)}) collective-permute-start(f32[2,3,136,128]{3,2,1,0:T(8,128)} %get-tuple-element.28), channel_id=1, source_target_pairs={{0,16},{8,24},{16,0},{24,8},{1,17},{9,25},{17,1},{25,9},{2,18},{10... | collective-permute-start | bytes 1253384 | tf_op jit(solution)/shard_map/ppermute | solution.py:396
  357.3 2.3 collective-permute-start.14
  359.6 33.9 %collective-permute-start.11 = (f32[128,128]{1,0:T(8,128)}, f32[128,128]{1,0:T(8,128)S(1)}, u32[]{:S(2)}, u32[]{:S(2)}) collective-permute-start(f32[128,128]{1,0:T(8,128)} %get-tuple-element.35), channel_id=1, source_target_pairs={{0,8},{8,16},{16,24},{24,0},{1,9},{9,17},{17,25},{25,1},{2,10},{10... | collective-permute-start | bytes 196616 | tf_op jit(solution)/shard_map/ppermute | solution.py:396
  360.1 34.9 %collective-permute-start.12 = (f32[128,128]{1,0:T(8,128)}, f32[128,128]{1,0:T(8,128)}, u32[]{:S(2)}, u32[]{:S(2)}) collective-permute-start(f32[128,128]{1,0:T(8,128)} %get-tuple-element.34), channel_id=1, source_target_pairs={{0,24},{8,0},{16,8},{24,16},{1,25},{9,1},{17,9},{25,17},{2,26},{10... | collective-permute-start | bytes 196616 | tf_op jit(solution)/shard_map/ppermute | solution.py:396
  395.1 1.0 copy-start.6
  (1 other events, 0.9 us)

commit v2 on v0

v2 whole, which is shorter than its diff:
```python
import functools

import jax
import jax.numpy as jnp
from jax import lax
from jax.experimental import pallas as pl
from jax.experimental.pallas import tpu as pltpu
from jax.sharding import PartitionSpec as P

CHEB = 16
LANES = 128
HALO = CHEB
TIME_STEP = 8.0
F32 = jnp.float32


def with_halo(cells, sides, width):
    for axis, dim in sides:
        count = lax.axis_size(axis)
        head = lax.slice_in_dim(cells, 0, width, axis=dim)
        tail = lax.slice_in_dim(cells, cells.shape[dim] - width, cells.shape[dim], axis=dim)
        cells = jnp.concatenate(
            [
                lax.ppermute(tail, axis, [(i, (i + 1) % count) for i in range(count)]),
                cells,
                lax.ppermute(head, axis, [((i + 1) % count, i) for i in range(count)]),
            ],
            axis=dim,
        )
    return cells


def region(arr, spatial, offset):
    extent = arr.shape[-3:]
    window = [slice(1, length - 1) for length in extent]
    window[spatial] = slice(offset, extent[spatial] - 2 + offset)
    leading = [slice(None)] * (arr.ndim - 3)
    return arr[tuple(leading + window)]


def apply_operator(padded, kpad):
    centre = region(padded, 0, 1)
    kcentre = region(kpad, 0, 1)
    summed = jnp.zeros_like(centre)
    for spatial in range(3):
        for offset in (0, 2):
            summed = summed + 0.5 * (kcentre + region(kpad, spatial, offset)) * (
                centre - region(padded, spatial, offset)
            )
    return centre + TIME_STEP * summed


def stepwise(conductivity, stored_state, row_scales, cotangent, upper_bound):
    upper = upper_bound[0]
    kpad = with_halo(conductivity, (("gx", 0), ("gy", 1), ("pa", 2)), 1)
    count = lax.axis_size("pa")
    partner = lax.ppermute(stored_state, "pa", [(i, (i + count // 2) % count) for i in range(count)])
    previous = partner.astype(F32) * row_scales[:, :, None]
    rhs = jnp.stack((previous, cotangent))
    theta = 0.5 * (upper + 1.0)
    delta = 0.5 * (upper - 1.0)
    sigma = theta / delta
    sides = (("gx", 1), ("gy", 2), ("pa", 3))

    def sweep(step, carry):
        solved, residual, direction, rho = carry
        padded = with_halo(direction, sides, 1)
        solved = solved + direction
        residual = residual - apply_operator(padded, kpad)
        rho_next = 1.0 / (2.0 * sigma - rho)
        direction = rho_next * rho * direction + 2.0 * rho_next / delta * residual
        return (solved, residual, direction, rho_next)

    start = (jnp.zeros_like(rhs), rhs, rhs / theta, 1.0 / sigma)
    solved, residual, _, _ = lax.fori_loop(0, CHEB, sweep, start)
    pair = with_halo(solved, sides, 1)
    centre = region(pair, 0, 1)
    summed = jnp.zeros_like(solved[0])
    for spatial in range(3):
        for offset in (0, 2):
            differ = centre - region(pair, spatial, offset)
            summed = summed + differ[0] * differ[1]
    return (-0.5 * TIME_STEP * summed, solved[1], solved[0], residual)


G = 4
BX = 8
BY = 128
BZ = 128
STRIP = BZ // G
NXL = G * BX // 2
TOP = 8 + HALO
ROWS = BY + 2 * TOP
MROWS = BY + 8
TILE = 8

FIRST = (0, 8, 0, 8)
HALF = (0, 1, 1, 0)


def roll(x, by):
    by %= LANES
    return pltpu.roll(x, by, 1) if by else x


def group_of(rows, strip):
    lane = lax.broadcasted_iota(jnp.int32, (rows, LANES), 1)
    return lax.rem(lane // STRIP - strip + G, G)


def pick(group, parts):
    out = parts[0]
    for b in range(1, G):
        out = jnp.where(group == b, parts[b], out)
    return out


def pack_kernel(strips, cond, stored, scales, cot, *outs):
    groups = [group_of(BY, strips[d]) for d in range(G)]
    for a in range(2):
        for n in range(3):
            parts = []
            for b in range(4):
                c = 4 * a + b
                if n == 1:
                    plane = stored[c].astype(F32) * scales[c]
                else:
                    plane = (cond if n == 0 else cot)[c]
                parts.append(roll(plane, 32 * b))
            for d in range(G):
                outs[d][n, a] = pick(groups[d], parts)


def edge_kernel(places, *refs):
    msgs, (to_left, to_right, head, tail) = refs[:G], refs[G:]
    lane = lax.broadcasted_iota(jnp.int32, (BY, LANES), 1)
    low = lax.rem(lane, STRIP) < STRIP // 2
    for n in range(3):
        for d in range(G):
            first, second = msgs[d][n, 0], msgs[d][n, 1]
            to_left[n, places[0, d]] = jnp.where(low, first, roll(second, 16))
            to_right[n, places[1, d]] = jnp.where(low, roll(second, -16), first)
            for a in range(2):
                head[n, d, a] = msgs[d][n, a, :HALO]
                tail[n, d, a] = msgs[d][n, a, BY - HALO :]


def unpack(get_brick, get_edge, group, low, put):
    for first, da, db in ((0, 0, 2), (8, 3, 1)):
        ra, rb = get_edge(1, da), get_edge(1, db)
        la, lb = get_edge(0, da), get_edge(0, db)
        for a in range(2):
            if a == 0:
                x = jnp.where(low, ra, roll(lb, 64))
                y = jnp.where(low, roll(rb, 64), la)
            else:
                x = jnp.where(low, roll(ra, -16), roll(lb, 80))
                y = jnp.where(low, roll(rb, 48), roll(la, 16))
            own, other = get_brick(da, a), roll(get_brick(db, a), 64)
            for b in range(4):
                parts = (own, x, other, y)
                whole = pick(group, [parts[(q - b) % 4] for q in range(4)])
                put(first + 4 * a + b, roll(whole, -32 * b))


def solve_kernel(strip, scalars, b0, b1, b2, b3, from_left, from_right, above, above_edge, below, below_edge, *refs):
    nf = 2
    bricks = (b0, b1, b2, b3)
    outs = refs[:G]
    refs = refs[G:]
    xa, xb, xc, rhs, stage_a, stage_b = (refs[nf * j : nf * (j + 1)] for j in range(6))
    kap, kx, ky, kz, diag = refs[6 * nf :]
    zero = jnp.zeros((TILE, LANES), F32)
    lane = lax.broadcasted_iota(jnp.int32, (TILE, LANES), 1)
    group = group_of(TILE, strip[0])
    low = lax.rem(lane, STRIP) < STRIP // 2
    targets = (kap, rhs[0], rhs[1])

    @pl.loop(0, BY // TILE)
    def _(t):
        r = pl.multiple_of(TILE * t, TILE)
        to = pl.multiple_of(TOP + TILE * t, TILE)
        edges = (from_left, from_right)
        for n, dst in enumerate(targets):

            def put(i, val):
                dst[i, pl.ds(to, TILE)] = val

            unpack(
                lambda d, a: bricks[d][n, a, pl.ds(r, TILE)],
                lambda side, d: edges[side][n, d, pl.ds(r, TILE)],
                group,
                low,
                put,
            )

    @pl.loop(0, HALO // TILE)
    def _(t):
        r = pl.multiple_of(TILE * t, TILE)
        for brick, edge, start in ((above, above_edge, TOP - HALO), (below, below_edge, TOP + BY)):
            to = pl.multiple_of(start + TILE * t, TILE)
            for n, dst in enumerate(targets):

                def put(i, val):
                    dst[i, pl.ds(to, TILE)] = val

                unpack(
                    lambda d, a: brick[n, d, a, pl.ds(r, TILE)],
                    lambda side, d: edge[side, n, d, pl.ds(r, TILE)],
                    group,
                    low,
                    put,
                )

    for i in range(NXL):
        for dst in (kap, ky, kz) + tuple(rhs) + tuple(xa) + tuple(xb) + tuple(xc):
            dst[i, 0:TILE] = zero
            dst[i, ROWS - TILE : ROWS] = zero

    @pl.loop(0, ROWS // TILE - 2)
    def _(t):
        r = pl.multiple_of(TILE + TILE * t, TILE)
        now = kap[0, pl.ds(r, TILE)]
        wrapped = roll(now, 64)
        for i in range(NXL):
            after = kap[i + 1, pl.ds(r, TILE)] if i + 1 < NXL else wrapped
            kx[i, pl.ds(r, TILE)] = 4.0 * (now + after)
            ky[i, pl.ds(r, TILE)] = 4.0 * (now + kap[i, pl.ds(r + 1, TILE)])
            kz[i, pl.ds(r, TILE)] = 4.0 * (now + roll(now, -1))
            now = after

    theta_inv = scalars[0, 0]

    @pl.loop(0, ROWS // TILE - 2)
    def _(t):
        r = pl.multiple_of(TILE + TILE * t, TILE)
        before = roll(kx[NXL - 1, pl.ds(r, TILE)], 64)
        for i in range(NXL):
            fx = kx[i, pl.ds(r, TILE)]
            fz = kz[i, pl.ds(r, TILE)]
            total = fx + before + ky[i, pl.ds(r, TILE)] + ky[i, pl.ds(r - 1, TILE)]
            diag[i, pl.ds(r, TILE)] = 1.0 + (total + (fz + roll(fz, 1)))
            before = fx
            for f in range(nf):
                xb[f][i, pl.ds(r, TILE)] = rhs[f][i, pl.ds(r, TILE)] * theta_inv
                xa[f][i, pl.ds(r, TILE)] = zero

    def along_lanes(cur, stage, r):
        for i in range(NXL):
            fz = kz[i, pl.ds(r, TILE)]
            for f in range(nf):
                x = cur[f][i, pl.ds(r, TILE)]
                stage[f][i] = (fz * roll(x, -1) + roll(fz * x, 1)) + rhs[f][i, pl.ds(r, TILE)]

    def advance(alpha, beta, old, cur, new, stage, r):
        now = [cur[f][0, pl.ds(r, TILE)] for f in range(nf)]
        wrapped = [roll(x, 64) for x in now]
        before = [roll(cur[f][NXL - 1, pl.ds(r, TILE)], 64) for f in range(nf)]
        fbefore = roll(kx[NXL - 1, pl.ds(r, TILE)], 64)
        for i in range(NXL):
            fx = kx[i, pl.ds(r, TILE)]
            fy = ky[i, pl.ds(r, TILE)]
            fym = ky[i, pl.ds(r - 1, TILE)]
            centre = (1.0 + alpha) - beta * diag[i, pl.ds(r, TILE)]
            for f in range(nf):
                x = now[f]
                after = cur[f][i + 1, pl.ds(r, TILE)] if i + 1 < NXL else wrapped[f]
                near = fx * after + fbefore * before[f]
                near = near + (fy * cur[f][i, pl.ds(r + 1, TILE)] + fym * cur[f][i, pl.ds(r - 1, TILE)])
                near = near + stage[f][i]
                new[f][i, pl.ds(r, TILE)] = centre * x - alpha * old[f][i, pl.ds(r, TILE)] + beta * near
                before[f] = x
                now[f] = after
            fbefore = fx

    def sweep(k, old, cur, new, span):
        alpha, beta = scalars[k, 0], scalars[k, 1]
        along_lanes(cur, stage_a, span[0])

        @pl.loop(0, span[1] // 2)
        def _(t):
            r = pl.multiple_of(span[0] + 2 * TILE * t, TILE)
            along_lanes(cur, stage_b, r + TILE)
            advance(alpha, beta, old, cur, new, stage_a, r)
            along_lanes(cur, stage_a, r + 2 * TILE)
            advance(alpha, beta, old, cur, new, stage_b, r + TILE)

    def three(k, spans):
        sweep(k, xa, xb, xc, spans[0])
        sweep(k + 1, xb, xc, xa, spans[1])
        sweep(k + 2, xc, xa, xb, spans[2])

    wide = (TILE, ROWS // TILE - 2)
    narrow = (2 * TILE, ROWS // TILE - 4)

    @pl.loop(0, 2)
    def _(m):
        three(1 + 3 * m, (wide,) * 3)

    three(7, (wide, narrow, narrow))

    @pl.loop(0, 2)
    def _(m):
        three(10 + 3 * m, (narrow,) * 3)

    sub = lax.broadcasted_iota(jnp.int32, (TILE, LANES), 0)
    inner = lax.rem(lax.rem(lane - STRIP * strip[0] + 2 * LANES, LANES) + 1, 64)

    def near_edge(width):
        return (inner < width) | ((inner >= 33) & (inner < 33 + width))

    masks = [near_edge(1), near_edge(2), near_edge(4)]

    def main_rows(f, first, row):
        rolled = [roll(xb[f][first + c, pl.ds(row, TILE)], 32 * (c % 4)) for c in range(BX)]
        out = []
        for h in range(2):
            out.append([pick(group, [rolled[4 * a + (q - 2 * h) % 4] for q in range(4)]) for a in range(2)])
        return out

    def side_rows(f, pair, first, row):
        tree = [xb[f][first + c, pl.ds(row, TILE)] for c in range(BX)]
        for level in range(3):
            tree = [
                jnp.where(masks[level], tree[j], roll(tree[j + 1], 1 << level)) for j in range(0, len(tree), 2)
            ]
        ends = roll(tree[0], 1)
        out = []
        for h in range(2):
            d = pair + 2 * h
            down, up = (BX * d + 31) % 32, (BX * d + 8) % 32
            down = roll(xb[f][down % NXL, pl.ds(row, TILE)], 64 * (h + 1 - down // NXL))
            up = roll(xb[f][up % NXL, pl.ds(row, TILE)], 96 + 64 * (h - up // NXL))
            parts = (ends, ends, down, up)
            out.append(pick(group, [parts[(q - 2 * h) % 4] for q in range(4)]))
        return out

    for f in range(nf):
        for pair in range(2):
            first = 8 * pair

            @pl.loop(0, BY // TILE)
            def _(t):
                row = pl.multiple_of(TOP + TILE * t, TILE)
                to = pl.ds(pl.multiple_of(TILE * t, TILE), TILE)
                mains = main_rows(f, first, row)
                sides = side_rows(f, pair, first, row)
                for h in range(2):
                    for a in range(2):
                        outs[pair + 2 * h][f, a, to] = mains[h][a]
                    outs[pair + 2 * h][f, 2, to] = sides[h]

            over = main_rows(f, first, TOP - TILE)
            under = main_rows(f, first, TOP + BY)
            for h in range(2):
                for a in range(2):
                    outs[pair + 2 * h][f, a, BY:MROWS] = jnp.where(
                        sub == 0, pltpu.roll(over[h][a], 1, 0), pltpu.roll(under[h][a], 1, 0)
                    )
                outs[pair + 2 * h][f, 2, BY:MROWS] = zero


def final_kernel(strips, m0, m1, m2, m3, cond, kdown, kup, kover, kunder, kzl, kzr, stored, scales, cot, grad, adjoint, state, residuals, xs, ends, kap):
    msgs = (m0, m1, m2, m3)
    lane = lax.broadcasted_iota(jnp.int32, (TILE, LANES), 1)
    owner = [[group_of(TILE, strips[d] + b) == 0 for b in range(4)] for d in range(G)]

    def choose(parts, b):
        out = parts[0]
        for d in range(1, G):
            out = jnp.where(owner[d][b], parts[d], out)
        return out

    def bricks(f, a, row):
        return [roll(msgs[d][f, a, pl.ds(row, TILE)], -64 * (d // 2)) for d in range(G)]

    for f in range(2):

        @pl.loop(0, BY // TILE)
        def _(t):
            row = pl.multiple_of(TILE * t, TILE)
            to = pl.ds(pl.multiple_of(TILE + TILE * t, TILE), TILE)
            for a in range(2):
                parts = bricks(f, a, row)
                for b in range(4):
                    xs[f, 1 + 4 * a + b, to] = roll(choose(parts, b), -32 * b)
            parts = bricks(f, 2, row)
            for d in range(G):
                ends[f, strips[d], pl.ds(row, TILE)] = parts[d]
            xs[f, 0, to] = roll(choose(parts, 2), -64)
            xs[f, 1 + BX, to] = roll(choose(parts, 3), -96)

        for a in range(2):
            parts = bricks(f, a, BY)
            for b in range(4):
                val = pltpu.roll(roll(choose(parts, b), -32 * b), 7, 0)
                xs[f, 1 + 4 * a + b, 0:TILE] = val
                xs[f, 1 + 4 * a + b, TILE + BY : 2 * TILE + BY] = val
    kap[0, TILE : TILE + BY] = kdown[...]
    kap[1 + BX, TILE : TILE + BY] = kup[...]
    for c in range(BX):
        kap[1 + c, TILE : TILE + BY] = cond[c]
        kap[1 + c, 0:TILE] = jnp.broadcast_to(kover[c : c + 1], (TILE, LANES))
        kap[1 + c, TILE + BY : 2 * TILE + BY] = jnp.broadcast_to(kunder[c : c + 1], (TILE, LANES))

    @pl.loop(0, BY // TILE)
    def _(t):
        r = pl.multiple_of(TILE * t, TILE)
        r8 = pl.multiple_of(TILE * t + TILE, TILE)
        at_r = pl.ds(r, TILE)
        low = [ends[f, 0, at_r] for f in range(2)]
        high = [ends[f, G - 1, at_r] for f in range(2)]
        for c in range(BX):
            k = kap[1 + c, pl.ds(r8, TILE)]
            x = [xs[f, 1 + c, pl.ds(r8, TILE)] for f in range(2)]
            total = [0.0, 0.0]
            product = 0.0

            def sides():
                for at in (c, c + 2):
                    yield kap[at, pl.ds(r8, TILE)], [xs[f, at, pl.ds(r8, TILE)] for f in range(2)]
                for off in (-1, 1):
                    yield kap[1 + c, pl.ds(r8 + off, TILE)], [xs[f, 1 + c, pl.ds(r8 + off, TILE)] for f in range(2)]
                yield (
                    jnp.where(lane == 0, kzl[c, at_r], roll(k, 1)),
                    [jnp.where(lane == 0, roll(low[f], -c), roll(x[f], 1)) for f in range(2)],
                )
                yield (
                    jnp.where(lane == LANES - 1, kzr[c, at_r], roll(k, -1)),
                    [jnp.where(lane == LANES - 1, roll(high[f], 126 - c), roll(x[f], -1)) for f in range(2)],
                )

            for kn, xn in sides():
                face = k + kn
                differ = [x[f] - xn[f] for f in range(2)]
                product = product + differ[0] * differ[1]
                for f in range(2):
                    total[f] = total[f] + face * differ[f]
            grad[c, at_r] = (-0.5 * TIME_STEP) * product
            state[c, at_r] = x[0]
            adjoint[c, at_r] = x[1]
            previous = stored[c, pl.ds(r, TILE)].astype(F32) * scales[c, at_r]
            residuals[0, c, at_r] = previous - (x[0] + (0.5 * TIME_STEP) * total[0])
            residuals[1, c, at_r] = cot[c, at_r] - (x[1] + (0.5 * TIME_STEP) * total[1])


def call(kernel, outs, smem, vmem, scratch=()):
    vm = pl.BlockSpec(memory_space=pltpu.VMEM)
    sm = pl.BlockSpec(memory_space=pltpu.SMEM)
    return pl.pallas_call(
        kernel,
        out_shape=[jax.ShapeDtypeStruct(shape, F32) for shape in outs],
        in_specs=[sm] * len(smem) + [vm] * len(vmem),
        out_specs=[vm] * len(outs),
        scratch_shapes=[pltpu.VMEM(shape, F32) for shape in scratch],
        compiler_params=pltpu.CompilerParams(vmem_limit_bytes=48 * 1024 * 1024),
    )(*smem, *vmem)


def shifted(x, axis, by):
    count = lax.axis_size(axis)
    return lax.ppermute(x, axis, [(i, (i + by) % count) for i in range(count)])


def around(x, by):
    order = [2 * g for g in range(G)] + [2 * g + 1 for g in reversed(range(G))]
    pairs = [(order[i], order[(i + by) % len(order)]) for i in range(len(order))]
    return lax.ppermute(x, ("gx", "pa"), pairs)


def chebyshev_scalars(upper):
    theta = 0.5 * (upper + 1.0)
    delta = 0.5 * (upper - 1.0)
    sigma = theta / delta
    rho = 1.0 / sigma
    rows = [(1.0 / theta, 0.0 * theta)]
    for _ in range(1, CHEB):
        rho_next = 1.0 / (2.0 * sigma - rho)
        rows.append((rho_next * rho, 2.0 * rho_next / delta))
        rho = rho_next
    return jnp.stack([jnp.stack(row) for row in rows])


def redistributed(conductivity, stored_state, row_scales, cotangent, upper_bound):
    g = lax.axis_index("gx")
    pa = lax.axis_index("pa")

    def strip_of(device):
        return jnp.where(pa == 0, device, G - 1 - device)

    steps = jnp.arange(G, dtype=jnp.int32)
    ahead = lax.rem(g + steps, G)
    behind = lax.rem(g - steps + G, G)
    scalars = chebyshev_scalars(upper_bound[0])
    stored = shifted(stored_state, "pa", 1)
    scales = row_scales[:, :, None]

    kdown = shifted(conductivity[BX - 1], "gx", 1)
    kup = shifted(conductivity[0], "gx", -1)
    kover = shifted(conductivity[:, BY - 1], "gy", 1)
    kunder = shifted(conductivity[:, 0], "gy", -1)
    kends = shifted(jnp.stack((conductivity[:, :, BZ - 1], conductivity[:, :, 0])), "pa", 1)

    brick = (3, 2, BY, LANES)
    parts = call(pack_kernel, [brick] * G, [strip_of(ahead)], [conductivity, stored, scales, cotangent])
    parts = [parts[0]] + [shifted(parts[d], "gx", d) for d in range(1, G)]

    strip = strip_of(g)
    left_g = jnp.where(pa == 0, jnp.maximum(g - 1, 0), jnp.minimum(g + 1, G - 1))
    right_g = jnp.where(pa == 0, jnp.minimum(g + 1, G - 1), jnp.maximum(g - 1, 0))
    places = lax.rem(jnp.stack((left_g - g + steps, right_g - g + steps)) + G, G)
    edge = (3, G, BY, LANES)
    rim = (3, G, 2, HALO, LANES)
    to_left, to_right, head, tail = call(edge_kernel, [edge, edge, rim, rim], [places], parts)
    from_right, from_left = around(to_left, -1), around(to_right, 1)
    below, above = shifted(head, "gy", -1), shifted(tail, "gy", 1)
    edges = jnp.stack((from_left, from_right))
    below_edge = shifted(edges[:, :, :, :HALO], "gy", -1)
    above_edge = shifted(edges[:, :, :, BY - HALO :], "gy", 1)
    field = (NXL, ROWS, LANES)
    solved = call(
        solve_kernel,
        [(2, 3, MROWS, LANES)] * G,
        [strip[None], scalars],
        [*parts, from_left, from_right, above, above_edge, below, below_edge],
        [field] * 8 + [(NXL, TILE, LANES)] * 4 + [field] * 5,
    )
    solved = [solved[0]] + [shifted(solved[d], "gx", d) for d in range(1, G)]
    out = (BX, BY, LANES)
    padded = (BX + 2, BY + 16, LANES)
    return call(
        final_kernel,
        [out, out, out, (2,) + out],
        [strip_of(behind)],
        [*solved, conductivity, kdown, kup, kover, kunder, kends[0][:, :, None], kends[1][:, :, None], stored, scales, cotangent],
        [(2,) + padded, (2, G, BY, LANES), padded],
    )


def body(conductivity, stored_state, row_scales, cotangent, upper_bound):
    strips_fit = (
        lax.axis_size("gx") == G
        and lax.axis_size("pa") == 2
        and conductivity.shape == (BX, BY, BZ)
    )
    run = redistributed if strips_fit else stepwise
    return tuple(run(conductivity, stored_state, row_scales, cotangent, upper_bound))


def solution(mesh):
    return jax.shard_map(
        body,
        mesh=mesh,
        in_specs=(
            P("gx", "gy", "pa"),
            P("gx", "gy", "pa"),
            P("gx", "gy"),
            P("gx", "gy", "pa"),
            P(),
        ),
        out_specs=(
            P("gx", "gy", "pa"),
            P("gx", "gy", "pa"),
            P("gx", "gy", "pa"),
            P(None, "gx", "gy", "pa"),
        ),
        check_vma=False,
    )
```

time: 756 us -> 200 us (0.26)
  other arithmetic: 187 us -> 0.69 us
  waiting for transfers between devices: 272 us -> 86.4 us
  starting transfers between devices: 188 us -> 18.6 us
  local copies, waits for them, and re-layouts: 97.9 us -> 9.8 us
  Pallas kernels: 0 us -> 80.9 us
    ppermute x205 -> x18, waiting for transfers between devices: 272 us -> 86.4 us  [the longest x16 70.6 us: shifted(): return lax.ppermute(x, axis, [(i, (i + by) % count) for i in range(count)])]
    ppermute x205 -> x18, starting transfers between devices: 188 us -> 18.6 us  [the longest x16 17.1 us: shifted(): return lax.ppermute(x, axis, [(i, (i + by) % count) for i in range(count)])]
    add x33 -> x1, other arithmetic: 118 us -> 0.01 us  [redistributed(): right_g - g + steps]
    pallas_call x0 -> x4, Pallas kernels: none -> 80.9 us  [call(): pl.pallas_call(kernel, out_shape=[jax.ShapeDtypeStruct(shape, F32) for sh...]
    slice x168 -> x2, local copies, waits for them, and re-layouts: 39.5 us -> 1.89 us  [the longest x1 1.11 us: redistributed(): conductivity[:, :, BZ - 1]]
    while x128 -> x0, local copies, waits for them, and re-layouts: 34.6 us -> none
    while x32 -> x0, other arithmetic: 32.5 us -> none
    ppermute x68 -> x0, local copies, waits for them, and re-layouts: 21.7 us -> none  [the longest x34 10.8 us: with_halo(): lax.ppermute(head, axis, [((i + 1) % count, i) for i in range(count)])]
  transfers between devices with their start and end apart: 205 -> 18, of which waited for: 183 -> 11; matrix products, arithmetic and copies ran while one was open for 10% -> 4% of each run, Pallas kernels for 0% -> 35%
where the time goes in v2:
time: 200 us; the launch traced here: 199 us
  waiting for transfers between devices  86.4 us (43%)
  Pallas kernels  80.9 us (40%)
  starting transfers between devices  18.6 us (9%)
  local copies, waits for them, and re-layouts  9.8 us (5%)
  between operations  2.84 us (1%)
    pallas_call x4, Pallas kernels, call(): pl.pallas_call(kernel, out_shape=[jax.ShapeDtypeStruct(shape, F32) for sh...  80.9 us
    ppermute x16, waiting for transfers between devices, shifted(): return lax.ppermute(x, axis, [(i, (i + by) % count) for i in range(count)])  70.6 us
    ppermute x16, starting transfers between devices, shifted(): return lax.ppermute(x, axis, [(i, (i + by) % count) for i in range(count)])  17.1 us
    ppermute x2, waiting for transfers between devices, around(): return lax.ppermute(x, ('gx', 'pa'), pairs)  15.9 us
    unnamed x28, local copies, waits for them, and re-layouts  5.89 us
  transfers between devices with their start and end apart: 18, of which 11 were waited for; matrix products, arithmetic and copies ran while one was open for 4% of the time, Pallas kernels for 35%

profile of v2, /device:TPU:8, one launch (start us, length us, event | category | flops | bytes accessed | tf_op | source)
XLA Modules:
  0.0 199.2 jit_solution(18135789742898835997)
XLA Ops:
  0.6 1.6 collective-permute-start
  4.0 5.0 %collective-permute-done.stored = bf16[8,128,128]{2,1,0:T(8,128)(2,1)S(1)} collective-permute-done((bf16[8,128,128]{2,1,0:T(8,128)(2,1)}, bf16[8,128,128]{2,1,0:T(8,128)(2,1)S(1)}, u32[]{:S(2)}, u32[]{:S(2)}) %collective-permute-start) | collective-permute-done | bytes 262176 | tf_op jit(solution)/shard_map/ppermute | solution.py:462
  10.0 2.1 %shard_map.84 = (f32[3,2,128,128]{3,2,1,0:T(8,128)S(1)}, f32[3,2,128,128]{3,2,1,0:T(8,128)}, f32[3,2,128,128]{3,2,1,0:T(8,128)S(1)}, f32[3,2,128,128]{3,2,1,0:T(8,128)S(1)}) custom-call(s32[4]{0:T(128)S(1)} %broadcast_select_fusion.strips, f32[8,128,128]{2,1,0:T(8,128)S(1)} %copy-done, bf16[8,128,128]{2,1,0:T(8,128)(2,1)S(1)} %collective-permute-done.stored, ...), custom_call_target="tpu_custom_call" | custom-call | tf_op jit(solution)/shard_map/pallas_call | solution.py:450
  12.1 1.6 collective-permute-start.1
  14.7 2.0 %collective-permute-start.3 = (f32[3,2,128,128]{3,2,1,0:T(8,128)S(1)}, f32[3,2,128,128]{3,2,1,0:T(8,128)S(1)}, u32[]{:S(2)}, u32[]{:S(2)}) collective-permute-start(f32[3,2,128,128]{3,2,1,0:T(8,128)S(1)} %get-tuple-element.19), channel_id=1, source_target_pairs={{0,24},{8,0},{16,8},{24,16},{1,25},{9,1},{17,9},{25,17},{2,26},{10... | collective-permute-start | bytes 1179656 | tf_op jit(solution)/shard_map/ppermute | solution.py:462
  19.9 1.2 copy.65
  21.1 1.2 copy.64
  22.5 18.0 %collective-permute-done.1.refs_1_.b1 = f32[3,2,128,128]{3,2,1,0:T(8,128)S(1)} collective-permute-done((f32[3,2,128,128]{3,2,1,0:T(8,128)}, f32[3,2,128,128]{3,2,1,0:T(8,128)S(1)}, u32[]{:S(2)}, u32[]{:S(2)}) %collective-permute-start.1) | collective-permute-done | bytes 393248 | tf_op jit(solution)/shard_map/ppermute | solution.py:462
  40.4 6.3 %collective-permute-done.2.refs_2_.b2 = f32[3,2,128,128]{3,2,1,0:T(8,128)S(1)} collective-permute-done((f32[3,2,128,128]{3,2,1,0:T(8,128)S(1)}, f32[3,2,128,128]{3,2,1,0:T(8,128)S(1)}, u32[]{:S(2)}, u32[]{:S(2)}) %collective-permute-start.2) | collective-permute-done | bytes 393248 | tf_op jit(solution)/shard_map/ppermute | solution.py:462
  46.7 1.8 collective-permute-done.3.refs_3_.b3
  48.5 2.2 %shard_map.85 = (f32[3,4,128,128]{3,2,1,0:T(8,128)}, f32[3,4,128,128]{3,2,1,0:T(8,128)}, f32[3,4,2,16,128]{4,3,2,1,0:T(8,128)S(1)}, f32[3,4,2,16,128]{4,3,2,1,0:T(8,128)S(1)}) custom-call(s32[2,4]{1,0:T(2,128)S(1)} %compare_select_fusion.places, f32[3,2,128,128]{3,2,1,0:T(8,128)S(1)} %get-tuple-element.16.refs_0_.b0, ...), custom_call_target="tpu_custom_call" | custom-call | tf_op jit(solution)/shard_map/pallas_call | solution.py:450
  51.4 1.4 collective-permute-start.5
  53.4 1.7 collective-permute-start.8
  55.2 15.3 %collective-permute-done.4.from_left = f32[3,4,128,128]{3,2,1,0:T(8,128)S(1)} collective-permute-done((f32[3,4,128,128]{3,2,1,0:T(8,128)}, f32[3,4,128,128]{3,2,1,0:T(8,128)S(1)}, u32[]{:S(2)}, u32[]{:S(2)}) %collective-permute-start.4) | collective-permute-done | bytes 786464 | tf_op jit(solution)/shard_map/ppermute | solution.py:468
  71.2 1.7 collective-permute-start.9
  73.5 3.0 %collective-permute-done.7.above_edge = f32[2,3,4,16,128]{4,3,2,1,0:T(8,128)S(1)} collective-permute-done((f32[2,3,4,16,128]{4,3,2,1,0:T(8,128)S(1)}, f32[2,3,4,16,128]{4,3,2,1,0:T(8,128)S(1)}, u32[]{:S(2)}, u32[]{:S(2)}) %collective-permute-start.7) | collective-permute-done | bytes 196640 | tf_op jit(solution)/shard_map/ppermute | solution.py:462
  77.3 66.2 %shard_map.86 = (f32[2,3,136,128]{3,2,1,0:T(8,128)S(1)}, f32[2,3,136,128]{3,2,1,0:T(8,128)}, f32[2,3,136,128]{3,2,1,0:T(8,128)}, f32[2,3,136,128]{3,2,1,0:T(8,128)}) custom-call(s32[1]{0:T(128)} %bitcast.strip, f32[16,2]{1,0:T(8,128)S(1)} %stack.273.scalars, f32[3,2,128,128]{3,2,1,0:T(8,128)S(1)} %get-tuple-element.16.refs_0_.b0, ...), custom_call_target="tpu_custom_call" | custom-call | tf_op jit(solution)/shard_map/pallas_call | solution.py:450
  144.3 3.5 %collective-permute-start.11 = (f32[2,3,136,128]{3,2,1,0:T(8,128)}, f32[2,3,136,128]{3,2,1,0:T(8,128)}, u32[]{:S(2)}, u32[]{:S(2)}) collective-permute-start(f32[2,3,136,128]{3,2,1,0:T(8,128)} %get-tuple-element.26), channel_id=1, source_target_pairs={{0,16},{8,24},{16,0},{24,8},{1,17},{9,25},{17,1},{25,9},{2,18},{10... | collective-permute-start | bytes 1253384 | tf_op jit(solution)/shard_map/ppermute | solution.py:462
  148.7 1.5 collective-permute-start.13
  150.2 1.3 collective-permute-done.17
  151.5 1.5 collective-permute-start.14
  153.4 30.8 %collective-permute-done.13.kdown = f32[128,128]{1,0:T(8,128)S(1)} collective-permute-done((f32[128,128]{1,0:T(8,128)}, f32[128,128]{1,0:T(8,128)S(1)}, u32[]{:S(2)}, u32[]{:S(2)}) %collective-permute-start.13) | collective-permute-done | bytes 65568 | tf_op jit(solution)/shard_map/ppermute | solution.py:462
  184.2 3.6 %collective-permute-done.14.kup = f32[128,128]{1,0:T(8,128)S(1)} collective-permute-done((f32[128,128]{1,0:T(8,128)S(1)}, f32[128,128]{1,0:T(8,128)S(1)}, u32[]{:S(2)}, u32[]{:S(2)}) %collective-permute-start.14) | collective-permute-done | bytes 65568 | tf_op jit(solution)/shard_map/ppermute | solution.py:462
  188.9 10.4 %shard_map.87 = (f32[8,128,128]{2,1,0:T(8,128)}, f32[8,128,128]{2,1,0:T(8,128)}, f32[8,128,128]{2,1,0:T(8,128)}, f32[2,8,128,128]{3,2,1,0:T(8,128)}) custom-call(s32[4]{0:T(128)S(1)} %broadcast_select_fusion.1.strips, f32[2,3,136,128]{3,2,1,0:T(8,128)S(1)} %copy-done.10, f32[2,3,136,128]{3,2,1,0:T(8,128)S(1)} %collective-permute-done.10.m1, ...), custom_call_target="tpu_custom_call" | custom-call | tf_op jit(solution)/shard_map/pallas_call | solution.py:450
  (66 shorter events, 11.6 us)
Async XLA Ops:
  0.6 8.3 %copy-start = (f32[8,128,128]{2,1,0:T(8,128)S(1)}, f32[8,128,128]{2,1,0:T(8,128)}, u32[]{:S(2)}) copy-start(f32[8,128,128]{2,1,0:T(8,128)} %cond.3) | copy-start | bytes 1572868
  0.6 8.3 %collective-permute-start = (bf16[8,128,128]{2,1,0:T(8,128)(2,1)}, bf16[8,128,128]{2,1,0:T(8,128)(2,1)S(1)}, u32[]{:S(2)}, u32[]{:S(2)}) collective-permute-start(bf16[8,128,128]{2,1,0:T(8,128)(2,1)} %param.6), channel_id=1, source_target_pairs={{0,1},{1,0},{2,3},{3,2},{4,5},{5,4},{6,7},{7,6},{8,9},{9,8},{10,11... | collective-permute-start | bytes 786440 | tf_op jit(solution)/shard_map/ppermute | solution.py:462
  3.0 144.8 %collective-permute-start.15 = (f32[8,128]{1,0:T(8,128)S(1)}, f32[8,128]{1,0:T(8,128)S(1)}, u32[]{:S(2)}, u32[]{:S(2)}) collective-permute-start(f32[8,128]{1,0:T(8,128)S(1)} %bitcast.91), channel_id=1, source_target_pairs={{0,2},{2,4},{4,6},{6,0},{1,3},{3,5},{5,7},{7,1},{8,10},{10,12},{12... | collective-permute-start | bytes 12296 | tf_op jit(solution)/shard_map/ppermute | solution.py:462
  12.1 28.3 %collective-permute-start.1 = (f32[3,2,128,128]{3,2,1,0:T(8,128)}, f32[3,2,128,128]{3,2,1,0:T(8,128)S(1)}, u32[]{:S(2)}, u32[]{:S(2)}) collective-permute-start(f32[3,2,128,128]{3,2,1,0:T(8,128)} %get-tuple-element.17), channel_id=1, source_target_pairs={{0,8},{8,16},{16,24},{24,0},{1,9},{9,17},{17,25},{25,1},{2,10},{10... | collective-permute-start | bytes 1179656 | tf_op jit(solution)/shard_map/ppermute | solution.py:462
  13.7 33.0 %collective-permute-start.2 = (f32[3,2,128,128]{3,2,1,0:T(8,128)S(1)}, f32[3,2,128,128]{3,2,1,0:T(8,128)S(1)}, u32[]{:S(2)}, u32[]{:S(2)}) collective-permute-start(f32[3,2,128,128]{3,2,1,0:T(8,128)S(1)} %get-tuple-element.18), channel_id=1, source_target_pairs={{0,16},{8,24},{16,0},{24,8},{1,17},{9,25},{17,1},{25,9},{2,18},{10... | collective-permute-start | bytes 1179656 | tf_op jit(solution)/shard_map/ppermute | solution.py:462
  14.7 33.8 %collective-permute-start.3 = (f32[3,2,128,128]{3,2,1,0:T(8,128)S(1)}, f32[3,2,128,128]{3,2,1,0:T(8,128)S(1)}, u32[]{:S(2)}, u32[]{:S(2)}) collective-permute-start(f32[3,2,128,128]{3,2,1,0:T(8,128)S(1)} %get-tuple-element.19), channel_id=1, source_target_pairs={{0,24},{8,0},{16,8},{24,16},{1,25},{9,1},{17,9},{25,17},{2,26},{10... | collective-permute-start | bytes 1179656 | tf_op jit(solution)/shard_map/ppermute | solution.py:462
  46.7 4.0 %copy-start.3 = (f32[3,2,128,128]{3,2,1,0:T(8,128)}, f32[3,2,128,128]{3,2,1,0:T(8,128)S(1)}, u32[]{:S(2)}) copy-start(f32[3,2,128,128]{3,2,1,0:T(8,128)S(1)} %collective-permute-done.2.refs_2_.b2) | copy-start | bytes 1179652
  50.7 19.7 %collective-permute-start.4 = (f32[3,4,128,128]{3,2,1,0:T(8,128)}, f32[3,4,128,128]{3,2,1,0:T(8,128)S(1)}, u32[]{:S(2)}, u32[]{:S(2)}) collective-permute-start(f32[3,4,128,128]{3,2,1,0:T(8,128)} %get-tuple-element.20), channel_id=1, source_target_pairs={{0,8},{8,16},{16,24},{24,25},{25,17},{17,9},{9,1},{1,0},{2,10},{10... | collective-permute-start | bytes 2359304 | tf_op jit(solution)/shard_map/ppermute | solution.py:468
  51.4 19.7 %collective-permute-start.5 = (f32[3,4,128,128]{3,2,1,0:T(8,128)}, f32[3,4,128,128]{3,2,1,0:T(8,128)S(1)}, u32[]{:S(2)}, u32[]{:S(2)}) collective-permute-start(f32[3,4,128,128]{3,2,1,0:T(8,128)} %get-tuple-element.21), channel_id=1, source_target_pairs={{0,1},{8,0},{16,8},{24,16},{25,24},{17,25},{9,17},{1,9},{2,3},{10,... | collective-permute-start | bytes 2359304 | tf_op jit(solution)/shard_map/ppermute | solution.py:468
  53.4 20.1 %collective-permute-start.6 = (f32[3,4,2,16,128]{4,3,2,1,0:T(8,128)}, f32[3,4,2,16,128]{4,3,2,1,0:T(8,128)S(1)}, u32[]{:S(2)}, u32[]{:S(2)}) collective-permute-start(f32[3,4,2,16,128]{4,3,2,1,0:T(8,128)} %copy-done.12), channel_id=1, source_target_pairs={{0,2},{2,4},{4,6},{6,0},{1,3},{3,5},{5,7},{7,1},{8,10},{10,12},{12... | collective-permute-start | bytes 589832 | tf_op jit(solution)/shard_map/ppermute | solution.py:462
  53.4 20.1 %collective-permute-start.8 = (f32[3,4,2,16,128]{4,3,2,1,0:T(8,128)}, f32[3,4,2,16,128]{4,3,2,1,0:T(8,128)S(1)}, u32[]{:S(2)}, u32[]{:S(2)}) collective-permute-start(f32[3,4,2,16,128]{4,3,2,1,0:T(8,128)} %copy-done.11), channel_id=1, source_target_pairs={{0,6},{2,0},{4,2},{6,4},{1,7},{3,1},{5,3},{7,5},{8,14},{10,8},{12,... | collective-permute-start | bytes 589832 | tf_op jit(solution)/shard_map/ppermute | solution.py:462
  71.1 6.3 %copy-start.4 = (f32[3,2,128,128]{3,2,1,0:T(8,128)S(1)}, f32[3,2,128,128]{3,2,1,0:T(8,128)}, u32[]{:S(2)}) copy-start(f32[3,2,128,128]{3,2,1,0:T(8,128)} %copy-done.3) | copy-start | bytes 1179652
  71.1 6.3 %copy-start.6 = (f32[3,2,128,128]{3,2,1,0:T(8,128)S(1)}, f32[3,2,128,128]{3,2,1,0:T(8,128)}, u32[]{:S(2)}) copy-start(f32[3,2,128,128]{3,2,1,0:T(8,128)} %copy-done.5) | copy-start | bytes 1179652
  71.1 5.4 %collective-permute-start.7 = (f32[2,3,4,16,128]{4,3,2,1,0:T(8,128)S(1)}, f32[2,3,4,16,128]{4,3,2,1,0:T(8,128)S(1)}, u32[]{:S(2)}, u32[]{:S(2)}) collective-permute-start(f32[2,3,4,16,128]{4,3,2,1,0:T(8,128)S(1)} %get-tuple-element.29), channel_id=1, source_target_pairs={{0,2},{2,4},{4,6},{6,0},{1,3},{3,5},{5,7},{7,1},{8,10},{10,12},{12... | collective-permute-start | bytes 589832 | tf_op jit(solution)/shard_map/ppermute | solution.py:462
  71.2 6.2 %collective-permute-start.9 = (f32[2,3,4,16,128]{4,3,2,1,0:T(8,128)S(1)}, f32[2,3,4,16,128]{4,3,2,1,0:T(8,128)S(1)}, u32[]{:S(2)}, u32[]{:S(2)}) collective-permute-start(f32[2,3,4,16,128]{4,3,2,1,0:T(8,128)S(1)} %get-tuple-element.28), channel_id=1, source_target_pairs={{0,6},{2,0},{4,2},{6,4},{1,7},{3,1},{5,3},{7,5},{8,14},{10,8},{12,... | collective-permute-start | bytes 589832 | tf_op jit(solution)/shard_map/ppermute | solution.py:462
  73.5 75.2 %collective-permute-start.16 = (f32[8,128]{1,0:T(8,128)S(1)}, f32[8,128]{1,0:T(8,128)S(1)}, u32[]{:S(2)}, u32[]{:S(2)}) collective-permute-start(f32[8,128]{1,0:T(8,128)S(1)} %bitcast.90), channel_id=1, source_target_pairs={{0,6},{2,0},{4,2},{6,4},{1,7},{3,1},{5,3},{7,5},{8,14},{10,8},{12,... | collective-permute-start | bytes 12296 | tf_op jit(solution)/shard_map/ppermute | solution.py:462
  144.3 43.5 %collective-permute-start.10 = (f32[2,3,136,128]{3,2,1,0:T(8,128)}, f32[2,3,136,128]{3,2,1,0:T(8,128)S(1)}, u32[]{:S(2)}, u32[]{:S(2)}) collective-permute-start(f32[2,3,136,128]{3,2,1,0:T(8,128)} %get-tuple-element.25), channel_id=1, source_target_pairs={{0,8},{8,16},{16,24},{24,0},{1,9},{9,17},{17,25},{25,1},{2,10},{10... | collective-permute-start | bytes 1253384 | tf_op jit(solution)/shard_map/ppermute | solution.py:462
  144.3 43.5 %collective-permute-start.11 = (f32[2,3,136,128]{3,2,1,0:T(8,128)}, f32[2,3,136,128]{3,2,1,0:T(8,128)}, u32[]{:S(2)}, u32[]{:S(2)}) collective-permute-start(f32[2,3,136,128]{3,2,1,0:T(8,128)} %get-tuple-element.26), channel_id=1, source_target_pairs={{0,16},{8,24},{16,0},{24,8},{1,17},{9,25},{17,1},{25,9},{2,18},{10... | collective-permute-start | bytes 1253384 | tf_op jit(solution)/shard_map/ppermute | solution.py:462
  147.8 40.1 %collective-permute-start.12 = (f32[2,3,136,128]{3,2,1,0:T(8,128)}, f32[2,3,136,128]{3,2,1,0:T(8,128)}, u32[]{:S(2)}, u32[]{:S(2)}) collective-permute-start(f32[2,3,136,128]{3,2,1,0:T(8,128)} %get-tuple-element.27), channel_id=1, source_target_pairs={{0,24},{8,0},{16,8},{24,16},{1,25},{9,1},{17,9},{25,17},{2,26},{10... | collective-permute-start | bytes 1253384 | tf_op jit(solution)/shard_map/ppermute | solution.py:462
  147.8 3.7 %collective-permute-start.17 = (f32[2,8,128]{2,1,0:T(8,128)S(1)}, f32[2,8,128]{2,1,0:T(8,128)S(1)}, u32[]{:S(2)}, u32[]{:S(2)}) collective-permute-start(f32[2,8,128]{2,1,0:T(8,128)S(1)} %pad_maximum_fusion.2), channel_id=1, source_target_pairs={{0,1},{1,0},{2,3},{3,2},{4,5},{5,4},{6,7},{7,6},{8,9},{9,8},{10,11... | collective-permute-start | bytes 24584 | tf_op jit(solution)/shard_map/ppermute | solution.py:462
  148.7 35.5 %collective-permute-start.13 = (f32[128,128]{1,0:T(8,128)}, f32[128,128]{1,0:T(8,128)S(1)}, u32[]{:S(2)}, u32[]{:S(2)}) collective-permute-start(f32[128,128]{1,0:T(8,128)} %get-tuple-element.35), channel_id=1, source_target_pairs={{0,8},{8,16},{16,24},{24,0},{1,9},{9,17},{17,25},{25,1},{2,10},{10... | collective-permute-start | bytes 196616 | tf_op jit(solution)/shard_map/ppermute | solution.py:462
  151.5 36.3 %collective-permute-start.14 = (f32[128,128]{1,0:T(8,128)S(1)}, f32[128,128]{1,0:T(8,128)S(1)}, u32[]{:S(2)}, u32[]{:S(2)}) collective-permute-start(f32[128,128]{1,0:T(8,128)S(1)} %get-tuple-element.34), channel_id=1, source_target_pairs={{0,24},{8,0},{16,8},{24,16},{1,25},{9,1},{17,9},{25,17},{2,26},{10... | collective-permute-start | bytes 196616 | tf_op jit(solution)/shard_map/ppermute | solution.py:462
  153.0 34.9 %copy-start.2 = (f32[8,128,128]{2,1,0:T(8,128)S(1)}, f32[8,128,128]{2,1,0:T(8,128)}, u32[]{:S(2)}) copy-start(f32[8,128,128]{2,1,0:T(8,128)} %cot.3) | copy-start | bytes 1572868
  153.2 34.7 %copy-start.8 = (bf16[8,128,128]{2,1,0:T(8,128)(2,1)S(1)}, bf16[8,128,128]{2,1,0:T(8,128)(2,1)}, u32[]{:S(2)}) copy-start(bf16[8,128,128]{2,1,0:T(8,128)(2,1)} %copy-done.7) | copy-start | bytes 786436
  (7 other events, 10.4 us)

commit v3 on v2

v3 whole, which is shorter than its diff:
```python
import functools

import jax
import jax.numpy as jnp
from jax import lax
from jax.experimental import pallas as pl
from jax.experimental.pallas import tpu as pltpu
from jax.sharding import PartitionSpec as P

CHEB = 16
LANES = 128
HALO = CHEB
TIME_STEP = 8.0
F32 = jnp.float32


def with_halo(cells, sides, width):
    for axis, dim in sides:
        count = lax.axis_size(axis)
        head = lax.slice_in_dim(cells, 0, width, axis=dim)
        tail = lax.slice_in_dim(cells, cells.shape[dim] - width, cells.shape[dim], axis=dim)
        cells = jnp.concatenate(
            [
                lax.ppermute(tail, axis, [(i, (i + 1) % count) for i in range(count)]),
                cells,
                lax.ppermute(head, axis, [((i + 1) % count, i) for i in range(count)]),
            ],
            axis=dim,
        )
    return cells


def region(arr, spatial, offset):
    extent = arr.shape[-3:]
    window = [slice(1, length - 1) for length in extent]
    window[spatial] = slice(offset, extent[spatial] - 2 + offset)
    leading = [slice(None)] * (arr.ndim - 3)
    return arr[tuple(leading + window)]


def apply_operator(padded, kpad):
    centre = region(padded, 0, 1)
    kcentre = region(kpad, 0, 1)
    summed = jnp.zeros_like(centre)
    for spatial in range(3):
        for offset in (0, 2):
            summed = summed + 0.5 * (kcentre + region(kpad, spatial, offset)) * (
                centre - region(padded, spatial, offset)
            )
    return centre + TIME_STEP * summed


def stepwise(conductivity, stored_state, row_scales, cotangent, upper_bound):
    upper = upper_bound[0]
    kpad = with_halo(conductivity, (("gx", 0), ("gy", 1), ("pa", 2)), 1)
    count = lax.axis_size("pa")
    partner = lax.ppermute(stored_state, "pa", [(i, (i + count // 2) % count) for i in range(count)])
    previous = partner.astype(F32) * row_scales[:, :, None]
    rhs = jnp.stack((previous, cotangent))
    theta = 0.5 * (upper + 1.0)
    delta = 0.5 * (upper - 1.0)
    sigma = theta / delta
    sides = (("gx", 1), ("gy", 2), ("pa", 3))

    def sweep(step, carry):
        solved, residual, direction, rho = carry
        padded = with_halo(direction, sides, 1)
        solved = solved + direction
        residual = residual - apply_operator(padded, kpad)
        rho_next = 1.0 / (2.0 * sigma - rho)
        direction = rho_next * rho * direction + 2.0 * rho_next / delta * residual
        return (solved, residual, direction, rho_next)

    start = (jnp.zeros_like(rhs), rhs, rhs / theta, 1.0 / sigma)
    solved, residual, _, _ = lax.fori_loop(0, CHEB, sweep, start)
    pair = with_halo(solved, sides, 1)
    centre = region(pair, 0, 1)
    summed = jnp.zeros_like(solved[0])
    for spatial in range(3):
        for offset in (0, 2):
            differ = centre - region(pair, spatial, offset)
            summed = summed + differ[0] * differ[1]
    return (-0.5 * TIME_STEP * summed, solved[1], solved[0], residual)


G = 4
BX = 8
BY = 128
BZ = 128
STRIP = BZ // G
TOP = 8 + HALO
ROWS = BY + 2 * TOP
MROWS = BY + 8
TILE = 8

BLOCK = (0, 3, 2, 1)
PLANES = BX


def roll(x, by):
    by %= LANES
    return pltpu.roll(x, by, 1) if by else x


def lanes_of(rows, strip):
    lane = lax.broadcasted_iota(jnp.int32, (rows, LANES), 1)
    return lax.rem(lane // STRIP - strip + 2 * G, G), lax.rem(lane, STRIP)


def pick(group, parts):
    out = parts[0]
    for b in range(1, G):
        out = jnp.where(group == b, parts[b], out)
    return out


def parity_order(transposed):
    src = lax.broadcasted_iota(jnp.int32, (LANES, LANES), 1 if transposed else 0)
    dst = lax.broadcasted_iota(jnp.int32, (LANES, LANES), 0 if transposed else 1)
    within = lax.rem(src, STRIP)
    place = src - within + 16 * lax.rem(within, 2) + within // 2
    return jnp.where(place == dst, 1.0, 0.0).astype(F32)


def reorder(x, order):
    return jnp.dot(x, order, precision=lax.Precision.HIGHEST, preferred_element_type=F32)


def pack_kernel(names, strips, *refs):
    ins, outs = refs[: len(refs) - G], refs[len(refs) - G :]
    order = parity_order(False)
    groups = [lanes_of(BY, strips[d])[0] for d in range(G)]
    for a in range(2):
        for n, name in enumerate(names):
            parts = []
            for b in range(4):
                c = 4 * a + b
                if name == "previous":
                    plane = ins[n][c].astype(F32) * ins[n + 1][c]
                else:
                    plane = ins[n][c]
                parts.append(roll(reorder(plane, order), 32 * b))
            for d in range(G):
                outs[d][n, a] = pick(groups[d], parts)


def edge_kernel(places, *refs):
    msgs, (to_left, to_right, head, tail) = refs[:G], refs[G:]
    lane = lax.broadcasted_iota(jnp.int32, (BY, LANES), 1)
    low = lax.rem(lane, 16) < 8
    for n in range(msgs[0].shape[0]):
        for d in range(G):
            first, second = msgs[d][n, 0], msgs[d][n, 1]
            to_left[n, places[0, d]] = jnp.where(low, first, roll(second, 8))
            to_right[n, places[1, d]] = jnp.where(low, roll(second, -8), first)
            for a in range(2):
                head[n, d, a] = msgs[d][n, a, :HALO]
                tail[n, d, a] = msgs[d][n, a, BY - HALO :]


def unpack(get_brick, get_edge, group, within, put):
    by_block = [BLOCK.index(q) for q in range(G)]
    edges = [[get_edge(side, d) for d in by_block] for side in range(2)]
    for a in range(2):
        far = 24 if a else 16
        own = [roll(get_brick(by_block[q], a), 32 * q) for q in range(G)]
        below = [roll(edges[0][q], 32 * q + far) for q in range(G)]
        above = [roll(edges[1][q], 32 * q - far) for q in range(G)]
        even = [
            jnp.where(within < 16, own[q], jnp.where(within < 24, above[q], below[(q + 1) % G])) for q in range(G)
        ]
        odd = [
            jnp.where(within < 8, above[(q - 1) % G], jnp.where(within < 16, below[q], own[q])) for q in range(G)
        ]
        for b in range(4):
            for e, parts in enumerate((even, odd)):
                whole = pick(group, [parts[(q - b) % G] for q in range(G)])
                put(4 * a + b, e, roll(whole, -32 * b - 16 * e))


def solve_kernel(nf, where, strip, scalars, *refs):
    stacks = []
    for _ in range(1 + max(stack for stack, _ in where)):
        stacks.append((refs[:G],) + tuple(refs[G : G + 6]))
        refs = refs[G + 6 :]
    outs = refs[:G]
    refs = refs[G:]
    xa, xb, xc, rhs, stage_a, stage_b = (refs[nf * j : nf * (j + 1)] for j in range(6))
    kap, kx, ky, kin, kout, diag = refs[6 * nf :]
    zero = jnp.zeros((TILE, LANES), F32)
    group, within = lanes_of(TILE, strip[0])
    targets = (kap,) + tuple(rhs)

    def put_at(dst, to):
        def put(i, e, val):
            dst[i, e, pl.ds(to, TILE)] = val

        return put

    @pl.loop(0, BY // TILE)
    def _(t):
        r = pl.multiple_of(TILE * t, TILE)
        to = pl.multiple_of(TOP + TILE * t, TILE)
        for dst, (stack, n) in zip(targets, where):
            bricks, from_left, from_right = stacks[stack][:3]
            sides = (from_left, from_right)
            unpack(
                lambda d, a: bricks[d][n, a, pl.ds(r, TILE)],
                lambda side, d: sides[side][n, d, pl.ds(r, TILE)],
                group,
                within,
                put_at(dst, to),
            )

    @pl.loop(0, HALO // TILE)
    def _(t):
        r = pl.multiple_of(TILE * t, TILE)
        for dst, (stack, n) in zip(targets, where):
            above, above_edge, below, below_edge = stacks[stack][3:]
            for brick, edge, start in ((above, above_edge, TOP - HALO), (below, below_edge, TOP + BY)):
                unpack(
                    lambda d, a: brick[n, d, a, pl.ds(r, TILE)],
                    lambda side, d: edge[side, n, d, pl.ds(r, TILE)],
                    group,
                    within,
                    put_at(dst, pl.multiple_of(start + TILE * t, TILE)),
                )

    for i in range(PLANES):
        for e in range(2):
            for dst in (kap, ky) + tuple(rhs) + tuple(xa) + tuple(xb) + tuple(xc):
                dst[i, e, 0:TILE] = zero
                dst[i, e, ROWS - TILE : ROWS] = zero
        for dst in (kin, kout):
            dst[i, 0:TILE] = zero
            dst[i, ROWS - TILE : ROWS] = zero

    @pl.loop(0, ROWS // TILE - 2)
    def _(t):
        r = pl.multiple_of(TILE + TILE * t, TILE)
        now = [kap[0, e, pl.ds(r, TILE)] for e in range(2)]
        wrapped = [roll(k, -32) for k in now]
        for i in range(PLANES):
            after = [kap[i + 1, e, pl.ds(r, TILE)] for e in range(2)] if i + 1 < PLANES else wrapped
            for e in range(2):
                kx[i, e, pl.ds(r, TILE)] = 4.0 * (now[e] + after[e])
                ky[i, e, pl.ds(r, TILE)] = 4.0 * (now[e] + kap[i, e, pl.ds(r + 1, TILE)])
            kin[i, pl.ds(r, TILE)] = 4.0 * (now[0] + now[1])
            kout[i, pl.ds(r, TILE)] = 4.0 * (now[1] + roll(now[0], -1))
            now = after

    theta_inv = scalars[0, 0]

    @pl.loop(0, ROWS // TILE - 2)
    def _(t):
        r = pl.multiple_of(TILE + TILE * t, TILE)
        before = [roll(kx[PLANES - 1, e, pl.ds(r, TILE)], 32) for e in range(2)]
        for i in range(PLANES):
            inner = kin[i, pl.ds(r, TILE)]
            outer = kout[i, pl.ds(r, TILE)]
            along = (inner + roll(outer, 1), inner + outer)
            for e in range(2):
                fx = kx[i, e, pl.ds(r, TILE)]
                total = fx + before[e] + ky[i, e, pl.ds(r, TILE)] + ky[i, e, pl.ds(r - 1, TILE)]
                diag[i, e, pl.ds(r, TILE)] = 1.0 + (total + along[e])
                before[e] = fx
                for f in range(nf):
                    xb[f][i, e, pl.ds(r, TILE)] = rhs[f][i, e, pl.ds(r, TILE)] * theta_inv
                    xa[f][i, e, pl.ds(r, TILE)] = zero

    def along_lanes(cur, stage, r):
        for i in range(PLANES):
            inner = kin[i, pl.ds(r, TILE)]
            outer = kout[i, pl.ds(r, TILE)]
            for f in range(nf):
                even, odd = (cur[f][i, e, pl.ds(r, TILE)] for e in range(2))
                stage[f][i, 0] = (inner * odd + roll(outer * odd, 1)) + rhs[f][i, 0, pl.ds(r, TILE)]
                stage[f][i, 1] = (inner * even + outer * roll(even, -1)) + rhs[f][i, 1, pl.ds(r, TILE)]

    def advance(alpha, beta, old, cur, new, stage, r):
        for e in range(2):
            now = [cur[f][0, e, pl.ds(r, TILE)] for f in range(nf)]
            wrapped = [roll(x, -32) for x in now]
            before = [roll(cur[f][PLANES - 1, e, pl.ds(r, TILE)], 32) for f in range(nf)]
            fbefore = roll(kx[PLANES - 1, e, pl.ds(r, TILE)], 32)
            for i in range(PLANES):
                fx = kx[i, e, pl.ds(r, TILE)]
                fy = ky[i, e, pl.ds(r, TILE)]
                fym = ky[i, e, pl.ds(r - 1, TILE)]
                centre = (1.0 + alpha) - beta * diag[i, e, pl.ds(r, TILE)]
                for f in range(nf):
                    x = now[f]
                    after = cur[f][i + 1, e, pl.ds(r, TILE)] if i + 1 < PLANES else wrapped[f]
                    near = fx * after + fbefore * before[f]
                    near = near + (fy * cur[f][i, e, pl.ds(r + 1, TILE)] + fym * cur[f][i, e, pl.ds(r - 1, TILE)])
                    near = near + stage[f][i, e]
                    new[f][i, e, pl.ds(r, TILE)] = centre * x - alpha * old[f][i, e, pl.ds(r, TILE)] + beta * near
                    before[f] = x
                    now[f] = after
                fbefore = fx

    def sweep(k, old, cur, new, span):
        alpha, beta = scalars[k, 0], scalars[k, 1]
        along_lanes(cur, stage_a, span[0])

        @pl.loop(0, span[1] // 2)
        def _(t):
            r = pl.multiple_of(span[0] + 2 * TILE * t, TILE)
            along_lanes(cur, stage_b, r + TILE)
            advance(alpha, beta, old, cur, new, stage_a, r)
            along_lanes(cur, stage_a, r + 2 * TILE)
            advance(alpha, beta, old, cur, new, stage_b, r + TILE)

    def three(k, spans):
        sweep(k, xa, xb, xc, spans[0])
        sweep(k + 1, xb, xc, xa, spans[1])
        sweep(k + 2, xc, xa, xb, spans[2])

    wide = (TILE, ROWS // TILE - 2)
    narrow = (2 * TILE, ROWS // TILE - 4)

    @pl.loop(0, 2)
    def _(m):
        three(1 + 3 * m, (wide,) * 3)

    three(7, (wide, narrow, narrow))

    @pl.loop(0, 2)
    def _(m):
        three(10 + 3 * m, (narrow,) * 3)

    def near_edge(width):
        below = lax.rem(within + 1, STRIP) < width
        return below | ((within >= 16) & (within < 16 + width))

    masks = [near_edge(1), near_edge(2), near_edge(4)]

    def pieces(f, row):
        out = []
        for i in range(PLANES):
            even, odd = (xb[f][i, e, pl.ds(row, TILE)] for e in range(2))
            out.append(jnp.where(within < 16, even, roll(odd, 16)))
        return out

    def main_rows(parts):
        parts = [roll(parts[i], 32 * (i % 4)) for i in range(PLANES)]
        return [[pick(group, [parts[4 * a + (q - d) % G] for q in range(G)]) for a in range(2)] for d in range(G)]

    def side_rows(f, parts, row):
        tree = [
            jnp.where(within == 31, xb[f][i, 1, pl.ds(row, TILE)], xb[f][i, 0, pl.ds(row, TILE)])
            for i in range(PLANES)
        ]
        for level in range(3):
            tree = [
                jnp.where(masks[level], tree[j], roll(tree[j + 1], 1 << level)) for j in range(0, len(tree), 2)
            ]
        ends = roll(tree[0], 1)
        groups = (ends, ends, roll(parts[PLANES - 1], 96), roll(parts[0], 64))
        return [pick(group, [groups[(q - d) % G] for q in range(G)]) for d in range(G)]

    @pl.loop(0, BY // TILE)
    def _(t):
        row = pl.multiple_of(TOP + TILE * t, TILE)
        to = pl.ds(pl.multiple_of(TILE * t, TILE), TILE)
        for f in range(nf):
            parts = pieces(f, row)
            mains, sides = main_rows(parts), side_rows(f, parts, row)
            for d in range(G):
                for a in range(2):
                    outs[d][f, a, to] = mains[d][a]
                outs[d][f, 2, to] = sides[d]

    sub = lax.broadcasted_iota(jnp.int32, (TILE, LANES), 0)
    for f in range(nf):
        over, under = main_rows(pieces(f, TOP - TILE)), main_rows(pieces(f, TOP + BY))
        for d in range(G):
            for a in range(2):
                outs[d][f, a, BY:MROWS] = jnp.where(
                    sub == 0, pltpu.roll(over[d][a], 1, 0), pltpu.roll(under[d][a], 1, 0)
                )
            outs[d][f, 2, BY:MROWS] = zero


def final_kernel(nstacks, strips, *refs):
    stacks = [refs[G * j : G * (j + 1)] for j in range(nstacks)]
    refs = refs[G * nstacks :]
    cond, kdown, kup, kover, kunder, kzl, kzr, stored, scales, cot = refs[:10]
    grad, adjoint, state, residuals, xs, ends, kap = refs[10:]
    fields = [(stack, n) for stack in stacks for n in range(2 // nstacks)]
    order = parity_order(True)
    wide = 4 * TILE

    def owners(rows):
        return [lanes_of(rows, strips[d])[0] for d in range(G)]

    def choose(owner, parts, b):
        out = parts[0]
        for d in range(1, G):
            out = jnp.where(owner[d] == b, parts[d], out)
        return out

    def bricks(f, a, row, rows):
        msgs, n = fields[f]
        return [roll(msgs[d][n, a, pl.ds(row, rows)], -32 * d) for d in range(G)]

    @pl.loop(0, BY // wide)
    def _(t):
        row = pl.multiple_of(wide * t, wide)
        to = pl.ds(pl.multiple_of(TILE + wide * t, TILE), wide)
        owner = owners(wide)
        for f in range(2):
            for a in range(2):
                parts = bricks(f, a, row, wide)
                for b in range(4):
                    xs[f, 1 + 4 * a + b, to] = reorder(roll(choose(owner, parts, b), -32 * b), order)
            parts = bricks(f, 2, row, wide)
            for d in range(G):
                ends[f, strips[d], pl.ds(row, wide)] = parts[d]
            xs[f, 0, to] = reorder(roll(choose(owner, parts, 2), -64), order)
            xs[f, 1 + BX, to] = reorder(roll(choose(owner, parts, 3), -96), order)

    owner = owners(TILE)
    for f in range(2):
        for a in range(2):
            parts = bricks(f, a, BY, TILE)
            for b in range(4):
                val = pltpu.roll(reorder(roll(choose(owner, parts, b), -32 * b), order), 7, 0)
                xs[f, 1 + 4 * a + b, 0:TILE] = val
                xs[f, 1 + 4 * a + b, TILE + BY : 2 * TILE + BY] = val
    kap[0, TILE : TILE + BY] = kdown[...]
    kap[1 + BX, TILE : TILE + BY] = kup[...]
    for c in range(BX):
        kap[1 + c, TILE : TILE + BY] = cond[c]
        kap[1 + c, 0:TILE] = jnp.broadcast_to(kover[c : c + 1], (TILE, LANES))
        kap[1 + c, TILE + BY : 2 * TILE + BY] = jnp.broadcast_to(kunder[c : c + 1], (TILE, LANES))
    lane = lax.broadcasted_iota(jnp.int32, (TILE, LANES), 1)

    @pl.loop(0, BY // TILE)
    def _(t):
        r = pl.multiple_of(TILE * t, TILE)
        r8 = pl.multiple_of(TILE * t + TILE, TILE)
        at_r = pl.ds(r, TILE)
        low = [ends[f, 0, at_r] for f in range(2)]
        high = [ends[f, G - 1, at_r] for f in range(2)]
        for c in range(BX):
            k = kap[1 + c, pl.ds(r8, TILE)]
            x = [xs[f, 1 + c, pl.ds(r8, TILE)] for f in range(2)]
            total = [0.0, 0.0]
            product = 0.0

            def sides():
                for at in (c, c + 2):
                    yield kap[at, pl.ds(r8, TILE)], [xs[f, at, pl.ds(r8, TILE)] for f in range(2)]
                for off in (-1, 1):
                    yield kap[1 + c, pl.ds(r8 + off, TILE)], [xs[f, 1 + c, pl.ds(r8 + off, TILE)] for f in range(2)]
                yield (
                    jnp.where(lane == 0, kzl[c, at_r], roll(k, 1)),
                    [jnp.where(lane == 0, roll(low[f], -c), roll(x[f], 1)) for f in range(2)],
                )
                yield (
                    jnp.where(lane == LANES - 1, kzr[c, at_r], roll(k, -1)),
                    [jnp.where(lane == LANES - 1, roll(high[f], 14 - c), roll(x[f], -1)) for f in range(2)],
                )

            for kn, xn in sides():
                face = k + kn
                differ = [x[f] - xn[f] for f in range(2)]
                product = product + differ[0] * differ[1]
                for f in range(2):
                    total[f] = total[f] + face * differ[f]
            grad[c, at_r] = (-0.5 * TIME_STEP) * product
            state[c, at_r] = x[0]
            adjoint[c, at_r] = x[1]
            previous = stored[c, pl.ds(r, TILE)].astype(F32) * scales[c, at_r]
            residuals[0, c, at_r] = previous - (x[0] + (0.5 * TIME_STEP) * total[0])
            residuals[1, c, at_r] = cot[c, at_r] - (x[1] + (0.5 * TIME_STEP) * total[1])


def call(kernel, outs, smem, vmem, scratch=()):
    vm = pl.BlockSpec(memory_space=pltpu.VMEM)
    sm = pl.BlockSpec(memory_space=pltpu.SMEM)
    return pl.pallas_call(
        kernel,
        out_shape=[jax.ShapeDtypeStruct(shape, F32) for shape in outs],
        in_specs=[sm] * len(smem) + [vm] * len(vmem),
        out_specs=[vm] * len(outs),
        scratch_shapes=[pltpu.VMEM(shape, F32) for shape in scratch],
        compiler_params=pltpu.CompilerParams(vmem_limit_bytes=48 * 1024 * 1024),
    )(*smem, *vmem)


def shifted(x, axis, by):
    count = lax.axis_size(axis)
    return lax.ppermute(x, axis, [(i, (i + by) % count) for i in range(count)])


def around(x, by):
    order = [2 * g for g in range(G)] + [2 * g + 1 for g in reversed(range(G))]
    pairs = [(order[i], order[(i + by) % len(order)]) for i in range(len(order))]
    return lax.ppermute(x, ("gx", "pa"), pairs)


def chebyshev_scalars(upper):
    theta = 0.5 * (upper + 1.0)
    delta = 0.5 * (upper - 1.0)
    sigma = theta / delta
    rho = 1.0 / sigma
    rows = [(1.0 / theta, 0.0 * theta)]
    for _ in range(1, CHEB):
        rho_next = 1.0 / (2.0 * sigma - rho)
        rows.append((rho_next * rho, 2.0 * rho_next / delta))
        rho = rho_next
    return jnp.stack([jnp.stack(row) for row in rows])


def redistributed(conductivity, stored_state, row_scales, cotangent, upper_bound):
    g = lax.axis_index("gx")
    pa = lax.axis_index("pa")

    def strip_of(device):
        return jnp.where(pa == 0, device, G - 1 - device)

    steps = jnp.arange(G, dtype=jnp.int32)
    ahead = lax.rem(g + steps, G)
    behind = lax.rem(g - steps + G, G)
    scalars = chebyshev_scalars(upper_bound[0])
    stored = shifted(stored_state, "pa", 1)
    scales = row_scales[:, :, None]

    kdown = shifted(conductivity[BX - 1], "gx", 1)
    kup = shifted(conductivity[0], "gx", -1)
    kover = shifted(conductivity[:, BY - 1], "gy", 1)
    kunder = shifted(conductivity[:, 0], "gy", -1)
    kends = shifted(jnp.stack((conductivity[:, :, BZ - 1], conductivity[:, :, 0])), "pa", 1)

    strip = strip_of(g)
    left_g = jnp.where(pa == 0, jnp.maximum(g - 1, 0), jnp.minimum(g + 1, G - 1))
    right_g = jnp.where(pa == 0, jnp.minimum(g + 1, G - 1), jnp.maximum(g - 1, 0))
    places = lax.rem(jnp.stack((left_g - g + steps, right_g - g + steps)) + G, G)

    def strips(names, arrays):
        count = len(names)
        pack = functools.partial(pack_kernel, names)
        parts = call(pack, [(count, 2, BY, LANES)] * G, [strip_of(ahead)], arrays)
        parts = [parts[0]] + [shifted(parts[d], "gx", d) for d in range(1, G)]
        edge = (count, G, BY, LANES)
        rim = (count, G, 2, HALO, LANES)
        to_left, to_right, head, tail = call(edge_kernel, [edge, edge, rim, rim], [places], parts)
        from_right, from_left = around(to_left, -1), around(to_right, 1)
        below, above = shifted(head, "gy", -1), shifted(tail, "gy", 1)
        edges = jnp.stack((from_left, from_right))
        below_edge = shifted(edges[:, :, :, :HALO], "gy", -1)
        above_edge = shifted(edges[:, :, :, BY - HALO :], "gy", 1)
        return [*parts, from_left, from_right, above, above_edge, below, below_edge]

    def solve(where, stacks):
        nf = len(where) - 1
        line = (PLANES, 2, ROWS, LANES)
        solved = call(
            functools.partial(solve_kernel, nf, where),
            [(nf, 3, MROWS, LANES)] * G,
            [strip[None], scalars],
            sum(stacks, []),
            [line] * (4 * nf)
            + [(PLANES, 2, TILE, LANES)] * (2 * nf)
            + [line] * 3
            + [(PLANES, ROWS, LANES)] * 2
            + [line],
        )
        return [solved[0]] + [shifted(solved[d], "gx", d) for d in range(1, G)]

    everything = strips(("conductivity", "cotangent", "previous"), [conductivity, cotangent, stored, scales])
    solved = solve(((0, 0), (0, 2), (0, 1)), [everything])
    out = (BX, BY, LANES)
    padded = (BX + 2, BY + 16, LANES)
    return call(
        functools.partial(final_kernel, 1),
        [out, out, out, (2,) + out],
        [strip_of(behind)],
        [*solved, conductivity, kdown, kup, kover, kunder, kends[0][:, :, None], kends[1][:, :, None], stored, scales, cotangent],
        [(2,) + padded, (2, G, BY, LANES), padded],
    )


def body(conductivity, stored_state, row_scales, cotangent, upper_bound):
    strips_fit = (
        lax.axis_size("gx") == G
        and lax.axis_size("pa") == 2
        and conductivity.shape == (BX, BY, BZ)
    )
    run = redistributed if strips_fit else stepwise
    return tuple(run(conductivity, stored_state, row_scales, cotangent, upper_bound))


def solution(mesh):
    return jax.shard_map(
        body,
        mesh=mesh,
        in_specs=(
            P("gx", "gy", "pa"),
            P("gx", "gy", "pa"),
            P("gx", "gy"),
            P("gx", "gy", "pa"),
            P(),
        ),
        out_specs=(
            P("gx", "gy", "pa"),
            P("gx", "gy", "pa"),
            P("gx", "gy", "pa"),
            P(None, "gx", "gy", "pa"),
        ),
        check_vma=False,
    )
```

time: 200 us -> 192 us (0.960)
  Pallas kernels: 80.9 us -> 73.4 us
    pallas_call x4, Pallas kernels: 80.9 us -> 73.4 us  [call(): pl.pallas_call(kernel, out_shape=[jax.ShapeDtypeStruct(shape, F32) for sh...]
  transfers between devices with their start and end apart: 18 -> 18, of which waited for: 11 -> 11; matrix products, arithmetic and copies ran while one was open for 4% -> 4% of each run, Pallas kernels for 35% -> 32%
where the time goes in v3:
time: 192 us
  waiting for transfers between devices  86.4 us (45%)
  Pallas kernels  73.4 us (38%)
  starting transfers between devices  18.6 us (10%)
  local copies, waits for them, and re-layouts  9.8 us (5%)
  between operations  2.84 us (1%)
    pallas_call x4, Pallas kernels, call(): pl.pallas_call(kernel, out_shape=[jax.ShapeDtypeStruct(shape, F32) for sh...  73.4 us
    ppermute x16, waiting for transfers between devices, shifted(): return lax.ppermute(x, axis, [(i, (i + by) % count) for i in range(count)])  70.6 us
    ppermute x16, starting transfers between devices, shifted(): return lax.ppermute(x, axis, [(i, (i + by) % count) for i in range(count)])  17.1 us
    ppermute x2, waiting for transfers between devices, around(): return lax.ppermute(x, ('gx', 'pa'), pairs)  15.9 us
    unnamed x28, local copies, waits for them, and re-layouts  5.89 us
  transfers between devices with their start and end apart: 18, of which 11 were waited for; matrix products, arithmetic and copies ran while one was open for 4% of the time, Pallas kernels for 32%

profile of v3, /device:TPU:8, one launch (start us, length us, event | category | flops | bytes accessed | tf_op | source)
XLA Modules:
  0.0 191.8 jit_solution(7645085479722054016)
XLA Ops:
  0.6 1.6 collective-permute-start
  4.0 5.0 %collective-permute-done.refs_2_.refs_11_ = bf16[8,128,128]{2,1,0:T(8,128)(2,1)S(1)} collective-permute-done((bf16[8,128,128]{2,1,0:T(8,128)(2,1)}, bf16[8,128,128]{2,1,0:T(8,128)(2,1)S(1)}, u32[]{:S(2)}, u32[]{:S(2)}) %collective-permute-start) | collective-permute-done | bytes 262176 | tf_op jit(solution)/shard_map/ppermute | solution.py:495
  10.0 2.9 %shard_map.84 = (f32[3,2,128,128]{3,2,1,0:T(8,128)S(1)}, f32[3,2,128,128]{3,2,1,0:T(8,128)}, f32[3,2,128,128]{3,2,1,0:T(8,128)S(1)}, f32[3,2,128,128]{3,2,1,0:T(8,128)S(1)}) custom-call(s32[4]{0:T(128)S(1)} %broadcast_select_fusion.strips, f32[8,128,128]{2,1,0:T(8,128)S(1)} %copy-done, f32[8,128,128]{2,1,0:T(8,128)S(1)} %copy-done.1, ...), custom_call_target="tpu_custom_call" | custom-call | tf_op jit(solution)/shard_map/pallas_call | solution.py:483
  12.9 1.6 collective-permute-start.1
  15.5 2.0 %collective-permute-start.3 = (f32[3,2,128,128]{3,2,1,0:T(8,128)S(1)}, f32[3,2,128,128]{3,2,1,0:T(8,128)S(1)}, u32[]{:S(2)}, u32[]{:S(2)}) collective-permute-start(f32[3,2,128,128]{3,2,1,0:T(8,128)S(1)} %get-tuple-element.19), channel_id=1, source_target_pairs={{0,24},{8,0},{16,8},{24,16},{1,25},{9,1},{17,9},{25,17},{2,26},{10... | collective-permute-start | bytes 1179656 | tf_op jit(solution)/shard_map/ppermute | solution.py:495
  20.7 1.2 copy.65
  21.9 1.2 copy.64
  23.2 18.0 %collective-permute-done.1.refs_1_ = f32[3,2,128,128]{3,2,1,0:T(8,128)S(1)} collective-permute-done((f32[3,2,128,128]{3,2,1,0:T(8,128)}, f32[3,2,128,128]{3,2,1,0:T(8,128)S(1)}, u32[]{:S(2)}, u32[]{:S(2)}) %collective-permute-start.1) | collective-permute-done | bytes 393248 | tf_op jit(solution)/shard_map/ppermute | solution.py:495
  41.2 6.3 %collective-permute-done.2.refs_2_ = f32[3,2,128,128]{3,2,1,0:T(8,128)S(1)} collective-permute-done((f32[3,2,128,128]{3,2,1,0:T(8,128)S(1)}, f32[3,2,128,128]{3,2,1,0:T(8,128)S(1)}, u32[]{:S(2)}, u32[]{:S(2)}) %collective-permute-start.2) | collective-permute-done | bytes 393248 | tf_op jit(solution)/shard_map/ppermute | solution.py:495
  47.5 1.8 collective-permute-done.3.refs_3_
  49.3 2.2 %shard_map.85 = (f32[3,4,128,128]{3,2,1,0:T(8,128)}, f32[3,4,128,128]{3,2,1,0:T(8,128)}, f32[3,4,2,16,128]{4,3,2,1,0:T(8,128)S(1)}, f32[3,4,2,16,128]{4,3,2,1,0:T(8,128)S(1)}) custom-call(s32[2,4]{1,0:T(2,128)S(1)} %compare_select_fusion.places, f32[3,2,128,128]{3,2,1,0:T(8,128)S(1)} %get-tuple-element.16.refs_0_, ...), custom_call_target="tpu_custom_call" | custom-call | tf_op jit(solution)/shard_map/pallas_call | solution.py:483
  52.2 1.4 collective-permute-start.5
  54.2 1.7 collective-permute-start.8
  56.0 15.3 %collective-permute-done.4.refs_4_ = f32[3,4,128,128]{3,2,1,0:T(8,128)S(1)} collective-permute-done((f32[3,4,128,128]{3,2,1,0:T(8,128)}, f32[3,4,128,128]{3,2,1,0:T(8,128)S(1)}, u32[]{:S(2)}, u32[]{:S(2)}) %collective-permute-start.4) | collective-permute-done | bytes 786464 | tf_op jit(solution)/shard_map/ppermute | solution.py:501
  71.9 1.7 collective-permute-start.9
  74.3 3.0 %collective-permute-done.7.refs_7_ = f32[2,3,4,16,128]{4,3,2,1,0:T(8,128)S(1)} collective-permute-done((f32[2,3,4,16,128]{4,3,2,1,0:T(8,128)S(1)}, f32[2,3,4,16,128]{4,3,2,1,0:T(8,128)S(1)}, u32[]{:S(2)}, u32[]{:S(2)}) %collective-permute-start.7) | collective-permute-done | bytes 196640 | tf_op jit(solution)/shard_map/ppermute | solution.py:495
  78.1 56.7 %shard_map.86 = (f32[2,3,136,128]{3,2,1,0:T(8,128)S(1)}, f32[2,3,136,128]{3,2,1,0:T(8,128)}, f32[2,3,136,128]{3,2,1,0:T(8,128)}, f32[2,3,136,128]{3,2,1,0:T(8,128)}) custom-call(s32[1]{0:T(128)} %bitcast.strip, f32[16,2]{1,0:T(8,128)S(1)} %stack.273.scalars, f32[3,2,128,128]{3,2,1,0:T(8,128)S(1)} %get-tuple-element.16.refs_0_, ...), custom_call_target="tpu_custom_call" | custom-call | tf_op jit(solution)/shard_map/pallas_call | solution.py:483
  135.6 3.5 %collective-permute-start.11 = (f32[2,3,136,128]{3,2,1,0:T(8,128)}, f32[2,3,136,128]{3,2,1,0:T(8,128)}, u32[]{:S(2)}, u32[]{:S(2)}) collective-permute-start(f32[2,3,136,128]{3,2,1,0:T(8,128)} %get-tuple-element.26), channel_id=1, source_target_pairs={{0,16},{8,24},{16,0},{24,8},{1,17},{9,25},{17,1},{25,9},{2,18},{10... | collective-permute-start | bytes 1253384 | tf_op jit(solution)/shard_map/ppermute | solution.py:495
  140.0 1.5 collective-permute-start.13
  141.4 1.3 collective-permute-done.17
  142.8 1.5 collective-permute-start.14
  144.7 30.8 %collective-permute-done.13.refs_5_ = f32[128,128]{1,0:T(8,128)S(1)} collective-permute-done((f32[128,128]{1,0:T(8,128)}, f32[128,128]{1,0:T(8,128)S(1)}, u32[]{:S(2)}, u32[]{:S(2)}) %collective-permute-start.13) | collective-permute-done | bytes 65568 | tf_op jit(solution)/shard_map/ppermute | solution.py:495
  175.5 3.6 %collective-permute-done.14.refs_6_ = f32[128,128]{1,0:T(8,128)S(1)} collective-permute-done((f32[128,128]{1,0:T(8,128)S(1)}, f32[128,128]{1,0:T(8,128)S(1)}, u32[]{:S(2)}, u32[]{:S(2)}) %collective-permute-start.14) | collective-permute-done | bytes 65568 | tf_op jit(solution)/shard_map/ppermute | solution.py:495
  180.1 11.6 %shard_map.87 = (f32[8,128,128]{2,1,0:T(8,128)}, f32[8,128,128]{2,1,0:T(8,128)}, f32[8,128,128]{2,1,0:T(8,128)}, f32[2,8,128,128]{3,2,1,0:T(8,128)}) custom-call(s32[4]{0:T(128)S(1)} %broadcast_select_fusion.1.strips, f32[2,3,136,128]{3,2,1,0:T(8,128)S(1)} %copy-done.10, f32[2,3,136,128]{3,2,1,0:T(8,128)S(1)} %collective-permute-done.10.refs_1_, ...), custom_call_target="tpu_custom_call" | custom-call | tf_op jit(solution)/shard_map/pallas_call | solution.py:483
  (66 shorter events, 11.6 us)
Async XLA Ops:
  0.6 8.3 %copy-start = (f32[8,128,128]{2,1,0:T(8,128)S(1)}, f32[8,128,128]{2,1,0:T(8,128)}, u32[]{:S(2)}) copy-start(f32[8,128,128]{2,1,0:T(8,128)} %refs_4_.1) | copy-start | bytes 1572868
  0.6 8.3 %collective-permute-start = (bf16[8,128,128]{2,1,0:T(8,128)(2,1)}, bf16[8,128,128]{2,1,0:T(8,128)(2,1)S(1)}, u32[]{:S(2)}, u32[]{:S(2)}) collective-permute-start(bf16[8,128,128]{2,1,0:T(8,128)(2,1)} %param.6), channel_id=1, source_target_pairs={{0,1},{1,0},{2,3},{3,2},{4,5},{5,4},{6,7},{7,6},{8,9},{9,8},{10,11... | collective-permute-start | bytes 786440 | tf_op jit(solution)/shard_map/ppermute | solution.py:495
  3.0 136.1 %collective-permute-start.15 = (f32[8,128]{1,0:T(8,128)S(1)}, f32[8,128]{1,0:T(8,128)S(1)}, u32[]{:S(2)}, u32[]{:S(2)}) collective-permute-start(f32[8,128]{1,0:T(8,128)S(1)} %bitcast.91), channel_id=1, source_target_pairs={{0,2},{2,4},{4,6},{6,0},{1,3},{3,5},{5,7},{7,1},{8,10},{10,12},{12... | collective-permute-start | bytes 12296 | tf_op jit(solution)/shard_map/ppermute | solution.py:495
  12.9 28.3 %collective-permute-start.1 = (f32[3,2,128,128]{3,2,1,0:T(8,128)}, f32[3,2,128,128]{3,2,1,0:T(8,128)S(1)}, u32[]{:S(2)}, u32[]{:S(2)}) collective-permute-start(f32[3,2,128,128]{3,2,1,0:T(8,128)} %get-tuple-element.17), channel_id=1, source_target_pairs={{0,8},{8,16},{16,24},{24,0},{1,9},{9,17},{17,25},{25,1},{2,10},{10... | collective-permute-start | bytes 1179656 | tf_op jit(solution)/shard_map/ppermute | solution.py:495
  14.5 33.0 %collective-permute-start.2 = (f32[3,2,128,128]{3,2,1,0:T(8,128)S(1)}, f32[3,2,128,128]{3,2,1,0:T(8,128)S(1)}, u32[]{:S(2)}, u32[]{:S(2)}) collective-permute-start(f32[3,2,128,128]{3,2,1,0:T(8,128)S(1)} %get-tuple-element.18), channel_id=1, source_target_pairs={{0,16},{8,24},{16,0},{24,8},{1,17},{9,25},{17,1},{25,9},{2,18},{10... | collective-permute-start | bytes 1179656 | tf_op jit(solution)/shard_map/ppermute | solution.py:495
  15.5 33.8 %collective-permute-start.3 = (f32[3,2,128,128]{3,2,1,0:T(8,128)S(1)}, f32[3,2,128,128]{3,2,1,0:T(8,128)S(1)}, u32[]{:S(2)}, u32[]{:S(2)}) collective-permute-start(f32[3,2,128,128]{3,2,1,0:T(8,128)S(1)} %get-tuple-element.19), channel_id=1, source_target_pairs={{0,24},{8,0},{16,8},{24,16},{1,25},{9,1},{17,9},{25,17},{2,26},{10... | collective-permute-start | bytes 1179656 | tf_op jit(solution)/shard_map/ppermute | solution.py:495
  47.5 4.0 %copy-start.3 = (f32[3,2,128,128]{3,2,1,0:T(8,128)}, f32[3,2,128,128]{3,2,1,0:T(8,128)S(1)}, u32[]{:S(2)}) copy-start(f32[3,2,128,128]{3,2,1,0:T(8,128)S(1)} %collective-permute-done.2.refs_2_) | copy-start | bytes 1179652
  51.5 19.7 %collective-permute-start.4 = (f32[3,4,128,128]{3,2,1,0:T(8,128)}, f32[3,4,128,128]{3,2,1,0:T(8,128)S(1)}, u32[]{:S(2)}, u32[]{:S(2)}) collective-permute-start(f32[3,4,128,128]{3,2,1,0:T(8,128)} %get-tuple-element.20), channel_id=1, source_target_pairs={{0,8},{8,16},{16,24},{24,25},{25,17},{17,9},{9,1},{1,0},{2,10},{10... | collective-permute-start | bytes 2359304 | tf_op jit(solution)/shard_map/ppermute | solution.py:501
  52.2 19.7 %collective-permute-start.5 = (f32[3,4,128,128]{3,2,1,0:T(8,128)}, f32[3,4,128,128]{3,2,1,0:T(8,128)S(1)}, u32[]{:S(2)}, u32[]{:S(2)}) collective-permute-start(f32[3,4,128,128]{3,2,1,0:T(8,128)} %get-tuple-element.21), channel_id=1, source_target_pairs={{0,1},{8,0},{16,8},{24,16},{25,24},{17,25},{9,17},{1,9},{2,3},{10,... | collective-permute-start | bytes 2359304 | tf_op jit(solution)/shard_map/ppermute | solution.py:501
  54.2 20.1 %collective-permute-start.6 = (f32[3,4,2,16,128]{4,3,2,1,0:T(8,128)}, f32[3,4,2,16,128]{4,3,2,1,0:T(8,128)S(1)}, u32[]{:S(2)}, u32[]{:S(2)}) collective-permute-start(f32[3,4,2,16,128]{4,3,2,1,0:T(8,128)} %copy-done.12), channel_id=1, source_target_pairs={{0,2},{2,4},{4,6},{6,0},{1,3},{3,5},{5,7},{7,1},{8,10},{10,12},{12... | collective-permute-start | bytes 589832 | tf_op jit(solution)/shard_map/ppermute | solution.py:495
  54.2 20.1 %collective-permute-start.8 = (f32[3,4,2,16,128]{4,3,2,1,0:T(8,128)}, f32[3,4,2,16,128]{4,3,2,1,0:T(8,128)S(1)}, u32[]{:S(2)}, u32[]{:S(2)}) collective-permute-start(f32[3,4,2,16,128]{4,3,2,1,0:T(8,128)} %copy-done.11), channel_id=1, source_target_pairs={{0,6},{2,0},{4,2},{6,4},{1,7},{3,1},{5,3},{7,5},{8,14},{10,8},{12,... | collective-permute-start | bytes 589832 | tf_op jit(solution)/shard_map/ppermute | solution.py:495
  71.8 6.3 %copy-start.4 = (f32[3,2,128,128]{3,2,1,0:T(8,128)S(1)}, f32[3,2,128,128]{3,2,1,0:T(8,128)}, u32[]{:S(2)}) copy-start(f32[3,2,128,128]{3,2,1,0:T(8,128)} %copy-done.3) | copy-start | bytes 1179652
  71.8 6.3 %copy-start.6 = (f32[3,2,128,128]{3,2,1,0:T(8,128)S(1)}, f32[3,2,128,128]{3,2,1,0:T(8,128)}, u32[]{:S(2)}) copy-start(f32[3,2,128,128]{3,2,1,0:T(8,128)} %copy-done.5) | copy-start | bytes 1179652
  71.9 5.4 %collective-permute-start.7 = (f32[2,3,4,16,128]{4,3,2,1,0:T(8,128)S(1)}, f32[2,3,4,16,128]{4,3,2,1,0:T(8,128)S(1)}, u32[]{:S(2)}, u32[]{:S(2)}) collective-permute-start(f32[2,3,4,16,128]{4,3,2,1,0:T(8,128)S(1)} %get-tuple-element.29), channel_id=1, source_target_pairs={{0,2},{2,4},{4,6},{6,0},{1,3},{3,5},{5,7},{7,1},{8,10},{10,12},{12... | collective-permute-start | bytes 589832 | tf_op jit(solution)/shard_map/ppermute | solution.py:495
  71.9 6.2 %collective-permute-start.9 = (f32[2,3,4,16,128]{4,3,2,1,0:T(8,128)S(1)}, f32[2,3,4,16,128]{4,3,2,1,0:T(8,128)S(1)}, u32[]{:S(2)}, u32[]{:S(2)}) collective-permute-start(f32[2,3,4,16,128]{4,3,2,1,0:T(8,128)S(1)} %get-tuple-element.28), channel_id=1, source_target_pairs={{0,6},{2,0},{4,2},{6,4},{1,7},{3,1},{5,3},{7,5},{8,14},{10,8},{12,... | collective-permute-start | bytes 589832 | tf_op jit(solution)/shard_map/ppermute | solution.py:495
  74.3 65.7 %collective-permute-start.16 = (f32[8,128]{1,0:T(8,128)S(1)}, f32[8,128]{1,0:T(8,128)S(1)}, u32[]{:S(2)}, u32[]{:S(2)}) collective-permute-start(f32[8,128]{1,0:T(8,128)S(1)} %bitcast.90), channel_id=1, source_target_pairs={{0,6},{2,0},{4,2},{6,4},{1,7},{3,1},{5,3},{7,5},{8,14},{10,8},{12,... | collective-permute-start | bytes 12296 | tf_op jit(solution)/shard_map/ppermute | solution.py:495
  135.5 43.5 %collective-permute-start.10 = (f32[2,3,136,128]{3,2,1,0:T(8,128)}, f32[2,3,136,128]{3,2,1,0:T(8,128)S(1)}, u32[]{:S(2)}, u32[]{:S(2)}) collective-permute-start(f32[2,3,136,128]{3,2,1,0:T(8,128)} %get-tuple-element.25), channel_id=1, source_target_pairs={{0,8},{8,16},{16,24},{24,0},{1,9},{9,17},{17,25},{25,1},{2,10},{10... | collective-permute-start | bytes 1253384 | tf_op jit(solution)/shard_map/ppermute | solution.py:495
  135.6 43.5 %collective-permute-start.11 = (f32[2,3,136,128]{3,2,1,0:T(8,128)}, f32[2,3,136,128]{3,2,1,0:T(8,128)}, u32[]{:S(2)}, u32[]{:S(2)}) collective-permute-start(f32[2,3,136,128]{3,2,1,0:T(8,128)} %get-tuple-element.26), channel_id=1, source_target_pairs={{0,16},{8,24},{16,0},{24,8},{1,17},{9,25},{17,1},{25,9},{2,18},{10... | collective-permute-start | bytes 1253384 | tf_op jit(solution)/shard_map/ppermute | solution.py:495
  139.0 40.1 %collective-permute-start.12 = (f32[2,3,136,128]{3,2,1,0:T(8,128)}, f32[2,3,136,128]{3,2,1,0:T(8,128)}, u32[]{:S(2)}, u32[]{:S(2)}) collective-permute-start(f32[2,3,136,128]{3,2,1,0:T(8,128)} %get-tuple-element.27), channel_id=1, source_target_pairs={{0,24},{8,0},{16,8},{24,16},{1,25},{9,1},{17,9},{25,17},{2,26},{10... | collective-permute-start | bytes 1253384 | tf_op jit(solution)/shard_map/ppermute | solution.py:495
  139.1 3.7 %collective-permute-start.17 = (f32[2,8,128]{2,1,0:T(8,128)S(1)}, f32[2,8,128]{2,1,0:T(8,128)S(1)}, u32[]{:S(2)}, u32[]{:S(2)}) collective-permute-start(f32[2,8,128]{2,1,0:T(8,128)S(1)} %pad_maximum_fusion.2), channel_id=1, source_target_pairs={{0,1},{1,0},{2,3},{3,2},{4,5},{5,4},{6,7},{7,6},{8,9},{9,8},{10,11... | collective-permute-start | bytes 24584 | tf_op jit(solution)/shard_map/ppermute | solution.py:495
  140.0 35.5 %collective-permute-start.13 = (f32[128,128]{1,0:T(8,128)}, f32[128,128]{1,0:T(8,128)S(1)}, u32[]{:S(2)}, u32[]{:S(2)}) collective-permute-start(f32[128,128]{1,0:T(8,128)} %get-tuple-element.35), channel_id=1, source_target_pairs={{0,8},{8,16},{16,24},{24,0},{1,9},{9,17},{17,25},{25,1},{2,10},{10... | collective-permute-start | bytes 196616 | tf_op jit(solution)/shard_map/ppermute | solution.py:495
  142.8 36.3 %collective-permute-start.14 = (f32[128,128]{1,0:T(8,128)S(1)}, f32[128,128]{1,0:T(8,128)S(1)}, u32[]{:S(2)}, u32[]{:S(2)}) collective-permute-start(f32[128,128]{1,0:T(8,128)S(1)} %get-tuple-element.34), channel_id=1, source_target_pairs={{0,24},{8,0},{16,8},{24,16},{1,25},{9,1},{17,9},{25,17},{2,26},{10... | collective-permute-start | bytes 196616 | tf_op jit(solution)/shard_map/ppermute | solution.py:495
  144.2 34.9 %copy-start.2 = (f32[8,128,128]{2,1,0:T(8,128)S(1)}, f32[8,128,128]{2,1,0:T(8,128)}, u32[]{:S(2)}) copy-start(f32[8,128,128]{2,1,0:T(8,128)} %refs_13_.1) | copy-start | bytes 1572868
  144.5 34.7 %copy-start.8 = (bf16[8,128,128]{2,1,0:T(8,128)(2,1)S(1)}, bf16[8,128,128]{2,1,0:T(8,128)(2,1)}, u32[]{:S(2)}) copy-start(bf16[8,128,128]{2,1,0:T(8,128)(2,1)} %copy-done.7) | copy-start | bytes 786436
  (7 other events, 11.2 us)

commit v4 on v3

--- a/solution.py
+++ b/solution.py
@@ -92,6 +92,7 @@
 ROWS = BY + 2 * TOP
 MROWS = BY + 8
 TILE = 8
+CHUNK = 32
 
 BLOCK = (0, 3, 2, 1)
 PLANES = BX
@@ -119,40 +120,54 @@
     dst = lax.broadcasted_iota(jnp.int32, (LANES, LANES), 0 if transposed else 1)
     within = lax.rem(src, STRIP)
     place = src - within + 16 * lax.rem(within, 2) + within // 2
-    return jnp.where(place == dst, 1.0, 0.0).astype(F32)
+    return jnp.where(place == dst, 1.0, 0.0).astype(jnp.bfloat16)
 
 
 def reorder(x, order):
-    return jnp.dot(x, order, precision=lax.Precision.HIGHEST, preferred_element_type=F32)
+    if x.dtype == jnp.bfloat16:
+        return jnp.dot(x, order, preferred_element_type=F32)
+    high = x.astype(jnp.bfloat16)
+    rest = x - high.astype(F32)
+    middle = rest.astype(jnp.bfloat16)
+    low = (rest - middle.astype(F32)).astype(jnp.bfloat16)
+    return (
+        jnp.dot(high, order, preferred_element_type=F32)
+        + jnp.dot(middle, order, preferred_element_type=F32)
+        + jnp.dot(low, order, preferred_element_type=F32)
+    )
 
 
 def pack_kernel(names, strips, *refs):
     ins, outs = refs[: len(refs) - G], refs[len(refs) - G :]
     order = parity_order(False)
     groups = [lanes_of(BY, strips[d])[0] for d in range(G)]
-    for a in range(2):
-        for n, name in enumerate(names):
+    for n, name in enumerate(names):
+        for a in range(2):
+            planes = reorder(ins[n][4 * a : 4 * a + 4].reshape(4 * BY, LANES), order)
             parts = []
             for b in range(4):
-                c = 4 * a + b
+                plane = planes[BY * b : BY * (b + 1)]
                 if name == "previous":
-                    plane = ins[n][c].astype(F32) * ins[n + 1][c]
-                else:
-                    plane = ins[n][c]
-                parts.append(roll(reorder(plane, order), 32 * b))
+                    plane = plane * ins[n + 1][4 * a + b]
+                parts.append(roll(plane, 32 * b))
             for d in range(G):
                 outs[d][n, a] = pick(groups[d], parts)
 
 
 def edge_kernel(places, *refs):
-    msgs, (to_left, to_right, head, tail) = refs[:G], refs[G:]
+    msgs, (to_left, to_right, head, tail) = refs[:G], refs[G : G + 4]
+    corners = refs[G + 4 :]
     lane = lax.broadcasted_iota(jnp.int32, (BY, LANES), 1)
     low = lax.rem(lane, 16) < 8
+    rows = (slice(BY - HALO, BY), slice(0, HALO))
     for n in range(msgs[0].shape[0]):
         for d in range(G):
             first, second = msgs[d][n, 0], msgs[d][n, 1]
-            to_left[n, places[0, d]] = jnp.where(low, first, roll(second, 8))
-            to_right[n, places[1, d]] = jnp.where(low, roll(second, -8), first)
+            edges = (jnp.where(low, first, roll(second, 8)), jnp.where(low, roll(second, -8), first))
+            for side, out in enumerate((to_left, to_right)):
+                out[n, places[side, d]] = edges[side]
+                for way in range(2):
+                    corners[2 * side + way][n, places[side, d]] = edges[side][rows[way]]
             for a in range(2):
                 head[n, d, a] = msgs[d][n, a, :HALO]
                 tail[n, d, a] = msgs[d][n, a, BY - HALO :]
@@ -181,50 +196,47 @@
 def solve_kernel(nf, where, strip, scalars, *refs):
     stacks = []
     for _ in range(1 + max(stack for stack, _ in where)):
-        stacks.append((refs[:G],) + tuple(refs[G : G + 6]))
-        refs = refs[G + 6 :]
+        stacks.append((refs[:G],) + tuple(refs[G : G + 8]))
+        refs = refs[G + 8 :]
     outs = refs[:G]
     refs = refs[G:]
-    xa, xb, xc, rhs, stage_a, stage_b = (refs[nf * j : nf * (j + 1)] for j in range(6))
-    kap, kx, ky, kin, kout, diag = refs[6 * nf :]
+    xa, xb, xc, rhs, turned = (refs[nf * j : nf * (j + 1)] for j in range(5))
+    kap, kx, ky, kin, kout, diag = refs[5 * nf :]
     zero = jnp.zeros((TILE, LANES), F32)
-    group, within = lanes_of(TILE, strip[0])
     targets = (kap,) + tuple(rhs)
 
-    def put_at(dst, to):
+    def put_at(dst, to, rows):
         def put(i, e, val):
-            dst[i, e, pl.ds(to, TILE)] = val
+            dst[i, e, pl.ds(to, rows)] = val
 
         return put
 
-    @pl.loop(0, BY // TILE)
+    @pl.loop(0, BY // CHUNK)
     def _(t):
-        r = pl.multiple_of(TILE * t, TILE)
-        to = pl.multiple_of(TOP + TILE * t, TILE)
+        r = pl.multiple_of(CHUNK * t, CHUNK)
+        to = pl.multiple_of(TOP + CHUNK * t, TILE)
+        group, within = lanes_of(CHUNK, strip[0])
         for dst, (stack, n) in zip(targets, where):
-            bricks, from_left, from_right = stacks[stack][:3]
-            sides = (from_left, from_right)
+            bricks, *sides = stacks[stack][:3]
             unpack(
-                lambda d, a: bricks[d][n, a, pl.ds(r, TILE)],
-                lambda side, d: sides[side][n, d, pl.ds(r, TILE)],
+                lambda d, a: bricks[d][n, a, pl.ds(r, CHUNK)],
+                lambda side, d: sides[side][n, d, pl.ds(r, CHUNK)],
                 group,
                 within,
-                put_at(dst, to),
+                put_at(dst, to, CHUNK),
             )
 
-    @pl.loop(0, HALO // TILE)
-    def _(t):
-        r = pl.multiple_of(TILE * t, TILE)
-        for dst, (stack, n) in zip(targets, where):
-            above, above_edge, below, below_edge = stacks[stack][3:]
-            for brick, edge, start in ((above, above_edge, TOP - HALO), (below, below_edge, TOP + BY)):
-                unpack(
-                    lambda d, a: brick[n, d, a, pl.ds(r, TILE)],
-                    lambda side, d: edge[side, n, d, pl.ds(r, TILE)],
-                    group,
-                    within,
-                    put_at(dst, pl.multiple_of(start + TILE * t, TILE)),
-                )
+    for dst, (stack, n) in zip(targets, where):
+        above, below, *corners = stacks[stack][3:]
+        group_halo, within_halo = lanes_of(HALO, strip[0])
+        for brick, edge, start in ((above, corners[:2], TOP - HALO), (below, corners[2:], TOP + BY)):
+            unpack(
+                lambda d, a: brick[n, d, a],
+                lambda side, d: edge[side][n, d],
+                group_halo,
+                within_halo,
+                put_at(dst, start, HALO),
+            )
 
     for i in range(PLANES):
         for e in range(2):
@@ -235,89 +247,95 @@
             dst[i, 0:TILE] = zero
             dst[i, ROWS - TILE : ROWS] = zero
 
-    @pl.loop(0, ROWS // TILE - 2)
+    theta_inv = scalars[0, 0]
+
+    @pl.loop(0, (ROWS // TILE - 2) // 2)
     def _(t):
-        r = pl.multiple_of(TILE + TILE * t, TILE)
-        now = [kap[0, e, pl.ds(r, TILE)] for e in range(2)]
-        wrapped = [roll(k, -32) for k in now]
+        rows = 2 * TILE
+        r = pl.multiple_of(TILE + rows * t, TILE)
+        at = pl.ds(r, rows)
+        first = [kap[0, e, at] for e in range(2)]
+        now = first
+        before = [4.0 * (k + roll(kap[PLANES - 1, e, at], 32)) for e, k in enumerate(first)]
         for i in range(PLANES):
-            after = [kap[i + 1, e, pl.ds(r, TILE)] for e in range(2)] if i + 1 < PLANES else wrapped
+            after = [kap[i + 1, e, at] if i + 1 < PLANES else roll(first[e], -32) for e in range(2)]
+            inner = 4.0 * (now[0] + now[1])
+            outer = 4.0 * (now[1] + roll(now[0], -1))
+            outer_before = 4.0 * (now[0] + roll(now[1], 1))
+            kin[i, at] = inner
+            kout[i, at] = outer
+            along = (inner + outer_before, inner + outer)
             for e in range(2):
-                kx[i, e, pl.ds(r, TILE)] = 4.0 * (now[e] + after[e])
-                ky[i, e, pl.ds(r, TILE)] = 4.0 * (now[e] + kap[i, e, pl.ds(r + 1, TILE)])
-            kin[i, pl.ds(r, TILE)] = 4.0 * (now[0] + now[1])
-            kout[i, pl.ds(r, TILE)] = 4.0 * (now[1] + roll(now[0], -1))
+                fx = 4.0 * (now[e] + after[e])
+                fy = 4.0 * (now[e] + kap[i, e, pl.ds(r + 1, rows)])
+                fym = 4.0 * (now[e] + kap[i, e, pl.ds(r - 1, rows)])
+                kx[i, e, at] = fx
+                ky[i, e, at] = fy
+                diag[i, e, at] = 1.0 + (fx + before[e] + (fy + fym) + along[e])
+                before[e] = fx
+                for f in range(nf):
+                    xb[f][i, e, at] = rhs[f][i, e, at] * theta_inv
+                    xa[f][i, e, at] = jnp.zeros((rows, LANES), F32)
             now = after
 
-    theta_inv = scalars[0, 0]
-
-    @pl.loop(0, ROWS // TILE - 2)
-    def _(t):
-        r = pl.multiple_of(TILE + TILE * t, TILE)
-        before = [roll(kx[PLANES - 1, e, pl.ds(r, TILE)], 32) for e in range(2)]
+    def turn_lanes(cur, r):
+        for f in range(nf):
+            for i in range(PLANES):
+                outer = kout[i, pl.ds(r, TILE)]
+                turned[f][i, 0] = roll(outer * cur[f][i, 1, pl.ds(r, TILE)], 1)
+                turned[f][i, 1] = roll(cur[f][i, 0, pl.ds(r, TILE)], -1)
+            for e in range(2):
+                last = kx[PLANES - 1, e, pl.ds(r, TILE)] * cur[f][PLANES - 1, e, pl.ds(r, TILE)]
+                turned[f][PLANES, e] = roll(last, 32)
+                turned[f][PLANES + 1, e] = roll(cur[f][0, e, pl.ds(r, TILE)], -32)
+
+    def advance(alpha, beta, old, cur, new, r):
+        now = [[cur[f][0, e, pl.ds(r, TILE)] for e in range(2)] for f in range(nf)]
+        before = [None] * nf
+        fbefore = None
         for i in range(PLANES):
+            fx = [kx[i, e, pl.ds(r, TILE)] for e in range(2)]
+            fy = [ky[i, e, pl.ds(r, TILE)] for e in range(2)]
+            fym = [ky[i, e, pl.ds(r - 1, TILE)] for e in range(2)]
             inner = kin[i, pl.ds(r, TILE)]
             outer = kout[i, pl.ds(r, TILE)]
-            along = (inner + roll(outer, 1), inner + outer)
-            for e in range(2):
-                fx = kx[i, e, pl.ds(r, TILE)]
-                total = fx + before[e] + ky[i, e, pl.ds(r, TILE)] + ky[i, e, pl.ds(r - 1, TILE)]
-                diag[i, e, pl.ds(r, TILE)] = 1.0 + (total + along[e])
-                before[e] = fx
-                for f in range(nf):
-                    xb[f][i, e, pl.ds(r, TILE)] = rhs[f][i, e, pl.ds(r, TILE)] * theta_inv
-                    xa[f][i, e, pl.ds(r, TILE)] = zero
-
-    def along_lanes(cur, stage, r):
-        for i in range(PLANES):
-            inner = kin[i, pl.ds(r, TILE)]
-            outer = kout[i, pl.ds(r, TILE)]
+            centre = [(1.0 + alpha) - beta * diag[i, e, pl.ds(r, TILE)] for e in range(2)]
             for f in range(nf):
-                even, odd = (cur[f][i, e, pl.ds(r, TILE)] for e in range(2))
-                stage[f][i, 0] = (inner * odd + roll(outer * odd, 1)) + rhs[f][i, 0, pl.ds(r, TILE)]
-                stage[f][i, 1] = (inner * even + outer * roll(even, -1)) + rhs[f][i, 1, pl.ds(r, TILE)]
-
-    def advance(alpha, beta, old, cur, new, stage, r):
-        for e in range(2):
-            now = [cur[f][0, e, pl.ds(r, TILE)] for f in range(nf)]
-            wrapped = [roll(x, -32) for x in now]
-            before = [roll(cur[f][PLANES - 1, e, pl.ds(r, TILE)], 32) for f in range(nf)]
-            fbefore = roll(kx[PLANES - 1, e, pl.ds(r, TILE)], 32)
-            for i in range(PLANES):
-                fx = kx[i, e, pl.ds(r, TILE)]
-                fy = ky[i, e, pl.ds(r, TILE)]
-                fym = ky[i, e, pl.ds(r - 1, TILE)]
-                centre = (1.0 + alpha) - beta * diag[i, e, pl.ds(r, TILE)]
-                for f in range(nf):
-                    x = now[f]
-                    after = cur[f][i + 1, e, pl.ds(r, TILE)] if i + 1 < PLANES else wrapped[f]
-                    near = fx * after + fbefore * before[f]
-                    near = near + (fy * cur[f][i, e, pl.ds(r + 1, TILE)] + fym * cur[f][i, e, pl.ds(r - 1, TILE)])
-                    near = near + stage[f][i, e]
-                    new[f][i, e, pl.ds(r, TILE)] = centre * x - alpha * old[f][i, e, pl.ds(r, TILE)] + beta * near
-                    before[f] = x
-                    now[f] = after
-                fbefore = fx
+                if i + 1 < PLANES:
+                    after = [cur[f][i + 1, e, pl.ds(r, TILE)] for e in range(2)]
+                else:
+                    after = [turned[f][PLANES + 1, e] for e in range(2)]
+                for e in range(2):
+                    x = now[f][e]
+                    near = fy[e] * cur[f][i, e, pl.ds(r + 1, TILE)] + fym[e] * cur[f][i, e, pl.ds(r - 1, TILE)]
+                    side = turned[f][i, e]
+                    near = near + (inner * now[f][1 - e] + (outer * side if e else side))
+                    behind = fbefore[e] * before[f][e] if i else turned[f][PLANES, e]
+                    near = near + (fx[e] * after[e] + behind)
+                    near = near + rhs[f][i, e, pl.ds(r, TILE)]
+                    new[f][i, e, pl.ds(r, TILE)] = centre[e] * x - alpha * old[f][i, e, pl.ds(r, TILE)] + beta * near
+                before[f] = now[f]
+                now[f] = after
+            fbefore = fx
 
     def sweep(k, old, cur, new, span):
         alpha, beta = scalars[k, 0], scalars[k, 1]
-        along_lanes(cur, stage_a, span[0])
-
-        @pl.loop(0, span[1] // 2)
+        turn_lanes(cur, span[0])
+
+        @pl.loop(0, span[1] // span[2])
         def _(t):
-            r = pl.multiple_of(span[0] + 2 * TILE * t, TILE)
-            along_lanes(cur, stage_b, r + TILE)
-            advance(alpha, beta, old, cur, new, stage_a, r)
-            along_lanes(cur, stage_a, r + 2 * TILE)
-            advance(alpha, beta, old, cur, new, stage_b, r + TILE)
+            for u in range(span[2]):
+                r = pl.multiple_of(span[0] + TILE * (span[2] * t + u), TILE)
+                advance(alpha, beta, old, cur, new, r)
+                turn_lanes(cur, r + TILE)
 
     def three(k, spans):
         sweep(k, xa, xb, xc, spans[0])
         sweep(k + 1, xb, xc, xa, spans[1])
         sweep(k + 2, xc, xa, xb, spans[2])
 
-    wide = (TILE, ROWS // TILE - 2)
-    narrow = (2 * TILE, ROWS // TILE - 4)
+    wide = (TILE, ROWS // TILE - 2, 4)
+    narrow = (2 * TILE, ROWS // TILE - 4, 3)
 
     @pl.loop(0, 2)
     def _(m):
@@ -329,43 +347,28 @@
     def _(m):
         three(10 + 3 * m, (narrow,) * 3)
 
-    def near_edge(width):
-        below = lax.rem(within + 1, STRIP) < width
-        return below | ((within >= 16) & (within < 16 + width))
-
-    masks = [near_edge(1), near_edge(2), near_edge(4)]
-
-    def pieces(f, row):
-        out = []
-        for i in range(PLANES):
-            even, odd = (xb[f][i, e, pl.ds(row, TILE)] for e in range(2))
-            out.append(jnp.where(within < 16, even, roll(odd, 16)))
-        return out
-
-    def main_rows(parts):
-        parts = [roll(parts[i], 32 * (i % 4)) for i in range(PLANES)]
-        return [[pick(group, [parts[4 * a + (q - d) % G] for q in range(G)]) for a in range(2)] for d in range(G)]
-
-    def side_rows(f, parts, row):
-        tree = [
-            jnp.where(within == 31, xb[f][i, 1, pl.ds(row, TILE)], xb[f][i, 0, pl.ds(row, TILE)])
-            for i in range(PLANES)
-        ]
+    def give(f, row, rows):
+        group, within = lanes_of(rows, strip[0])
+        at = pl.ds(row, rows)
+        whole = [[xb[f][i, e, at] for e in range(2)] for i in range(PLANES)]
+        parts = [jnp.where(within < 16, even, roll(odd, 16)) for even, odd in whole]
+        turned = [roll(parts[i], 32 * (i % 4)) for i in range(PLANES)]
+        mains = [[pick(group, [turned[4 * a + (q - d) % G] for q in range(G)]) for a in range(2)] for d in range(G)]
+        tree = [jnp.where(within == 31, odd, even) for even, odd in whole]
         for level in range(3):
-            tree = [
-                jnp.where(masks[level], tree[j], roll(tree[j + 1], 1 << level)) for j in range(0, len(tree), 2)
-            ]
+            width = 1 << level
+            keep = (lax.rem(within + 1, STRIP) < width) | ((within >= 16) & (within < 16 + width))
+            tree = [jnp.where(keep, tree[j], roll(tree[j + 1], width)) for j in range(0, len(tree), 2)]
         ends = roll(tree[0], 1)
         groups = (ends, ends, roll(parts[PLANES - 1], 96), roll(parts[0], 64))
-        return [pick(group, [groups[(q - d) % G] for q in range(G)]) for d in range(G)]
-
-    @pl.loop(0, BY // TILE)
+        sides = [pick(group, [groups[(q - d) % G] for q in range(G)]) for d in range(G)]
+        return mains, sides
+
+    @pl.loop(0, BY // CHUNK)
     def _(t):
-        row = pl.multiple_of(TOP + TILE * t, TILE)
-        to = pl.ds(pl.multiple_of(TILE * t, TILE), TILE)
+        to = pl.ds(pl.multiple_of(CHUNK * t, CHUNK), CHUNK)
         for f in range(nf):
-            parts = pieces(f, row)
-            mains, sides = main_rows(parts), side_rows(f, parts, row)
+            mains, sides = give(f, pl.multiple_of(TOP + CHUNK * t, TILE), CHUNK)
             for d in range(G):
                 for a in range(2):
                     outs[d][f, a, to] = mains[d][a]
@@ -373,7 +376,7 @@
 
     sub = lax.broadcasted_iota(jnp.int32, (TILE, LANES), 0)
     for f in range(nf):
-        over, under = main_rows(pieces(f, TOP - TILE)), main_rows(pieces(f, TOP + BY))
+        over, under = give(f, TOP - TILE, TILE)[0], give(f, TOP + BY, TILE)[0]
         for d in range(G):
             for a in range(2):
                 outs[d][f, a, BY:MROWS] = jnp.where(
@@ -389,7 +392,6 @@
     grad, adjoint, state, residuals, xs, ends, kap = refs[10:]
     fields = [(stack, n) for stack in stacks for n in range(2 // nstacks)]
     order = parity_order(True)
-    wide = 4 * TILE
 
     def owners(rows):
         return [lanes_of(rows, strips[d])[0] for d in range(G)]
@@ -404,30 +406,35 @@
         msgs, n = fields[f]
         return [roll(msgs[d][n, a, pl.ds(row, rows)], -32 * d) for d in range(G)]
 
-    @pl.loop(0, BY // wide)
+    @pl.loop(0, BY // CHUNK)
     def _(t):
-        row = pl.multiple_of(wide * t, wide)
-        to = pl.ds(pl.multiple_of(TILE + wide * t, TILE), wide)
-        owner = owners(wide)
+        row = pl.multiple_of(CHUNK * t, CHUNK)
+        to = pl.ds(pl.multiple_of(TILE + CHUNK * t, TILE), CHUNK)
+        owner = owners(CHUNK)
         for f in range(2):
+            whole = []
             for a in range(2):
-                parts = bricks(f, a, row, wide)
-                for b in range(4):
-                    xs[f, 1 + 4 * a + b, to] = reorder(roll(choose(owner, parts, b), -32 * b), order)
-            parts = bricks(f, 2, row, wide)
+                parts = bricks(f, a, row, CHUNK)
+                whole += [roll(choose(owner, parts, b), -32 * b) for b in range(4)]
+            parts = bricks(f, 2, row, CHUNK)
             for d in range(G):
-                ends[f, strips[d], pl.ds(row, wide)] = parts[d]
-            xs[f, 0, to] = reorder(roll(choose(owner, parts, 2), -64), order)
-            xs[f, 1 + BX, to] = reorder(roll(choose(owner, parts, 3), -96), order)
+                ends[f, strips[d], pl.ds(row, CHUNK)] = parts[d]
+            whole += [roll(choose(owner, parts, b), -32 * b) for b in (2, 3)]
+            ordered = reorder(jnp.concatenate(whole, axis=0), order)
+            for j, at in enumerate([*range(1, 1 + BX), 0, 1 + BX]):
+                xs[f, at, to] = ordered[CHUNK * j : CHUNK * (j + 1)]
 
     owner = owners(TILE)
     for f in range(2):
+        whole = []
         for a in range(2):
             parts = bricks(f, a, BY, TILE)
-            for b in range(4):
-                val = pltpu.roll(reorder(roll(choose(owner, parts, b), -32 * b), order), 7, 0)
-                xs[f, 1 + 4 * a + b, 0:TILE] = val
-                xs[f, 1 + 4 * a + b, TILE + BY : 2 * TILE + BY] = val
+            whole += [roll(choose(owner, parts, b), -32 * b) for b in range(4)]
+        ordered = reorder(jnp.concatenate(whole, axis=0), order)
+        for c in range(BX):
+            val = pltpu.roll(ordered[TILE * c : TILE * (c + 1)], 7, 0)
+            xs[f, 1 + c, 0:TILE] = val
+            xs[f, 1 + c, TILE + BY : 2 * TILE + BY] = val
     kap[0, TILE : TILE + BY] = kdown[...]
     kap[1 + BX, TILE : TILE + BY] = kup[...]
     for c in range(BX):
@@ -495,10 +502,18 @@
     return lax.ppermute(x, axis, [(i, (i + by) % count) for i in range(count)])
 
 
-def around(x, by):
-    order = [2 * g for g in range(G)] + [2 * g + 1 for g in reversed(range(G))]
-    pairs = [(order[i], order[(i + by) % len(order)]) for i in range(len(order))]
-    return lax.ppermute(x, ("gx", "pa"), pairs)
+def around(x, by, rows=0):
+    order = [(g, 0) for g in range(G)] + [(g, 1) for g in reversed(range(G))]
+    count = lax.axis_size("gy")
+    if rows == 0:
+        pairs = [(2 * g + p, 2 * order[(i + by) % len(order)][0] + order[(i + by) % len(order)][1]) for i, (g, p) in enumerate(order)]
+        return lax.ppermute(x, ("gx", "pa"), pairs)
+    pairs = []
+    for i, (g, p) in enumerate(order):
+        to_g, to_p = order[(i + by) % len(order)]
+        for y in range(count):
+            pairs.append(((g * count + y) * 2 + p, (to_g * count + (y + rows) % count) * 2 + to_p))
+    return lax.ppermute(x, ("gx", "gy", "pa"), pairs)
 
 
 def chebyshev_scalars(upper):
@@ -546,13 +561,19 @@
         parts = [parts[0]] + [shifted(parts[d], "gx", d) for d in range(1, G)]
         edge = (count, G, BY, LANES)
         rim = (count, G, 2, HALO, LANES)
-        to_left, to_right, head, tail = call(edge_kernel, [edge, edge, rim, rim], [places], parts)
+        corner = (count, G, HALO, LANES)
+        to_left, to_right, head, tail, left_down, left_up, right_down, right_up = call(
+            edge_kernel, [edge, edge, rim, rim] + [corner] * 4, [places], parts
+        )
         from_right, from_left = around(to_left, -1), around(to_right, 1)
         below, above = shifted(head, "gy", -1), shifted(tail, "gy", 1)
-        edges = jnp.stack((from_left, from_right))
-        below_edge = shifted(edges[:, :, :, :HALO], "gy", -1)
-        above_edge = shifted(edges[:, :, :, BY - HALO :], "gy", 1)
-        return [*parts, from_left, from_right, above, above_edge, below, below_edge]
+        corners = [
+            around(right_down, 1, 1),
+            around(left_down, -1, 1),
+            around(right_up, 1, -1),
+            around(left_up, -1, -1),
+        ]
+        return [*parts, from_left, from_right, above, below, *corners]
 
     def solve(where, stacks):
         nf = len(where) - 1
@@ -563,22 +584,24 @@
             [strip[None], scalars],
             sum(stacks, []),
             [line] * (4 * nf)
-            + [(PLANES, 2, TILE, LANES)] * (2 * nf)
+            + [(PLANES + 2, 2, TILE, LANES)] * nf
             + [line] * 3
             + [(PLANES, ROWS, LANES)] * 2
             + [line],
         )
         return [solved[0]] + [shifted(solved[d], "gx", d) for d in range(1, G)]
 
-    everything = strips(("conductivity", "cotangent", "previous"), [conductivity, cotangent, stored, scales])
-    solved = solve(((0, 0), (0, 2), (0, 1)), [everything])
+    first = strips(("conductivity", "cotangent"), [conductivity, cotangent])
+    second = strips(("previous",), [stored, scales])
+    solved_adjoint = solve(((0, 0), (0, 1)), [first])
+    solved_state = solve(((0, 0), (1, 0)), [first, second])
     out = (BX, BY, LANES)
     padded = (BX + 2, BY + 16, LANES)
     return call(
-        functools.partial(final_kernel, 1),
+        functools.partial(final_kernel, 2),
         [out, out, out, (2,) + out],
         [strip_of(behind)],
-        [*solved, conductivity, kdown, kup, kover, kunder, kends[0][:, :, None], kends[1][:, :, None], stored, scales, cotangent],
+        [*solved_state, *solved_adjoint, conductivity, kdown, kup, kover, kunder, kends[0][:, :, None], kends[1][:, :, None], stored, scales, cotangent],
         [(2,) + padded, (2, G, BY, LANES), padded],
     )
 

time: 192 us -> 196 us (1.021)
  waiting for transfers between devices: 86.4 us -> 54.8 us
  starting transfers between devices: 18.6 us -> 41.8 us
  local copies, waits for them, and re-layouts: 9.8 us -> 24.8 us
  Pallas kernels: 73.4 us -> 65.8 us
  other arithmetic: 0.69 us -> 4.55 us
    ppermute x16 -> x22, waiting for transfers between devices: 70.6 us -> 44.9 us  [shifted(): return lax.ppermute(x, axis, [(i, (i + by) % count) for i in range(count)])]
    ppermute x2 -> x4, waiting for transfers between devices: 15.9 us -> 0.01 us  [around(): return lax.ppermute(x, ('gx', 'pa'), pairs)]
    unnamed x28 -> x70, local copies, waits for them, and re-layouts: 5.89 us -> 20.3 us
    ppermute x16 -> x22, starting transfers between devices: 17.1 us -> 27.9 us  [shifted(): return lax.ppermute(x, axis, [(i, (i + by) % count) for i in range(count)])]
    ppermute x0 -> x8, waiting for transfers between devices: none -> 9.9 us  [around(): return lax.ppermute(x, ('gx', 'gy', 'pa'), pairs)]
    ppermute x0 -> x8, starting transfers between devices: none -> 8.02 us  [around(): return lax.ppermute(x, ('gx', 'gy', 'pa'), pairs)]
    pallas_call x4 -> x7, Pallas kernels: 73.4 us -> 65.8 us  [call(): pl.pallas_call(kernel, out_shape=[jax.ShapeDtypeStruct(shape, F32) for sh...]
    ppermute x2 -> x4, starting transfers between devices: 1.48 us -> 5.85 us  [around(): return lax.ppermute(x, ('gx', 'pa'), pairs)]
  transfers between devices with their start and end apart: 18 -> 34, of which waited for: 11 -> 16; matrix products, arithmetic and copies ran while one was open for 4% -> 6% of each run, Pallas kernels for 32% -> 29%
where the time goes in v4:
time: 196 us; the launch traced here: 195 us
  Pallas kernels  65.8 us (34%)
  waiting for transfers between devices  54.8 us (28%)
  starting transfers between devices  41.8 us (21%)
  local copies, waits for them, and re-layouts  24.8 us (13%)
  other arithmetic  4.55 us (2%)
  between operations  2.91 us (1%)
    pallas_call x7, Pallas kernels, call(): pl.pallas_call(kernel, out_shape=[jax.ShapeDtypeStruct(shape, F32) for sh...  65.8 us
    ppermute x22, waiting for transfers between devices, shifted(): return lax.ppermute(x, axis, [(i, (i + by) % count) for i in range(count)])  44.9 us
    ppermute x22, starting transfers between devices, shifted(): return lax.ppermute(x, axis, [(i, (i + by) % count) for i in range(count)])  27.9 us
    unnamed x70, local copies, waits for them, and re-layouts  20.3 us
    ppermute x8, waiting for transfers between devices, around(): return lax.ppermute(x, ('gx', 'gy', 'pa'), pairs)  9.9 us
    ppermute x8, starting transfers between devices, around(): return lax.ppermute(x, ('gx', 'gy', 'pa'), pairs)  8.02 us
    ppermute x4, starting transfers between devices, around(): return lax.ppermute(x, ('gx', 'pa'), pairs)  5.85 us
    another operation x8, other arithmetic, chebyshev_scalars(): return jnp.stack([jnp.stack(row) for row in rows])  4.51 us
  transfers between devices with their start and end apart: 34, of which 16 were waited for; matrix products, arithmetic and copies ran while one was open for 6% of the time, Pallas kernels for 29%

profile of v4, /device:TPU:8, one launch (start us, length us, event | category | flops | bytes accessed | tf_op | source)
XLA Modules:
  0.0 194.6 jit_solution(6426838764048660838)
XLA Ops:
  6.7 1.9 %collective-permute-start.2 = (f32[2,2,128,128]{3,2,1,0:T(8,128)S(1)}, f32[2,2,128,128]{3,2,1,0:T(8,128)S(1)}, u32[]{:S(2)}, u32[]{:S(2)}) collective-permute-start(f32[2,2,128,128]{3,2,1,0:T(8,128)S(1)} %get-tuple-element.39), channel_id=1, source_target_pairs={{0,24},{8,0},{16,8},{24,16},{1,25},{9,1},{17,9},{25,17},{2,26},{10... | collective-permute-start | bytes 786440 | tf_op jit(solution)/shard_map/ppermute | solution.py:502
  14.4 9.2 %collective-permute-done.refs_1_ = f32[2,2,128,128]{3,2,1,0:T(8,128)S(1)} collective-permute-done((f32[2,2,128,128]{3,2,1,0:T(8,128)S(1)}, f32[2,2,128,128]{3,2,1,0:T(8,128)S(1)}, u32[]{:S(2)}, u32[]{:S(2)}) %collective-permute-start) | collective-permute-done | bytes 262176 | tf_op jit(solution)/shard_map/ppermute | solution.py:502
  23.6 4.5 %collective-permute-done.1.refs_2_ = f32[2,2,128,128]{3,2,1,0:T(8,128)S(1)} collective-permute-done((f32[2,2,128,128]{3,2,1,0:T(8,128)S(1)}, f32[2,2,128,128]{3,2,1,0:T(8,128)S(1)}, u32[]{:S(2)}, u32[]{:S(2)}) %collective-permute-start.1) | collective-permute-done | bytes 262176 | tf_op jit(solution)/shard_map/ppermute | solution.py:502
  28.0 1.8 collective-permute-done.2.refs_3_
  31.6 2.7 %collective-permute-start.8 = (f32[2,4,16,128]{3,2,1,0:T(8,128)S(1)}, f32[2,4,16,128]{3,2,1,0:T(8,128)S(1)}, u32[]{:S(2)}, u32[]{:S(2)}) collective-permute-start(f32[2,4,16,128]{3,2,1,0:T(8,128)S(1)} %get-tuple-element.45), channel_id=1, source_target_pairs={{0,3},{2,5},{4,7},{6,1},{8,2},{10,4},{12,6},{14,0},{16,10},{18,12}... | collective-permute-start | bytes 196616 | tf_op jit(solution)/shard_map/ppermute | solution.py:516
  37.5 2.3 %collective-permute-start.13 = (f32[1,2,128,128]{3,2,1,0:T(8,128)S(1)}, f32[1,2,128,128]{3,2,1,0:T(8,128)S(1)}, u32[]{:S(2)}, u32[]{:S(2)}) collective-permute-start(f32[1,2,128,128]{3,2,1,0:T(8,128)S(1)} %get-tuple-element.50), channel_id=1, source_target_pairs={{0,16},{8,24},{16,0},{24,8},{1,17},{9,25},{17,1},{25,9},{2,18},{10... | collective-permute-start | bytes 393224 | tf_op jit(solution)/shard_map/ppermute | solution.py:502
  46.8 2.6 %collective-permute-start.3 = (f32[2,4,128,128]{3,2,1,0:T(8,128)}, f32[2,4,128,128]{3,2,1,0:T(8,128)S(1)}, u32[]{:S(2)}, u32[]{:S(2)}) collective-permute-start(f32[2,4,128,128]{3,2,1,0:T(8,128)} %get-tuple-element.40), channel_id=1, source_target_pairs={{0,8},{8,16},{16,24},{24,25},{25,17},{17,9},{9,1},{1,0},{2,10},{10... | collective-permute-start | bytes 1572872 | tf_op jit(solution)/shard_map/ppermute | solution.py:510
  55.2 8.4 %collective-permute-done.10.refs_11_ = f32[2,4,16,128]{3,2,1,0:T(8,128)S(1)} collective-permute-done((f32[2,4,16,128]{3,2,1,0:T(8,128)}, f32[2,4,16,128]{3,2,1,0:T(8,128)S(1)}, u32[]{:S(2)}, u32[]{:S(2)}) %collective-permute-start.10) | collective-permute-done | bytes 65568 | tf_op jit(solution)/shard_map/ppermute | solution.py:516
  64.2 2.1 %collective-permute-start.19 = (f32[1,4,16,128]{3,2,1,0:T(8,128)}, f32[1,4,16,128]{3,2,1,0:T(8,128)}, u32[]{:S(2)}, u32[]{:S(2)}) collective-permute-start(f32[1,4,16,128]{3,2,1,0:T(8,128)} %get-tuple-element.56), channel_id=1, source_target_pairs={{0,10},{2,12},{4,14},{6,8},{8,18},{10,20},{12,22},{14,16},{16,26},... | collective-permute-start | bytes 98312 | tf_op jit(solution)/shard_map/ppermute | solution.py:516
  66.4 3.1 %collective-permute-start.21 = (f32[1,4,16,128]{3,2,1,0:T(8,128)}, f32[1,4,16,128]{3,2,1,0:T(8,128)}, u32[]{:S(2)}, u32[]{:S(2)}) collective-permute-start(f32[1,4,16,128]{3,2,1,0:T(8,128)} %get-tuple-element.58), channel_id=1, source_target_pairs={{0,14},{2,8},{4,10},{6,12},{8,22},{10,16},{12,18},{14,20},{16,30},... | collective-permute-start | bytes 98312 | tf_op jit(solution)/shard_map/ppermute | solution.py:516
  73.4 1.8 copy.66
  75.2 1.8 copy.65
  78.2 3.0 %collective-permute-start.17 = (f32[1,4,2,16,128]{4,3,2,1,0:T(8,128)}, f32[1,4,2,16,128]{4,3,2,1,0:T(8,128)S(1)}, u32[]{:S(2)}, u32[]{:S(2)}) collective-permute-start(f32[1,4,2,16,128]{4,3,2,1,0:T(8,128)} %copy-done.27), channel_id=1, source_target_pairs={{0,2},{2,4},{4,6},{6,0},{1,3},{3,5},{5,7},{7,1},{8,10},{10,12},{12... | collective-permute-start | bytes 196616 | tf_op jit(solution)/shard_map/ppermute | solution.py:502
  93.9 26.2 %shard_map.88 = (f32[1,3,136,128]{3,2,1,0:T(8,128)S(1)}, f32[1,3,136,128]{3,2,1,0:T(8,128)S(1)}, f32[1,3,136,128]{3,2,1,0:T(8,128)}, f32[1,3,136,128]{3,2,1,0:T(8,128)}) custom-call(s32[1]{0:T(128)} %bitcast.strip, f32[16,2]{1,0:T(8,128)S(1)} %stack.264.scalars, f32[2,2,128,128]{3,2,1,0:T(8,128)S(1)} %get-tuple-element.36.refs_0_, ...), custom_call_target="tpu_custom_call" | custom-call | tf_op jit(solution)/shard_map/pallas_call | solution.py:490
  120.1 1.8 collective-permute-start.23
  122.7 25.7 %shard_map.89 = (f32[1,3,136,128]{3,2,1,0:T(8,128)S(1)}, f32[1,3,136,128]{3,2,1,0:T(8,128)}, f32[1,3,136,128]{3,2,1,0:T(8,128)}, f32[1,3,136,128]{3,2,1,0:T(8,128)}) custom-call(s32[1]{0:T(128)} %bitcast.strip, f32[16,2]{1,0:T(8,128)S(1)} %stack.264.scalars, f32[2,2,128,128]{3,2,1,0:T(8,128)S(1)} %get-tuple-element.36.refs_0_, ...), custom_call_target="tpu_custom_call" | custom-call | tf_op jit(solution)/shard_map/pallas_call | solution.py:490
  149.1 2.9 %collective-permute-start.24 = (f32[1,3,136,128]{3,2,1,0:T(8,128)}, f32[1,3,136,128]{3,2,1,0:T(8,128)S(1)}, u32[]{:S(2)}, u32[]{:S(2)}) collective-permute-start(f32[1,3,136,128]{3,2,1,0:T(8,128)} %get-tuple-element.62), channel_id=1, source_target_pairs={{0,16},{8,24},{16,0},{24,8},{1,17},{9,25},{17,1},{25,9},{2,18},{10... | collective-permute-start | bytes 626696 | tf_op jit(solution)/shard_map/ppermute | solution.py:502
  152.6 2.0 %collective-permute-start.26 = (f32[1,3,136,128]{3,2,1,0:T(8,128)}, f32[1,3,136,128]{3,2,1,0:T(8,128)}, u32[]{:S(2)}, u32[]{:S(2)}) collective-permute-start(f32[1,3,136,128]{3,2,1,0:T(8,128)} %get-tuple-element.65), channel_id=1, source_target_pairs={{0,8},{8,16},{16,24},{24,0},{1,9},{9,17},{17,25},{25,1},{2,10},{10... | collective-permute-start | bytes 626696 | tf_op jit(solution)/shard_map/ppermute | solution.py:502
  155.3 1.9 collective-permute-start.27
  157.6 8.5 %collective-permute-done.24.refs_2_ = f32[1,3,136,128]{3,2,1,0:T(8,128)S(1)} collective-permute-done((f32[1,3,136,128]{3,2,1,0:T(8,128)}, f32[1,3,136,128]{3,2,1,0:T(8,128)S(1)}, u32[]{:S(2)}, u32[]{:S(2)}) %collective-permute-start.24) | collective-permute-done | bytes 208928 | tf_op jit(solution)/shard_map/ppermute | solution.py:502
  166.2 9.2 %collective-permute-done.25.refs_3_ = f32[1,3,136,128]{3,2,1,0:T(8,128)} collective-permute-done((f32[1,3,136,128]{3,2,1,0:T(8,128)}, f32[1,3,136,128]{3,2,1,0:T(8,128)}, u32[]{:S(2)}, u32[]{:S(2)}) %collective-permute-start.25) | collective-permute-done | bytes 208928 | tf_op jit(solution)/shard_map/ppermute | solution.py:502
  175.4 2.6 %collective-permute-done.26.refs_5_ = f32[1,3,136,128]{3,2,1,0:T(8,128)} collective-permute-done((f32[1,3,136,128]{3,2,1,0:T(8,128)}, f32[1,3,136,128]{3,2,1,0:T(8,128)}, u32[]{:S(2)}, u32[]{:S(2)}) %collective-permute-start.26) | collective-permute-done | bytes 208928 | tf_op jit(solution)/shard_map/ppermute | solution.py:502
  178.0 4.4 %collective-permute-done.27.refs_6_ = f32[1,3,136,128]{3,2,1,0:T(8,128)} collective-permute-done((f32[1,3,136,128]{3,2,1,0:T(8,128)}, f32[1,3,136,128]{3,2,1,0:T(8,128)}, u32[]{:S(2)}, u32[]{:S(2)}) %collective-permute-start.27) | collective-permute-done | bytes 208928 | tf_op jit(solution)/shard_map/ppermute | solution.py:502
  186.9 7.7 %shard_map.90 = (f32[8,128,128]{2,1,0:T(8,128)}, f32[8,128,128]{2,1,0:T(8,128)}, f32[8,128,128]{2,1,0:T(8,128)}, f32[2,8,128,128]{3,2,1,0:T(8,128)}) custom-call(s32[4]{0:T(128)S(1)} %broadcast_select_fusion.1.strips, f32[1,3,136,128]{3,2,1,0:T(8,128)S(1)} %copy-done.13, f32[1,3,136,128]{3,2,1,0:T(8,128)S(1)} %collective-permute-done.23.refs_1_, ...), custom_call_target="tpu_custom_call" | custom-call | tf_op jit(solution)/shard_map/pallas_call | solution.py:490
  (142 shorter events, 53.5 us)
Async XLA Ops:
  4.0 19.6 %collective-permute-start = (f32[2,2,128,128]{3,2,1,0:T(8,128)S(1)}, f32[2,2,128,128]{3,2,1,0:T(8,128)S(1)}, u32[]{:S(2)}, u32[]{:S(2)}) collective-permute-start(f32[2,2,128,128]{3,2,1,0:T(8,128)S(1)} %get-tuple-element.37), channel_id=1, source_target_pairs={{0,8},{8,16},{16,24},{24,0},{1,9},{9,17},{17,25},{25,1},{2,10},{10... | collective-permute-start | bytes 786440 | tf_op jit(solution)/shard_map/ppermute | solution.py:502
  5.6 22.4 %collective-permute-start.1 = (f32[2,2,128,128]{3,2,1,0:T(8,128)S(1)}, f32[2,2,128,128]{3,2,1,0:T(8,128)S(1)}, u32[]{:S(2)}, u32[]{:S(2)}) collective-permute-start(f32[2,2,128,128]{3,2,1,0:T(8,128)S(1)} %get-tuple-element.38), channel_id=1, source_target_pairs={{0,16},{8,24},{16,0},{24,8},{1,17},{9,25},{17,1},{25,9},{2,18},{10... | collective-permute-start | bytes 786440 | tf_op jit(solution)/shard_map/ppermute | solution.py:502
  6.7 23.1 %collective-permute-start.2 = (f32[2,2,128,128]{3,2,1,0:T(8,128)S(1)}, f32[2,2,128,128]{3,2,1,0:T(8,128)S(1)}, u32[]{:S(2)}, u32[]{:S(2)}) collective-permute-start(f32[2,2,128,128]{3,2,1,0:T(8,128)S(1)} %get-tuple-element.39), channel_id=1, source_target_pairs={{0,24},{8,0},{16,8},{24,16},{1,25},{9,1},{17,9},{25,17},{2,26},{10... | collective-permute-start | bytes 786440 | tf_op jit(solution)/shard_map/ppermute | solution.py:502
  8.7 25.8 %collective-permute-start.11 = (bf16[8,128,128]{2,1,0:T(8,128)(2,1)S(1)}, bf16[8,128,128]{2,1,0:T(8,128)(2,1)S(1)}, u32[]{:S(2)}, u32[]{:S(2)}) collective-permute-start(bf16[8,128,128]{2,1,0:T(8,128)(2,1)S(1)} %copy-done.33), channel_id=1, source_target_pairs={{0,1},{1,0},{2,3},{3,2},{4,5},{5,4},{6,7},{7,6},{8,9},{9,8},{10,11... | collective-permute-start | bytes 786440 | tf_op jit(solution)/shard_map/ppermute | solution.py:502
  37.5 12.0 %collective-permute-start.13 = (f32[1,2,128,128]{3,2,1,0:T(8,128)S(1)}, f32[1,2,128,128]{3,2,1,0:T(8,128)S(1)}, u32[]{:S(2)}, u32[]{:S(2)}) collective-permute-start(f32[1,2,128,128]{3,2,1,0:T(8,128)S(1)} %get-tuple-element.50), channel_id=1, source_target_pairs={{0,16},{8,24},{16,0},{24,8},{1,17},{9,25},{17,1},{25,9},{2,18},{10... | collective-permute-start | bytes 393224 | tf_op jit(solution)/shard_map/ppermute | solution.py:502
  40.4 11.1 %collective-permute-start.14 = (f32[1,2,128,128]{3,2,1,0:T(8,128)}, f32[1,2,128,128]{3,2,1,0:T(8,128)}, u32[]{:S(2)}, u32[]{:S(2)}) collective-permute-start(f32[1,2,128,128]{3,2,1,0:T(8,128)} %get-tuple-element.51), channel_id=1, source_target_pairs={{0,24},{8,0},{16,8},{24,16},{1,25},{9,1},{17,9},{25,17},{2,26},{10... | collective-permute-start | bytes 393224 | tf_op jit(solution)/shard_map/ppermute | solution.py:502
  41.9 24.4 %collective-permute-start.5 = (f32[2,4,2,16,128]{4,3,2,1,0:T(8,128)}, f32[2,4,2,16,128]{4,3,2,1,0:T(8,128)S(1)}, u32[]{:S(2)}, u32[]{:S(2)}) collective-permute-start(f32[2,4,2,16,128]{4,3,2,1,0:T(8,128)} %get-tuple-element.42), channel_id=1, source_target_pairs={{0,2},{2,4},{4,6},{6,0},{1,3},{3,5},{5,7},{7,1},{8,10},{10,12},{12... | collective-permute-start | bytes 393224 | tf_op jit(solution)/shard_map/ppermute | solution.py:502
  43.0 23.4 %collective-permute-start.6 = (f32[2,4,2,16,128]{4,3,2,1,0:T(8,128)}, f32[2,4,2,16,128]{4,3,2,1,0:T(8,128)S(1)}, u32[]{:S(2)}, u32[]{:S(2)}) collective-permute-start(f32[2,4,2,16,128]{4,3,2,1,0:T(8,128)} %get-tuple-element.43), channel_id=1, source_target_pairs={{0,6},{2,0},{4,2},{6,4},{1,7},{3,1},{5,3},{7,5},{8,14},{10,8},{12,... | collective-permute-start | bytes 393224 | tf_op jit(solution)/shard_map/ppermute | solution.py:502
  46.8 42.7 %collective-permute-start.3 = (f32[2,4,128,128]{3,2,1,0:T(8,128)}, f32[2,4,128,128]{3,2,1,0:T(8,128)S(1)}, u32[]{:S(2)}, u32[]{:S(2)}) collective-permute-start(f32[2,4,128,128]{3,2,1,0:T(8,128)} %get-tuple-element.40), channel_id=1, source_target_pairs={{0,8},{8,16},{16,24},{24,25},{25,17},{17,9},{9,1},{1,0},{2,10},{10... | collective-permute-start | bytes 1572872 | tf_op jit(solution)/shard_map/ppermute | solution.py:510
  49.5 40.2 %collective-permute-start.4 = (f32[2,4,128,128]{3,2,1,0:T(8,128)}, f32[2,4,128,128]{3,2,1,0:T(8,128)S(1)}, u32[]{:S(2)}, u32[]{:S(2)}) collective-permute-start(f32[2,4,128,128]{3,2,1,0:T(8,128)} %copy-done.22), channel_id=1, source_target_pairs={{0,1},{8,0},{16,8},{24,16},{25,24},{17,25},{9,17},{1,9},{2,3},{10,... | collective-permute-start | bytes 1572872 | tf_op jit(solution)/shard_map/ppermute | solution.py:510
  51.5 12.1 %collective-permute-start.10 = (f32[2,4,16,128]{3,2,1,0:T(8,128)}, f32[2,4,16,128]{3,2,1,0:T(8,128)S(1)}, u32[]{:S(2)}, u32[]{:S(2)}) collective-permute-start(f32[2,4,16,128]{3,2,1,0:T(8,128)} %copy-done.26), channel_id=1, source_target_pairs={{0,7},{2,1},{4,3},{6,5},{8,6},{10,0},{12,2},{14,4},{16,14},{18,8},... | collective-permute-start | bytes 196616 | tf_op jit(solution)/shard_map/ppermute | solution.py:516
  70.3 16.9 %collective-permute-start.15 = (f32[1,4,128,128]{3,2,1,0:T(8,128)}, f32[1,4,128,128]{3,2,1,0:T(8,128)}, u32[]{:S(2)}, u32[]{:S(2)}) collective-permute-start(f32[1,4,128,128]{3,2,1,0:T(8,128)} %copy-done.24), channel_id=1, source_target_pairs={{0,8},{8,16},{16,24},{24,25},{25,17},{17,9},{9,1},{1,0},{2,10},{10... | collective-permute-start | bytes 786440 | tf_op jit(solution)/shard_map/ppermute | solution.py:510
  71.4 16.5 %collective-permute-start.16 = (f32[1,4,128,128]{3,2,1,0:T(8,128)}, f32[1,4,128,128]{3,2,1,0:T(8,128)}, u32[]{:S(2)}, u32[]{:S(2)}) collective-permute-start(f32[1,4,128,128]{3,2,1,0:T(8,128)} %copy-done.23), channel_id=1, source_target_pairs={{0,1},{8,0},{16,8},{24,16},{25,24},{17,25},{9,17},{1,9},{2,3},{10,... | collective-permute-start | bytes 786440 | tf_op jit(solution)/shard_map/ppermute | solution.py:510
  85.9 66.1 %collective-permute-start.29 = (f32[128,128]{1,0:T(8,128)}, f32[128,128]{1,0:T(8,128)S(1)}, u32[]{:S(2)}, u32[]{:S(2)}) collective-permute-start(f32[128,128]{1,0:T(8,128)} %get-tuple-element.73), channel_id=1, source_target_pairs={{0,8},{8,16},{16,24},{24,0},{1,9},{9,17},{17,25},{25,1},{2,10},{10... | collective-permute-start | bytes 196616 | tf_op jit(solution)/shard_map/ppermute | solution.py:502
  87.2 67.4 %collective-permute-start.30 = (f32[128,128]{1,0:T(8,128)}, f32[128,128]{1,0:T(8,128)S(1)}, u32[]{:S(2)}, u32[]{:S(2)}) collective-permute-start(f32[128,128]{1,0:T(8,128)} %get-tuple-element.72), channel_id=1, source_target_pairs={{0,24},{8,0},{16,8},{24,16},{1,25},{9,1},{17,9},{25,17},{2,26},{10... | collective-permute-start | bytes 196616 | tf_op jit(solution)/shard_map/ppermute | solution.py:502
  87.9 33.9 %collective-permute-start.31 = (f32[8,128]{1,0:T(8,128)}, f32[8,128]{1,0:T(8,128)S(1)}, u32[]{:S(2)}, u32[]{:S(2)}) collective-permute-start(f32[8,128]{1,0:T(8,128)} %bitcast.53), channel_id=1, source_target_pairs={{0,2},{2,4},{4,6},{6,0},{1,3},{3,5},{5,7},{7,1},{8,10},{10,12},{12... | collective-permute-start | bytes 12296 | tf_op jit(solution)/shard_map/ppermute | solution.py:502
  89.5 59.5 %collective-permute-start.32 = (f32[8,128]{1,0:T(8,128)S(1)}, f32[8,128]{1,0:T(8,128)S(1)}, u32[]{:S(2)}, u32[]{:S(2)}) collective-permute-start(f32[8,128]{1,0:T(8,128)S(1)} %bitcast.86), channel_id=1, source_target_pairs={{0,6},{2,0},{4,2},{6,4},{1,7},{3,1},{5,3},{7,5},{8,14},{10,8},{12,... | collective-permute-start | bytes 12296 | tf_op jit(solution)/shard_map/ppermute | solution.py:502
  120.1 37.1 %collective-permute-start.23 = (f32[1,3,136,128]{3,2,1,0:T(8,128)S(1)}, f32[1,3,136,128]{3,2,1,0:T(8,128)S(1)}, u32[]{:S(2)}, u32[]{:S(2)}) collective-permute-start(f32[1,3,136,128]{3,2,1,0:T(8,128)S(1)} %get-tuple-element.61), channel_id=1, source_target_pairs={{0,8},{8,16},{16,24},{24,0},{1,9},{9,17},{17,25},{25,1},{2,10},{10... | collective-permute-start | bytes 626696 | tf_op jit(solution)/shard_map/ppermute | solution.py:502
  121.8 30.2 %collective-permute-start.33 = (f32[2,8,128]{2,1,0:T(8,128)S(1)}, f32[2,8,128]{2,1,0:T(8,128)S(1)}, u32[]{:S(2)}, u32[]{:S(2)}) collective-permute-start(f32[2,8,128]{2,1,0:T(8,128)S(1)} %pad_maximum_fusion), channel_id=1, source_target_pairs={{0,1},{1,0},{2,3},{3,2},{4,5},{5,4},{6,7},{7,6},{8,9},{9,8},{10,11... | collective-permute-start | bytes 24584 | tf_op jit(solution)/shard_map/ppermute | solution.py:502
  149.1 17.1 %collective-permute-start.24 = (f32[1,3,136,128]{3,2,1,0:T(8,128)}, f32[1,3,136,128]{3,2,1,0:T(8,128)S(1)}, u32[]{:S(2)}, u32[]{:S(2)}) collective-permute-start(f32[1,3,136,128]{3,2,1,0:T(8,128)} %get-tuple-element.62), channel_id=1, source_target_pairs={{0,16},{8,24},{16,0},{24,8},{1,17},{9,25},{17,1},{25,9},{2,18},{10... | collective-permute-start | bytes 626696 | tf_op jit(solution)/shard_map/ppermute | solution.py:502
  152.0 23.4 %collective-permute-start.25 = (f32[1,3,136,128]{3,2,1,0:T(8,128)}, f32[1,3,136,128]{3,2,1,0:T(8,128)}, u32[]{:S(2)}, u32[]{:S(2)}) collective-permute-start(f32[1,3,136,128]{3,2,1,0:T(8,128)} %get-tuple-element.63), channel_id=1, source_target_pairs={{0,24},{8,0},{16,8},{24,16},{1,25},{9,1},{17,9},{25,17},{2,26},{10... | collective-permute-start | bytes 626696 | tf_op jit(solution)/shard_map/ppermute | solution.py:502
  152.6 25.4 %collective-permute-start.26 = (f32[1,3,136,128]{3,2,1,0:T(8,128)}, f32[1,3,136,128]{3,2,1,0:T(8,128)}, u32[]{:S(2)}, u32[]{:S(2)}) collective-permute-start(f32[1,3,136,128]{3,2,1,0:T(8,128)} %get-tuple-element.65), channel_id=1, source_target_pairs={{0,8},{8,16},{16,24},{24,0},{1,9},{9,17},{17,25},{25,1},{2,10},{10... | collective-permute-start | bytes 626696 | tf_op jit(solution)/shard_map/ppermute | solution.py:502
  155.3 27.2 %collective-permute-start.27 = (f32[1,3,136,128]{3,2,1,0:T(8,128)}, f32[1,3,136,128]{3,2,1,0:T(8,128)}, u32[]{:S(2)}, u32[]{:S(2)}) collective-permute-start(f32[1,3,136,128]{3,2,1,0:T(8,128)} %get-tuple-element.66), channel_id=1, source_target_pairs={{0,16},{8,24},{16,0},{24,8},{1,17},{9,25},{17,1},{25,9},{2,18},{10... | collective-permute-start | bytes 626696 | tf_op jit(solution)/shard_map/ppermute | solution.py:502
  157.1 26.2 %collective-permute-start.28 = (f32[1,3,136,128]{3,2,1,0:T(8,128)}, f32[1,3,136,128]{3,2,1,0:T(8,128)}, u32[]{:S(2)}, u32[]{:S(2)}) collective-permute-start(f32[1,3,136,128]{3,2,1,0:T(8,128)} %get-tuple-element.67), channel_id=1, source_target_pairs={{0,24},{8,0},{16,8},{24,16},{1,25},{9,1},{17,9},{25,17},{2,26},{10... | collective-permute-start | bytes 626696 | tf_op jit(solution)/shard_map/ppermute | solution.py:502
  (44 other events, 258.7 us)

commit v5 on v4

v5 whole, which is shorter than its diff:
```python
import functools

import jax
import jax.numpy as jnp
from jax import lax
from jax.experimental import pallas as pl
from jax.experimental.pallas import tpu as pltpu
from jax.sharding import PartitionSpec as P

CHEB = 16
LANES = 128
HALO = CHEB
TIME_STEP = 8.0
F32 = jnp.float32


def with_halo(cells, sides, width):
    for axis, dim in sides:
        count = lax.axis_size(axis)
        head = lax.slice_in_dim(cells, 0, width, axis=dim)
        tail = lax.slice_in_dim(cells, cells.shape[dim] - width, cells.shape[dim], axis=dim)
        cells = jnp.concatenate(
            [
                lax.ppermute(tail, axis, [(i, (i + 1) % count) for i in range(count)]),
                cells,
                lax.ppermute(head, axis, [((i + 1) % count, i) for i in range(count)]),
            ],
            axis=dim,
        )
    return cells


def region(arr, spatial, offset):
    extent = arr.shape[-3:]
    window = [slice(1, length - 1) for length in extent]
    window[spatial] = slice(offset, extent[spatial] - 2 + offset)
    leading = [slice(None)] * (arr.ndim - 3)
    return arr[tuple(leading + window)]


def apply_operator(padded, kpad):
    centre = region(padded, 0, 1)
    kcentre = region(kpad, 0, 1)
    summed = jnp.zeros_like(centre)
    for spatial in range(3):
        for offset in (0, 2):
            summed = summed + 0.5 * (kcentre + region(kpad, spatial, offset)) * (
                centre - region(padded, spatial, offset)
            )
    return centre + TIME_STEP * summed


def stepwise(conductivity, stored_state, row_scales, cotangent, upper_bound):
    upper = upper_bound[0]
    kpad = with_halo(conductivity, (("gx", 0), ("gy", 1), ("pa", 2)), 1)
    count = lax.axis_size("pa")
    partner = lax.ppermute(stored_state, "pa", [(i, (i + count // 2) % count) for i in range(count)])
    previous = partner.astype(F32) * row_scales[:, :, None]
    rhs = jnp.stack((previous, cotangent))
    theta = 0.5 * (upper + 1.0)
    delta = 0.5 * (upper - 1.0)
    sigma = theta / delta
    sides = (("gx", 1), ("gy", 2), ("pa", 3))

    def sweep(step, carry):
        solved, residual, direction, rho = carry
        padded = with_halo(direction, sides, 1)
        solved = solved + direction
        residual = residual - apply_operator(padded, kpad)
        rho_next = 1.0 / (2.0 * sigma - rho)
        direction = rho_next * rho * direction + 2.0 * rho_next / delta * residual
        return (solved, residual, direction, rho_next)

    start = (jnp.zeros_like(rhs), rhs, rhs / theta, 1.0 / sigma)
    solved, residual, _, _ = lax.fori_loop(0, CHEB, sweep, start)
    pair = with_halo(solved, sides, 1)
    centre = region(pair, 0, 1)
    summed = jnp.zeros_like(solved[0])
    for spatial in range(3):
        for offset in (0, 2):
            differ = centre - region(pair, spatial, offset)
            summed = summed + differ[0] * differ[1]
    return (-0.5 * TIME_STEP * summed, solved[1], solved[0], residual)


G = 4
BX = 8
BY = 128
BZ = 128
STRIP = BZ // G
TOP = 8 + HALO
ROWS = BY + 2 * TOP
EXTENDED = BY + 2 * HALO
GROUP = BY + 8
SIDES = 2 * GROUP
FIELD = SIDES + BY
KAP = FIELD + BY
BOTH = KAP + 16
TILE = 8
CHUNK = 32

BLOCK = (0, 3, 2, 1)
PLANES = BX


def roll(x, by):
    by %= LANES
    return pltpu.roll(x, by, 1) if by else x


def lanes_of(rows, strip):
    lane = lax.broadcasted_iota(jnp.int32, (rows, LANES), 1)
    return lax.rem(lane // STRIP - strip + 2 * G, G), lax.rem(lane, STRIP)


def pick(group, parts):
    out = parts[0]
    for b in range(1, G):
        out = jnp.where(group == b, parts[b], out)
    return out


def parity_order(transposed):
    src = lax.broadcasted_iota(jnp.int32, (LANES, LANES), 1 if transposed else 0)
    dst = lax.broadcasted_iota(jnp.int32, (LANES, LANES), 0 if transposed else 1)
    within = lax.rem(src, STRIP)
    place = src - within + 16 * lax.rem(within, 2) + within // 2
    return jnp.where(place == dst, 1.0, 0.0).astype(jnp.bfloat16)


def reorder(x, order):
    if x.dtype == jnp.bfloat16:
        return jnp.dot(x, order, preferred_element_type=F32)
    high = x.astype(jnp.bfloat16)
    rest = x - high.astype(F32)
    middle = rest.astype(jnp.bfloat16)
    low = (rest - middle.astype(F32)).astype(jnp.bfloat16)
    return (
        jnp.dot(high, order, preferred_element_type=F32)
        + jnp.dot(middle, order, preferred_element_type=F32)
        + jnp.dot(low, order, preferred_element_type=F32)
    )


def pack_kernel(strips, *refs):
    ins, outs = refs[: len(refs) - G], refs[len(refs) - G :]
    order = parity_order(False)
    groups = [lanes_of(BY, strips[d])[0] for d in range(G)]
    for n, array in enumerate(ins):
        for a in range(2):
            planes = reorder(array[4 * a : 4 * a + 4].reshape(4 * BY, LANES), order)
            parts = [roll(planes[BY * b : BY * (b + 1)], 32 * b) for b in range(4)]
            for d in range(G):
                outs[d][n, a] = pick(groups[d], parts)


def pack_previous_kernel(strips, stored, scales, above, below, *outs):
    order = parity_order(False)
    for rows, start, array in ((BY, HALO, stored), (HALO, 0, above), (HALO, HALO + BY, below)):
        groups = [lanes_of(rows, strips[d])[0] for d in range(G)]
        for a in range(2):
            planes = reorder(array[4 * a : 4 * a + 4].reshape(4 * rows, LANES), order)
            parts = []
            for b in range(4):
                plane = planes[rows * b : rows * (b + 1)]
                if array is stored:
                    plane = plane * scales[4 * a + b]
                parts.append(roll(plane, 32 * b))
            for d in range(G):
                outs[d][0, a, start : start + rows] = pick(groups[d], parts)


def edge_kernel(places, *refs):
    msgs, (to_left, to_right), rims = refs[:G], refs[G : G + 2], refs[G + 2 :]
    length = msgs[0].shape[2]
    lane = lax.broadcasted_iota(jnp.int32, (length, LANES), 1)
    low = lax.rem(lane, 16) < 8
    rows = (slice(length - HALO, length), slice(0, HALO))
    for n in range(msgs[0].shape[0]):
        for d in range(G):
            first, second = msgs[d][n, 0], msgs[d][n, 1]
            edges = (jnp.where(low, first, roll(second, 8)), jnp.where(low, roll(second, -8), first))
            for side, out in enumerate((to_left, to_right)):
                out[n, places[side, d]] = edges[side]
            if rims:
                head, tail, *corners = rims
                for side in range(2):
                    for way in range(2):
                        corners[2 * side + way][n, places[side, d]] = edges[side][rows[way]]
                for a in range(2):
                    head[n, d, a] = msgs[d][n, a, :HALO]
                    tail[n, d, a] = msgs[d][n, a, length - HALO :]


def unpack(get_brick, get_edge, group, within, put):
    by_block = [BLOCK.index(q) for q in range(G)]
    edges = [[get_edge(side, d) for d in by_block] for side in range(2)]
    for a in range(2):
        far = 24 if a else 16
        own = [roll(get_brick(by_block[q], a), 32 * q) for q in range(G)]
        below = [roll(edges[0][q], 32 * q + far) for q in range(G)]
        above = [roll(edges[1][q], 32 * q - far) for q in range(G)]
        even = [
            jnp.where(within < 16, own[q], jnp.where(within < 24, above[q], below[(q + 1) % G])) for q in range(G)
        ]
        odd = [
            jnp.where(within < 8, above[(q - 1) % G], jnp.where(within < 16, below[q], own[q])) for q in range(G)
        ]
        for b in range(4):
            for e, parts in enumerate((even, odd)):
                whole = pick(group, [parts[(q - b) % G] for q in range(G)])
                put(4 * a + b, e, roll(whole, -32 * b - 16 * e))


def solve_kernel(sizes, where, give_kap, strip, upper, *refs):
    stacks = []
    for size in sizes:
        stacks.append((refs[:G],) + tuple(refs[G:size]))
        refs = refs[size:]
    outs = refs[:G]
    rhs, xa, xb, xc, turned, kap, kx, ky, kin, kout, diag, steps = refs[G:]
    zero = jnp.zeros((TILE, LANES), F32)
    targets = (kap, rhs)

    theta = 0.5 * (jnp.full((TILE, LANES), upper[0]) + 1.0)
    delta = 0.5 * (jnp.full((TILE, LANES), upper[0]) - 1.0)
    sigma = theta / delta
    rho = 1.0 / sigma
    for k in range(1, CHEB):
        rho_next = 1.0 / (2.0 * sigma - rho)
        steps[k, 0] = rho_next * rho
        steps[k, 1] = 2.0 * rho_next / delta
        rho = rho_next
    theta_inv = 1.0 / (0.5 * (jnp.full((2 * TILE, LANES), upper[0]) + 1.0))

    def put_at(dst, to, rows):
        def put(i, e, val):
            dst[i, e, pl.ds(to, rows)] = val

        return put

    for dst, (stack, n) in zip(targets, where):
        bricks, *sides = stacks[stack][:3]
        start = TOP - (bricks[0].shape[2] - BY) // 2

        @pl.loop(0, bricks[0].shape[2] // CHUNK)
        def _(t):
            at = pl.ds(pl.multiple_of(CHUNK * t, CHUNK), CHUNK)
            group, within = lanes_of(CHUNK, strip[0])
            unpack(
                lambda d, a: bricks[d][n, a, at],
                lambda side, d: sides[side][n, d, at],
                group,
                within,
                put_at(dst, pl.multiple_of(start + CHUNK * t, TILE), CHUNK),
            )

        if stacks[stack][3:]:
            above, below, *corners = stacks[stack][3:]
            group_halo, within_halo = lanes_of(HALO, strip[0])
            for brick, edge, start in ((above, corners[:2], TOP - HALO), (below, corners[2:], TOP + BY)):
                unpack(
                    lambda d, a: brick[n, d, a],
                    lambda side, d: edge[side][n, d],
                    group_halo,
                    within_halo,
                    put_at(dst, start, HALO),
                )

    for i in range(PLANES):
        for e in range(2):
            for dst in (kap, ky, rhs, xa, xb, xc):
                dst[i, e, 0:TILE] = zero
                dst[i, e, ROWS - TILE : ROWS] = zero
        for dst in (kin, kout):
            dst[i, 0:TILE] = zero
            dst[i, ROWS - TILE : ROWS] = zero

    @pl.loop(0, (ROWS // TILE - 2) // 2)
    def _(t):
        rows = 2 * TILE
        r = pl.multiple_of(TILE + rows * t, TILE)
        at = pl.ds(r, rows)
        first = [kap[0, e, at] for e in range(2)]
        now = first
        before = [4.0 * (k + roll(kap[PLANES - 1, e, at], 32)) for e, k in enumerate(first)]
        for i in range(PLANES):
            after = [kap[i + 1, e, at] if i + 1 < PLANES else roll(first[e], -32) for e in range(2)]
            inner = 4.0 * (now[0] + now[1])
            outer = 4.0 * (now[1] + roll(now[0], -1))
            outer_before = 4.0 * (now[0] + roll(now[1], 1))
            kin[i, at] = inner
            kout[i, at] = outer
            along = (inner + outer_before, inner + outer)
            for e in range(2):
                fx = 4.0 * (now[e] + after[e])
                fy = 4.0 * (now[e] + kap[i, e, pl.ds(r + 1, rows)])
                fym = 4.0 * (now[e] + kap[i, e, pl.ds(r - 1, rows)])
                kx[i, e, at] = fx
                ky[i, e, at] = fy
                diag[i, e, at] = 1.0 + (fx + before[e] + (fy + fym) + along[e])
                before[e] = fx
                xb[i, e, at] = rhs[i, e, at] * theta_inv
                xa[i, e, at] = jnp.zeros((rows, LANES), F32)
            now = after

    def turn_lanes(cur, r):
        at = pl.ds(r, TILE)
        for i in range(PLANES):
            turned[i, 0] = roll(kout[i, at] * cur[i, 1, at], 1)
            turned[i, 1] = roll(cur[i, 0, at], -1)
        for e in range(2):
            turned[PLANES, e] = roll(kx[PLANES - 1, e, at] * cur[PLANES - 1, e, at], 32)
            turned[PLANES + 1, e] = roll(cur[0, e, at], -32)

    def advance(alpha, beta, old, cur, new, r):
        at = pl.ds(r, TILE)
        now = [cur[0, e, at] for e in range(2)]
        before = fbefore = None
        for i in range(PLANES):
            fx = [kx[i, e, at] for e in range(2)]
            inner, outer = kin[i, at], kout[i, at]
            if i + 1 < PLANES:
                after = [cur[i + 1, e, at] for e in range(2)]
            else:
                after = [turned[PLANES + 1, e] for e in range(2)]
            for e in range(2):
                near = ky[i, e, at] * cur[i, e, pl.ds(r + 1, TILE)]
                near = near + ky[i, e, pl.ds(r - 1, TILE)] * cur[i, e, pl.ds(r - 1, TILE)]
                side = turned[i, e]
                near = near + (inner * now[1 - e] + (outer * side if e else side))
                behind = fbefore[e] * before[e] if i else turned[PLANES, e]
                near = near + (fx[e] * after[e] + behind)
                near = near + rhs[i, e, at]
                centre = (1.0 + alpha) - beta * diag[i, e, at]
                new[i, e, at] = centre * now[e] - alpha * old[i, e, at] + beta * near
            before, now, fbefore = now, after, fx

    def sweep(k, old, cur, new, span):
        alpha, beta = steps[k, 0], steps[k, 1]
        turn_lanes(cur, span[0])

        @pl.loop(0, span[1] // span[2])
        def _(t):
            for u in range(span[2]):
                r = pl.multiple_of(span[0] + TILE * (span[2] * t + u), TILE)
                advance(alpha, beta, old, cur, new, r)
                turn_lanes(cur, r + TILE)

    def three(k, spans):
        sweep(k, xa, xb, xc, spans[0])
        sweep(k + 1, xb, xc, xa, spans[1])
        sweep(k + 2, xc, xa, xb, spans[2])

    wide = (TILE, ROWS // TILE - 2, 4)
    narrow = (2 * TILE, ROWS // TILE - 4, 3)

    @pl.loop(0, 2)
    def _(m):
        three(1 + 3 * m, (wide,) * 3)

    three(7, (wide, narrow, narrow))

    @pl.loop(0, 2)
    def _(m):
        three(10 + 3 * m, (narrow,) * 3)

    def mains(whole, group, within):
        parts = [jnp.where(within < 16, even, roll(odd, 16)) for even, odd in whole]
        turned = [roll(parts[i], 32 * (i % 4)) for i in range(PLANES)]
        return parts, [
            [pick(group, [turned[4 * a + (q - d) % G] for q in range(G)]) for a in range(2)] for d in range(G)
        ]

    def beside(whole, parts, group, within):
        tree = [jnp.where(within == 31, odd, even) for even, odd in whole]
        for level in range(3):
            width = 1 << level
            keep = (lax.rem(within + 1, STRIP) < width) | ((within >= 16) & (within < 16 + width))
            tree = [jnp.where(keep, tree[j], roll(tree[j + 1], width)) for j in range(0, len(tree), 2)]
        ends = roll(tree[0], 1)
        groups = (ends, ends, roll(parts[PLANES - 1], 96), roll(parts[0], 64))
        return [pick(group, [groups[(q - d) % G] for q in range(G)]) for d in range(G)]

    def load(field, row, rows):
        return [[field[i, e, pl.ds(row, rows)] for e in range(2)] for i in range(PLANES)]

    @pl.loop(0, BY // CHUNK)
    def _(t):
        row = pl.multiple_of(TOP + CHUNK * t, TILE)
        group, within = lanes_of(CHUNK, strip[0])

        def to(start):
            return pl.ds(pl.multiple_of(start + CHUNK * t, TILE), CHUNK)

        for field, start in ((xb, SIDES),) + (((kap, FIELD),) if give_kap else ()):
            whole = load(field, row, CHUNK)
            parts, main = mains(whole, group, within)
            sides = beside(whole, parts, group, within)
            for d in range(G):
                outs[d][to(start)] = sides[d]
                if field is xb:
                    for a in range(2):
                        outs[d][to(GROUP * a)] = main[d][a]

    sub = lax.broadcasted_iota(jnp.int32, (TILE, LANES), 0)
    group, within = lanes_of(TILE, strip[0])
    for field in (xb, kap) if give_kap else (xb,):
        over = mains(load(field, TOP - TILE, TILE), group, within)[1]
        under = mains(load(field, TOP + BY, TILE), group, within)[1]
        for d in range(G):
            for a in range(2):
                to = GROUP * a + BY if field is xb else KAP + TILE * a
                outs[d][to : to + TILE] = jnp.where(
                    sub == 0, pltpu.roll(over[d][a], 1, 0), pltpu.roll(under[d][a], 1, 0)
                )


def collect(strips, msgs, padded, ends, base, own):
    order = parity_order(True)

    def owners(rows):
        return [lanes_of(rows, strips[d])[0] for d in range(G)]

    def choose(owner, parts, b):
        out = parts[0]
        for d in range(1, G):
            out = jnp.where(owner[d] == b, parts[d], out)
        return roll(out, -32 * b)

    def bricks(row, rows):
        return [roll(msgs[d][pl.ds(row, rows)], -32 * d) for d in range(G)]

    sides_at, tiles_at = (SIDES, (BY, GROUP + BY)) if own is None else (FIELD, (KAP, KAP + TILE))

    @pl.loop(0, BY // CHUNK)
    def _(t):
        to = pl.ds(pl.multiple_of(TILE + CHUNK * t, TILE), CHUNK)
        owner = owners(CHUNK)
        whole, places = [], []
        if own is None:
            for a in range(2):
                parts = bricks(pl.multiple_of(GROUP * a + CHUNK * t, TILE), CHUNK)
                whole += [choose(owner, parts, b) for b in range(4)]
                places += [1 + 4 * a + b for b in range(4)]
        else:
            for c in range(BX):
                padded[1 + c, to] = own[c, pl.ds(pl.multiple_of(CHUNK * t, CHUNK), CHUNK)]
        parts = bricks(pl.multiple_of(sides_at + CHUNK * t, TILE), CHUNK)
        for side, end in enumerate((0, G - 1)):
            val = parts[0]
            for d in range(1, G):
                val = jnp.where(strips[d] == end, parts[d], val)
            ends[side, pl.ds(pl.multiple_of(CHUNK * t, CHUNK), CHUNK)] = val
        whole += [choose(owner, parts, b) for b in (2, 3)]
        places += [0, 1 + BX]
        ordered = reorder(jnp.concatenate(whole, axis=0), order)
        for j, at in enumerate(places):
            padded[at, to] = ordered[CHUNK * j : CHUNK * (j + 1)]

    owner = owners(TILE)
    whole = []
    for a in range(2):
        parts = bricks(tiles_at[a], TILE)
        whole += [choose(owner, parts, b) for b in range(4)]
    ordered = reorder(jnp.concatenate(whole, axis=0), order)
    for c in range(BX):
        val = pltpu.roll(ordered[TILE * c : TILE * (c + 1)], 7, 0)
        padded[1 + c, 0:TILE] = val
        padded[1 + c, TILE + BY : 2 * TILE + BY] = val


def around_cell(padded, ends, c, t):
    lane = lax.broadcasted_iota(jnp.int32, (TILE, LANES), 1)
    r = pl.multiple_of(TILE * t, TILE)
    r8 = pl.multiple_of(TILE * t + TILE, TILE)
    cell = padded[1 + c, pl.ds(r8, TILE)]
    low, high = (ends[side, pl.ds(r, TILE)] for side in range(2))
    return cell, (
        padded[c, pl.ds(r8, TILE)],
        padded[c + 2, pl.ds(r8, TILE)],
        padded[1 + c, pl.ds(r8 - 1, TILE)],
        padded[1 + c, pl.ds(r8 + 1, TILE)],
        jnp.where(lane == 0, roll(low, -c), roll(cell, 1)),
        jnp.where(lane == LANES - 1, roll(high, 14 - c), roll(cell, -1)),
    )


def adjoint_kernel(strips, m0, m1, m2, m3, cond, cot, adjoint, residual, padded, ends, kap, kends):
    collect(strips, (m0, m1, m2, m3), padded, ends, 0, None)
    collect(strips, (m0, m1, m2, m3), kap, kends, 0, cond)

    @pl.loop(0, BY // TILE)
    def _(t):
        at = pl.ds(pl.multiple_of(TILE * t, TILE), TILE)
        for c in range(BX):
            k, knear = around_cell(kap, kends, c, t)
            x, xnear = around_cell(padded, ends, c, t)
            total = 0.0
            for kn, xn in zip(knear, xnear):
                total = total + (k + kn) * (x - xn)
            adjoint[c, at] = x
            residual[c, at] = cot[c, at] - (x + (0.5 * TIME_STEP) * total)


def state_kernel(strips, m0, m1, m2, m3, stored, scales, adj, adj_ends, kap, kends, adj_residual, grad, state, residuals, padded, ends):
    collect(strips, (m0, m1, m2, m3), padded, ends, 0, None)

    @pl.loop(0, BY // TILE)
    def _(t):
        at = pl.ds(pl.multiple_of(TILE * t, TILE), TILE)
        for c in range(BX):
            k, knear = around_cell(kap, kends, c, t)
            x, xnear = around_cell(padded, ends, c, t)
            y, ynear = around_cell(adj, adj_ends, c, t)
            total = product = 0.0
            for kn, xn, yn in zip(knear, xnear, ynear):
                differ = x - xn
                total = total + (k + kn) * differ
                product = product + differ * (y - yn)
            grad[c, at] = (-0.5 * TIME_STEP) * product
            state[c, at] = x
            previous = stored[c, at].astype(F32) * scales[c, at]
            residuals[0, c, at] = previous - (x + (0.5 * TIME_STEP) * total)
            residuals[1, c, at] = adj_residual[c, at]


def call(kernel, outs, smem, vmem, scratch=(), micros=2):
    vm = pl.BlockSpec(memory_space=pltpu.VMEM)
    sm = pl.BlockSpec(memory_space=pltpu.SMEM)
    return pl.pallas_call(
        kernel,
        out_shape=[jax.ShapeDtypeStruct(shape, F32) for shape in outs],
        in_specs=[sm] * len(smem) + [vm] * len(vmem),
        out_specs=[vm] * len(outs),
        scratch_shapes=[pltpu.VMEM(shape, F32) for shape in scratch],
        compiler_params=pltpu.CompilerParams(vmem_limit_bytes=48 * 1024 * 1024),
        cost_estimate=pl.CostEstimate(flops=0, bytes_accessed=micros * 3_000_000, transcendentals=0),
    )(*smem, *vmem)


def shifted(x, axis, by):
    count = lax.axis_size(axis)
    return lax.ppermute(x, axis, [(i, (i + by) % count) for i in range(count)])


def around(x, by, rows=0):
    order = [(g, 0) for g in range(G)] + [(g, 1) for g in reversed(range(G))]
    count = lax.axis_size("gy")
    if rows == 0:
        pairs = [(2 * g + p, 2 * order[(i + by) % len(order)][0] + order[(i + by) % len(order)][1]) for i, (g, p) in enumerate(order)]
        return lax.ppermute(x, ("gx", "pa"), pairs)
    pairs = []
    for i, (g, p) in enumerate(order):
        to_g, to_p = order[(i + by) % len(order)]
        for y in range(count):
            pairs.append(((g * count + y) * 2 + p, (to_g * count + (y + rows) % count) * 2 + to_p))
    return lax.ppermute(x, ("gx", "gy", "pa"), pairs)


def redistributed(conductivity, stored_state, row_scales, cotangent, upper_bound):
    g = lax.axis_index("gx")
    pa = lax.axis_index("pa")

    def strip_of(device):
        return jnp.where(pa == 0, device, G - 1 - device)

    steps = jnp.arange(G, dtype=jnp.int32)
    ahead = lax.rem(g + steps, G)
    behind = lax.rem(g - steps + G, G)
    stored = shifted(stored_state, "pa", 1)
    scales = row_scales[:, :, None]

    strip = strip_of(g)
    left_g = jnp.where(pa == 0, jnp.maximum(g - 1, 0), jnp.minimum(g + 1, G - 1))
    right_g = jnp.where(pa == 0, jnp.minimum(g + 1, G - 1), jnp.maximum(g - 1, 0))
    places = lax.rem(jnp.stack((left_g - g + steps, right_g - g + steps)) + G, G)

    def strips(kernel, shape, arrays, with_rims):
        count, _, rows, _ = shape
        parts = call(kernel, [shape] * G, [strip_of(ahead)], arrays)
        parts = [parts[0]] + [shifted(parts[d], "gx", d) for d in range(1, G)]
        edge = (count, G, rows, LANES)
        rim = (count, G, 2, HALO, LANES)
        corner = (count, G, HALO, LANES)
        to_left, to_right, *rims = call(
            edge_kernel, [edge, edge] + ([rim, rim] + [corner] * 4 if with_rims else []), [places], parts
        )
        halos = [around(to_right, 1), around(to_left, -1)]
        if with_rims:
            head, tail, left_down, left_up, right_down, right_up = rims
            halos += [shifted(tail, "gy", 1), shifted(head, "gy", -1)]
            halos += [
                around(right_down, 1, 1),
                around(left_down, -1, 1),
                around(right_up, 1, -1),
                around(left_up, -1, -1),
            ]
        return [*parts, *halos]

    def solve(where, stacks, give_kap):
        line = (PLANES, 2, ROWS, LANES)
        half = (PLANES, ROWS, LANES)
        solved = call(
            functools.partial(solve_kernel, [len(stack) for stack in stacks], where, give_kap),
            [(BOTH if give_kap else FIELD, LANES)] * G,
            [strip[None], upper_bound],
            sum(stacks, []),
            [line] * 4
            + [(PLANES + 2, 2, TILE, LANES)]
            + [line] * 3
            + [half, half, line]
            + [(CHEB, 2, TILE, LANES)],
            micros=25,
        )
        return [solved[0]] + [shifted(solved[d], "gx", d) for d in range(1, G)]

    first = strips(pack_kernel, (2, 2, BY, LANES), [conductivity, cotangent], True)
    above = shifted(stored[:, BY - HALO :].astype(F32) * scales[:, BY - HALO :], "gy", 1)
    below = shifted(stored[:, :HALO].astype(F32) * scales[:, :HALO], "gy", -1)
    second = strips(pack_previous_kernel, (1, 2, EXTENDED, LANES), [stored, scales, above, below], False)
    solved_adjoint = solve(((0, 0), (0, 1)), [first], True)
    solved_state = solve(((0, 0), (1, 0)), [first, second], False)

    out = (BX, BY, LANES)
    padded = (BX + 2, BY + 16, LANES)
    ends = (2, BY, LANES)
    here = strip_of(behind)
    adjoint, adj_residual, adj, adj_ends, kap, kends = call(
        adjoint_kernel,
        [out, out, padded, ends, padded, ends],
        [here],
        [*solved_adjoint, conductivity, cotangent],
    )
    grad, state, residuals = call(
        state_kernel,
        [out, out, (2,) + out],
        [here],
        [*solved_state, stored, scales, adj, adj_ends, kap, kends, adj_residual],
        [padded, ends],
    )
    return grad, adjoint, state, residuals


def body(conductivity, stored_state, row_scales, cotangent, upper_bound):
    strips_fit = (
        lax.axis_size("gx") == G
        and lax.axis_size("pa") == 2
        and conductivity.shape == (BX, BY, BZ)
    )
    run = redistributed if strips_fit else stepwise
    return tuple(run(conductivity, stored_state, row_scales, cotangent, upper_bound))


def solution(mesh):
    return jax.shard_map(
        body,
        mesh=mesh,
        in_specs=(
            P("gx", "gy", "pa"),
            P("gx", "gy", "pa"),
            P("gx", "gy"),
            P("gx", "gy", "pa"),
            P(),
        ),
        out_specs=(
            P("gx", "gy", "pa"),
            P("gx", "gy", "pa"),
            P("gx", "gy", "pa"),
            P(None, "gx", "gy", "pa"),
        ),
        check_vma=False,
    )
```

time: 196 us -> 162 us (0.83)
  starting transfers between devices: 41.8 us -> 24.7 us
  local copies, waits for them, and re-layouts: 24.8 us -> 10.5 us
  Pallas kernels: 65.8 us -> 70.5 us
  other arithmetic: 4.55 us -> 0.13 us
    unnamed x70 -> x44, local copies, waits for them, and re-layouts: 20.3 us -> 10.2 us
    ppermute x22 -> x17, starting transfers between devices: 27.9 us -> 18.1 us  [shifted(): return lax.ppermute(x, axis, [(i, (i + by) % count) for i in range(count)])]
    ppermute x8 -> x4, starting transfers between devices: 8.02 us -> 2.52 us  [around(): return lax.ppermute(x, ('gx', 'gy', 'pa'), pairs)]
    pallas_call x7 -> x8, Pallas kernels: 65.8 us -> 70.5 us  [call(): pl.pallas_call(kernel, out_shape=[jax.ShapeDtypeStruct(shape, F32) for sh...]
    another operation x9 -> x0, other arithmetic: 4.51 us -> none  [the longest x8 4.51 us: chebyshev_scalars(): return jnp.stack([jnp.stack(row) for row in rows])]
    ppermute x8 -> x4, waiting for transfers between devices: 9.9 us -> 8.76 us  [around(): return lax.ppermute(x, ('gx', 'gy', 'pa'), pairs)]
    ppermute x22 -> x17, waiting for transfers between devices: 44.9 us -> 45.8 us  [shifted(): return lax.ppermute(x, axis, [(i, (i + by) % count) for i in range(count)])]
  transfers between devices with their start and end apart: 34 -> 25, of which waited for: 16 -> 12; matrix products, arithmetic and copies ran while one was open for 6% -> 0% of each run, Pallas kernels for 29% -> 40%
where the time goes in v5:
time: 162 us
  Pallas kernels  70.5 us (44%)
  waiting for transfers between devices  54.6 us (34%)
  starting transfers between devices  24.7 us (15%)
  local copies, waits for them, and re-layouts  10.5 us (6%)
    pallas_call x8, Pallas kernels, call(): pl.pallas_call(kernel, out_shape=[jax.ShapeDtypeStruct(shape, F32) for sh...  70.5 us
    ppermute x17, waiting for transfers between devices, shifted(): return lax.ppermute(x, axis, [(i, (i + by) % count) for i in range(count)])  45.8 us
    ppermute x17, starting transfers between devices, shifted(): return lax.ppermute(x, axis, [(i, (i + by) % count) for i in range(count)])  18.1 us
    unnamed x44, local copies, waits for them, and re-layouts  10.2 us
    ppermute x4, waiting for transfers between devices, around(): return lax.ppermute(x, ('gx', 'gy', 'pa'), pairs)  8.76 us
    ppermute x4, starting transfers between devices, around(): return lax.ppermute(x, ('gx', 'pa'), pairs)  4.09 us
  transfers between devices with their start and end apart: 25, of which 12 were waited for; matrix products, arithmetic and copies ran while one was open for 0% of the time, Pallas kernels for 40%

profile of v5, /device:TPU:8, one launch (start us, length us, event | category | flops | bytes accessed | tf_op | source)
XLA Modules:
  0.0 161.9 jit_solution(18079527737897754552)
XLA Ops:
  0.6 1.6 collective-permute-start.11
  5.6 1.6 collective-permute-start
  8.4 1.8 %collective-permute-start.2 = (f32[2,2,128,128]{3,2,1,0:T(8,128)S(1)}, f32[2,2,128,128]{3,2,1,0:T(8,128)S(1)}, u32[]{:S(2)}, u32[]{:S(2)}) collective-permute-start(f32[2,2,128,128]{3,2,1,0:T(8,128)S(1)} %get-tuple-element.42), channel_id=1, source_target_pairs={{0,24},{8,0},{16,8},{24,16},{1,25},{9,1},{17,9},{25,17},{2,26},{10... | collective-permute-start | bytes 786440 | tf_op jit(solution)/shard_map/ppermute | solution.py:544
  11.0 14.2 %collective-permute-done.refs_1_ = f32[2,2,128,128]{3,2,1,0:T(8,128)S(1)} collective-permute-done((f32[2,2,128,128]{3,2,1,0:T(8,128)S(1)}, f32[2,2,128,128]{3,2,1,0:T(8,128)S(1)}, u32[]{:S(2)}, u32[]{:S(2)}) %collective-permute-start) | collective-permute-done | bytes 262176 | tf_op jit(solution)/shard_map/ppermute | solution.py:544
  25.2 4.2 %collective-permute-done.1.refs_2_ = f32[2,2,128,128]{3,2,1,0:T(8,128)S(1)} collective-permute-done((f32[2,2,128,128]{3,2,1,0:T(8,128)S(1)}, f32[2,2,128,128]{3,2,1,0:T(8,128)S(1)}, u32[]{:S(2)}, u32[]{:S(2)}) %collective-permute-start.1) | collective-permute-done | bytes 262176 | tf_op jit(solution)/shard_map/ppermute | solution.py:544
  29.3 1.8 %collective-permute-done.2.refs_3_ = f32[2,2,128,128]{3,2,1,0:T(8,128)S(1)} collective-permute-done((f32[2,2,128,128]{3,2,1,0:T(8,128)S(1)}, f32[2,2,128,128]{3,2,1,0:T(8,128)S(1)}, u32[]{:S(2)}, u32[]{:S(2)}) %collective-permute-start.2) | collective-permute-done | bytes 262176 | tf_op jit(solution)/shard_map/ppermute | solution.py:544
  31.1 1.9 %shard_map.85 = (f32[2,4,128,128]{3,2,1,0:T(8,128)}, f32[2,4,128,128]{3,2,1,0:T(8,128)}, f32[2,4,2,16,128]{4,3,2,1,0:T(8,128)}, f32[2,4,2,16,128]{4,3,2,1,0:T(8,...) custom-call(s32[2,4]{1,0:T(2,128)S(1)} %compare_select_fusion.places, ...), custom_call_target="tpu_custom_call" | custom-call | bytes 6000000 | tf_op jit(solution)/shard_map/pallas_call | solution.py:531
  33.1 2.0 %collective-permute-start.4 = (f32[2,4,128,128]{3,2,1,0:T(8,128)}, f32[2,4,128,128]{3,2,1,0:T(8,128)S(1)}, u32[]{:S(2)}, u32[]{:S(2)}) collective-permute-start(f32[2,4,128,128]{3,2,1,0:T(8,128)} %get-tuple-element.44), channel_id=1, source_target_pairs={{0,1},{8,0},{16,8},{24,16},{25,24},{17,25},{9,17},{1,9},{2,3},{10,... | collective-permute-start | bytes 1572872 | tf_op jit(solution)/shard_map/ppermute | solution.py:552
  36.7 1.3 collective-permute-done.13.below
  41.9 6.7 %collective-permute-done.7.refs_8_ = f32[2,4,16,128]{3,2,1,0:T(8,128)S(1)} collective-permute-done((f32[2,4,16,128]{3,2,1,0:T(8,128)}, f32[2,4,16,128]{3,2,1,0:T(8,128)S(1)}, u32[]{:S(2)}, u32[]{:S(2)}) %collective-permute-start.7) | collective-permute-done | bytes 65568 | tf_op jit(solution)/shard_map/ppermute | solution.py:558
  50.4 2.1 %collective-permute-start.15 = (f32[1,2,160,128]{3,2,1,0:T(8,128)S(1)}, f32[1,2,160,128]{3,2,1,0:T(8,128)S(1)}, u32[]{:S(2)}, u32[]{:S(2)}) collective-permute-start(f32[1,2,160,128]{3,2,1,0:T(8,128)S(1)} %get-tuple-element.53), channel_id=1, source_target_pairs={{0,16},{8,24},{16,0},{24,8},{1,17},{9,25},{17,1},{25,9},{2,18},{10... | collective-permute-start | bytes 491528 | tf_op jit(solution)/shard_map/ppermute | solution.py:544
  53.1 3.0 %collective-permute-done.14.refs_1_.refs_13_ = f32[1,2,160,128]{3,2,1,0:T(8,128)S(1)} collective-permute-done((f32[1,2,160,128]{3,2,1,0:T(8,128)S(1)}, f32[1,2,160,128]{3,2,1,0:T(8,128)S(1)}, u32[]{:S(2)}, u32[]{:S(2)}) %collective-permute-start.14) | collective-permute-done | bytes 163872 | tf_op jit(solution)/shard_map/ppermute | solution.py:544
  56.1 8.2 %collective-permute-done.15.refs_2_.refs_14_ = f32[1,2,160,128]{3,2,1,0:T(8,128)S(1)} collective-permute-done((f32[1,2,160,128]{3,2,1,0:T(8,128)S(1)}, f32[1,2,160,128]{3,2,1,0:T(8,128)S(1)}, u32[]{:S(2)}, u32[]{:S(2)}) %collective-permute-start.15) | collective-permute-done | bytes 163872 | tf_op jit(solution)/shard_map/ppermute | solution.py:544
  65.7 1.6 shard_map.87
  67.3 2.1 %collective-permute-done.10.refs_11_ = f32[2,4,16,128]{3,2,1,0:T(8,128)S(1)} collective-permute-done((f32[2,4,16,128]{3,2,1,0:T(8,128)S(1)}, f32[2,4,16,128]{3,2,1,0:T(8,128)S(1)}, u32[]{:S(2)}, u32[]{:S(2)}) %collective-permute-start.10) | collective-permute-done | bytes 65568 | tf_op jit(solution)/shard_map/ppermute | solution.py:558
  77.6 25.7 %shard_map.89 = (f32[544,128]{1,0:T(8,128)S(1)}, f32[544,128]{1,0:T(8,128)S(1)}, f32[544,128]{1,0:T(8,128)S(1)}, f32[544,128]{1,0:T(8,128)S(1)}) custom-call(s32[1]{0:T(128)} %bitcast.strip, f32[1]{0:T(128)S(6)} %copy.11.upper, f32[2,2,128,128]{3,2,1,0:T(8,128)S(1)} %get-tuple-element.39.refs_0_, f32[2,2,128,128]{3,2,1,0:T(8,128)S(1)} %collective-permute-done.refs_1_, ...), custom_call_target="tpu_custom_call" | custom-call | bytes 75000000 | tf_op jit(solution)/shard_map/pallas_call | solution.py:531
  104.5 1.6 %collective-permute-start.23 = (f32[544,128]{1,0:T(8,128)S(1)}, f32[544,128]{1,0:T(8,128)S(1)}, u32[]{:S(2)}, u32[]{:S(2)}) collective-permute-start(f32[544,128]{1,0:T(8,128)S(1)} %get-tuple-element.63), channel_id=1, source_target_pairs={{0,16},{8,24},{16,0},{24,8},{1,17},{9,25},{17,1},{25,9},{2,18},{10... | collective-permute-start | bytes 835592 | tf_op jit(solution)/shard_map/ppermute | solution.py:544
  106.1 1.8 %collective-permute-start.24 = (f32[544,128]{1,0:T(8,128)S(1)}, f32[544,128]{1,0:T(8,128)S(1)}, u32[]{:S(2)}, u32[]{:S(2)}) collective-permute-start(f32[544,128]{1,0:T(8,128)S(1)} %get-tuple-element.64), channel_id=1, source_target_pairs={{0,24},{8,0},{16,8},{24,16},{1,25},{9,1},{17,9},{25,17},{2,26},{10... | collective-permute-start | bytes 835592 | tf_op jit(solution)/shard_map/ppermute | solution.py:544
  108.0 25.9 %shard_map.88 = (f32[400,128]{1,0:T(8,128)S(1)}, f32[400,128]{1,0:T(8,128)S(1)}, f32[400,128]{1,0:T(8,128)S(1)}, f32[400,128]{1,0:T(8,128)S(1)}) custom-call(s32[1]{0:T(128)} %bitcast.strip, f32[1]{0:T(128)S(6)} %copy.11.upper, f32[2,2,128,128]{3,2,1,0:T(8,128)S(1)} %get-tuple-element.39.refs_0_, f32[2,2,128,128]{3,2,1,0:T(8,128)S(1)} %collective-permute-done.refs_1_, ...), custom_call_target="tpu_custom_call" | custom-call | bytes 75000000 | tf_op jit(solution)/shard_map/pallas_call | solution.py:531
  134.1 3.1 %collective-permute-start.20 = (f32[400,128]{1,0:T(8,128)S(1)}, f32[400,128]{1,0:T(8,128)S(1)}, u32[]{:S(2)}, u32[]{:S(2)}) collective-permute-start(f32[400,128]{1,0:T(8,128)S(1)} %get-tuple-element.59), channel_id=1, source_target_pairs={{0,16},{8,24},{16,0},{24,8},{1,17},{9,25},{17,1},{25,9},{2,18},{10... | collective-permute-start | bytes 614408 | tf_op jit(solution)/shard_map/ppermute | solution.py:544
  137.3 6.7 %shard_map.90 = (f32[8,128,128]{2,1,0:T(8,128)}, f32[8,128,128]{2,1,0:T(8,128)S(1)}, f32[10,144,128]{2,1,0:T(8,128)S(1)}, f32[2,128,128]{2,1,0:T(8,128)S(1)}, f3...) custom-call(s32[4]{0:T(128)S(1)} %broadcast_select_fusion.1.strips, f32[544,128]{1,0:T(8,128)S(1)} %get-tuple-element.61.m0, ...), custom_call_target="tpu_custom_call" | custom-call | bytes 6000000 | tf_op jit(solution)/shard_map/pallas_call | solution.py:531
  144.0 8.0 %collective-permute-done.20.m2 = f32[400,128]{1,0:T(8,128)S(1)} collective-permute-done((f32[400,128]{1,0:T(8,128)S(1)}, f32[400,128]{1,0:T(8,128)S(1)}, u32[]{:S(2)}, u32[]{:S(2)}) %collective-permute-start.20) | collective-permute-done | bytes 204832 | tf_op jit(solution)/shard_map/ppermute | solution.py:544
  152.0 3.3 %collective-permute-done.21.m3 = f32[400,128]{1,0:T(8,128)S(1)} collective-permute-done((f32[400,128]{1,0:T(8,128)S(1)}, f32[400,128]{1,0:T(8,128)S(1)}, u32[]{:S(2)}, u32[]{:S(2)}) %collective-permute-start.21) | collective-permute-done | bytes 204832 | tf_op jit(solution)/shard_map/ppermute | solution.py:544
  155.4 6.5 %shard_map.91 = (f32[8,128,128]{2,1,0:T(8,128)}, f32[8,128,128]{2,1,0:T(8,128)}, f32[2,8,128,128]{3,2,1,0:T(8,128)}) custom-call(s32[4]{0:T(128)S(1)} %broadcast_select_fusion.1.strips, f32[400,128]{1,0:T(8,128)S(1)} %get-tuple-element.57.m0, f32[400,128]{1,0:T(8,128)S(1)} %collective-permute-done.19.m1, f32[400,128]{1,0:T(8,128)S(1)} %collective-permute-done.20.m2, ...), custom_call_target="tpu_custom_call" | custom-call | bytes 6000000 | tf_op jit(solution)/shard_map/pallas_call | solution.py:531
  (85 shorter events, 23.6 us)
Async XLA Ops:
  0.6 34.5 %collective-permute-start.11 = (bf16[8,128,128]{2,1,0:T(8,128)(2,1)}, bf16[8,128,128]{2,1,0:T(8,128)(2,1)S(1)}, u32[]{:S(2)}, u32[]{:S(2)}) collective-permute-start(bf16[8,128,128]{2,1,0:T(8,128)(2,1)} %param.6), channel_id=1, source_target_pairs={{0,1},{1,0},{2,3},{3,2},{4,5},{5,4},{6,7},{7,6},{8,9},{9,8},{10,11... | collective-permute-start | bytes 786440 | tf_op jit(solution)/shard_map/ppermute | solution.py:544
  5.6 19.6 %collective-permute-start = (f32[2,2,128,128]{3,2,1,0:T(8,128)S(1)}, f32[2,2,128,128]{3,2,1,0:T(8,128)S(1)}, u32[]{:S(2)}, u32[]{:S(2)}) collective-permute-start(f32[2,2,128,128]{3,2,1,0:T(8,128)S(1)} %get-tuple-element.40), channel_id=1, source_target_pairs={{0,8},{8,16},{16,24},{24,0},{1,9},{9,17},{17,25},{25,1},{2,10},{10... | collective-permute-start | bytes 786440 | tf_op jit(solution)/shard_map/ppermute | solution.py:544
  7.2 22.1 %collective-permute-start.1 = (f32[2,2,128,128]{3,2,1,0:T(8,128)S(1)}, f32[2,2,128,128]{3,2,1,0:T(8,128)S(1)}, u32[]{:S(2)}, u32[]{:S(2)}) collective-permute-start(f32[2,2,128,128]{3,2,1,0:T(8,128)S(1)} %get-tuple-element.41), channel_id=1, source_target_pairs={{0,16},{8,24},{16,0},{24,8},{1,17},{9,25},{17,1},{25,9},{2,18},{10... | collective-permute-start | bytes 786440 | tf_op jit(solution)/shard_map/ppermute | solution.py:544
  8.4 22.7 %collective-permute-start.2 = (f32[2,2,128,128]{3,2,1,0:T(8,128)S(1)}, f32[2,2,128,128]{3,2,1,0:T(8,128)S(1)}, u32[]{:S(2)}, u32[]{:S(2)}) collective-permute-start(f32[2,2,128,128]{3,2,1,0:T(8,128)S(1)} %get-tuple-element.42), channel_id=1, source_target_pairs={{0,24},{8,0},{16,8},{24,16},{1,25},{9,1},{17,9},{25,17},{2,26},{10... | collective-permute-start | bytes 786440 | tf_op jit(solution)/shard_map/ppermute | solution.py:544
  33.0 40.3 %collective-permute-start.3 = (f32[2,4,128,128]{3,2,1,0:T(8,128)}, f32[2,4,128,128]{3,2,1,0:T(8,128)S(1)}, u32[]{:S(2)}, u32[]{:S(2)}) collective-permute-start(f32[2,4,128,128]{3,2,1,0:T(8,128)} %get-tuple-element.43), channel_id=1, source_target_pairs={{0,8},{8,16},{16,24},{24,25},{25,17},{17,9},{9,1},{1,0},{2,10},{10... | collective-permute-start | bytes 1572872 | tf_op jit(solution)/shard_map/ppermute | solution.py:552
  33.1 40.3 %collective-permute-start.4 = (f32[2,4,128,128]{3,2,1,0:T(8,128)}, f32[2,4,128,128]{3,2,1,0:T(8,128)S(1)}, u32[]{:S(2)}, u32[]{:S(2)}) collective-permute-start(f32[2,4,128,128]{3,2,1,0:T(8,128)} %get-tuple-element.44), channel_id=1, source_target_pairs={{0,1},{8,0},{16,8},{24,16},{25,24},{17,25},{9,17},{1,9},{2,3},{10,... | collective-permute-start | bytes 1572872 | tf_op jit(solution)/shard_map/ppermute | solution.py:552
  35.8 3.9 %collective-permute-start.12 = (f32[8,16,128]{2,1,0:T(8,128)S(1)}, f32[8,16,128]{2,1,0:T(8,128)S(1)}, u32[]{:S(2)}, u32[]{:S(2)}) collective-permute-start(f32[8,16,128]{2,1,0:T(8,128)S(1)} %get-tuple-element.75), channel_id=1, source_target_pairs={{0,2},{2,4},{4,6},{6,0},{1,3},{3,5},{5,7},{7,1},{8,10},{10,12},{12... | collective-permute-start | bytes 196616 | tf_op jit(solution)/shard_map/ppermute | solution.py:544
  35.8 12.7 %collective-permute-start.7 = (f32[2,4,16,128]{3,2,1,0:T(8,128)}, f32[2,4,16,128]{3,2,1,0:T(8,128)S(1)}, u32[]{:S(2)}, u32[]{:S(2)}) collective-permute-start(f32[2,4,16,128]{3,2,1,0:T(8,128)} %get-tuple-element.47), channel_id=1, source_target_pairs={{0,10},{2,12},{4,14},{6,8},{8,18},{10,20},{12,22},{14,16},{16,26},... | collective-permute-start | bytes 196616 | tf_op jit(solution)/shard_map/ppermute | solution.py:558
  38.0 11.8 %collective-permute-start.8 = (f32[2,4,16,128]{3,2,1,0:T(8,128)}, f32[2,4,16,128]{3,2,1,0:T(8,128)S(1)}, u32[]{:S(2)}, u32[]{:S(2)}) collective-permute-start(f32[2,4,16,128]{3,2,1,0:T(8,128)} %get-tuple-element.48), channel_id=1, source_target_pairs={{0,3},{2,5},{4,7},{6,1},{8,2},{10,4},{12,6},{14,0},{16,10},{18,12}... | collective-permute-start | bytes 196616 | tf_op jit(solution)/shard_map/ppermute | solution.py:558
  39.7 12.8 %collective-permute-start.9 = (f32[2,4,16,128]{3,2,1,0:T(8,128)S(1)}, f32[2,4,16,128]{3,2,1,0:T(8,128)S(1)}, u32[]{:S(2)}, u32[]{:S(2)}) collective-permute-start(f32[2,4,16,128]{3,2,1,0:T(8,128)S(1)} %get-tuple-element.49), channel_id=1, source_target_pairs={{0,14},{2,8},{4,10},{6,12},{8,22},{10,16},{12,18},{14,20},{16,30},... | collective-permute-start | bytes 196616 | tf_op jit(solution)/shard_map/ppermute | solution.py:558
  49.1 7.0 %collective-permute-start.14 = (f32[1,2,160,128]{3,2,1,0:T(8,128)S(1)}, f32[1,2,160,128]{3,2,1,0:T(8,128)S(1)}, u32[]{:S(2)}, u32[]{:S(2)}) collective-permute-start(f32[1,2,160,128]{3,2,1,0:T(8,128)S(1)} %get-tuple-element.52), channel_id=1, source_target_pairs={{0,8},{8,16},{16,24},{24,0},{1,9},{9,17},{17,25},{25,1},{2,10},{10... | collective-permute-start | bytes 491528 | tf_op jit(solution)/shard_map/ppermute | solution.py:544
  50.4 14.0 %collective-permute-start.15 = (f32[1,2,160,128]{3,2,1,0:T(8,128)S(1)}, f32[1,2,160,128]{3,2,1,0:T(8,128)S(1)}, u32[]{:S(2)}, u32[]{:S(2)}) collective-permute-start(f32[1,2,160,128]{3,2,1,0:T(8,128)S(1)} %get-tuple-element.53), channel_id=1, source_target_pairs={{0,16},{8,24},{16,0},{24,8},{1,17},{9,25},{17,1},{25,9},{2,18},{10... | collective-permute-start | bytes 491528 | tf_op jit(solution)/shard_map/ppermute | solution.py:544
  53.1 12.6 %collective-permute-start.16 = (f32[1,2,160,128]{3,2,1,0:T(8,128)S(1)}, f32[1,2,160,128]{3,2,1,0:T(8,128)S(1)}, u32[]{:S(2)}, u32[]{:S(2)}) collective-permute-start(f32[1,2,160,128]{3,2,1,0:T(8,128)S(1)} %get-tuple-element.54), channel_id=1, source_target_pairs={{0,24},{8,0},{16,8},{24,16},{1,25},{9,1},{17,9},{25,17},{2,26},{10... | collective-permute-start | bytes 491528 | tf_op jit(solution)/shard_map/ppermute | solution.py:544
  56.1 14.8 %collective-permute-start.5 = (f32[2,4,2,16,128]{4,3,2,1,0:T(8,128)S(1)}, f32[2,4,2,16,128]{4,3,2,1,0:T(8,128)S(1)}, u32[]{:S(2)}, u32[]{:S(2)}) collective-permute-start(f32[2,4,2,16,128]{4,3,2,1,0:T(8,128)S(1)} %copy-done.18), channel_id=1, source_target_pairs={{0,2},{2,4},{4,6},{6,0},{1,3},{3,5},{5,7},{7,1},{8,10},{10,12},{12... | collective-permute-start | bytes 393224 | tf_op jit(solution)/shard_map/ppermute | solution.py:544
  64.3 9.0 %collective-permute-start.6 = (f32[2,4,2,16,128]{4,3,2,1,0:T(8,128)}, f32[2,4,2,16,128]{4,3,2,1,0:T(8,128)}, u32[]{:S(2)}, u32[]{:S(2)}) collective-permute-start(f32[2,4,2,16,128]{4,3,2,1,0:T(8,128)} %get-tuple-element.46), channel_id=1, source_target_pairs={{0,6},{2,0},{4,2},{6,4},{1,7},{3,1},{5,3},{7,5},{8,14},{10,8},{12,... | collective-permute-start | bytes 393224 | tf_op jit(solution)/shard_map/ppermute | solution.py:544
  65.7 3.7 %collective-permute-start.10 = (f32[2,4,16,128]{3,2,1,0:T(8,128)S(1)}, f32[2,4,16,128]{3,2,1,0:T(8,128)S(1)}, u32[]{:S(2)}, u32[]{:S(2)}) collective-permute-start(f32[2,4,16,128]{3,2,1,0:T(8,128)S(1)} %copy-done.20), channel_id=1, source_target_pairs={{0,7},{2,1},{4,3},{6,5},{8,6},{10,0},{12,2},{14,4},{16,14},{18,8},... | collective-permute-start | bytes 196616 | tf_op jit(solution)/shard_map/ppermute | solution.py:558
  70.0 37.9 %collective-permute-start.17 = (f32[1,4,160,128]{3,2,1,0:T(8,128)}, f32[1,4,160,128]{3,2,1,0:T(8,128)}, u32[]{:S(2)}, u32[]{:S(2)}) collective-permute-start(f32[1,4,160,128]{3,2,1,0:T(8,128)} %get-tuple-element.55), channel_id=1, source_target_pairs={{0,8},{8,16},{16,24},{24,25},{25,17},{17,9},{9,1},{1,0},{2,10},{10... | collective-permute-start | bytes 983048 | tf_op jit(solution)/shard_map/ppermute | solution.py:552
  71.6 36.3 %collective-permute-start.18 = (f32[1,4,160,128]{3,2,1,0:T(8,128)}, f32[1,4,160,128]{3,2,1,0:T(8,128)}, u32[]{:S(2)}, u32[]{:S(2)}) collective-permute-start(f32[1,4,160,128]{3,2,1,0:T(8,128)} %get-tuple-element.56), channel_id=1, source_target_pairs={{0,1},{8,0},{16,8},{24,16},{25,24},{17,25},{9,17},{1,9},{2,3},{10,... | collective-permute-start | bytes 983048 | tf_op jit(solution)/shard_map/ppermute | solution.py:552
  103.3 33.9 %collective-permute-start.22 = (f32[544,128]{1,0:T(8,128)S(1)}, f32[544,128]{1,0:T(8,128)S(1)}, u32[]{:S(2)}, u32[]{:S(2)}) collective-permute-start(f32[544,128]{1,0:T(8,128)S(1)} %get-tuple-element.62), channel_id=1, source_target_pairs={{0,8},{8,16},{16,24},{24,0},{1,9},{9,17},{17,25},{25,1},{2,10},{10... | collective-permute-start | bytes 835592 | tf_op jit(solution)/shard_map/ppermute | solution.py:544
  104.5 32.8 %collective-permute-start.23 = (f32[544,128]{1,0:T(8,128)S(1)}, f32[544,128]{1,0:T(8,128)S(1)}, u32[]{:S(2)}, u32[]{:S(2)}) collective-permute-start(f32[544,128]{1,0:T(8,128)S(1)} %get-tuple-element.63), channel_id=1, source_target_pairs={{0,16},{8,24},{16,0},{24,8},{1,17},{9,25},{17,1},{25,9},{2,18},{10... | collective-permute-start | bytes 835592 | tf_op jit(solution)/shard_map/ppermute | solution.py:544
  106.1 31.1 %collective-permute-start.24 = (f32[544,128]{1,0:T(8,128)S(1)}, f32[544,128]{1,0:T(8,128)S(1)}, u32[]{:S(2)}, u32[]{:S(2)}) collective-permute-start(f32[544,128]{1,0:T(8,128)S(1)} %get-tuple-element.64), channel_id=1, source_target_pairs={{0,24},{8,0},{16,8},{24,16},{1,25},{9,1},{17,9},{25,17},{2,26},{10... | collective-permute-start | bytes 835592 | tf_op jit(solution)/shard_map/ppermute | solution.py:544
  133.9 10.1 %collective-permute-start.19 = (f32[400,128]{1,0:T(8,128)S(1)}, f32[400,128]{1,0:T(8,128)S(1)}, u32[]{:S(2)}, u32[]{:S(2)}) collective-permute-start(f32[400,128]{1,0:T(8,128)S(1)} %get-tuple-element.58), channel_id=1, source_target_pairs={{0,8},{8,16},{16,24},{24,0},{1,9},{9,17},{17,25},{25,1},{2,10},{10... | collective-permute-start | bytes 614408 | tf_op jit(solution)/shard_map/ppermute | solution.py:544
  134.1 17.9 %collective-permute-start.20 = (f32[400,128]{1,0:T(8,128)S(1)}, f32[400,128]{1,0:T(8,128)S(1)}, u32[]{:S(2)}, u32[]{:S(2)}) collective-permute-start(f32[400,128]{1,0:T(8,128)S(1)} %get-tuple-element.59), channel_id=1, source_target_pairs={{0,16},{8,24},{16,0},{24,8},{1,17},{9,25},{17,1},{25,9},{2,18},{10... | collective-permute-start | bytes 614408 | tf_op jit(solution)/shard_map/ppermute | solution.py:544
  137.2 18.1 %collective-permute-start.21 = (f32[400,128]{1,0:T(8,128)S(1)}, f32[400,128]{1,0:T(8,128)S(1)}, u32[]{:S(2)}, u32[]{:S(2)}) collective-permute-start(f32[400,128]{1,0:T(8,128)S(1)} %get-tuple-element.60), channel_id=1, source_target_pairs={{0,24},{8,0},{16,8},{24,16},{1,25},{9,1},{17,9},{25,17},{2,26},{10... | collective-permute-start | bytes 614408 | tf_op jit(solution)/shard_map/ppermute | solution.py:544
  (23 other events, 215.2 us)

commit v6 on v5

--- a/solution.py
+++ b/solution.py
@@ -154,20 +154,33 @@
                 outs[d][n, a] = pick(groups[d], parts)
 
 
-def pack_previous_kernel(strips, stored, scales, above, below, *outs):
-    order = parity_order(False)
-    for rows, start, array in ((BY, HALO, stored), (HALO, 0, above), (HALO, HALO + BY, below)):
+def pack_previous_kernel(strips, both, above, below, *outs):
+    src = lax.broadcasted_iota(jnp.int32, (2 * LANES, 2 * LANES), 0)
+    dst = lax.broadcasted_iota(jnp.int32, (2 * LANES, 2 * LANES), 1)
+    place = LANES * lax.rem(src, 2) + 64 * (src // LANES) + lax.rem(src, LANES) // 2
+    order = jnp.where(place == dst, 1.0, 0.0).astype(jnp.bfloat16)
+
+    def give(planes, rows, start):
         groups = [lanes_of(rows, strips[d])[0] for d in range(G)]
-        for a in range(2):
-            planes = reorder(array[4 * a : 4 * a + 4].reshape(4 * rows, LANES), order)
-            parts = []
-            for b in range(4):
-                plane = planes[rows * b : rows * (b + 1)]
-                if array is stored:
-                    plane = plane * scales[4 * a + b]
-                parts.append(roll(plane, 32 * b))
+        for m in range(4):
+            pieces = []
+            for i in (2 * m, 2 * m + 1):
+                pair = planes[rows * i : rows * (i + 1)]
+                for e in range(2):
+                    pieces.append(pair[:, LANES * e : LANES * (e + 1)])
             for d in range(G):
-                outs[d][0, a, start : start + rows] = pick(groups[d], parts)
+                turned = [pltpu.roll(pieces[k], lax.rem(16 * strips[d] + 32 * k + 8, LANES), 1) for k in range(4)]
+                outs[d][m, pl.ds(start, rows)] = pick(groups[d], turned)
+
+    @pl.loop(0, BY // CHUNK)
+    def _(t):
+        r = pl.multiple_of(CHUNK * t, CHUNK)
+        halves = [both[half, :, pl.ds(r, CHUNK)].reshape(BX * CHUNK, LANES) for half in range(2)]
+        give(reorder(jnp.concatenate(halves, axis=1), order), CHUNK, pl.multiple_of(HALO + CHUNK * t, HALO))
+
+    for start, array in ((0, above), (HALO + BY, below)):
+        halves = [array[half].reshape(BX * HALO, LANES) for half in range(2)]
+        give(reorder(jnp.concatenate(halves, axis=1), order), HALO, start)
 
 
 def edge_kernel(places, *refs):
@@ -212,7 +225,17 @@
                 put(4 * a + b, e, roll(whole, -32 * b - 16 * e))
 
 
-def solve_kernel(sizes, where, give_kap, strip, upper, *refs):
+def unpack_strip(get, group, put):
+    by_block = [BLOCK.index(q) for q in range(G)]
+    for m in range(4):
+        turned = [roll(get(by_block[q], m), 32 * q) for q in range(G)]
+        for k in range(4):
+            whole = pick(group, [turned[(q - k) % G] for q in range(G)])
+            put(2 * m + k // 2, k % 2, roll(whole, -32 * k - 8))
+
+
+def solve_kernel(sizes, give_kap, strip, upper, *refs):
+    refs, finish = fetch(refs, sum(sizes))
     stacks = []
     for size in sizes:
         stacks.append((refs[:G],) + tuple(refs[G:size]))
@@ -239,11 +262,35 @@
 
         return put
 
-    for dst, (stack, n) in zip(targets, where):
-        bricks, *sides = stacks[stack][:3]
-        start = TOP - (bricks[0].shape[2] - BY) // 2
-
-        @pl.loop(0, bricks[0].shape[2] // CHUNK)
+    for i in range(PLANES):
+        for e in range(2):
+            for dst in (kap, ky, rhs, xa, xb, xc):
+                dst[i, e, 0:TILE] = zero
+                dst[i, e, ROWS - TILE : ROWS] = zero
+        for dst in (kin, kout):
+            dst[i, 0:TILE] = zero
+            dst[i, ROWS - TILE : ROWS] = zero
+
+    finish()
+
+    for n, dst in enumerate(targets):
+        bricks, *sides = stacks[0][:3]
+        if n == 1 and len(stacks) > 1:
+            strips_here = stacks[1][0]
+
+            @pl.loop(0, EXTENDED // CHUNK)
+            def _(t):
+                at = pl.ds(pl.multiple_of(CHUNK * t, CHUNK), CHUNK)
+                group, _ = lanes_of(CHUNK, strip[0])
+                unpack_strip(
+                    lambda d, m: strips_here[d][m, at],
+                    group,
+                    put_at(dst, pl.multiple_of(TOP - HALO + CHUNK * t, TILE), CHUNK),
+                )
+
+            continue
+
+        @pl.loop(0, BY // CHUNK)
         def _(t):
             at = pl.ds(pl.multiple_of(CHUNK * t, CHUNK), CHUNK)
             group, within = lanes_of(CHUNK, strip[0])
@@ -252,29 +299,19 @@
                 lambda side, d: sides[side][n, d, at],
                 group,
                 within,
-                put_at(dst, pl.multiple_of(start + CHUNK * t, TILE), CHUNK),
+                put_at(dst, pl.multiple_of(TOP + CHUNK * t, TILE), CHUNK),
             )
 
-        if stacks[stack][3:]:
-            above, below, *corners = stacks[stack][3:]
-            group_halo, within_halo = lanes_of(HALO, strip[0])
-            for brick, edge, start in ((above, corners[:2], TOP - HALO), (below, corners[2:], TOP + BY)):
-                unpack(
-                    lambda d, a: brick[n, d, a],
-                    lambda side, d: edge[side][n, d],
-                    group_halo,
-                    within_halo,
-                    put_at(dst, start, HALO),
-                )
-
-    for i in range(PLANES):
-        for e in range(2):
-            for dst in (kap, ky, rhs, xa, xb, xc):
-                dst[i, e, 0:TILE] = zero
-                dst[i, e, ROWS - TILE : ROWS] = zero
-        for dst in (kin, kout):
-            dst[i, 0:TILE] = zero
-            dst[i, ROWS - TILE : ROWS] = zero
+        above, below, *corners = stacks[0][3:]
+        group_halo, within_halo = lanes_of(HALO, strip[0])
+        for brick, edge, start in ((above, corners[:2], TOP - HALO), (below, corners[2:], TOP + BY)):
+            unpack(
+                lambda d, a: brick[n, d, a],
+                lambda side, d: edge[side][n, d],
+                group_halo,
+                within_halo,
+                put_at(dst, start, HALO),
+            )
 
     @pl.loop(0, (ROWS // TILE - 2) // 2)
     def _(t):
@@ -503,7 +540,7 @@
             residual[c, at] = cot[c, at] - (x + (0.5 * TIME_STEP) * total)
 
 
-def state_kernel(strips, m0, m1, m2, m3, stored, scales, adj, adj_ends, kap, kends, adj_residual, grad, state, residuals, padded, ends):
+def state_kernel(strips, m0, m1, m2, m3, previous, adj, adj_ends, kap, kends, adj_residual, grad, state, residuals, padded, ends):
     collect(strips, (m0, m1, m2, m3), padded, ends, 0, None)
 
     @pl.loop(0, BY // TILE)
@@ -520,20 +557,47 @@
                 product = product + differ * (y - yn)
             grad[c, at] = (-0.5 * TIME_STEP) * product
             state[c, at] = x
-            previous = stored[c, at].astype(F32) * scales[c, at]
-            residuals[0, c, at] = previous - (x + (0.5 * TIME_STEP) * total)
+            residuals[0, c, at] = previous[0, c, at] - (x + (0.5 * TIME_STEP) * total)
             residuals[1, c, at] = adj_residual[c, at]
 
 
-def call(kernel, outs, smem, vmem, scratch=(), micros=2):
+def fetch(refs, count):
+    away, here, sems = refs[:count], refs[len(refs) - count - 1 : -1], refs[-1]
+    copies = [pltpu.make_async_copy(a, h, sems.at[j]) for j, (a, h) in enumerate(zip(away, here))]
+    for copy in copies:
+        copy.start()
+
+    def finish():
+        for copy in copies:
+            copy.wait()
+
+    return (*here, *refs[count : len(refs) - count - 1]), finish
+
+
+def fetched(flags, smem, kernel, *refs):
+    ins, rest = refs[smem : smem + len(flags)], refs[smem + len(flags) :]
+    away = [ref for ref, flag in zip(ins, flags) if flag]
+    inner, finish = fetch((*away, *rest), len(away))
+    finish()
+    here = iter(inner[: len(away)])
+    ins = [next(here) if flag else ref for ref, flag in zip(ins, flags)]
+    kernel(*refs[:smem], *ins, *inner[len(away) :])
+
+
+def call(kernel, outs, smem, vmem, scratch=(), micros=2, fetches=False):
     vm = pl.BlockSpec(memory_space=pltpu.VMEM)
     sm = pl.BlockSpec(memory_space=pltpu.SMEM)
+    hbm = pl.BlockSpec(memory_space=pltpu.HBM)
+    flags = [x.shape[-1] == LANES for x in vmem]
+    copies = [pltpu.VMEM(x.shape, x.dtype) for x, flag in zip(vmem, flags) if flag]
     return pl.pallas_call(
-        kernel,
+        kernel if fetches else functools.partial(fetched, flags, len(smem), kernel),
         out_shape=[jax.ShapeDtypeStruct(shape, F32) for shape in outs],
-        in_specs=[sm] * len(smem) + [vm] * len(vmem),
+        in_specs=[sm] * len(smem) + [hbm if flag else vm for flag in flags],
         out_specs=[vm] * len(outs),
-        scratch_shapes=[pltpu.VMEM(shape, F32) for shape in scratch],
+        scratch_shapes=[pltpu.VMEM(shape, F32) for shape in scratch]
+        + copies
+        + [pltpu.SemaphoreType.DMA((len(copies),))],
         compiler_params=pltpu.CompilerParams(vmem_limit_bytes=48 * 1024 * 1024),
         cost_estimate=pl.CostEstimate(flops=0, bytes_accessed=micros * 3_000_000, transcendentals=0),
     )(*smem, *vmem)
@@ -576,33 +640,45 @@
     right_g = jnp.where(pa == 0, jnp.minimum(g + 1, G - 1), jnp.maximum(g - 1, 0))
     places = lax.rem(jnp.stack((left_g - g + steps, right_g - g + steps)) + G, G)
 
-    def strips(kernel, shape, arrays, with_rims):
-        count, _, rows, _ = shape
-        parts = call(kernel, [shape] * G, [strip_of(ahead)], arrays)
-        parts = [parts[0]] + [shifted(parts[d], "gx", d) for d in range(1, G)]
-        edge = (count, G, rows, LANES)
-        rim = (count, G, 2, HALO, LANES)
-        corner = (count, G, HALO, LANES)
-        to_left, to_right, *rims = call(
-            edge_kernel, [edge, edge] + ([rim, rim] + [corner] * 4 if with_rims else []), [places], parts
-        )
-        halos = [around(to_right, 1), around(to_left, -1)]
-        if with_rims:
-            head, tail, left_down, left_up, right_down, right_up = rims
-            halos += [shifted(tail, "gy", 1), shifted(head, "gy", -1)]
-            halos += [
-                around(right_down, 1, 1),
-                around(left_down, -1, 1),
-                around(right_up, 1, -1),
-                around(left_up, -1, -1),
-            ]
-        return [*parts, *halos]
-
-    def solve(where, stacks, give_kap):
+    brick = (2, 2, BY, LANES)
+    parts = call(pack_kernel, [brick] * G, [strip_of(ahead)], [conductivity, cotangent])
+    parts = [parts[0]] + [shifted(parts[d], "gx", d) for d in range(1, G)]
+    both = jnp.stack((stored, stored_state)).astype(F32) * scales
+    above = shifted(both[:, :, BY - HALO :], "gy", 1)
+    below = shifted(both[:, :, :HALO], "gy", -1)
+    messages = call(
+        pack_previous_kernel,
+        [(4, EXTENDED, LANES)] * G,
+        [strip_of(ahead)],
+        [both, above, below],
+    )
+    parts, messages = lax.optimization_barrier((parts, messages))
+    edge = (2, G, BY, LANES)
+    rim = (2, G, 2, HALO, LANES)
+    corner = (2, G, HALO, LANES)
+    to_left, to_right, head, tail, left_down, left_up, right_down, right_up = call(
+        edge_kernel, [edge, edge, rim, rim] + [corner] * 4, [places], parts
+    )
+    halos = [
+        around(to_right, 1),
+        around(to_left, -1),
+        shifted(tail, "gy", 1),
+        shifted(head, "gy", -1),
+        around(right_down, 1, 1),
+        around(left_down, -1, 1),
+        around(right_up, 1, -1),
+        around(left_up, -1, -1),
+    ]
+
+    messages, halos = lax.optimization_barrier((messages, halos))
+    first = [*parts, *halos]
+    second = [messages[0]] + [shifted(messages[d], "gx", d) for d in range(1, G)]
+
+    def solve(stacks, give_kap):
         line = (PLANES, 2, ROWS, LANES)
         half = (PLANES, ROWS, LANES)
         solved = call(
-            functools.partial(solve_kernel, [len(stack) for stack in stacks], where, give_kap),
+            functools.partial(solve_kernel, [len(stack) for stack in stacks], give_kap),
             [(BOTH if give_kap else FIELD, LANES)] * G,
             [strip[None], upper_bound],
             sum(stacks, []),
@@ -612,15 +688,12 @@
             + [half, half, line]
             + [(CHEB, 2, TILE, LANES)],
             micros=25,
+            fetches=True,
         )
         return [solved[0]] + [shifted(solved[d], "gx", d) for d in range(1, G)]
 
-    first = strips(pack_kernel, (2, 2, BY, LANES), [conductivity, cotangent], True)
-    above = shifted(stored[:, BY - HALO :].astype(F32) * scales[:, BY - HALO :], "gy", 1)
-    below = shifted(stored[:, :HALO].astype(F32) * scales[:, :HALO], "gy", -1)
-    second = strips(pack_previous_kernel, (1, 2, EXTENDED, LANES), [stored, scales, above, below], False)
-    solved_adjoint = solve(((0, 0), (0, 1)), [first], True)
-    solved_state = solve(((0, 0), (1, 0)), [first, second], False)
+    solved_adjoint = solve([first], True)
+    solved_state = solve([first, second], False)
 
     out = (BX, BY, LANES)
     padded = (BX + 2, BY + 16, LANES)
@@ -636,7 +709,7 @@
         state_kernel,
         [out, out, (2,) + out],
         [here],
-        [*solved_state, stored, scales, adj, adj_ends, kap, kends, adj_residual],
+        [*solved_state, both, adj, adj_ends, kap, kends, adj_residual],
         [padded, ends],
     )
     return grad, adjoint, state, residuals

time: 162 us -> 146 us (0.901)
  waiting for transfers between devices: 54.6 us -> 36.6 us
  local copies, waits for them, and re-layouts: 10.5 us -> 6.42 us
  Pallas kernels: 70.5 us -> 74.3 us
  starting transfers between devices: 24.7 us -> 26.5 us
    ppermute x17, waiting for transfers between devices: 45.8 us -> 22.6 us  [shifted(): return lax.ppermute(x, axis, [(i, (i + by) % count) for i in range(count)])]
    ppermute x4, waiting for transfers between devices: 8.76 us -> 13.9 us  [around(): return lax.ppermute(x, ('gx', 'gy', 'pa'), pairs)]
    pallas_call x8 -> x7, Pallas kernels: 70.5 us -> 74.3 us  [call(): pl.pallas_call(kernel if fetches else functools.partial(fetched, flags, l...]
    unnamed x44 -> x24, local copies, waits for them, and re-layouts: 10.2 us -> 6.4 us
    ppermute x17, starting transfers between devices: 18.1 us -> 21.2 us  [shifted(): return lax.ppermute(x, axis, [(i, (i + by) % count) for i in range(count)])]
    ppermute x4 -> x2, starting transfers between devices: 4.09 us -> 2.07 us  [around(): return lax.ppermute(x, ('gx', 'pa'), pairs)]
  transfers between devices with their start and end apart: 25 -> 23, of which waited for: 12 -> 10; matrix products, arithmetic and copies ran while one was open for 0% -> 0% of each run, Pallas kernels for 40% -> 45%
where the time goes in v6:
time: 146 us
  Pallas kernels  74.3 us (51%)
  waiting for transfers between devices  36.6 us (25%)
  starting transfers between devices  26.5 us (18%)
  local copies, waits for them, and re-layouts  6.42 us (4%)
  between operations  1.48 us (1%)
    pallas_call x7, Pallas kernels, call(): pl.pallas_call(kernel if fetches else functools.partial(fetched, flags, l...  74.3 us
    ppermute x17, waiting for transfers between devices, shifted(): return lax.ppermute(x, axis, [(i, (i + by) % count) for i in range(count)])  22.6 us
    ppermute x17, starting transfers between devices, shifted(): return lax.ppermute(x, axis, [(i, (i + by) % count) for i in range(count)])  21.2 us
    ppermute x4, waiting for transfers between devices, around(): return lax.ppermute(x, ('gx', 'gy', 'pa'), pairs)  13.9 us
    unnamed x24, local copies, waits for them, and re-layouts  6.4 us
    ppermute x4, starting transfers between devices, around(): return lax.ppermute(x, ('gx', 'gy', 'pa'), pairs)  3.14 us
  transfers between devices with their start and end apart: 23, of which 10 were waited for; matrix products, arithmetic and copies ran while one was open for 0% of the time, Pallas kernels for 45%

profile of v6, /device:TPU:8, one launch (start us, length us, event | category | flops | bytes accessed | tf_op | source)
XLA Modules:
  0.0 145.5 jit_solution(11397074797131987107)
XLA Ops:
  5.7 1.6 %collective-permute-start = (f32[2,2,128,128]{3,2,1,0:T(8,128)S(1)}, f32[2,2,128,128]{3,2,1,0:T(8,128)S(1)}, u32[]{:S(2)}, u32[]{:S(2)}) collective-permute-start(f32[2,2,128,128]{3,2,1,0:T(8,128)S(1)} %get-tuple-element.58), channel_id=1, source_target_pairs={{0,8},{8,16},{16,24},{24,0},{1,9},{9,17},{17,25},{25,1},{2,10},{10... | collective-permute-start | bytes 786440 | tf_op jit(solution)/shard_map/ppermute | solution.py:608
  8.5 1.8 %collective-permute-start.2 = (f32[2,2,128,128]{3,2,1,0:T(8,128)S(1)}, f32[2,2,128,128]{3,2,1,0:T(8,128)S(1)}, u32[]{:S(2)}, u32[]{:S(2)}) collective-permute-start(f32[2,2,128,128]{3,2,1,0:T(8,128)S(1)} %get-tuple-element.60), channel_id=1, source_target_pairs={{0,24},{8,0},{16,8},{24,16},{1,25},{9,1},{17,9},{25,17},{2,26},{10... | collective-permute-start | bytes 786440 | tf_op jit(solution)/shard_map/ppermute | solution.py:608
  11.8 2.4 %collective-permute-done.5.refs_3_ = f32[2,8,16,128]{3,2,1,0:T(8,128)S(1)} collective-permute-done((f32[2,8,16,128]{3,2,1,0:T(8,128)S(1)}, f32[2,8,16,128]{3,2,1,0:T(8,128)S(1)}, u32[]{:S(2)}, u32[]{:S(2)}) %collective-permute-start.5) | collective-permute-done | bytes 131104 | tf_op jit(solution)/shard_map/ppermute | solution.py:608
  14.2 2.9 %collective-permute-done.4.refs_2_ = f32[2,8,16,128]{3,2,1,0:T(8,128)S(1)} collective-permute-done((f32[2,8,16,128]{3,2,1,0:T(8,128)S(1)}, f32[2,8,16,128]{3,2,1,0:T(8,128)S(1)}, u32[]{:S(2)}, u32[]{:S(2)}) %collective-permute-start.4) | collective-permute-done | bytes 131104 | tf_op jit(solution)/shard_map/ppermute | solution.py:608
  17.2 4.8 %shard_map.85 = (f32[4,160,128]{2,1,0:T(8,128)S(1)}, f32[4,160,128]{2,1,0:T(8,128)}, f32[4,160,128]{2,1,0:T(8,128)}, f32[4,160,128]{2,1,0:T(8,128)}) custom-call(s32[4]{0:T(128)S(1)} %broadcast_select_fusion.refs_0_, f32[2,8,128,128]{3,2,1,0:T(8,128)S(1)} %convert_multiply_fusion.refs_1_.refs_5_, f32[2,8,16,128]{3,2,1,0:T(8,128)S(1)} %collective-permute-done.4.refs_2_, ...), custom_call_target="tpu_custom_call" | custom-call | bytes 6000000 | tf_op jit(solution)/shard_map/pallas_call | solution.py:593
  22.6 2.6 %collective-permute-done.refs_2_.refs_1_ = f32[2,2,128,128]{3,2,1,0:T(8,128)S(1)} collective-permute-done((f32[2,2,128,128]{3,2,1,0:T(8,128)S(1)}, f32[2,2,128,128]{3,2,1,0:T(8,128)S(1)}, u32[]{:S(2)}, u32[]{:S(2)}) %collective-permute-start) | collective-permute-done | bytes 262176 | tf_op jit(solution)/shard_map/ppermute | solution.py:608
  25.3 4.2 %collective-permute-done.1.refs_3_.refs_2_ = f32[2,2,128,128]{3,2,1,0:T(8,128)S(1)} collective-permute-done((f32[2,2,128,128]{3,2,1,0:T(8,128)S(1)}, f32[2,2,128,128]{3,2,1,0:T(8,128)S(1)}, u32[]{:S(2)}, u32[]{:S(2)}) %collective-permute-start.1) | collective-permute-done | bytes 262176 | tf_op jit(solution)/shard_map/ppermute | solution.py:608
  29.4 1.8 %collective-permute-done.2.refs_4_.refs_3_ = f32[2,2,128,128]{3,2,1,0:T(8,128)S(1)} collective-permute-done((f32[2,2,128,128]{3,2,1,0:T(8,128)S(1)}, f32[2,2,128,128]{3,2,1,0:T(8,128)S(1)}, u32[]{:S(2)}, u32[]{:S(2)}) %collective-permute-start.2) | collective-permute-done | bytes 262176 | tf_op jit(solution)/shard_map/ppermute | solution.py:608
  32.3 2.0 %collective-permute-start.7 = (f32[2,4,128,128]{3,2,1,0:T(8,128)S(1)}, f32[2,4,128,128]{3,2,1,0:T(8,128)S(1)}, u32[]{:S(2)}, u32[]{:S(2)}) collective-permute-start(f32[2,4,128,128]{3,2,1,0:T(8,128)S(1)} %get-tuple-element.74), channel_id=1, source_target_pairs={{0,1},{8,0},{16,8},{24,16},{25,24},{17,25},{9,17},{1,9},{2,3},{10,... | collective-permute-start | bytes 1572872 | tf_op jit(solution)/shard_map/ppermute | solution.py:616
  34.3 2.7 %collective-permute-start.11 = (f32[2,4,16,128]{3,2,1,0:T(8,128)S(1)}, f32[2,4,16,128]{3,2,1,0:T(8,128)S(1)}, u32[]{:S(2)}, u32[]{:S(2)}) collective-permute-start(f32[2,4,16,128]{3,2,1,0:T(8,128)S(1)} %get-tuple-element.78), channel_id=1, source_target_pairs={{0,3},{2,5},{4,7},{6,1},{8,2},{10,4},{12,6},{14,0},{16,10},{18,12}... | collective-permute-start | bytes 196616 | tf_op jit(solution)/shard_map/ppermute | solution.py:622
  37.1 10.4 %collective-permute-done.10.refs_8_ = f32[2,4,16,128]{3,2,1,0:T(8,128)S(1)} collective-permute-done((f32[2,4,16,128]{3,2,1,0:T(8,128)S(1)}, f32[2,4,16,128]{3,2,1,0:T(8,128)S(1)}, u32[]{:S(2)}, u32[]{:S(2)}) %collective-permute-start.10) | collective-permute-done | bytes 65568 | tf_op jit(solution)/shard_map/ppermute | solution.py:622
  50.3 3.5 %collective-permute-done.13.refs_11_ = f32[2,4,16,128]{3,2,1,0:T(8,128)S(1)} collective-permute-done((f32[2,4,16,128]{3,2,1,0:T(8,128)S(1)}, f32[2,4,16,128]{3,2,1,0:T(8,128)S(1)}, u32[]{:S(2)}, u32[]{:S(2)}) %collective-permute-start.13) | collective-permute-done | bytes 65568 | tf_op jit(solution)/shard_map/ppermute | solution.py:622
  55.3 3.0 %collective-permute-start.15 = (f32[4,160,128]{2,1,0:T(8,128)}, f32[4,160,128]{2,1,0:T(8,128)}, u32[]{:S(2)}, u32[]{:S(2)}) collective-permute-start(f32[4,160,128]{2,1,0:T(8,128)} %get-tuple-element.91), channel_id=1, source_target_pairs={{0,16},{8,24},{16,0},{24,8},{1,17},{9,25},{17,1},{25,9},{2,18},{10... | collective-permute-start | bytes 983048 | tf_op jit(solution)/shard_map/ppermute | solution.py:608
  60.6 25.7 %shard_map.88 = (f32[544,128]{1,0:T(8,128)S(1)}, f32[544,128]{1,0:T(8,128)S(1)}, f32[544,128]{1,0:T(8,128)S(1)}, f32[544,128]{1,0:T(8,128)S(1)}) custom-call(s32[1]{0:T(128)} %bitcast.strip, f32[1]{0:T(128)S(6)} %copy.9.upper, f32[2,2,128,128]{3,2,1,0:T(8,128)S(1)} %get-tuple-element.65.refs_1_.refs_0_, ...), custom_call_target="tpu_custom_call" | custom-call | bytes 75000000 | tf_op jit(solution)/shard_map/pallas_call | solution.py:593
  86.3 2.1 %collective-permute-start.20 = (f32[544,128]{1,0:T(8,128)S(1)}, f32[544,128]{1,0:T(8,128)S(1)}, u32[]{:S(2)}, u32[]{:S(2)}) collective-permute-start(f32[544,128]{1,0:T(8,128)S(1)} %get-tuple-element.98), channel_id=1, source_target_pairs={{0,8},{8,16},{16,24},{24,0},{1,9},{9,17},{17,25},{25,1},{2,10},{10... | collective-permute-start | bytes 835592 | tf_op jit(solution)/shard_map/ppermute | solution.py:608
  88.3 1.8 %collective-permute-start.21 = (f32[544,128]{1,0:T(8,128)S(1)}, f32[544,128]{1,0:T(8,128)S(1)}, u32[]{:S(2)}, u32[]{:S(2)}) collective-permute-start(f32[544,128]{1,0:T(8,128)S(1)} %get-tuple-element.99), channel_id=1, source_target_pairs={{0,16},{8,24},{16,0},{24,8},{1,17},{9,25},{17,1},{25,9},{2,18},{10... | collective-permute-start | bytes 835592 | tf_op jit(solution)/shard_map/ppermute | solution.py:608
  90.2 26.1 %shard_map.87 = (f32[400,128]{1,0:T(8,128)S(1)}, f32[400,128]{1,0:T(8,128)S(1)}, f32[400,128]{1,0:T(8,128)S(1)}, f32[400,128]{1,0:T(8,128)S(1)}) custom-call(s32[1]{0:T(128)} %bitcast.strip, f32[1]{0:T(128)S(6)} %copy.9.upper, f32[2,2,128,128]{3,2,1,0:T(8,128)S(1)} %get-tuple-element.65.refs_1_.refs_0_, ...), custom_call_target="tpu_custom_call" | custom-call | bytes 75000000 | tf_op jit(solution)/shard_map/pallas_call | solution.py:593
  116.3 2.1 %collective-permute-start.17 = (f32[400,128]{1,0:T(8,128)S(1)}, f32[400,128]{1,0:T(8,128)S(1)}, u32[]{:S(2)}, u32[]{:S(2)}) collective-permute-start(f32[400,128]{1,0:T(8,128)S(1)} %get-tuple-element.94), channel_id=1, source_target_pairs={{0,8},{8,16},{16,24},{24,0},{1,9},{9,17},{17,25},{25,1},{2,10},{10... | collective-permute-start | bytes 614408 | tf_op jit(solution)/shard_map/ppermute | solution.py:608
  118.4 2.9 %collective-permute-start.18 = (f32[400,128]{1,0:T(8,128)S(1)}, f32[400,128]{1,0:T(8,128)S(1)}, u32[]{:S(2)}, u32[]{:S(2)}) collective-permute-start(f32[400,128]{1,0:T(8,128)S(1)} %get-tuple-element.95), channel_id=1, source_target_pairs={{0,16},{8,24},{16,0},{24,8},{1,17},{9,25},{17,1},{25,9},{2,18},{10... | collective-permute-start | bytes 614408 | tf_op jit(solution)/shard_map/ppermute | solution.py:608
  121.3 7.0 %shard_map.89 = (f32[8,128,128]{2,1,0:T(8,128)}, f32[8,128,128]{2,1,0:T(8,128)S(1)}, f32[10,144,128]{2,1,0:T(8,128)S(1)}, f32[2,128,128]{2,1,0:T(8,128)S(1)}, f3...) custom-call(s32[4]{0:T(128)S(1)} %broadcast_select_fusion.1.refs_0_, f32[544,128]{1,0:T(8,128)S(1)} %get-tuple-element.97.refs_1_, ...), custom_call_target="tpu_custom_call" | custom-call | bytes 6000000 | tf_op jit(solution)/shard_map/pallas_call | solution.py:593
  128.3 4.3 %collective-permute-done.17.refs_2_ = f32[400,128]{1,0:T(8,128)S(1)} collective-permute-done((f32[400,128]{1,0:T(8,128)S(1)}, f32[400,128]{1,0:T(8,128)S(1)}, u32[]{:S(2)}, u32[]{:S(2)}) %collective-permute-start.17) | collective-permute-done | bytes 204832 | tf_op jit(solution)/shard_map/ppermute | solution.py:608
  132.7 2.3 %collective-permute-done.18.refs_3_ = f32[400,128]{1,0:T(8,128)S(1)} collective-permute-done((f32[400,128]{1,0:T(8,128)S(1)}, f32[400,128]{1,0:T(8,128)S(1)}, u32[]{:S(2)}, u32[]{:S(2)}) %collective-permute-start.18) | collective-permute-done | bytes 204832 | tf_op jit(solution)/shard_map/ppermute | solution.py:608
  135.0 2.1 %collective-permute-done.19.refs_4_ = f32[400,128]{1,0:T(8,128)S(1)} collective-permute-done((f32[400,128]{1,0:T(8,128)S(1)}, f32[400,128]{1,0:T(8,128)S(1)}, u32[]{:S(2)}, u32[]{:S(2)}) %collective-permute-start.19) | collective-permute-done | bytes 204832 | tf_op jit(solution)/shard_map/ppermute | solution.py:608
  137.0 8.5 %shard_map.90 = (f32[8,128,128]{2,1,0:T(8,128)}, f32[8,128,128]{2,1,0:T(8,128)}, f32[2,8,128,128]{3,2,1,0:T(8,128)}) custom-call(s32[4]{0:T(128)S(1)} %broadcast_select_fusion.1.refs_0_, f32[400,128]{1,0:T(8,128)S(1)} %get-tuple-element.93.refs_1_, f32[400,128]{1,0:T(8,128)S(1)} %collective-permute-done.17.refs_2_, ...), custom_call_target="tpu_custom_call" | custom-call | bytes 6000000 | tf_op jit(solution)/shard_map/pallas_call | solution.py:593
  (59 shorter events, 15.6 us)
Async XLA Ops:
  0.6 9.7 %collective-permute-start.3 = (bf16[8,128,128]{2,1,0:T(8,128)(2,1)}, bf16[8,128,128]{2,1,0:T(8,128)(2,1)S(1)}, u32[]{:S(2)}, u32[]{:S(2)}) collective-permute-start(bf16[8,128,128]{2,1,0:T(8,128)(2,1)} %param.6), channel_id=1, source_target_pairs={{0,1},{1,0},{2,3},{3,2},{4,5},{5,4},{6,7},{7,6},{8,9},{9,8},{10,11... | collective-permute-start | bytes 786440 | tf_op jit(solution)/shard_map/ppermute | solution.py:608
  5.7 19.6 %collective-permute-start = (f32[2,2,128,128]{3,2,1,0:T(8,128)S(1)}, f32[2,2,128,128]{3,2,1,0:T(8,128)S(1)}, u32[]{:S(2)}, u32[]{:S(2)}) collective-permute-start(f32[2,2,128,128]{3,2,1,0:T(8,128)S(1)} %get-tuple-element.58), channel_id=1, source_target_pairs={{0,8},{8,16},{16,24},{24,0},{1,9},{9,17},{17,25},{25,1},{2,10},{10... | collective-permute-start | bytes 786440 | tf_op jit(solution)/shard_map/ppermute | solution.py:608
  7.3 22.1 %collective-permute-start.1 = (f32[2,2,128,128]{3,2,1,0:T(8,128)S(1)}, f32[2,2,128,128]{3,2,1,0:T(8,128)S(1)}, u32[]{:S(2)}, u32[]{:S(2)}) collective-permute-start(f32[2,2,128,128]{3,2,1,0:T(8,128)S(1)} %get-tuple-element.59), channel_id=1, source_target_pairs={{0,16},{8,24},{16,0},{24,8},{1,17},{9,25},{17,1},{25,9},{2,18},{10... | collective-permute-start | bytes 786440 | tf_op jit(solution)/shard_map/ppermute | solution.py:608
  8.5 22.7 %collective-permute-start.2 = (f32[2,2,128,128]{3,2,1,0:T(8,128)S(1)}, f32[2,2,128,128]{3,2,1,0:T(8,128)S(1)}, u32[]{:S(2)}, u32[]{:S(2)}) collective-permute-start(f32[2,2,128,128]{3,2,1,0:T(8,128)S(1)} %get-tuple-element.60), channel_id=1, source_target_pairs={{0,24},{8,0},{16,8},{24,16},{1,25},{9,1},{17,9},{25,17},{2,26},{10... | collective-permute-start | bytes 786440 | tf_op jit(solution)/shard_map/ppermute | solution.py:608
  11.3 3.0 %collective-permute-start.5 = (f32[2,8,16,128]{3,2,1,0:T(8,128)S(1)}, f32[2,8,16,128]{3,2,1,0:T(8,128)S(1)}, u32[]{:S(2)}, u32[]{:S(2)}) collective-permute-start(f32[2,8,16,128]{3,2,1,0:T(8,128)S(1)} %get-tuple-element.110), channel_id=1, source_target_pairs={{0,6},{2,0},{4,2},{6,4},{1,7},{3,1},{5,3},{7,5},{8,14},{10,8},{12,... | collective-permute-start | bytes 393224 | tf_op jit(solution)/shard_map/ppermute | solution.py:608
  11.3 5.8 %collective-permute-start.4 = (f32[2,8,16,128]{3,2,1,0:T(8,128)S(1)}, f32[2,8,16,128]{3,2,1,0:T(8,128)S(1)}, u32[]{:S(2)}, u32[]{:S(2)}) collective-permute-start(f32[2,8,16,128]{3,2,1,0:T(8,128)S(1)} %get-tuple-element.111), channel_id=1, source_target_pairs={{0,2},{2,4},{4,6},{6,0},{1,3},{3,5},{5,7},{7,1},{8,10},{10,12},{12... | collective-permute-start | bytes 393224 | tf_op jit(solution)/shard_map/ppermute | solution.py:608
  32.2 22.2 %collective-permute-start.6 = (f32[2,4,128,128]{3,2,1,0:T(8,128)S(1)}, f32[2,4,128,128]{3,2,1,0:T(8,128)S(1)}, u32[]{:S(2)}, u32[]{:S(2)}) collective-permute-start(f32[2,4,128,128]{3,2,1,0:T(8,128)S(1)} %get-tuple-element.73), channel_id=1, source_target_pairs={{0,8},{8,16},{16,24},{24,25},{25,17},{17,9},{9,1},{1,0},{2,10},{10... | collective-permute-start | bytes 1572872 | tf_op jit(solution)/shard_map/ppermute | solution.py:616
  32.3 22.1 %collective-permute-start.7 = (f32[2,4,128,128]{3,2,1,0:T(8,128)S(1)}, f32[2,4,128,128]{3,2,1,0:T(8,128)S(1)}, u32[]{:S(2)}, u32[]{:S(2)}) collective-permute-start(f32[2,4,128,128]{3,2,1,0:T(8,128)S(1)} %get-tuple-element.74), channel_id=1, source_target_pairs={{0,1},{8,0},{16,8},{24,16},{25,24},{17,25},{9,17},{1,9},{2,3},{10,... | collective-permute-start | bytes 1572872 | tf_op jit(solution)/shard_map/ppermute | solution.py:616
  34.3 13.2 %collective-permute-start.10 = (f32[2,4,16,128]{3,2,1,0:T(8,128)S(1)}, f32[2,4,16,128]{3,2,1,0:T(8,128)S(1)}, u32[]{:S(2)}, u32[]{:S(2)}) collective-permute-start(f32[2,4,16,128]{3,2,1,0:T(8,128)S(1)} %get-tuple-element.77), channel_id=1, source_target_pairs={{0,10},{2,12},{4,14},{6,8},{8,18},{10,20},{12,22},{14,16},{16,26},... | collective-permute-start | bytes 196616 | tf_op jit(solution)/shard_map/ppermute | solution.py:622
  34.3 13.8 %collective-permute-start.11 = (f32[2,4,16,128]{3,2,1,0:T(8,128)S(1)}, f32[2,4,16,128]{3,2,1,0:T(8,128)S(1)}, u32[]{:S(2)}, u32[]{:S(2)}) collective-permute-start(f32[2,4,16,128]{3,2,1,0:T(8,128)S(1)} %get-tuple-element.78), channel_id=1, source_target_pairs={{0,3},{2,5},{4,7},{6,1},{8,2},{10,4},{12,6},{14,0},{16,10},{18,12}... | collective-permute-start | bytes 196616 | tf_op jit(solution)/shard_map/ppermute | solution.py:622
  37.0 12.3 %collective-permute-start.12 = (f32[2,4,16,128]{3,2,1,0:T(8,128)S(1)}, f32[2,4,16,128]{3,2,1,0:T(8,128)S(1)}, u32[]{:S(2)}, u32[]{:S(2)}) collective-permute-start(f32[2,4,16,128]{3,2,1,0:T(8,128)S(1)} %get-tuple-element.79), channel_id=1, source_target_pairs={{0,14},{2,8},{4,10},{6,12},{8,22},{10,16},{12,18},{14,20},{16,30},... | collective-permute-start | bytes 196616 | tf_op jit(solution)/shard_map/ppermute | solution.py:622
  47.5 6.9 %collective-permute-start.8 = (f32[2,4,2,16,128]{4,3,2,1,0:T(8,128)S(1)}, f32[2,4,2,16,128]{4,3,2,1,0:T(8,128)S(1)}, u32[]{:S(2)}, u32[]{:S(2)}) collective-permute-start(f32[2,4,2,16,128]{4,3,2,1,0:T(8,128)S(1)} %get-tuple-element.75), channel_id=1, source_target_pairs={{0,2},{2,4},{4,6},{6,0},{1,3},{3,5},{5,7},{7,1},{8,10},{10,12},{12... | collective-permute-start | bytes 393224 | tf_op jit(solution)/shard_map/ppermute | solution.py:608
  48.1 6.3 %collective-permute-start.9 = (f32[2,4,2,16,128]{4,3,2,1,0:T(8,128)S(1)}, f32[2,4,2,16,128]{4,3,2,1,0:T(8,128)S(1)}, u32[]{:S(2)}, u32[]{:S(2)}) collective-permute-start(f32[2,4,2,16,128]{4,3,2,1,0:T(8,128)S(1)} %get-tuple-element.76), channel_id=1, source_target_pairs={{0,6},{2,0},{4,2},{6,4},{1,7},{3,1},{5,3},{7,5},{8,14},{10,8},{12,... | collective-permute-start | bytes 393224 | tf_op jit(solution)/shard_map/ppermute | solution.py:608
  49.9 3.9 %collective-permute-start.13 = (f32[2,4,16,128]{3,2,1,0:T(8,128)S(1)}, f32[2,4,16,128]{3,2,1,0:T(8,128)S(1)}, u32[]{:S(2)}, u32[]{:S(2)}) collective-permute-start(f32[2,4,16,128]{3,2,1,0:T(8,128)S(1)} %get-tuple-element.80), channel_id=1, source_target_pairs={{0,7},{2,1},{4,3},{6,5},{8,6},{10,0},{12,2},{14,4},{16,14},{18,8},... | collective-permute-start | bytes 196616 | tf_op jit(solution)/shard_map/ppermute | solution.py:622
  54.4 35.7 %collective-permute-start.14 = (f32[4,160,128]{2,1,0:T(8,128)}, f32[4,160,128]{2,1,0:T(8,128)}, u32[]{:S(2)}, u32[]{:S(2)}) collective-permute-start(f32[4,160,128]{2,1,0:T(8,128)} %get-tuple-element.90), channel_id=1, source_target_pairs={{0,8},{8,16},{16,24},{24,0},{1,9},{9,17},{17,25},{25,1},{2,10},{10... | collective-permute-start | bytes 983048 | tf_op jit(solution)/shard_map/ppermute | solution.py:608
  55.3 34.9 %collective-permute-start.15 = (f32[4,160,128]{2,1,0:T(8,128)}, f32[4,160,128]{2,1,0:T(8,128)}, u32[]{:S(2)}, u32[]{:S(2)}) collective-permute-start(f32[4,160,128]{2,1,0:T(8,128)} %get-tuple-element.91), channel_id=1, source_target_pairs={{0,16},{8,24},{16,0},{24,8},{1,17},{9,25},{17,1},{25,9},{2,18},{10... | collective-permute-start | bytes 983048 | tf_op jit(solution)/shard_map/ppermute | solution.py:608
  58.3 31.9 %collective-permute-start.16 = (f32[4,160,128]{2,1,0:T(8,128)}, f32[4,160,128]{2,1,0:T(8,128)}, u32[]{:S(2)}, u32[]{:S(2)}) collective-permute-start(f32[4,160,128]{2,1,0:T(8,128)} %get-tuple-element.92), channel_id=1, source_target_pairs={{0,24},{8,0},{16,8},{24,16},{1,25},{9,1},{17,9},{25,17},{2,26},{10... | collective-permute-start | bytes 983048 | tf_op jit(solution)/shard_map/ppermute | solution.py:608
  86.3 35.0 %collective-permute-start.20 = (f32[544,128]{1,0:T(8,128)S(1)}, f32[544,128]{1,0:T(8,128)S(1)}, u32[]{:S(2)}, u32[]{:S(2)}) collective-permute-start(f32[544,128]{1,0:T(8,128)S(1)} %get-tuple-element.98), channel_id=1, source_target_pairs={{0,8},{8,16},{16,24},{24,0},{1,9},{9,17},{17,25},{25,1},{2,10},{10... | collective-permute-start | bytes 835592 | tf_op jit(solution)/shard_map/ppermute | solution.py:608
  88.3 33.0 %collective-permute-start.21 = (f32[544,128]{1,0:T(8,128)S(1)}, f32[544,128]{1,0:T(8,128)S(1)}, u32[]{:S(2)}, u32[]{:S(2)}) collective-permute-start(f32[544,128]{1,0:T(8,128)S(1)} %get-tuple-element.99), channel_id=1, source_target_pairs={{0,16},{8,24},{16,0},{24,8},{1,17},{9,25},{17,1},{25,9},{2,18},{10... | collective-permute-start | bytes 835592 | tf_op jit(solution)/shard_map/ppermute | solution.py:608
  90.2 31.2 %copy-start.3 = (f32[8,128,128]{2,1,0:T(8,128)S(1)}, f32[8,128,128]{2,1,0:T(8,128)}, u32[]{:S(2)}) copy-start(f32[8,128,128]{2,1,0:T(8,128)} %refs_6_.1) | copy-start | bytes 1572868
  90.2 31.2 %collective-permute-start.22 = (f32[544,128]{1,0:T(8,128)S(1)}, f32[544,128]{1,0:T(8,128)S(1)}, u32[]{:S(2)}, u32[]{:S(2)}) collective-permute-start(f32[544,128]{1,0:T(8,128)S(1)} %get-tuple-element.100), channel_id=1, source_target_pairs={{0,24},{8,0},{16,8},{24,16},{1,25},{9,1},{17,9},{25,17},{2,26},{10... | collective-permute-start | bytes 835592 | tf_op jit(solution)/shard_map/ppermute | solution.py:608
  116.3 16.4 %collective-permute-start.17 = (f32[400,128]{1,0:T(8,128)S(1)}, f32[400,128]{1,0:T(8,128)S(1)}, u32[]{:S(2)}, u32[]{:S(2)}) collective-permute-start(f32[400,128]{1,0:T(8,128)S(1)} %get-tuple-element.94), channel_id=1, source_target_pairs={{0,8},{8,16},{16,24},{24,0},{1,9},{9,17},{17,25},{25,1},{2,10},{10... | collective-permute-start | bytes 614408 | tf_op jit(solution)/shard_map/ppermute | solution.py:608
  118.4 16.6 %collective-permute-start.18 = (f32[400,128]{1,0:T(8,128)S(1)}, f32[400,128]{1,0:T(8,128)S(1)}, u32[]{:S(2)}, u32[]{:S(2)}) collective-permute-start(f32[400,128]{1,0:T(8,128)S(1)} %get-tuple-element.95), channel_id=1, source_target_pairs={{0,16},{8,24},{16,0},{24,8},{1,17},{9,25},{17,1},{25,9},{2,18},{10... | collective-permute-start | bytes 614408 | tf_op jit(solution)/shard_map/ppermute | solution.py:608
  121.3 15.8 %collective-permute-start.19 = (f32[400,128]{1,0:T(8,128)S(1)}, f32[400,128]{1,0:T(8,128)S(1)}, u32[]{:S(2)}, u32[]{:S(2)}) collective-permute-start(f32[400,128]{1,0:T(8,128)S(1)} %get-tuple-element.96), channel_id=1, source_target_pairs={{0,24},{8,0},{16,8},{24,16},{1,25},{9,1},{17,9},{25,17},{2,26},{10... | collective-permute-start | bytes 614408 | tf_op jit(solution)/shard_map/ppermute | solution.py:608
  (11 other events, 73.2 us)

commit v7 on v6

--- a/solution.py
+++ b/solution.py
@@ -184,25 +184,17 @@
 
 
 def edge_kernel(places, *refs):
-    msgs, (to_left, to_right), rims = refs[:G], refs[G : G + 2], refs[G + 2 :]
-    length = msgs[0].shape[2]
-    lane = lax.broadcasted_iota(jnp.int32, (length, LANES), 1)
+    msgs, (to_left, to_right, head, tail) = refs[:G], refs[G:]
+    lane = lax.broadcasted_iota(jnp.int32, (BY, LANES), 1)
     low = lax.rem(lane, 16) < 8
-    rows = (slice(length - HALO, length), slice(0, HALO))
     for n in range(msgs[0].shape[0]):
         for d in range(G):
             first, second = msgs[d][n, 0], msgs[d][n, 1]
-            edges = (jnp.where(low, first, roll(second, 8)), jnp.where(low, roll(second, -8), first))
-            for side, out in enumerate((to_left, to_right)):
-                out[n, places[side, d]] = edges[side]
-            if rims:
-                head, tail, *corners = rims
-                for side in range(2):
-                    for way in range(2):
-                        corners[2 * side + way][n, places[side, d]] = edges[side][rows[way]]
-                for a in range(2):
-                    head[n, d, a] = msgs[d][n, a, :HALO]
-                    tail[n, d, a] = msgs[d][n, a, length - HALO :]
+            to_left[n, places[0, d]] = jnp.where(low, first, roll(second, 8))
+            to_right[n, places[1, d]] = jnp.where(low, roll(second, -8), first)
+            for a in range(2):
+                head[n, d, a] = msgs[d][n, a, :HALO]
+                tail[n, d, a] = msgs[d][n, a, BY - HALO :]
 
 
 def unpack(get_brick, get_edge, group, within, put):
@@ -234,16 +226,16 @@
             put(2 * m + k // 2, k % 2, roll(whole, -32 * k - 8))
 
 
-def solve_kernel(sizes, give_kap, strip, upper, *refs):
-    refs, finish = fetch(refs, sum(sizes))
-    stacks = []
-    for size in sizes:
-        stacks.append((refs[:G],) + tuple(refs[G:size]))
-        refs = refs[size:]
-    outs = refs[:G]
-    rhs, xa, xb, xc, turned, kap, kx, ky, kin, kout, diag, steps = refs[G:]
+def solve_kernel(adjoint, strip, upper, *refs):
+    if adjoint:
+        bricks, (from_left, from_right, above, below, above_edge, below_edge) = refs[:G], refs[G : G + 6]
+        outs, coefficients, (kap, *scratch) = refs[G + 6 : 2 * G + 6], refs[2 * G + 6 : 2 * G + 11], refs[2 * G + 11 :]
+    else:
+        strips_here, coefficients = refs[:G], refs[G : G + 5]
+        outs, scratch = refs[G + 5 : 2 * G + 5], refs[2 * G + 5 :]
+    kx, ky, kin, kout, diag = coefficients
+    rhs, xa, xb, xc, turned, steps = scratch
     zero = jnp.zeros((TILE, LANES), F32)
-    targets = (kap, rhs)
 
     theta = 0.5 * (jnp.full((TILE, LANES), upper[0]) + 1.0)
     delta = 0.5 * (jnp.full((TILE, LANES), upper[0]) - 1.0)
@@ -264,53 +256,49 @@
 
     for i in range(PLANES):
         for e in range(2):
-            for dst in (kap, ky, rhs, xa, xb, xc):
+            for dst in (rhs, xa, xb, xc) + ((kap, ky) if adjoint else ()):
                 dst[i, e, 0:TILE] = zero
                 dst[i, e, ROWS - TILE : ROWS] = zero
-        for dst in (kin, kout):
+        for dst in (kin, kout) if adjoint else ():
             dst[i, 0:TILE] = zero
             dst[i, ROWS - TILE : ROWS] = zero
 
-    finish()
-
-    for n, dst in enumerate(targets):
-        bricks, *sides = stacks[0][:3]
-        if n == 1 and len(stacks) > 1:
-            strips_here = stacks[1][0]
-
-            @pl.loop(0, EXTENDED // CHUNK)
-            def _(t):
-                at = pl.ds(pl.multiple_of(CHUNK * t, CHUNK), CHUNK)
-                group, _ = lanes_of(CHUNK, strip[0])
-                unpack_strip(
-                    lambda d, m: strips_here[d][m, at],
-                    group,
-                    put_at(dst, pl.multiple_of(TOP - HALO + CHUNK * t, TILE), CHUNK),
-                )
-
-            continue
+    if adjoint:
+        sides, corners = (from_left, from_right), (above_edge, below_edge)
 
         @pl.loop(0, BY // CHUNK)
         def _(t):
             at = pl.ds(pl.multiple_of(CHUNK * t, CHUNK), CHUNK)
             group, within = lanes_of(CHUNK, strip[0])
-            unpack(
-                lambda d, a: bricks[d][n, a, at],
-                lambda side, d: sides[side][n, d, at],
+            for n, dst in enumerate((kap, rhs)):
+                unpack(
+                    lambda d, a: bricks[d][n, a, at],
+                    lambda side, d: sides[side][n, d, at],
+                    group,
+                    within,
+                    put_at(dst, pl.multiple_of(TOP + CHUNK * t, TILE), CHUNK),
+                )
+
+        group_halo, within_halo = lanes_of(HALO, strip[0])
+        for n, dst in enumerate((kap, rhs)):
+            for brick, edge, start in ((above, above_edge, TOP - HALO), (below, below_edge, TOP + BY)):
+                unpack(
+                    lambda d, a: brick[n, d, a],
+                    lambda side, d: edge[side, n, d],
+                    group_halo,
+                    within_halo,
+                    put_at(dst, start, HALO),
+                )
+    else:
+
+        @pl.loop(0, EXTENDED // CHUNK)
+        def _(t):
+            at = pl.ds(pl.multiple_of(CHUNK * t, CHUNK), CHUNK)
+            group, _ = lanes_of(CHUNK, strip[0])
+            unpack_strip(
+                lambda d, m: strips_here[d][m, at],
                 group,
-                within,
-                put_at(dst, pl.multiple_of(TOP + CHUNK * t, TILE), CHUNK),
-            )
-
-        above, below, *corners = stacks[0][3:]
-        group_halo, within_halo = lanes_of(HALO, strip[0])
-        for brick, edge, start in ((above, corners[:2], TOP - HALO), (below, corners[2:], TOP + BY)):
-            unpack(
-                lambda d, a: brick[n, d, a],
-                lambda side, d: edge[side][n, d],
-                group_halo,
-                within_halo,
-                put_at(dst, start, HALO),
+                put_at(rhs, pl.multiple_of(TOP - HALO + CHUNK * t, TILE), CHUNK),
             )
 
     @pl.loop(0, (ROWS // TILE - 2) // 2)
@@ -318,6 +306,12 @@
         rows = 2 * TILE
         r = pl.multiple_of(TILE + rows * t, TILE)
         at = pl.ds(r, rows)
+        for i in range(PLANES):
+            for e in range(2):
+                xb[i, e, at] = rhs[i, e, at] * theta_inv
+                xa[i, e, at] = jnp.zeros((rows, LANES), F32)
+        if not adjoint:
+            return
         first = [kap[0, e, at] for e in range(2)]
         now = first
         before = [4.0 * (k + roll(kap[PLANES - 1, e, at], 32)) for e, k in enumerate(first)]
@@ -337,8 +331,6 @@
                 ky[i, e, at] = fy
                 diag[i, e, at] = 1.0 + (fx + before[e] + (fy + fym) + along[e])
                 before[e] = fx
-                xb[i, e, at] = rhs[i, e, at] * theta_inv
-                xa[i, e, at] = jnp.zeros((rows, LANES), F32)
             now = after
 
     def turn_lanes(cur, r):
@@ -430,7 +422,7 @@
         def to(start):
             return pl.ds(pl.multiple_of(start + CHUNK * t, TILE), CHUNK)
 
-        for field, start in ((xb, SIDES),) + (((kap, FIELD),) if give_kap else ()):
+        for field, start in ((xb, SIDES),) + (((kap, FIELD),) if adjoint else ()):
             whole = load(field, row, CHUNK)
             parts, main = mains(whole, group, within)
             sides = beside(whole, parts, group, within)
@@ -442,7 +434,7 @@
 
     sub = lax.broadcasted_iota(jnp.int32, (TILE, LANES), 0)
     group, within = lanes_of(TILE, strip[0])
-    for field in (xb, kap) if give_kap else (xb,):
+    for field in (xb, kap) if adjoint else (xb,):
         over = mains(load(field, TOP - TILE, TILE), group, within)[1]
         under = mains(load(field, TOP + BY, TILE), group, within)[1]
         for d in range(G):
@@ -561,44 +553,16 @@
             residuals[1, c, at] = adj_residual[c, at]
 
 
-def fetch(refs, count):
-    away, here, sems = refs[:count], refs[len(refs) - count - 1 : -1], refs[-1]
-    copies = [pltpu.make_async_copy(a, h, sems.at[j]) for j, (a, h) in enumerate(zip(away, here))]
-    for copy in copies:
-        copy.start()
-
-    def finish():
-        for copy in copies:
-            copy.wait()
-
-    return (*here, *refs[count : len(refs) - count - 1]), finish
-
-
-def fetched(flags, smem, kernel, *refs):
-    ins, rest = refs[smem : smem + len(flags)], refs[smem + len(flags) :]
-    away = [ref for ref, flag in zip(ins, flags) if flag]
-    inner, finish = fetch((*away, *rest), len(away))
-    finish()
-    here = iter(inner[: len(away)])
-    ins = [next(here) if flag else ref for ref, flag in zip(ins, flags)]
-    kernel(*refs[:smem], *ins, *inner[len(away) :])
-
-
-def call(kernel, outs, smem, vmem, scratch=(), micros=2, fetches=False):
+def call(kernel, outs, smem, vmem, scratch=(), micros=2, mebibytes=16):
     vm = pl.BlockSpec(memory_space=pltpu.VMEM)
     sm = pl.BlockSpec(memory_space=pltpu.SMEM)
-    hbm = pl.BlockSpec(memory_space=pltpu.HBM)
-    flags = [x.shape[-1] == LANES for x in vmem]
-    copies = [pltpu.VMEM(x.shape, x.dtype) for x, flag in zip(vmem, flags) if flag]
     return pl.pallas_call(
-        kernel if fetches else functools.partial(fetched, flags, len(smem), kernel),
+        kernel,
         out_shape=[jax.ShapeDtypeStruct(shape, F32) for shape in outs],
-        in_specs=[sm] * len(smem) + [hbm if flag else vm for flag in flags],
+        in_specs=[sm] * len(smem) + [vm] * len(vmem),
         out_specs=[vm] * len(outs),
-        scratch_shapes=[pltpu.VMEM(shape, F32) for shape in scratch]
-        + copies
-        + [pltpu.SemaphoreType.DMA((len(copies),))],
-        compiler_params=pltpu.CompilerParams(vmem_limit_bytes=48 * 1024 * 1024),
+        scratch_shapes=[pltpu.VMEM(shape, F32) for shape in scratch],
+        compiler_params=pltpu.CompilerParams(vmem_limit_bytes=mebibytes * 1024 * 1024),
         cost_estimate=pl.CostEstimate(flops=0, bytes_accessed=micros * 3_000_000, transcendentals=0),
     )(*smem, *vmem)
 
@@ -608,18 +572,9 @@
     return lax.ppermute(x, axis, [(i, (i + by) % count) for i in range(count)])
 
 
-def around(x, by, rows=0):
-    order = [(g, 0) for g in range(G)] + [(g, 1) for g in reversed(range(G))]
-    count = lax.axis_size("gy")
-    if rows == 0:
-        pairs = [(2 * g + p, 2 * order[(i + by) % len(order)][0] + order[(i + by) % len(order)][1]) for i, (g, p) in enumerate(order)]
-        return lax.ppermute(x, ("gx", "pa"), pairs)
-    pairs = []
-    for i, (g, p) in enumerate(order):
-        to_g, to_p = order[(i + by) % len(order)]
-        for y in range(count):
-            pairs.append(((g * count + y) * 2 + p, (to_g * count + (y + rows) % count) * 2 + to_p))
-    return lax.ppermute(x, ("gx", "gy", "pa"), pairs)
+def around(x, by):
+    order = [2 * g for g in range(G)] + [2 * g + 1 for g in reversed(range(G))]
+    return lax.ppermute(x, ("gx", "pa"), [(at, order[(i + by) % len(order)]) for i, at in enumerate(order)])
 
 
 def redistributed(conductivity, stored_state, row_scales, cotangent, upper_bound):
@@ -632,9 +587,6 @@
     steps = jnp.arange(G, dtype=jnp.int32)
     ahead = lax.rem(g + steps, G)
     behind = lax.rem(g - steps + G, G)
-    stored = shifted(stored_state, "pa", 1)
-    scales = row_scales[:, :, None]
-
     strip = strip_of(g)
     left_g = jnp.where(pa == 0, jnp.maximum(g - 1, 0), jnp.minimum(g + 1, G - 1))
     right_g = jnp.where(pa == 0, jnp.minimum(g + 1, G - 1), jnp.maximum(g - 1, 0))
@@ -642,8 +594,10 @@
 
     brick = (2, 2, BY, LANES)
     parts = call(pack_kernel, [brick] * G, [strip_of(ahead)], [conductivity, cotangent])
+    parts, stored_state = lax.optimization_barrier((parts, stored_state))
     parts = [parts[0]] + [shifted(parts[d], "gx", d) for d in range(1, G)]
-    both = jnp.stack((stored, stored_state)).astype(F32) * scales
+    stored = shifted(stored_state, "pa", 1)
+    both = jnp.stack((stored, stored_state)).astype(F32) * row_scales[:, :, None]
     above = shifted(both[:, :, BY - HALO :], "gy", 1)
     below = shifted(both[:, :, :HALO], "gy", -1)
     messages = call(
@@ -655,45 +609,43 @@
     parts, messages = lax.optimization_barrier((parts, messages))
     edge = (2, G, BY, LANES)
     rim = (2, G, 2, HALO, LANES)
-    corner = (2, G, HALO, LANES)
-    to_left, to_right, head, tail, left_down, left_up, right_down, right_up = call(
-        edge_kernel, [edge, edge, rim, rim] + [corner] * 4, [places], parts
-    )
-    halos = [
-        around(to_right, 1),
-        around(to_left, -1),
-        shifted(tail, "gy", 1),
-        shifted(head, "gy", -1),
-        around(right_down, 1, 1),
-        around(left_down, -1, 1),
-        around(right_up, 1, -1),
-        around(left_up, -1, -1),
-    ]
-
+    to_left, to_right, head, tail = call(edge_kernel, [edge, edge, rim, rim], [places], parts)
+    from_left, from_right = around(to_right, 1), around(to_left, -1)
+    above, below = shifted(tail, "gy", 1), shifted(head, "gy", -1)
+    edges = [jnp.stack((from_left[:, :, at], from_right[:, :, at])) for at in (slice(BY - HALO, BY), slice(0, HALO))]
+    halos = [from_left, from_right, above, below, shifted(edges[0], "gy", 1), shifted(edges[1], "gy", -1)]
     messages, halos = lax.optimization_barrier((messages, halos))
-    first = [*parts, *halos]
     second = [messages[0]] + [shifted(messages[d], "gx", d) for d in range(1, G)]
 
-    def solve(stacks, give_kap):
-        line = (PLANES, 2, ROWS, LANES)
-        half = (PLANES, ROWS, LANES)
-        solved = call(
-            functools.partial(solve_kernel, [len(stack) for stack in stacks], give_kap),
-            [(BOTH if give_kap else FIELD, LANES)] * G,
-            [strip[None], upper_bound],
-            sum(stacks, []),
-            [line] * 4
-            + [(PLANES + 2, 2, TILE, LANES)]
-            + [line] * 3
-            + [half, half, line]
-            + [(CHEB, 2, TILE, LANES)],
+    line = (PLANES, 2, ROWS, LANES)
+    half = (PLANES, ROWS, LANES)
+    lines = [line] * 4 + [(PLANES + 2, 2, TILE, LANES), (CHEB, 2, TILE, LANES)]
+    setup = [strip[None], upper_bound]
+
+    def home(solved):
+        return [solved[0]] + [shifted(solved[d], "gx", d) for d in range(1, G)]
+
+    *solved_adjoint, kx, ky, kin, kout, diag = call(
+        functools.partial(solve_kernel, True),
+        [(BOTH, LANES)] * G + [line, line, half, half, line],
+        setup,
+        [*parts, *halos],
+        [line] + lines,
+        micros=25,
+        mebibytes=24,
+    )
+    solved_adjoint = home(solved_adjoint)
+    solved_state = home(
+        call(
+            functools.partial(solve_kernel, False),
+            [(FIELD, LANES)] * G,
+            setup,
+            [*second, kx, ky, kin, kout, diag],
+            lines,
             micros=25,
-            fetches=True,
+            mebibytes=24,
         )
-        return [solved[0]] + [shifted(solved[d], "gx", d) for d in range(1, G)]
-
-    solved_adjoint = solve([first], True)
-    solved_state = solve([first, second], False)
+    )
 
     out = (BX, BY, LANES)
     padded = (BX + 2, BY + 16, LANES)

time: 146 us -> 145 us (level)
  Pallas kernels: 74.3 us -> 71.9 us
  local copies, waits for them, and re-layouts: 6.42 us -> 8.34 us
    ppermute x6 -> x2, waiting for transfers between devices: 13.9 us -> 10.1 us  [around(): lax.ppermute(x, ('gx', 'pa'), [(at, order[(i + by) % len(order)]) for i,...]
    ppermute x17 -> x19, waiting for transfers between devices: 22.6 us -> 26 us  [shifted(): return lax.ppermute(x, axis, [(i, (i + by) % count) for i in range(count)])]
    ppermute x6 -> x2, starting transfers between devices: 5.21 us -> 2.07 us  [around(): lax.ppermute(x, ('gx', 'pa'), [(at, order[(i + by) % len(order)]) for i,...]
    pallas_call x7, Pallas kernels: 74.3 us -> 71.9 us  [call(): pl.pallas_call(kernel, out_shape=[jax.ShapeDtypeStruct(shape, F32) for sh...]
    ppermute x17 -> x19, starting transfers between devices: 21.2 us -> 23.3 us  [shifted(): return lax.ppermute(x, axis, [(i, (i + by) % count) for i in range(count)])]
    unnamed x24, local copies, waits for them, and re-layouts: 6.4 us -> 8.3 us
  transfers between devices with their start and end apart: 23 -> 21, of which waited for: 10 -> 12; matrix products, arithmetic and copies ran while one was open for 0% -> 1% of each run, Pallas kernels for 45% -> 44%
where the time goes in v7:
time: 145 us; the launch traced here: 144 us
  Pallas kernels  71.9 us (50%)
  waiting for transfers between devices  36.2 us (25%)
  starting transfers between devices  25.3 us (17%)
  local copies, waits for them, and re-layouts  8.34 us (6%)
  between operations  1.48 us (1%)
    pallas_call x7, Pallas kernels, call(): pl.pallas_call(kernel, out_shape=[jax.ShapeDtypeStruct(shape, F32) for sh...  71.9 us
    ppermute x19, waiting for transfers between devices, shifted(): return lax.ppermute(x, axis, [(i, (i + by) % count) for i in range(count)])  26 us
    ppermute x19, starting transfers between devices, shifted(): return lax.ppermute(x, axis, [(i, (i + by) % count) for i in range(count)])  23.3 us
    ppermute x2, waiting for transfers between devices, around(): lax.ppermute(x, ('gx', 'pa'), [(at, order[(i + by) % len(order)]) for i,...  10.1 us
    unnamed x24, local copies, waits for them, and re-layouts  8.3 us
  transfers between devices with their start and end apart: 21, of which 12 were waited for; matrix products, arithmetic and copies ran while one was open for 1% of the time, Pallas kernels for 44%

profile of v7, /device:TPU:8, one launch (start us, length us, event | category | flops | bytes accessed | tf_op | source)
XLA Modules:
  0.0 144.5 jit_solution(13807470179727207290)
XLA Ops:
  4.0 1.6 %collective-permute-start.3 = (bf16[8,128,128]{2,1,0:T(8,128)(2,1)}, bf16[8,128,128]{2,1,0:T(8,128)(2,1)S(1)}, u32[]{:S(2)}, u32[]{:S(2)}) collective-permute-start(bf16[8,128,128]{2,1,0:T(8,128)(2,1)} %param.6), channel_id=1, source_target_pairs={{0,1},{1,0},{2,3},{3,2},{4,5},{5,4},{6,7},{7,6},{8,9},{9,8},{10,11... | collective-permute-start | bytes 786440 | tf_op jit(solution)/shard_map/ppermute | solution.py:572
  8.4 1.8 %collective-permute-start.2 = (f32[2,2,128,128]{3,2,1,0:T(8,128)S(1)}, f32[2,2,128,128]{3,2,1,0:T(8,128)S(1)}, u32[]{:S(2)}, u32[]{:S(2)}) collective-permute-start(f32[2,2,128,128]{3,2,1,0:T(8,128)S(1)} %get-tuple-element.68), channel_id=1, source_target_pairs={{0,24},{8,0},{16,8},{24,16},{1,25},{9,1},{17,9},{25,17},{2,26},{10... | collective-permute-start | bytes 786440 | tf_op jit(solution)/shard_map/ppermute | solution.py:572
  10.2 2.1 %collective-permute-done.3 = bf16[8,128,128]{2,1,0:T(8,128)(2,1)S(1)} collective-permute-done((bf16[8,128,128]{2,1,0:T(8,128)(2,1)}, bf16[8,128,128]{2,1,0:T(8,128)(2,1)S(1)}, u32[]{:S(2)}, u32[]{:S(2)}) %collective-permute-start.3) | collective-permute-done | bytes 262176 | tf_op jit(solution)/shard_map/ppermute | solution.py:572
  14.1 2.5 %collective-permute-done.5.below = f32[2,8,16,128]{3,2,1,0:T(8,128)S(1)} collective-permute-done((f32[2,8,16,128]{3,2,1,0:T(8,128)S(1)}, f32[2,8,16,128]{3,2,1,0:T(8,128)S(1)}, u32[]{:S(2)}, u32[]{:S(2)}) %collective-permute-start.5) | collective-permute-done | bytes 131104 | tf_op jit(solution)/shard_map/ppermute | solution.py:572
  16.6 2.8 %collective-permute-done.4.above = f32[2,8,16,128]{3,2,1,0:T(8,128)S(1)} collective-permute-done((f32[2,8,16,128]{3,2,1,0:T(8,128)S(1)}, f32[2,8,16,128]{3,2,1,0:T(8,128)S(1)}, u32[]{:S(2)}, u32[]{:S(2)}) %collective-permute-start.4) | collective-permute-done | bytes 131104 | tf_op jit(solution)/shard_map/ppermute | solution.py:572
  19.4 4.3 %shard_map.85 = (f32[4,160,128]{2,1,0:T(8,128)S(1)}, f32[4,160,128]{2,1,0:T(8,128)}, f32[4,160,128]{2,1,0:T(8,128)}, f32[4,160,128]{2,1,0:T(8,128)}) custom-call(s32[4]{0:T(128)S(1)} %broadcast_select_fusion.strips, f32[2,8,128,128]{3,2,1,0:T(8,128)S(1)} %convert_multiply_fusion.both.previous, f32[2,8,16,128]{3,2,1,0:T(8,128)S(1)} %collective-permute-done.4.above, ...), custom_call_target="tpu_custom_call" | custom-call | bytes 6000000 | tf_op jit(solution)/shard_map/pallas_call | solution.py:559
  25.1 4.2 %collective-permute-done.1.refs_2_ = f32[2,2,128,128]{3,2,1,0:T(8,128)S(1)} collective-permute-done((f32[2,2,128,128]{3,2,1,0:T(8,128)S(1)}, f32[2,2,128,128]{3,2,1,0:T(8,128)S(1)}, u32[]{:S(2)}, u32[]{:S(2)}) %collective-permute-start.1) | collective-permute-done | bytes 262176 | tf_op jit(solution)/shard_map/ppermute | solution.py:572
  29.3 1.8 %collective-permute-done.2.refs_3_ = f32[2,2,128,128]{3,2,1,0:T(8,128)S(1)} collective-permute-done((f32[2,2,128,128]{3,2,1,0:T(8,128)S(1)}, f32[2,2,128,128]{3,2,1,0:T(8,128)S(1)}, u32[]{:S(2)}, u32[]{:S(2)}) %collective-permute-start.2) | collective-permute-done | bytes 262176 | tf_op jit(solution)/shard_map/ppermute | solution.py:572
  32.0 2.0 %collective-permute-start.7 = (f32[2,4,128,128]{3,2,1,0:T(8,128)S(1)}, f32[2,4,128,128]{3,2,1,0:T(8,128)S(1)}, u32[]{:S(2)}, u32[]{:S(2)}) collective-permute-start(f32[2,4,128,128]{3,2,1,0:T(8,128)S(1)} %get-tuple-element.83), channel_id=1, source_target_pairs={{0,1},{8,0},{16,8},{24,16},{25,24},{17,25},{9,17},{1,9},{2,3},{10,... | collective-permute-start | bytes 1572872 | tf_op jit(solution)/shard_map/ppermute | solution.py:577
  34.1 1.7 %collective-permute-start.9 = (f32[2,4,2,16,128]{4,3,2,1,0:T(8,128)S(1)}, f32[2,4,2,16,128]{4,3,2,1,0:T(8,128)S(1)}, u32[]{:S(2)}, u32[]{:S(2)}) collective-permute-start(f32[2,4,2,16,128]{4,3,2,1,0:T(8,128)S(1)} %get-tuple-element.85), channel_id=1, source_target_pairs={{0,6},{2,0},{4,2},{6,4},{1,7},{3,1},{5,3},{7,5},{8,14},{10,8},{12,... | collective-permute-start | bytes 393224 | tf_op jit(solution)/shard_map/ppermute | solution.py:572
  35.8 10.1 %collective-permute-done.6.refs_4_ = f32[2,4,128,128]{3,2,1,0:T(8,128)S(1)} collective-permute-done((f32[2,4,128,128]{3,2,1,0:T(8,128)S(1)}, f32[2,4,128,128]{3,2,1,0:T(8,128)S(1)}, u32[]{:S(2)}, u32[]{:S(2)}) %collective-permute-start.6) | collective-permute-done | bytes 524320 | tf_op jit(solution)/shard_map/ppermute | solution.py:577
  46.0 1.8 %collective-permute-start.11 = (f32[2,2,4,16,128]{4,3,2,1,0:T(8,128)S(1)}, f32[2,2,4,16,128]{4,3,2,1,0:T(8,128)S(1)}, u32[]{:S(2)}, u32[]{:S(2)}) collective-permute-start(f32[2,2,4,16,128]{4,3,2,1,0:T(8,128)S(1)} %pad_maximum_fusion.1), channel_id=1, source_target_pairs={{0,6},{2,0},{4,2},{6,4},{1,7},{3,1},{5,3},{7,5},{8,14},{10,8},{12,... | collective-permute-start | bytes 393224 | tf_op jit(solution)/shard_map/ppermute | solution.py:572
  52.2 3.6 %collective-permute-start.13 = (f32[4,160,128]{2,1,0:T(8,128)}, f32[4,160,128]{2,1,0:T(8,128)}, u32[]{:S(2)}, u32[]{:S(2)}) collective-permute-start(f32[4,160,128]{2,1,0:T(8,128)} %get-tuple-element.88), channel_id=1, source_target_pairs={{0,16},{8,24},{16,0},{24,8},{1,17},{9,25},{17,1},{25,9},{2,18},{10... | collective-permute-start | bytes 983048 | tf_op jit(solution)/shard_map/ppermute | solution.py:572
  60.0 27.3 %shard_map.87 = (f32[544,128]{1,0:T(8,128)S(1)}, f32[544,128]{1,0:T(8,128)S(1)}, f32[544,128]{1,0:T(8,128)S(1)}, f32[544,128]{1,0:T(8,128)S(1)}, f32[8,2,176,128...) custom-call(s32[1]{0:T(128)} %bitcast.strip, ...), custom_call_target="tpu_custom_call" | custom-call | bytes 75000000 | tf_op jit(solution)/shard_map/pallas_call | solution.py:559
  87.4 2.1 %collective-permute-start.18 = (f32[544,128]{1,0:T(8,128)S(1)}, f32[544,128]{1,0:T(8,128)S(1)}, u32[]{:S(2)}, u32[]{:S(2)}) collective-permute-start(f32[544,128]{1,0:T(8,128)S(1)} %get-tuple-element.106), channel_id=1, source_target_pairs={{0,8},{8,16},{16,24},{24,0},{1,9},{9,17},{17,25},{25,1},{2,10},{10... | collective-permute-start | bytes 835592 | tf_op jit(solution)/shard_map/ppermute | solution.py:572
  89.5 1.8 %collective-permute-start.19 = (f32[544,128]{1,0:T(8,128)S(1)}, f32[544,128]{1,0:T(8,128)S(1)}, u32[]{:S(2)}, u32[]{:S(2)}) collective-permute-start(f32[544,128]{1,0:T(8,128)S(1)} %get-tuple-element.107), channel_id=1, source_target_pairs={{0,16},{8,24},{16,0},{24,8},{1,17},{9,25},{17,1},{25,9},{2,18},{10... | collective-permute-start | bytes 835592 | tf_op jit(solution)/shard_map/ppermute | solution.py:572
  91.3 25.2 %shard_map.88 = (f32[400,128]{1,0:T(8,128)S(1)}, f32[400,128]{1,0:T(8,128)S(1)}, f32[400,128]{1,0:T(8,128)S(1)}, f32[400,128]{1,0:T(8,128)S(1)}) custom-call(s32[1]{0:T(128)} %bitcast.strip, f32[1]{0:T(128)S(6)} %copy.9.upper, f32[4,160,128]{2,1,0:T(8,128)S(1)} %get-tuple-element.86.refs_0_, f32[4,160,128]{2,1,0:T(8,128)} %collective-permute-done.12.refs_1_, ...), custom_call_target="tpu_custom_call" | custom-call | bytes 75000000 | tf_op jit(solution)/shard_map/pallas_call | solution.py:559
  116.5 2.1 %collective-permute-start.15 = (f32[400,128]{1,0:T(8,128)S(1)}, f32[400,128]{1,0:T(8,128)S(1)}, u32[]{:S(2)}, u32[]{:S(2)}) collective-permute-start(f32[400,128]{1,0:T(8,128)S(1)} %get-tuple-element.102), channel_id=1, source_target_pairs={{0,8},{8,16},{16,24},{24,0},{1,9},{9,17},{17,25},{25,1},{2,10},{10... | collective-permute-start | bytes 614408 | tf_op jit(solution)/shard_map/ppermute | solution.py:572
  118.6 2.9 %collective-permute-start.16 = (f32[400,128]{1,0:T(8,128)S(1)}, f32[400,128]{1,0:T(8,128)S(1)}, u32[]{:S(2)}, u32[]{:S(2)}) collective-permute-start(f32[400,128]{1,0:T(8,128)S(1)} %get-tuple-element.103), channel_id=1, source_target_pairs={{0,16},{8,24},{16,0},{24,8},{1,17},{9,25},{17,1},{25,9},{2,18},{10... | collective-permute-start | bytes 614408 | tf_op jit(solution)/shard_map/ppermute | solution.py:572
  121.5 6.7 %shard_map.89 = (f32[8,128,128]{2,1,0:T(8,128)}, f32[8,128,128]{2,1,0:T(8,128)S(1)}, f32[10,144,128]{2,1,0:T(8,128)S(1)}, f32[2,128,128]{2,1,0:T(8,128)S(1)}, f3...) custom-call(s32[4]{0:T(128)S(1)} %broadcast_select_fusion.1.strips, f32[544,128]{1,0:T(8,128)S(1)} %get-tuple-element.105.m0, ...), custom_call_target="tpu_custom_call" | custom-call | bytes 6000000 | tf_op jit(solution)/shard_map/pallas_call | solution.py:559
  128.2 4.6 %collective-permute-done.15.m1 = f32[400,128]{1,0:T(8,128)S(1)} collective-permute-done((f32[400,128]{1,0:T(8,128)S(1)}, f32[400,128]{1,0:T(8,128)S(1)}, u32[]{:S(2)}, u32[]{:S(2)}) %collective-permute-start.15) | collective-permute-done | bytes 204832 | tf_op jit(solution)/shard_map/ppermute | solution.py:572
  132.8 3.0 %collective-permute-done.16.m2 = f32[400,128]{1,0:T(8,128)S(1)} collective-permute-done((f32[400,128]{1,0:T(8,128)S(1)}, f32[400,128]{1,0:T(8,128)S(1)}, u32[]{:S(2)}, u32[]{:S(2)}) %collective-permute-start.16) | collective-permute-done | bytes 204832 | tf_op jit(solution)/shard_map/ppermute | solution.py:572
  135.8 2.3 %collective-permute-done.17.m3 = f32[400,128]{1,0:T(8,128)S(1)} collective-permute-done((f32[400,128]{1,0:T(8,128)S(1)}, f32[400,128]{1,0:T(8,128)S(1)}, u32[]{:S(2)}, u32[]{:S(2)}) %collective-permute-start.17) | collective-permute-done | bytes 204832 | tf_op jit(solution)/shard_map/ppermute | solution.py:572
  138.2 6.3 %shard_map.90 = (f32[8,128,128]{2,1,0:T(8,128)}, f32[8,128,128]{2,1,0:T(8,128)}, f32[2,8,128,128]{3,2,1,0:T(8,128)}) custom-call(s32[4]{0:T(128)S(1)} %broadcast_select_fusion.1.strips, f32[400,128]{1,0:T(8,128)S(1)} %get-tuple-element.101.m0, f32[400,128]{1,0:T(8,128)S(1)} %collective-permute-done.15.m1, f32[400,128]{1,0:T(8,128)S(1)} %collective-permute-done.16.m2, ...), custom_call_target="tpu_custom_call" | custom-call | bytes 6000000 | tf_op jit(solution)/shard_map/pallas_call | solution.py:559
  (59 shorter events, 18.4 us)
Async XLA Ops:
  0.7 1.0 copy-start
  4.0 8.3 %collective-permute-start.3 = (bf16[8,128,128]{2,1,0:T(8,128)(2,1)}, bf16[8,128,128]{2,1,0:T(8,128)(2,1)S(1)}, u32[]{:S(2)}, u32[]{:S(2)}) collective-permute-start(bf16[8,128,128]{2,1,0:T(8,128)(2,1)} %param.6), channel_id=1, source_target_pairs={{0,1},{1,0},{2,3},{3,2},{4,5},{5,4},{6,7},{7,6},{8,9},{9,8},{10,11... | collective-permute-start | bytes 786440 | tf_op jit(solution)/shard_map/ppermute | solution.py:572
  5.6 19.6 %collective-permute-start = (f32[2,2,128,128]{3,2,1,0:T(8,128)S(1)}, f32[2,2,128,128]{3,2,1,0:T(8,128)S(1)}, u32[]{:S(2)}, u32[]{:S(2)}) collective-permute-start(f32[2,2,128,128]{3,2,1,0:T(8,128)S(1)} %get-tuple-element.66), channel_id=1, source_target_pairs={{0,8},{8,16},{16,24},{24,0},{1,9},{9,17},{17,25},{25,1},{2,10},{10... | collective-permute-start | bytes 786440 | tf_op jit(solution)/shard_map/ppermute | solution.py:572
  7.1 22.1 %collective-permute-start.1 = (f32[2,2,128,128]{3,2,1,0:T(8,128)S(1)}, f32[2,2,128,128]{3,2,1,0:T(8,128)S(1)}, u32[]{:S(2)}, u32[]{:S(2)}) collective-permute-start(f32[2,2,128,128]{3,2,1,0:T(8,128)S(1)} %get-tuple-element.67), channel_id=1, source_target_pairs={{0,16},{8,24},{16,0},{24,8},{1,17},{9,25},{17,1},{25,9},{2,18},{10... | collective-permute-start | bytes 786440 | tf_op jit(solution)/shard_map/ppermute | solution.py:572
  8.4 22.7 %collective-permute-start.2 = (f32[2,2,128,128]{3,2,1,0:T(8,128)S(1)}, f32[2,2,128,128]{3,2,1,0:T(8,128)S(1)}, u32[]{:S(2)}, u32[]{:S(2)}) collective-permute-start(f32[2,2,128,128]{3,2,1,0:T(8,128)S(1)} %get-tuple-element.68), channel_id=1, source_target_pairs={{0,24},{8,0},{16,8},{24,16},{1,25},{9,1},{17,9},{25,17},{2,26},{10... | collective-permute-start | bytes 786440 | tf_op jit(solution)/shard_map/ppermute | solution.py:572
  13.5 3.1 %collective-permute-start.5 = (f32[2,8,16,128]{3,2,1,0:T(8,128)S(1)}, f32[2,8,16,128]{3,2,1,0:T(8,128)S(1)}, u32[]{:S(2)}, u32[]{:S(2)}) collective-permute-start(f32[2,8,16,128]{3,2,1,0:T(8,128)S(1)} %get-tuple-element.118), channel_id=1, source_target_pairs={{0,6},{2,0},{4,2},{6,4},{1,7},{3,1},{5,3},{7,5},{8,14},{10,8},{12,... | collective-permute-start | bytes 393224 | tf_op jit(solution)/shard_map/ppermute | solution.py:572
  13.6 5.8 %collective-permute-start.4 = (f32[2,8,16,128]{3,2,1,0:T(8,128)S(1)}, f32[2,8,16,128]{3,2,1,0:T(8,128)S(1)}, u32[]{:S(2)}, u32[]{:S(2)}) collective-permute-start(f32[2,8,16,128]{3,2,1,0:T(8,128)S(1)} %get-tuple-element.119), channel_id=1, source_target_pairs={{0,2},{2,4},{4,6},{6,0},{1,3},{3,5},{5,7},{7,1},{8,10},{10,12},{12... | collective-permute-start | bytes 393224 | tf_op jit(solution)/shard_map/ppermute | solution.py:572
  32.0 13.9 %collective-permute-start.6 = (f32[2,4,128,128]{3,2,1,0:T(8,128)S(1)}, f32[2,4,128,128]{3,2,1,0:T(8,128)S(1)}, u32[]{:S(2)}, u32[]{:S(2)}) collective-permute-start(f32[2,4,128,128]{3,2,1,0:T(8,128)S(1)} %get-tuple-element.82), channel_id=1, source_target_pairs={{0,8},{8,16},{16,24},{24,25},{25,17},{17,9},{9,1},{1,0},{2,10},{10... | collective-permute-start | bytes 1572872 | tf_op jit(solution)/shard_map/ppermute | solution.py:577
  32.0 13.9 %collective-permute-start.7 = (f32[2,4,128,128]{3,2,1,0:T(8,128)S(1)}, f32[2,4,128,128]{3,2,1,0:T(8,128)S(1)}, u32[]{:S(2)}, u32[]{:S(2)}) collective-permute-start(f32[2,4,128,128]{3,2,1,0:T(8,128)S(1)} %get-tuple-element.83), channel_id=1, source_target_pairs={{0,1},{8,0},{16,8},{24,16},{25,24},{17,25},{9,17},{1,9},{2,3},{10,... | collective-permute-start | bytes 1572872 | tf_op jit(solution)/shard_map/ppermute | solution.py:577
  34.0 13.8 %collective-permute-start.8 = (f32[2,4,2,16,128]{4,3,2,1,0:T(8,128)S(1)}, f32[2,4,2,16,128]{4,3,2,1,0:T(8,128)S(1)}, u32[]{:S(2)}, u32[]{:S(2)}) collective-permute-start(f32[2,4,2,16,128]{4,3,2,1,0:T(8,128)S(1)} %get-tuple-element.84), channel_id=1, source_target_pairs={{0,2},{2,4},{4,6},{6,0},{1,3},{3,5},{5,7},{7,1},{8,10},{10,12},{12... | collective-permute-start | bytes 393224 | tf_op jit(solution)/shard_map/ppermute | solution.py:572
  34.1 14.4 %collective-permute-start.9 = (f32[2,4,2,16,128]{4,3,2,1,0:T(8,128)S(1)}, f32[2,4,2,16,128]{4,3,2,1,0:T(8,128)S(1)}, u32[]{:S(2)}, u32[]{:S(2)}) collective-permute-start(f32[2,4,2,16,128]{4,3,2,1,0:T(8,128)S(1)} %get-tuple-element.85), channel_id=1, source_target_pairs={{0,6},{2,0},{4,2},{6,4},{1,7},{3,1},{5,3},{7,5},{8,14},{10,8},{12,... | collective-permute-start | bytes 393224 | tf_op jit(solution)/shard_map/ppermute | solution.py:572
  46.0 4.4 %collective-permute-start.10 = (f32[2,2,4,16,128]{4,3,2,1,0:T(8,128)S(1)}, f32[2,2,4,16,128]{4,3,2,1,0:T(8,128)S(1)}, u32[]{:S(2)}, u32[]{:S(2)}) collective-permute-start(f32[2,2,4,16,128]{4,3,2,1,0:T(8,128)S(1)} %pad_maximum_fusion), channel_id=1, source_target_pairs={{0,2},{2,4},{4,6},{6,0},{1,3},{3,5},{5,7},{7,1},{8,10},{10,12},{12... | collective-permute-start | bytes 393224 | tf_op jit(solution)/shard_map/ppermute | solution.py:572
  46.0 5.0 %collective-permute-start.11 = (f32[2,2,4,16,128]{4,3,2,1,0:T(8,128)S(1)}, f32[2,2,4,16,128]{4,3,2,1,0:T(8,128)S(1)}, u32[]{:S(2)}, u32[]{:S(2)}) collective-permute-start(f32[2,2,4,16,128]{4,3,2,1,0:T(8,128)S(1)} %pad_maximum_fusion.1), channel_id=1, source_target_pairs={{0,6},{2,0},{4,2},{6,4},{1,7},{3,1},{5,3},{7,5},{8,14},{10,8},{12,... | collective-permute-start | bytes 393224 | tf_op jit(solution)/shard_map/ppermute | solution.py:572
  51.7 39.5 %collective-permute-start.12 = (f32[4,160,128]{2,1,0:T(8,128)}, f32[4,160,128]{2,1,0:T(8,128)}, u32[]{:S(2)}, u32[]{:S(2)}) collective-permute-start(f32[4,160,128]{2,1,0:T(8,128)} %get-tuple-element.87), channel_id=1, source_target_pairs={{0,8},{8,16},{16,24},{24,0},{1,9},{9,17},{17,25},{25,1},{2,10},{10... | collective-permute-start | bytes 983048 | tf_op jit(solution)/shard_map/ppermute | solution.py:572
  52.2 39.1 %collective-permute-start.13 = (f32[4,160,128]{2,1,0:T(8,128)}, f32[4,160,128]{2,1,0:T(8,128)}, u32[]{:S(2)}, u32[]{:S(2)}) collective-permute-start(f32[4,160,128]{2,1,0:T(8,128)} %get-tuple-element.88), channel_id=1, source_target_pairs={{0,16},{8,24},{16,0},{24,8},{1,17},{9,25},{17,1},{25,9},{2,18},{10... | collective-permute-start | bytes 983048 | tf_op jit(solution)/shard_map/ppermute | solution.py:572
  55.8 35.5 %collective-permute-start.14 = (f32[4,160,128]{2,1,0:T(8,128)}, f32[4,160,128]{2,1,0:T(8,128)}, u32[]{:S(2)}, u32[]{:S(2)}) collective-permute-start(f32[4,160,128]{2,1,0:T(8,128)} %get-tuple-element.89), channel_id=1, source_target_pairs={{0,24},{8,0},{16,8},{24,16},{1,25},{9,1},{17,9},{25,17},{2,26},{10... | collective-permute-start | bytes 983048 | tf_op jit(solution)/shard_map/ppermute | solution.py:572
  87.4 34.1 %collective-permute-start.18 = (f32[544,128]{1,0:T(8,128)S(1)}, f32[544,128]{1,0:T(8,128)S(1)}, u32[]{:S(2)}, u32[]{:S(2)}) collective-permute-start(f32[544,128]{1,0:T(8,128)S(1)} %get-tuple-element.106), channel_id=1, source_target_pairs={{0,8},{8,16},{16,24},{24,0},{1,9},{9,17},{17,25},{25,1},{2,10},{10... | collective-permute-start | bytes 835592 | tf_op jit(solution)/shard_map/ppermute | solution.py:572
  89.5 32.0 %collective-permute-start.19 = (f32[544,128]{1,0:T(8,128)S(1)}, f32[544,128]{1,0:T(8,128)S(1)}, u32[]{:S(2)}, u32[]{:S(2)}) collective-permute-start(f32[544,128]{1,0:T(8,128)S(1)} %get-tuple-element.107), channel_id=1, source_target_pairs={{0,16},{8,24},{16,0},{24,8},{1,17},{9,25},{17,1},{25,9},{2,18},{10... | collective-permute-start | bytes 835592 | tf_op jit(solution)/shard_map/ppermute | solution.py:572
  91.3 30.3 %collective-permute-start.20 = (f32[544,128]{1,0:T(8,128)S(1)}, f32[544,128]{1,0:T(8,128)S(1)}, u32[]{:S(2)}, u32[]{:S(2)}) collective-permute-start(f32[544,128]{1,0:T(8,128)S(1)} %get-tuple-element.108), channel_id=1, source_target_pairs={{0,24},{8,0},{16,8},{24,16},{1,25},{9,1},{17,9},{25,17},{2,26},{10... | collective-permute-start | bytes 835592 | tf_op jit(solution)/shard_map/ppermute | solution.py:572
  91.3 30.2 %copy-start.1 = (f32[8,128,128]{2,1,0:T(8,128)S(1)}, f32[8,128,128]{2,1,0:T(8,128)}, u32[]{:S(2)}) copy-start(f32[8,128,128]{2,1,0:T(8,128)} %cond.1) | copy-start | bytes 1572868
  91.3 30.2 %copy-start.3 = (f32[8,128,128]{2,1,0:T(8,128)S(1)}, f32[8,128,128]{2,1,0:T(8,128)}, u32[]{:S(2)}) copy-start(f32[8,128,128]{2,1,0:T(8,128)} %cot.1) | copy-start | bytes 1572868
  116.5 16.3 %collective-permute-start.15 = (f32[400,128]{1,0:T(8,128)S(1)}, f32[400,128]{1,0:T(8,128)S(1)}, u32[]{:S(2)}, u32[]{:S(2)}) collective-permute-start(f32[400,128]{1,0:T(8,128)S(1)} %get-tuple-element.102), channel_id=1, source_target_pairs={{0,8},{8,16},{16,24},{24,0},{1,9},{9,17},{17,25},{25,1},{2,10},{10... | collective-permute-start | bytes 614408 | tf_op jit(solution)/shard_map/ppermute | solution.py:572
  118.6 17.3 %collective-permute-start.16 = (f32[400,128]{1,0:T(8,128)S(1)}, f32[400,128]{1,0:T(8,128)S(1)}, u32[]{:S(2)}, u32[]{:S(2)}) collective-permute-start(f32[400,128]{1,0:T(8,128)S(1)} %get-tuple-element.103), channel_id=1, source_target_pairs={{0,16},{8,24},{16,0},{24,8},{1,17},{9,25},{17,1},{25,9},{2,18},{10... | collective-permute-start | bytes 614408 | tf_op jit(solution)/shard_map/ppermute | solution.py:572
  121.5 16.7 %collective-permute-start.17 = (f32[400,128]{1,0:T(8,128)S(1)}, f32[400,128]{1,0:T(8,128)S(1)}, u32[]{:S(2)}, u32[]{:S(2)}) collective-permute-start(f32[400,128]{1,0:T(8,128)S(1)} %get-tuple-element.104), channel_id=1, source_target_pairs={{0,24},{8,0},{16,8},{24,16},{1,25},{9,1},{17,9},{25,17},{2,26},{10... | collective-permute-start | bytes 614408 | tf_op jit(solution)/shard_map/ppermute | solution.py:572
  (9 other events, 7.3 us)

commit v8 on v7

--- a/solution.py
+++ b/solution.py
@@ -381,8 +381,8 @@
         sweep(k + 1, xb, xc, xa, spans[1])
         sweep(k + 2, xc, xa, xb, spans[2])
 
-    wide = (TILE, ROWS // TILE - 2, 4)
-    narrow = (2 * TILE, ROWS // TILE - 4, 3)
+    wide = (TILE, ROWS // TILE - 2, ROWS // TILE - 2)
+    narrow = (2 * TILE, ROWS // TILE - 4, ROWS // TILE - 4)
 
     @pl.loop(0, 2)
     def _(m):
@@ -614,7 +614,7 @@
     above, below = shifted(tail, "gy", 1), shifted(head, "gy", -1)
     edges = [jnp.stack((from_left[:, :, at], from_right[:, :, at])) for at in (slice(BY - HALO, BY), slice(0, HALO))]
     halos = [from_left, from_right, above, below, shifted(edges[0], "gy", 1), shifted(edges[1], "gy", -1)]
-    messages, halos = lax.optimization_barrier((messages, halos))
+    messages, halos[0] = lax.optimization_barrier((messages, halos[0]))
     second = [messages[0]] + [shifted(messages[d], "gx", d) for d in range(1, G)]
 
     line = (PLANES, 2, ROWS, LANES)

time: 145 us -> 140 us (0.966)
  local copies, waits for them, and re-layouts: 8.34 us -> 5.23 us
  waiting for transfers between devices: 36.2 us -> 33.8 us
    unnamed x24 -> x16, local copies, waits for them, and re-layouts: 8.3 us -> 5.2 us
    ppermute x19, waiting for transfers between devices: 26 us -> 23.6 us  [shifted(): return lax.ppermute(x, axis, [(i, (i + by) % count) for i in range(count)])]
  transfers between devices with their start and end apart: 21 -> 21, of which waited for: 12 -> 11; matrix products, arithmetic and copies ran while one was open for 1% -> 2% of each run, Pallas kernels for 44% -> 45%
where the time goes in v8:
time: 140 us
  Pallas kernels  71.7 us (51%)
  waiting for transfers between devices  33.8 us (24%)
  starting transfers between devices  25.5 us (18%)
  local copies, waits for them, and re-layouts  5.23 us (4%)
  other arithmetic  2.53 us (2%)
  between operations  1.47 us (1%)
    pallas_call x7, Pallas kernels, call(): pl.pallas_call(kernel, out_shape=[jax.ShapeDtypeStruct(shape, F32) for sh...  71.7 us
    ppermute x19, waiting for transfers between devices, shifted(): return lax.ppermute(x, axis, [(i, (i + by) % count) for i in range(count)])  23.6 us
    ppermute x19, starting transfers between devices, shifted(): return lax.ppermute(x, axis, [(i, (i + by) % count) for i in range(count)])  23.4 us
    ppermute x2, waiting for transfers between devices, around(): lax.ppermute(x, ('gx', 'pa'), [(at, order[(i + by) % len(order)]) for i,...  10.1 us
    unnamed x16, local copies, waits for them, and re-layouts  5.2 us
  transfers between devices with their start and end apart: 21, of which 11 were waited for; matrix products, arithmetic and copies ran while one was open for 2% of the time, Pallas kernels for 45%

profile of v8, /device:TPU:8, one launch (start us, length us, event | category | flops | bytes accessed | tf_op | source)
XLA Modules:
  0.0 140.1 jit_solution(3865449448264071550)
XLA Ops:
  4.0 1.6 %collective-permute-start.3 = (bf16[8,128,128]{2,1,0:T(8,128)(2,1)}, bf16[8,128,128]{2,1,0:T(8,128)(2,1)S(1)}, u32[]{:S(2)}, u32[]{:S(2)}) collective-permute-start(bf16[8,128,128]{2,1,0:T(8,128)(2,1)} %param.6), channel_id=1, source_target_pairs={{0,1},{1,0},{2,3},{3,2},{4,5},{5,4},{6,7},{7,6},{8,9},{9,8},{10,11... | collective-permute-start | bytes 786440 | tf_op jit(solution)/shard_map/ppermute | solution.py:572
  8.4 1.8 %collective-permute-start.2 = (f32[2,2,128,128]{3,2,1,0:T(8,128)S(1)}, f32[2,2,128,128]{3,2,1,0:T(8,128)S(1)}, u32[]{:S(2)}, u32[]{:S(2)}) collective-permute-start(f32[2,2,128,128]{3,2,1,0:T(8,128)S(1)} %get-tuple-element.63), channel_id=1, source_target_pairs={{0,24},{8,0},{16,8},{24,16},{1,25},{9,1},{17,9},{25,17},{2,26},{10... | collective-permute-start | bytes 786440 | tf_op jit(solution)/shard_map/ppermute | solution.py:572
  10.2 2.1 %collective-permute-done.3 = bf16[8,128,128]{2,1,0:T(8,128)(2,1)S(1)} collective-permute-done((bf16[8,128,128]{2,1,0:T(8,128)(2,1)}, bf16[8,128,128]{2,1,0:T(8,128)(2,1)S(1)}, u32[]{:S(2)}, u32[]{:S(2)}) %collective-permute-start.3) | collective-permute-done | bytes 262176 | tf_op jit(solution)/shard_map/ppermute | solution.py:572
  14.1 2.5 %collective-permute-done.5.below = f32[2,8,16,128]{3,2,1,0:T(8,128)S(1)} collective-permute-done((f32[2,8,16,128]{3,2,1,0:T(8,128)S(1)}, f32[2,8,16,128]{3,2,1,0:T(8,128)S(1)}, u32[]{:S(2)}, u32[]{:S(2)}) %collective-permute-start.5) | collective-permute-done | bytes 131104 | tf_op jit(solution)/shard_map/ppermute | solution.py:572
  16.6 2.8 %collective-permute-done.4.above = f32[2,8,16,128]{3,2,1,0:T(8,128)S(1)} collective-permute-done((f32[2,8,16,128]{3,2,1,0:T(8,128)S(1)}, f32[2,8,16,128]{3,2,1,0:T(8,128)S(1)}, u32[]{:S(2)}, u32[]{:S(2)}) %collective-permute-start.4) | collective-permute-done | bytes 131104 | tf_op jit(solution)/shard_map/ppermute | solution.py:572
  19.4 4.3 %shard_map.85 = (f32[4,160,128]{2,1,0:T(8,128)S(1)}, f32[4,160,128]{2,1,0:T(8,128)}, f32[4,160,128]{2,1,0:T(8,128)}, f32[4,160,128]{2,1,0:T(8,128)}) custom-call(s32[4]{0:T(128)S(1)} %broadcast_select_fusion.strips, f32[2,8,128,128]{3,2,1,0:T(8,128)S(1)} %convert_multiply_fusion.both.previous, f32[2,8,16,128]{3,2,1,0:T(8,128)S(1)} %collective-permute-done.4.above, ...), custom_call_target="tpu_custom_call" | custom-call | bytes 6000000 | tf_op jit(solution)/shard_map/pallas_call | solution.py:559
  25.1 4.2 %collective-permute-done.1.refs_2_ = f32[2,2,128,128]{3,2,1,0:T(8,128)S(1)} collective-permute-done((f32[2,2,128,128]{3,2,1,0:T(8,128)S(1)}, f32[2,2,128,128]{3,2,1,0:T(8,128)S(1)}, u32[]{:S(2)}, u32[]{:S(2)}) %collective-permute-start.1) | collective-permute-done | bytes 262176 | tf_op jit(solution)/shard_map/ppermute | solution.py:572
  29.3 1.8 %collective-permute-done.2.refs_3_ = f32[2,2,128,128]{3,2,1,0:T(8,128)S(1)} collective-permute-done((f32[2,2,128,128]{3,2,1,0:T(8,128)S(1)}, f32[2,2,128,128]{3,2,1,0:T(8,128)S(1)}, u32[]{:S(2)}, u32[]{:S(2)}) %collective-permute-start.2) | collective-permute-done | bytes 262176 | tf_op jit(solution)/shard_map/ppermute | solution.py:572
  32.0 2.0 %collective-permute-start.10 = (f32[2,4,128,128]{3,2,1,0:T(8,128)S(1)}, f32[2,4,128,128]{3,2,1,0:T(8,128)S(1)}, u32[]{:S(2)}, u32[]{:S(2)}) collective-permute-start(f32[2,4,128,128]{3,2,1,0:T(8,128)S(1)} %get-tuple-element.83), channel_id=1, source_target_pairs={{0,1},{8,0},{16,8},{24,16},{25,24},{17,25},{9,17},{1,9},{2,3},{10,... | collective-permute-start | bytes 1572872 | tf_op jit(solution)/shard_map/ppermute | solution.py:577
  34.0 1.7 %collective-permute-start.12 = (f32[2,4,2,16,128]{4,3,2,1,0:T(8,128)S(1)}, f32[2,4,2,16,128]{4,3,2,1,0:T(8,128)S(1)}, u32[]{:S(2)}, u32[]{:S(2)}) collective-permute-start(f32[2,4,2,16,128]{4,3,2,1,0:T(8,128)S(1)} %get-tuple-element.85), channel_id=1, source_target_pairs={{0,6},{2,0},{4,2},{6,4},{1,7},{3,1},{5,3},{7,5},{8,14},{10,8},{12,... | collective-permute-start | bytes 393224 | tf_op jit(solution)/shard_map/ppermute | solution.py:572
  35.8 10.1 %collective-permute-done.6.refs_4_ = f32[2,4,128,128]{3,2,1,0:T(8,128)S(1)} collective-permute-done((f32[2,4,128,128]{3,2,1,0:T(8,128)S(1)}, f32[2,4,128,128]{3,2,1,0:T(8,128)S(1)}, u32[]{:S(2)}, u32[]{:S(2)}) %collective-permute-start.6) | collective-permute-done | bytes 524320 | tf_op jit(solution)/shard_map/ppermute | solution.py:577
  47.3 1.7 %collective-permute-start.14 = (f32[2,2,4,16,128]{4,3,2,1,0:T(8,128)}, f32[2,2,4,16,128]{4,3,2,1,0:T(8,128)}, u32[]{:S(2)}, u32[]{:S(2)}) collective-permute-start(f32[2,2,4,16,128]{4,3,2,1,0:T(8,128)} %pad_maximum_fusion.1), channel_id=1, source_target_pairs={{0,6},{2,0},{4,2},{6,4},{1,7},{3,1},{5,3},{7,5},{8,14},{10,8},{12,... | collective-permute-start | bytes 393224 | tf_op jit(solution)/shard_map/ppermute | solution.py:572
  50.1 3.6 %collective-permute-start.8 = (f32[4,160,128]{2,1,0:T(8,128)}, f32[4,160,128]{2,1,0:T(8,128)}, u32[]{:S(2)}, u32[]{:S(2)}) collective-permute-start(f32[4,160,128]{2,1,0:T(8,128)} %get-tuple-element.80), channel_id=1, source_target_pairs={{0,16},{8,24},{16,0},{24,8},{1,17},{9,25},{17,1},{25,9},{2,18},{10... | collective-permute-start | bytes 983048 | tf_op jit(solution)/shard_map/ppermute | solution.py:572
  56.9 27.6 %shard_map.87 = (f32[544,128]{1,0:T(8,128)S(1)}, f32[544,128]{1,0:T(8,128)S(1)}, f32[544,128]{1,0:T(8,128)S(1)}, f32[544,128]{1,0:T(8,128)S(1)}, f32[8,2,176,128...) custom-call(s32[1]{0:T(128)} %bitcast.strip, ...), custom_call_target="tpu_custom_call" | custom-call | bytes 75000000 | tf_op jit(solution)/shard_map/pallas_call | solution.py:559
  84.4 2.3 %collective-permute-start.18 = (f32[544,128]{1,0:T(8,128)S(1)}, f32[544,128]{1,0:T(8,128)S(1)}, u32[]{:S(2)}, u32[]{:S(2)}) collective-permute-start(f32[544,128]{1,0:T(8,128)S(1)} %get-tuple-element.96), channel_id=1, source_target_pairs={{0,8},{8,16},{16,24},{24,0},{1,9},{9,17},{17,25},{25,1},{2,10},{10... | collective-permute-start | bytes 835592 | tf_op jit(solution)/shard_map/ppermute | solution.py:572
  86.7 1.8 %collective-permute-start.19 = (f32[544,128]{1,0:T(8,128)S(1)}, f32[544,128]{1,0:T(8,128)S(1)}, u32[]{:S(2)}, u32[]{:S(2)}) collective-permute-start(f32[544,128]{1,0:T(8,128)S(1)} %get-tuple-element.97), channel_id=1, source_target_pairs={{0,16},{8,24},{16,0},{24,8},{1,17},{9,25},{17,1},{25,9},{2,18},{10... | collective-permute-start | bytes 835592 | tf_op jit(solution)/shard_map/ppermute | solution.py:572
  88.6 24.7 %shard_map.88 = (f32[400,128]{1,0:T(8,128)S(1)}, f32[400,128]{1,0:T(8,128)S(1)}, f32[400,128]{1,0:T(8,128)S(1)}, f32[400,128]{1,0:T(8,128)S(1)}) custom-call(s32[1]{0:T(128)} %bitcast.strip, f32[1]{0:T(128)S(6)} %copy.9.upper, f32[4,160,128]{2,1,0:T(8,128)S(1)} %get-tuple-element.78.refs_0_, f32[4,160,128]{2,1,0:T(8,128)} %collective-permute-done.7.refs_1_, ...), custom_call_target="tpu_custom_call" | custom-call | bytes 75000000 | tf_op jit(solution)/shard_map/pallas_call | solution.py:559
  113.3 2.1 %collective-permute-start.15 = (f32[400,128]{1,0:T(8,128)S(1)}, f32[400,128]{1,0:T(8,128)S(1)}, u32[]{:S(2)}, u32[]{:S(2)}) collective-permute-start(f32[400,128]{1,0:T(8,128)S(1)} %get-tuple-element.92), channel_id=1, source_target_pairs={{0,8},{8,16},{16,24},{24,0},{1,9},{9,17},{17,25},{25,1},{2,10},{10... | collective-permute-start | bytes 614408 | tf_op jit(solution)/shard_map/ppermute | solution.py:572
  115.3 2.9 %collective-permute-start.16 = (f32[400,128]{1,0:T(8,128)S(1)}, f32[400,128]{1,0:T(8,128)S(1)}, u32[]{:S(2)}, u32[]{:S(2)}) collective-permute-start(f32[400,128]{1,0:T(8,128)S(1)} %get-tuple-element.93), channel_id=1, source_target_pairs={{0,16},{8,24},{16,0},{24,8},{1,17},{9,25},{17,1},{25,9},{2,18},{10... | collective-permute-start | bytes 614408 | tf_op jit(solution)/shard_map/ppermute | solution.py:572
  118.3 6.7 %shard_map.89 = (f32[8,128,128]{2,1,0:T(8,128)}, f32[8,128,128]{2,1,0:T(8,128)S(1)}, f32[10,144,128]{2,1,0:T(8,128)S(1)}, f32[2,128,128]{2,1,0:T(8,128)S(1)}, f3...) custom-call(s32[4]{0:T(128)S(1)} %broadcast_select_fusion.1.strips, f32[544,128]{1,0:T(8,128)S(1)} %get-tuple-element.95.m0, ...), custom_call_target="tpu_custom_call" | custom-call | bytes 6000000 | tf_op jit(solution)/shard_map/pallas_call | solution.py:559
  125.0 4.3 %collective-permute-done.15.m1 = f32[400,128]{1,0:T(8,128)S(1)} collective-permute-done((f32[400,128]{1,0:T(8,128)S(1)}, f32[400,128]{1,0:T(8,128)S(1)}, u32[]{:S(2)}, u32[]{:S(2)}) %collective-permute-start.15) | collective-permute-done | bytes 204832 | tf_op jit(solution)/shard_map/ppermute | solution.py:572
  129.3 2.2 %collective-permute-done.16.m2 = f32[400,128]{1,0:T(8,128)S(1)} collective-permute-done((f32[400,128]{1,0:T(8,128)S(1)}, f32[400,128]{1,0:T(8,128)S(1)}, u32[]{:S(2)}, u32[]{:S(2)}) %collective-permute-start.16) | collective-permute-done | bytes 204832 | tf_op jit(solution)/shard_map/ppermute | solution.py:572
  131.5 2.4 %collective-permute-done.17.m3 = f32[400,128]{1,0:T(8,128)S(1)} collective-permute-done((f32[400,128]{1,0:T(8,128)S(1)}, f32[400,128]{1,0:T(8,128)S(1)}, u32[]{:S(2)}, u32[]{:S(2)}) %collective-permute-start.17) | collective-permute-done | bytes 204832 | tf_op jit(solution)/shard_map/ppermute | solution.py:572
  133.8 6.3 %shard_map.90 = (f32[8,128,128]{2,1,0:T(8,128)}, f32[8,128,128]{2,1,0:T(8,128)}, f32[2,8,128,128]{3,2,1,0:T(8,128)}) custom-call(s32[4]{0:T(128)S(1)} %broadcast_select_fusion.1.strips, f32[400,128]{1,0:T(8,128)S(1)} %get-tuple-element.91.m0, f32[400,128]{1,0:T(8,128)S(1)} %collective-permute-done.15.m1, f32[400,128]{1,0:T(8,128)S(1)} %collective-permute-done.16.m2, ...), custom_call_target="tpu_custom_call" | custom-call | bytes 6000000 | tf_op jit(solution)/shard_map/pallas_call | solution.py:559
  (51 shorter events, 15.3 us)
Async XLA Ops:
  0.7 1.0 copy-start
  4.0 8.3 %collective-permute-start.3 = (bf16[8,128,128]{2,1,0:T(8,128)(2,1)}, bf16[8,128,128]{2,1,0:T(8,128)(2,1)S(1)}, u32[]{:S(2)}, u32[]{:S(2)}) collective-permute-start(bf16[8,128,128]{2,1,0:T(8,128)(2,1)} %param.6), channel_id=1, source_target_pairs={{0,1},{1,0},{2,3},{3,2},{4,5},{5,4},{6,7},{7,6},{8,9},{9,8},{10,11... | collective-permute-start | bytes 786440 | tf_op jit(solution)/shard_map/ppermute | solution.py:572
  5.6 19.6 %collective-permute-start = (f32[2,2,128,128]{3,2,1,0:T(8,128)S(1)}, f32[2,2,128,128]{3,2,1,0:T(8,128)S(1)}, u32[]{:S(2)}, u32[]{:S(2)}) collective-permute-start(f32[2,2,128,128]{3,2,1,0:T(8,128)S(1)} %get-tuple-element.61), channel_id=1, source_target_pairs={{0,8},{8,16},{16,24},{24,0},{1,9},{9,17},{17,25},{25,1},{2,10},{10... | collective-permute-start | bytes 786440 | tf_op jit(solution)/shard_map/ppermute | solution.py:572
  7.1 22.1 %collective-permute-start.1 = (f32[2,2,128,128]{3,2,1,0:T(8,128)S(1)}, f32[2,2,128,128]{3,2,1,0:T(8,128)S(1)}, u32[]{:S(2)}, u32[]{:S(2)}) collective-permute-start(f32[2,2,128,128]{3,2,1,0:T(8,128)S(1)} %get-tuple-element.62), channel_id=1, source_target_pairs={{0,16},{8,24},{16,0},{24,8},{1,17},{9,25},{17,1},{25,9},{2,18},{10... | collective-permute-start | bytes 786440 | tf_op jit(solution)/shard_map/ppermute | solution.py:572
  8.4 22.7 %collective-permute-start.2 = (f32[2,2,128,128]{3,2,1,0:T(8,128)S(1)}, f32[2,2,128,128]{3,2,1,0:T(8,128)S(1)}, u32[]{:S(2)}, u32[]{:S(2)}) collective-permute-start(f32[2,2,128,128]{3,2,1,0:T(8,128)S(1)} %get-tuple-element.63), channel_id=1, source_target_pairs={{0,24},{8,0},{16,8},{24,16},{1,25},{9,1},{17,9},{25,17},{2,26},{10... | collective-permute-start | bytes 786440 | tf_op jit(solution)/shard_map/ppermute | solution.py:572
  13.5 3.1 %collective-permute-start.5 = (f32[2,8,16,128]{3,2,1,0:T(8,128)S(1)}, f32[2,8,16,128]{3,2,1,0:T(8,128)S(1)}, u32[]{:S(2)}, u32[]{:S(2)}) collective-permute-start(f32[2,8,16,128]{3,2,1,0:T(8,128)S(1)} %get-tuple-element.108), channel_id=1, source_target_pairs={{0,6},{2,0},{4,2},{6,4},{1,7},{3,1},{5,3},{7,5},{8,14},{10,8},{12,... | collective-permute-start | bytes 393224 | tf_op jit(solution)/shard_map/ppermute | solution.py:572
  13.6 5.8 %collective-permute-start.4 = (f32[2,8,16,128]{3,2,1,0:T(8,128)S(1)}, f32[2,8,16,128]{3,2,1,0:T(8,128)S(1)}, u32[]{:S(2)}, u32[]{:S(2)}) collective-permute-start(f32[2,8,16,128]{3,2,1,0:T(8,128)S(1)} %get-tuple-element.109), channel_id=1, source_target_pairs={{0,2},{2,4},{4,6},{6,0},{1,3},{3,5},{5,7},{7,1},{8,10},{10,12},{12... | collective-permute-start | bytes 393224 | tf_op jit(solution)/shard_map/ppermute | solution.py:572
  32.0 13.9 %collective-permute-start.6 = (f32[2,4,128,128]{3,2,1,0:T(8,128)S(1)}, f32[2,4,128,128]{3,2,1,0:T(8,128)S(1)}, u32[]{:S(2)}, u32[]{:S(2)}) collective-permute-start(f32[2,4,128,128]{3,2,1,0:T(8,128)S(1)} %get-tuple-element.77), channel_id=1, source_target_pairs={{0,8},{8,16},{16,24},{24,25},{25,17},{17,9},{9,1},{1,0},{2,10},{10... | collective-permute-start | bytes 1572872 | tf_op jit(solution)/shard_map/ppermute | solution.py:577
  32.0 13.9 %collective-permute-start.10 = (f32[2,4,128,128]{3,2,1,0:T(8,128)S(1)}, f32[2,4,128,128]{3,2,1,0:T(8,128)S(1)}, u32[]{:S(2)}, u32[]{:S(2)}) collective-permute-start(f32[2,4,128,128]{3,2,1,0:T(8,128)S(1)} %get-tuple-element.83), channel_id=1, source_target_pairs={{0,1},{8,0},{16,8},{24,16},{25,24},{17,25},{9,17},{1,9},{2,3},{10,... | collective-permute-start | bytes 1572872 | tf_op jit(solution)/shard_map/ppermute | solution.py:577
  34.0 15.4 %collective-permute-start.11 = (f32[2,4,2,16,128]{4,3,2,1,0:T(8,128)S(1)}, f32[2,4,2,16,128]{4,3,2,1,0:T(8,128)S(1)}, u32[]{:S(2)}, u32[]{:S(2)}) collective-permute-start(f32[2,4,2,16,128]{4,3,2,1,0:T(8,128)S(1)} %get-tuple-element.84), channel_id=1, source_target_pairs={{0,2},{2,4},{4,6},{6,0},{1,3},{3,5},{5,7},{7,1},{8,10},{10,12},{12... | collective-permute-start | bytes 393224 | tf_op jit(solution)/shard_map/ppermute | solution.py:572
  34.0 19.7 %collective-permute-start.12 = (f32[2,4,2,16,128]{4,3,2,1,0:T(8,128)S(1)}, f32[2,4,2,16,128]{4,3,2,1,0:T(8,128)S(1)}, u32[]{:S(2)}, u32[]{:S(2)}) collective-permute-start(f32[2,4,2,16,128]{4,3,2,1,0:T(8,128)S(1)} %get-tuple-element.85), channel_id=1, source_target_pairs={{0,6},{2,0},{4,2},{6,4},{1,7},{3,1},{5,3},{7,5},{8,14},{10,8},{12,... | collective-permute-start | bytes 393224 | tf_op jit(solution)/shard_map/ppermute | solution.py:572
  46.6 8.4 %collective-permute-start.13 = (f32[2,2,4,16,128]{4,3,2,1,0:T(8,128)}, f32[2,2,4,16,128]{4,3,2,1,0:T(8,128)}, u32[]{:S(2)}, u32[]{:S(2)}) collective-permute-start(f32[2,2,4,16,128]{4,3,2,1,0:T(8,128)} %pad_maximum_fusion), channel_id=1, source_target_pairs={{0,2},{2,4},{4,6},{6,0},{1,3},{3,5},{5,7},{7,1},{8,10},{10,12},{12... | collective-permute-start | bytes 393224 | tf_op jit(solution)/shard_map/ppermute | solution.py:572
  47.3 7.8 %collective-permute-start.14 = (f32[2,2,4,16,128]{4,3,2,1,0:T(8,128)}, f32[2,2,4,16,128]{4,3,2,1,0:T(8,128)}, u32[]{:S(2)}, u32[]{:S(2)}) collective-permute-start(f32[2,2,4,16,128]{4,3,2,1,0:T(8,128)} %pad_maximum_fusion.1), channel_id=1, source_target_pairs={{0,6},{2,0},{4,2},{6,4},{1,7},{3,1},{5,3},{7,5},{8,14},{10,8},{12,... | collective-permute-start | bytes 393224 | tf_op jit(solution)/shard_map/ppermute | solution.py:572
  49.0 39.5 %collective-permute-start.7 = (f32[4,160,128]{2,1,0:T(8,128)}, f32[4,160,128]{2,1,0:T(8,128)}, u32[]{:S(2)}, u32[]{:S(2)}) collective-permute-start(f32[4,160,128]{2,1,0:T(8,128)} %get-tuple-element.79), channel_id=1, source_target_pairs={{0,8},{8,16},{16,24},{24,0},{1,9},{9,17},{17,25},{25,1},{2,10},{10... | collective-permute-start | bytes 983048 | tf_op jit(solution)/shard_map/ppermute | solution.py:572
  50.1 38.5 %collective-permute-start.8 = (f32[4,160,128]{2,1,0:T(8,128)}, f32[4,160,128]{2,1,0:T(8,128)}, u32[]{:S(2)}, u32[]{:S(2)}) collective-permute-start(f32[4,160,128]{2,1,0:T(8,128)} %get-tuple-element.80), channel_id=1, source_target_pairs={{0,16},{8,24},{16,0},{24,8},{1,17},{9,25},{17,1},{25,9},{2,18},{10... | collective-permute-start | bytes 983048 | tf_op jit(solution)/shard_map/ppermute | solution.py:572
  54.4 34.2 %collective-permute-start.9 = (f32[4,160,128]{2,1,0:T(8,128)}, f32[4,160,128]{2,1,0:T(8,128)}, u32[]{:S(2)}, u32[]{:S(2)}) collective-permute-start(f32[4,160,128]{2,1,0:T(8,128)} %get-tuple-element.81), channel_id=1, source_target_pairs={{0,24},{8,0},{16,8},{24,16},{1,25},{9,1},{17,9},{25,17},{2,26},{10... | collective-permute-start | bytes 983048 | tf_op jit(solution)/shard_map/ppermute | solution.py:572
  84.4 33.8 %collective-permute-start.18 = (f32[544,128]{1,0:T(8,128)S(1)}, f32[544,128]{1,0:T(8,128)S(1)}, u32[]{:S(2)}, u32[]{:S(2)}) collective-permute-start(f32[544,128]{1,0:T(8,128)S(1)} %get-tuple-element.96), channel_id=1, source_target_pairs={{0,8},{8,16},{16,24},{24,0},{1,9},{9,17},{17,25},{25,1},{2,10},{10... | collective-permute-start | bytes 835592 | tf_op jit(solution)/shard_map/ppermute | solution.py:572
  86.7 31.5 %collective-permute-start.19 = (f32[544,128]{1,0:T(8,128)S(1)}, f32[544,128]{1,0:T(8,128)S(1)}, u32[]{:S(2)}, u32[]{:S(2)}) collective-permute-start(f32[544,128]{1,0:T(8,128)S(1)} %get-tuple-element.97), channel_id=1, source_target_pairs={{0,16},{8,24},{16,0},{24,8},{1,17},{9,25},{17,1},{25,9},{2,18},{10... | collective-permute-start | bytes 835592 | tf_op jit(solution)/shard_map/ppermute | solution.py:572
  88.5 29.7 %collective-permute-start.20 = (f32[544,128]{1,0:T(8,128)S(1)}, f32[544,128]{1,0:T(8,128)S(1)}, u32[]{:S(2)}, u32[]{:S(2)}) collective-permute-start(f32[544,128]{1,0:T(8,128)S(1)} %get-tuple-element.98), channel_id=1, source_target_pairs={{0,24},{8,0},{16,8},{24,16},{1,25},{9,1},{17,9},{25,17},{2,26},{10... | collective-permute-start | bytes 835592 | tf_op jit(solution)/shard_map/ppermute | solution.py:572
  88.6 29.7 %copy-start.1 = (f32[8,128,128]{2,1,0:T(8,128)S(1)}, f32[8,128,128]{2,1,0:T(8,128)}, u32[]{:S(2)}) copy-start(f32[8,128,128]{2,1,0:T(8,128)} %cond.1) | copy-start | bytes 1572868
  88.6 29.7 %copy-start.3 = (f32[8,128,128]{2,1,0:T(8,128)S(1)}, f32[8,128,128]{2,1,0:T(8,128)}, u32[]{:S(2)}) copy-start(f32[8,128,128]{2,1,0:T(8,128)} %cot.1) | copy-start | bytes 1572868
  113.3 16.0 %collective-permute-start.15 = (f32[400,128]{1,0:T(8,128)S(1)}, f32[400,128]{1,0:T(8,128)S(1)}, u32[]{:S(2)}, u32[]{:S(2)}) collective-permute-start(f32[400,128]{1,0:T(8,128)S(1)} %get-tuple-element.92), channel_id=1, source_target_pairs={{0,8},{8,16},{16,24},{24,0},{1,9},{9,17},{17,25},{25,1},{2,10},{10... | collective-permute-start | bytes 614408 | tf_op jit(solution)/shard_map/ppermute | solution.py:572
  115.3 16.1 %collective-permute-start.16 = (f32[400,128]{1,0:T(8,128)S(1)}, f32[400,128]{1,0:T(8,128)S(1)}, u32[]{:S(2)}, u32[]{:S(2)}) collective-permute-start(f32[400,128]{1,0:T(8,128)S(1)} %get-tuple-element.93), channel_id=1, source_target_pairs={{0,16},{8,24},{16,0},{24,8},{1,17},{9,25},{17,1},{25,9},{2,18},{10... | collective-permute-start | bytes 614408 | tf_op jit(solution)/shard_map/ppermute | solution.py:572
  118.3 15.6 %collective-permute-start.17 = (f32[400,128]{1,0:T(8,128)S(1)}, f32[400,128]{1,0:T(8,128)S(1)}, u32[]{:S(2)}, u32[]{:S(2)}) collective-permute-start(f32[400,128]{1,0:T(8,128)S(1)} %get-tuple-element.94), channel_id=1, source_target_pairs={{0,24},{8,0},{16,8},{24,16},{1,25},{9,1},{17,9},{25,17},{2,26},{10... | collective-permute-start | bytes 614408 | tf_op jit(solution)/shard_map/ppermute | solution.py:572
  (5 other events, 4.2 us)

commit v9 on v7

--- a/solution.py
+++ b/solution.py
@@ -98,6 +98,7 @@
 BOTH = KAP + 16
 TILE = 8
 CHUNK = 32
+WIDE = 16
 
 BLOCK = (0, 3, 2, 1)
 PLANES = BX
@@ -499,54 +500,66 @@
         padded[1 + c, TILE + BY : 2 * TILE + BY] = val
 
 
-def around_cell(padded, ends, c, t):
-    lane = lax.broadcasted_iota(jnp.int32, (TILE, LANES), 1)
-    r = pl.multiple_of(TILE * t, TILE)
-    r8 = pl.multiple_of(TILE * t + TILE, TILE)
-    cell = padded[1 + c, pl.ds(r8, TILE)]
-    low, high = (ends[side, pl.ds(r, TILE)] for side in range(2))
-    return cell, (
-        padded[c, pl.ds(r8, TILE)],
-        padded[c + 2, pl.ds(r8, TILE)],
-        padded[1 + c, pl.ds(r8 - 1, TILE)],
-        padded[1 + c, pl.ds(r8 + 1, TILE)],
+def across(padded, c, t):
+    r8 = pl.multiple_of(WIDE * t + TILE, TILE)
+    return padded[1 + c, pl.ds(r8, WIDE)], [
+        padded[c, pl.ds(r8, WIDE)],
+        padded[c + 2, pl.ds(r8, WIDE)],
+        padded[1 + c, pl.ds(r8 - 1, WIDE)],
+        padded[1 + c, pl.ds(r8 + 1, WIDE)],
+    ]
+
+
+def along(cell, ends, c, t):
+    lane = lax.broadcasted_iota(jnp.int32, (WIDE, LANES), 1)
+    low, high = (ends[side, pl.ds(pl.multiple_of(WIDE * t, WIDE), WIDE)] for side in range(2))
+    return [
         jnp.where(lane == 0, roll(low, -c), roll(cell, 1)),
         jnp.where(lane == LANES - 1, roll(high, 14 - c), roll(cell, -1)),
-    )
-
-
-def adjoint_kernel(strips, m0, m1, m2, m3, cond, cot, adjoint, residual, padded, ends, kap, kends):
+    ]
+
+
+def adjoint_kernel(strips, m0, m1, m2, m3, cond, cot, adjoint, residual, padded, kap, faces, differences, ends, kends):
     collect(strips, (m0, m1, m2, m3), padded, ends, 0, None)
     collect(strips, (m0, m1, m2, m3), kap, kends, 0, cond)
 
-    @pl.loop(0, BY // TILE)
+    @pl.loop(0, BY // WIDE)
     def _(t):
-        at = pl.ds(pl.multiple_of(TILE * t, TILE), TILE)
+        at = pl.ds(pl.multiple_of(WIDE * t, WIDE), WIDE)
         for c in range(BX):
-            k, knear = around_cell(kap, kends, c, t)
-            x, xnear = around_cell(padded, ends, c, t)
+            k, knear = across(kap, c, t)
+            x, xnear = across(padded, c, t)
             total = 0.0
             for kn, xn in zip(knear, xnear):
                 total = total + (k + kn) * (x - xn)
+            for side, (kn, xn) in enumerate(zip(along(k, kends, c, t), along(x, ends, c, t))):
+                face, differ = k + kn, x - xn
+                faces[side, c, at] = face
+                differences[side, c, at] = differ
+                total = total + face * differ
             adjoint[c, at] = x
             residual[c, at] = cot[c, at] - (x + (0.5 * TIME_STEP) * total)
 
 
-def state_kernel(strips, m0, m1, m2, m3, previous, adj, adj_ends, kap, kends, adj_residual, grad, state, residuals, padded, ends):
+def state_kernel(strips, m0, m1, m2, m3, previous, adj, kap, faces, differences, adj_residual, grad, state, residuals, padded, ends):
     collect(strips, (m0, m1, m2, m3), padded, ends, 0, None)
 
-    @pl.loop(0, BY // TILE)
+    @pl.loop(0, BY // WIDE)
     def _(t):
-        at = pl.ds(pl.multiple_of(TILE * t, TILE), TILE)
+        at = pl.ds(pl.multiple_of(WIDE * t, WIDE), WIDE)
         for c in range(BX):
-            k, knear = around_cell(kap, kends, c, t)
-            x, xnear = around_cell(padded, ends, c, t)
-            y, ynear = around_cell(adj, adj_ends, c, t)
+            k, knear = across(kap, c, t)
+            x, xnear = across(padded, c, t)
+            y, ynear = across(adj, c, t)
             total = product = 0.0
             for kn, xn, yn in zip(knear, xnear, ynear):
                 differ = x - xn
                 total = total + (k + kn) * differ
                 product = product + differ * (y - yn)
+            for side, xn in enumerate(along(x, ends, c, t)):
+                differ = x - xn
+                total = total + faces[side, c, at] * differ
+                product = product + differ * differences[side, c, at]
             grad[c, at] = (-0.5 * TIME_STEP) * product
             state[c, at] = x
             residuals[0, c, at] = previous[0, c, at] - (x + (0.5 * TIME_STEP) * total)
@@ -598,24 +611,25 @@
     parts = [parts[0]] + [shifted(parts[d], "gx", d) for d in range(1, G)]
     stored = shifted(stored_state, "pa", 1)
     both = jnp.stack((stored, stored_state)).astype(F32) * row_scales[:, :, None]
-    above = shifted(both[:, :, BY - HALO :], "gy", 1)
-    below = shifted(both[:, :, :HALO], "gy", -1)
+    above_rows = shifted(both[:, :, BY - HALO :], "gy", 1)
+    below_rows = shifted(both[:, :, :HALO], "gy", -1)
+    parts, above_rows, below_rows = lax.optimization_barrier((parts, above_rows, below_rows))
+    edge = (2, G, BY, LANES)
+    rim = (2, G, 2, HALO, LANES)
+    to_left, to_right, head, tail = call(edge_kernel, [edge, edge, rim, rim], [places], parts)
+    to_left, below_rows = lax.optimization_barrier((to_left, below_rows))
     messages = call(
         pack_previous_kernel,
         [(4, EXTENDED, LANES)] * G,
         [strip_of(ahead)],
-        [both, above, below],
+        [both, above_rows, below_rows],
     )
-    parts, messages = lax.optimization_barrier((parts, messages))
-    edge = (2, G, BY, LANES)
-    rim = (2, G, 2, HALO, LANES)
-    to_left, to_right, head, tail = call(edge_kernel, [edge, edge, rim, rim], [places], parts)
     from_left, from_right = around(to_right, 1), around(to_left, -1)
+    from_left, from_right, own = lax.optimization_barrier((from_left, from_right, messages[0]))
     above, below = shifted(tail, "gy", 1), shifted(head, "gy", -1)
     edges = [jnp.stack((from_left[:, :, at], from_right[:, :, at])) for at in (slice(BY - HALO, BY), slice(0, HALO))]
     halos = [from_left, from_right, above, below, shifted(edges[0], "gy", 1), shifted(edges[1], "gy", -1)]
-    messages, halos = lax.optimization_barrier((messages, halos))
-    second = [messages[0]] + [shifted(messages[d], "gx", d) for d in range(1, G)]
+    second = [own] + [shifted(messages[d], "gx", d) for d in range(1, G)]
 
     line = (PLANES, 2, ROWS, LANES)
     half = (PLANES, ROWS, LANES)
@@ -651,17 +665,18 @@
     padded = (BX + 2, BY + 16, LANES)
     ends = (2, BY, LANES)
     here = strip_of(behind)
-    adjoint, adj_residual, adj, adj_ends, kap, kends = call(
+    adjoint, adj_residual, adj, kap, faces, differences = call(
         adjoint_kernel,
-        [out, out, padded, ends, padded, ends],
+        [out, out, padded, padded, (2,) + out, (2,) + out],
         [here],
         [*solved_adjoint, conductivity, cotangent],
+        [ends, ends],
     )
     grad, state, residuals = call(
         state_kernel,
         [out, out, (2,) + out],
         [here],
-        [*solved_state, both, adj, adj_ends, kap, kends, adj_residual],
+        [*solved_state, both, adj, kap, faces, differences, adj_residual],
         [padded, ends],
     )
     return grad, adjoint, state, residuals

time: 145 us -> 140 us (0.966)
  local copies, waits for them, and re-layouts: 8.34 us -> 5.24 us
    ppermute x2, waiting for transfers between devices: 10.1 us -> 5.83 us  [around(): lax.ppermute(x, ('gx', 'pa'), [(at, order[(i + by) % len(order)]) for i,...]
    unnamed x24 -> x16, local copies, waits for them, and re-layouts: 8.3 us -> 5.2 us
    ppermute x19, waiting for transfers between devices: 26 us -> 29 us  [shifted(): return lax.ppermute(x, axis, [(i, (i + by) % count) for i in range(count)])]
  transfers between devices with their start and end apart: 21 -> 21, of which waited for: 12 -> 9; matrix products, arithmetic and copies ran while one was open for 1% -> 2% of each run, Pallas kernels for 44% -> 46%
where the time goes in v9:
time: 140 us; the launch traced here: 139 us
  Pallas kernels  70.7 us (50%)
  waiting for transfers between devices  34.9 us (25%)
  starting transfers between devices  24.7 us (18%)
  local copies, waits for them, and re-layouts  5.24 us (4%)
  other arithmetic  2.53 us (2%)
  between operations  1.48 us (1%)
    pallas_call x7, Pallas kernels, call(): pl.pallas_call(kernel, out_shape=[jax.ShapeDtypeStruct(shape, F32) for sh...  70.7 us
    ppermute x19, waiting for transfers between devices, shifted(): return lax.ppermute(x, axis, [(i, (i + by) % count) for i in range(count)])  29 us
    ppermute x19, starting transfers between devices, shifted(): return lax.ppermute(x, axis, [(i, (i + by) % count) for i in range(count)])  22.6 us
    ppermute x2, waiting for transfers between devices, around(): lax.ppermute(x, ('gx', 'pa'), [(at, order[(i + by) % len(order)]) for i,...  5.83 us
    unnamed x16, local copies, waits for them, and re-layouts  5.2 us
  transfers between devices with their start and end apart: 21, of which 9 were waited for; matrix products, arithmetic and copies ran while one was open for 2% of the time, Pallas kernels for 46%

profile of v9, /device:TPU:8, one launch (start us, length us, event | category | flops | bytes accessed | tf_op | source)
XLA Modules:
  0.0 139.5 jit_solution(7352417525321793626)
XLA Ops:
  4.0 1.6 %collective-permute-start.3 = (bf16[8,128,128]{2,1,0:T(8,128)(2,1)}, bf16[8,128,128]{2,1,0:T(8,128)(2,1)S(1)}, u32[]{:S(2)}, u32[]{:S(2)}) collective-permute-start(bf16[8,128,128]{2,1,0:T(8,128)(2,1)} %param.6), channel_id=1, source_target_pairs={{0,1},{1,0},{2,3},{3,2},{4,5},{5,4},{6,7},{7,6},{8,9},{9,8},{10,11... | collective-permute-start | bytes 786440 | tf_op jit(solution)/shard_map/ppermute | solution.py:585
  5.6 1.6 %collective-permute-start = (f32[2,2,128,128]{3,2,1,0:T(8,128)S(1)}, f32[2,2,128,128]{3,2,1,0:T(8,128)S(1)}, u32[]{:S(2)}, u32[]{:S(2)}) collective-permute-start(f32[2,2,128,128]{3,2,1,0:T(8,128)S(1)} %get-tuple-element.59), channel_id=1, source_target_pairs={{0,8},{8,16},{16,24},{24,0},{1,9},{9,17},{17,25},{25,1},{2,10},{10... | collective-permute-start | bytes 786440 | tf_op jit(solution)/shard_map/ppermute | solution.py:585
  8.4 1.8 %collective-permute-start.2 = (f32[2,2,128,128]{3,2,1,0:T(8,128)S(1)}, f32[2,2,128,128]{3,2,1,0:T(8,128)S(1)}, u32[]{:S(2)}, u32[]{:S(2)}) collective-permute-start(f32[2,2,128,128]{3,2,1,0:T(8,128)S(1)} %get-tuple-element.61), channel_id=1, source_target_pairs={{0,24},{8,0},{16,8},{24,16},{1,25},{9,1},{17,9},{25,17},{2,26},{10... | collective-permute-start | bytes 786440 | tf_op jit(solution)/shard_map/ppermute | solution.py:585
  10.2 2.1 %collective-permute-done.3 = bf16[8,128,128]{2,1,0:T(8,128)(2,1)S(1)} collective-permute-done((bf16[8,128,128]{2,1,0:T(8,128)(2,1)}, bf16[8,128,128]{2,1,0:T(8,128)(2,1)S(1)}, u32[]{:S(2)}, u32[]{:S(2)}) %collective-permute-start.3) | collective-permute-done | bytes 262176 | tf_op jit(solution)/shard_map/ppermute | solution.py:585
  14.1 11.0 %collective-permute-done.refs_1_ = f32[2,2,128,128]{3,2,1,0:T(8,128)S(1)} collective-permute-done((f32[2,2,128,128]{3,2,1,0:T(8,128)S(1)}, f32[2,2,128,128]{3,2,1,0:T(8,128)S(1)}, u32[]{:S(2)}, u32[]{:S(2)}) %collective-permute-start) | collective-permute-done | bytes 262176 | tf_op jit(solution)/shard_map/ppermute | solution.py:585
  25.1 4.2 %collective-permute-done.1.refs_2_ = f32[2,2,128,128]{3,2,1,0:T(8,128)S(1)} collective-permute-done((f32[2,2,128,128]{3,2,1,0:T(8,128)S(1)}, f32[2,2,128,128]{3,2,1,0:T(8,128)S(1)}, u32[]{:S(2)}, u32[]{:S(2)}) %collective-permute-start.1) | collective-permute-done | bytes 262176 | tf_op jit(solution)/shard_map/ppermute | solution.py:585
  29.3 1.8 %collective-permute-done.2.refs_3_ = f32[2,2,128,128]{3,2,1,0:T(8,128)S(1)} collective-permute-done((f32[2,2,128,128]{3,2,1,0:T(8,128)S(1)}, f32[2,2,128,128]{3,2,1,0:T(8,128)S(1)}, u32[]{:S(2)}, u32[]{:S(2)}) %collective-permute-start.2) | collective-permute-done | bytes 262176 | tf_op jit(solution)/shard_map/ppermute | solution.py:585
  32.0 2.0 %collective-permute-start.6 = (f32[2,4,128,128]{3,2,1,0:T(8,128)S(1)}, f32[2,4,128,128]{3,2,1,0:T(8,128)S(1)}, u32[]{:S(2)}, u32[]{:S(2)}) collective-permute-start(f32[2,4,128,128]{3,2,1,0:T(8,128)S(1)} %get-tuple-element.67), channel_id=1, source_target_pairs={{0,8},{8,16},{16,24},{24,25},{25,17},{17,9},{9,1},{1,0},{2,10},{10... | collective-permute-start | bytes 1572872 | tf_op jit(solution)/shard_map/ppermute | solution.py:590
  34.1 1.7 %collective-permute-start.12 = (f32[2,4,2,16,128]{4,3,2,1,0:T(8,128)S(1)}, f32[2,4,2,16,128]{4,3,2,1,0:T(8,128)S(1)}, u32[]{:S(2)}, u32[]{:S(2)}) collective-permute-start(f32[2,4,2,16,128]{4,3,2,1,0:T(8,128)S(1)} %get-tuple-element.81), channel_id=1, source_target_pairs={{0,6},{2,0},{4,2},{6,4},{1,7},{3,1},{5,3},{7,5},{8,14},{10,8},{12,... | collective-permute-start | bytes 393224 | tf_op jit(solution)/shard_map/ppermute | solution.py:585
  35.8 4.3 %shard_map.86 = (f32[4,160,128]{2,1,0:T(8,128)S(1)}, f32[4,160,128]{2,1,0:T(8,128)}, f32[4,160,128]{2,1,0:T(8,128)}, f32[4,160,128]{2,1,0:T(8,128)}) custom-call(s32[4]{0:T(128)S(1)} %broadcast_select_fusion.strips, f32[2,8,128,128]{3,2,1,0:T(8,128)S(1)} %convert_multiply_fusion.both.previous, f32[2,8,16,128]{3,2,1,0:T(8,128)S(1)} %collective-permute-done.4.above, ...), custom_call_target="tpu_custom_call" | custom-call | bytes 6000000 | tf_op jit(solution)/shard_map/pallas_call | solution.py:572
  40.1 5.8 %collective-permute-done.7.refs_5_ = f32[2,4,128,128]{3,2,1,0:T(8,128)S(1)} collective-permute-done((f32[2,4,128,128]{3,2,1,0:T(8,128)S(1)}, f32[2,4,128,128]{3,2,1,0:T(8,128)S(1)}, u32[]{:S(2)}, u32[]{:S(2)}) %collective-permute-start.7) | collective-permute-done | bytes 524320 | tf_op jit(solution)/shard_map/ppermute | solution.py:590
  47.3 1.7 %collective-permute-start.14 = (f32[2,2,4,16,128]{4,3,2,1,0:T(8,128)}, f32[2,2,4,16,128]{4,3,2,1,0:T(8,128)}, u32[]{:S(2)}, u32[]{:S(2)}) collective-permute-start(f32[2,2,4,16,128]{4,3,2,1,0:T(8,128)} %pad_maximum_fusion.1), channel_id=1, source_target_pairs={{0,6},{2,0},{4,2},{6,4},{1,7},{3,1},{5,3},{7,5},{8,14},{10,8},{12,... | collective-permute-start | bytes 393224 | tf_op jit(solution)/shard_map/ppermute | solution.py:585
  49.0 1.7 %collective-permute-start.8 = (f32[4,160,128]{2,1,0:T(8,128)}, f32[4,160,128]{2,1,0:T(8,128)}, u32[]{:S(2)}, u32[]{:S(2)}) collective-permute-start(f32[4,160,128]{2,1,0:T(8,128)} %get-tuple-element.75), channel_id=1, source_target_pairs={{0,8},{8,16},{16,24},{24,0},{1,9},{9,17},{17,25},{25,1},{2,10},{10... | collective-permute-start | bytes 983048 | tf_op jit(solution)/shard_map/ppermute | solution.py:585
  56.3 28.3 %shard_map.87 = (f32[544,128]{1,0:T(8,128)S(1)}, f32[544,128]{1,0:T(8,128)S(1)}, f32[544,128]{1,0:T(8,128)S(1)}, f32[544,128]{1,0:T(8,128)S(1)}, f32[8,2,176,128...) custom-call(s32[1]{0:T(128)} %bitcast.strip, ...), custom_call_target="tpu_custom_call" | custom-call | bytes 75000000 | tf_op jit(solution)/shard_map/pallas_call | solution.py:572
  84.5 1.5 %collective-permute-start.18 = (f32[544,128]{1,0:T(8,128)S(1)}, f32[544,128]{1,0:T(8,128)S(1)}, u32[]{:S(2)}, u32[]{:S(2)}) collective-permute-start(f32[544,128]{1,0:T(8,128)S(1)} %get-tuple-element.92), channel_id=1, source_target_pairs={{0,8},{8,16},{16,24},{24,0},{1,9},{9,17},{17,25},{25,1},{2,10},{10... | collective-permute-start | bytes 835592 | tf_op jit(solution)/shard_map/ppermute | solution.py:585
  86.0 3.6 %collective-permute-start.19 = (f32[544,128]{1,0:T(8,128)S(1)}, f32[544,128]{1,0:T(8,128)S(1)}, u32[]{:S(2)}, u32[]{:S(2)}) collective-permute-start(f32[544,128]{1,0:T(8,128)S(1)} %get-tuple-element.93), channel_id=1, source_target_pairs={{0,16},{8,24},{16,0},{24,8},{1,17},{9,25},{17,1},{25,9},{2,18},{10... | collective-permute-start | bytes 835592 | tf_op jit(solution)/shard_map/ppermute | solution.py:585
  89.6 25.2 %shard_map.88 = (f32[400,128]{1,0:T(8,128)S(1)}, f32[400,128]{1,0:T(8,128)S(1)}, f32[400,128]{1,0:T(8,128)S(1)}, f32[400,128]{1,0:T(8,128)S(1)}) custom-call(s32[1]{0:T(128)} %bitcast.strip, f32[1]{0:T(128)S(6)} %copy.9.upper, f32[4,160,128]{2,1,0:T(8,128)S(1)} %get-tuple-element.74.refs_0_, f32[4,160,128]{2,1,0:T(8,128)} %collective-permute-done.8.refs_1_, ...), custom_call_target="tpu_custom_call" | custom-call | bytes 75000000 | tf_op jit(solution)/shard_map/pallas_call | solution.py:572
  114.8 2.1 %collective-permute-start.15 = (f32[400,128]{1,0:T(8,128)S(1)}, f32[400,128]{1,0:T(8,128)S(1)}, u32[]{:S(2)}, u32[]{:S(2)}) collective-permute-start(f32[400,128]{1,0:T(8,128)S(1)} %get-tuple-element.88), channel_id=1, source_target_pairs={{0,8},{8,16},{16,24},{24,0},{1,9},{9,17},{17,25},{25,1},{2,10},{10... | collective-permute-start | bytes 614408 | tf_op jit(solution)/shard_map/ppermute | solution.py:585
  116.9 1.8 %collective-permute-start.16 = (f32[400,128]{1,0:T(8,128)S(1)}, f32[400,128]{1,0:T(8,128)S(1)}, u32[]{:S(2)}, u32[]{:S(2)}) collective-permute-start(f32[400,128]{1,0:T(8,128)S(1)} %get-tuple-element.89), channel_id=1, source_target_pairs={{0,16},{8,24},{16,0},{24,8},{1,17},{9,25},{17,1},{25,9},{2,18},{10... | collective-permute-start | bytes 614408 | tf_op jit(solution)/shard_map/ppermute | solution.py:585
  118.8 6.1 %shard_map.89 = (f32[8,128,128]{2,1,0:T(8,128)}, f32[8,128,128]{2,1,0:T(8,128)S(1)}, f32[10,144,128]{2,1,0:T(8,128)S(1)}, f32[10,144,128]{2,1,0:T(8,128)S(1)}, f...) custom-call(s32[4]{0:T(128)S(1)} %broadcast_select_fusion.1.strips, f32[544,128]{1,0:T(8,128)S(1)} %get-tuple-element.91.m0, ...), custom_call_target="tpu_custom_call" | custom-call | bytes 6000000 | tf_op jit(solution)/shard_map/pallas_call | solution.py:572
  124.8 5.7 %collective-permute-done.15.m1 = f32[400,128]{1,0:T(8,128)S(1)} collective-permute-done((f32[400,128]{1,0:T(8,128)S(1)}, f32[400,128]{1,0:T(8,128)S(1)}, u32[]{:S(2)}, u32[]{:S(2)}) %collective-permute-start.15) | collective-permute-done | bytes 204832 | tf_op jit(solution)/shard_map/ppermute | solution.py:585
  130.6 2.2 %collective-permute-done.16.m2 = f32[400,128]{1,0:T(8,128)S(1)} collective-permute-done((f32[400,128]{1,0:T(8,128)S(1)}, f32[400,128]{1,0:T(8,128)S(1)}, u32[]{:S(2)}, u32[]{:S(2)}) %collective-permute-start.16) | collective-permute-done | bytes 204832 | tf_op jit(solution)/shard_map/ppermute | solution.py:585
  132.8 2.0 %collective-permute-done.17.m3 = f32[400,128]{1,0:T(8,128)S(1)} collective-permute-done((f32[400,128]{1,0:T(8,128)S(1)}, f32[400,128]{1,0:T(8,128)S(1)}, u32[]{:S(2)}, u32[]{:S(2)}) %collective-permute-start.17) | collective-permute-done | bytes 204832 | tf_op jit(solution)/shard_map/ppermute | solution.py:585
  134.7 4.8 %shard_map.90 = (f32[8,128,128]{2,1,0:T(8,128)}, f32[8,128,128]{2,1,0:T(8,128)}, f32[2,8,128,128]{3,2,1,0:T(8,128)}) custom-call(s32[4]{0:T(128)S(1)} %broadcast_select_fusion.1.strips, f32[400,128]{1,0:T(8,128)S(1)} %get-tuple-element.87.m0, f32[400,128]{1,0:T(8,128)S(1)} %collective-permute-done.15.m1, f32[400,128]{1,0:T(8,128)S(1)} %collective-permute-done.16.m2, ...), custom_call_target="tpu_custom_call" | custom-call | bytes 6000000 | tf_op jit(solution)/shard_map/pallas_call | solution.py:572
  (51 shorter events, 13.6 us)
Async XLA Ops:
  0.7 1.0 copy-start
  4.0 8.3 %collective-permute-start.3 = (bf16[8,128,128]{2,1,0:T(8,128)(2,1)}, bf16[8,128,128]{2,1,0:T(8,128)(2,1)S(1)}, u32[]{:S(2)}, u32[]{:S(2)}) collective-permute-start(bf16[8,128,128]{2,1,0:T(8,128)(2,1)} %param.6), channel_id=1, source_target_pairs={{0,1},{1,0},{2,3},{3,2},{4,5},{5,4},{6,7},{7,6},{8,9},{9,8},{10,11... | collective-permute-start | bytes 786440 | tf_op jit(solution)/shard_map/ppermute | solution.py:585
  5.6 19.6 %collective-permute-start = (f32[2,2,128,128]{3,2,1,0:T(8,128)S(1)}, f32[2,2,128,128]{3,2,1,0:T(8,128)S(1)}, u32[]{:S(2)}, u32[]{:S(2)}) collective-permute-start(f32[2,2,128,128]{3,2,1,0:T(8,128)S(1)} %get-tuple-element.59), channel_id=1, source_target_pairs={{0,8},{8,16},{16,24},{24,0},{1,9},{9,17},{17,25},{25,1},{2,10},{10... | collective-permute-start | bytes 786440 | tf_op jit(solution)/shard_map/ppermute | solution.py:585
  7.1 22.1 %collective-permute-start.1 = (f32[2,2,128,128]{3,2,1,0:T(8,128)S(1)}, f32[2,2,128,128]{3,2,1,0:T(8,128)S(1)}, u32[]{:S(2)}, u32[]{:S(2)}) collective-permute-start(f32[2,2,128,128]{3,2,1,0:T(8,128)S(1)} %get-tuple-element.60), channel_id=1, source_target_pairs={{0,16},{8,24},{16,0},{24,8},{1,17},{9,25},{17,1},{25,9},{2,18},{10... | collective-permute-start | bytes 786440 | tf_op jit(solution)/shard_map/ppermute | solution.py:585
  8.4 22.7 %collective-permute-start.2 = (f32[2,2,128,128]{3,2,1,0:T(8,128)S(1)}, f32[2,2,128,128]{3,2,1,0:T(8,128)S(1)}, u32[]{:S(2)}, u32[]{:S(2)}) collective-permute-start(f32[2,2,128,128]{3,2,1,0:T(8,128)S(1)} %get-tuple-element.61), channel_id=1, source_target_pairs={{0,24},{8,0},{16,8},{24,16},{1,25},{9,1},{17,9},{25,17},{2,26},{10... | collective-permute-start | bytes 786440 | tf_op jit(solution)/shard_map/ppermute | solution.py:585
  13.5 17.6 %collective-permute-start.5 = (f32[2,8,16,128]{3,2,1,0:T(8,128)S(1)}, f32[2,8,16,128]{3,2,1,0:T(8,128)S(1)}, u32[]{:S(2)}, u32[]{:S(2)}) collective-permute-start(f32[2,8,16,128]{3,2,1,0:T(8,128)S(1)} %get-tuple-element.104), channel_id=1, source_target_pairs={{0,6},{2,0},{4,2},{6,4},{1,7},{3,1},{5,3},{7,5},{8,14},{10,8},{12,... | collective-permute-start | bytes 393224 | tf_op jit(solution)/shard_map/ppermute | solution.py:585
  13.6 17.5 %collective-permute-start.4 = (f32[2,8,16,128]{3,2,1,0:T(8,128)S(1)}, f32[2,8,16,128]{3,2,1,0:T(8,128)S(1)}, u32[]{:S(2)}, u32[]{:S(2)}) collective-permute-start(f32[2,8,16,128]{3,2,1,0:T(8,128)S(1)} %get-tuple-element.105), channel_id=1, source_target_pairs={{0,2},{2,4},{4,6},{6,0},{1,3},{3,5},{5,7},{7,1},{8,10},{10,12},{12... | collective-permute-start | bytes 393224 | tf_op jit(solution)/shard_map/ppermute | solution.py:585
  32.0 13.9 %collective-permute-start.7 = (f32[2,4,128,128]{3,2,1,0:T(8,128)S(1)}, f32[2,4,128,128]{3,2,1,0:T(8,128)S(1)}, u32[]{:S(2)}, u32[]{:S(2)}) collective-permute-start(f32[2,4,128,128]{3,2,1,0:T(8,128)S(1)} %get-tuple-element.70), channel_id=1, source_target_pairs={{0,1},{8,0},{16,8},{24,16},{25,24},{17,25},{9,17},{1,9},{2,3},{10,... | collective-permute-start | bytes 1572872 | tf_op jit(solution)/shard_map/ppermute | solution.py:590
  32.0 13.9 %collective-permute-start.6 = (f32[2,4,128,128]{3,2,1,0:T(8,128)S(1)}, f32[2,4,128,128]{3,2,1,0:T(8,128)S(1)}, u32[]{:S(2)}, u32[]{:S(2)}) collective-permute-start(f32[2,4,128,128]{3,2,1,0:T(8,128)S(1)} %get-tuple-element.67), channel_id=1, source_target_pairs={{0,8},{8,16},{16,24},{24,25},{25,17},{17,9},{9,1},{1,0},{2,10},{10... | collective-permute-start | bytes 1572872 | tf_op jit(solution)/shard_map/ppermute | solution.py:590
  34.1 16.7 %collective-permute-start.11 = (f32[2,4,2,16,128]{4,3,2,1,0:T(8,128)S(1)}, f32[2,4,2,16,128]{4,3,2,1,0:T(8,128)S(1)}, u32[]{:S(2)}, u32[]{:S(2)}) collective-permute-start(f32[2,4,2,16,128]{4,3,2,1,0:T(8,128)S(1)} %get-tuple-element.80), channel_id=1, source_target_pairs={{0,2},{2,4},{4,6},{6,0},{1,3},{3,5},{5,7},{7,1},{8,10},{10,12},{12... | collective-permute-start | bytes 393224 | tf_op jit(solution)/shard_map/ppermute | solution.py:585
  34.1 18.5 %collective-permute-start.12 = (f32[2,4,2,16,128]{4,3,2,1,0:T(8,128)S(1)}, f32[2,4,2,16,128]{4,3,2,1,0:T(8,128)S(1)}, u32[]{:S(2)}, u32[]{:S(2)}) collective-permute-start(f32[2,4,2,16,128]{4,3,2,1,0:T(8,128)S(1)} %get-tuple-element.81), channel_id=1, source_target_pairs={{0,6},{2,0},{4,2},{6,4},{1,7},{3,1},{5,3},{7,5},{8,14},{10,8},{12,... | collective-permute-start | bytes 393224 | tf_op jit(solution)/shard_map/ppermute | solution.py:585
  46.6 7.8 %collective-permute-start.13 = (f32[2,2,4,16,128]{4,3,2,1,0:T(8,128)}, f32[2,2,4,16,128]{4,3,2,1,0:T(8,128)}, u32[]{:S(2)}, u32[]{:S(2)}) collective-permute-start(f32[2,2,4,16,128]{4,3,2,1,0:T(8,128)} %pad_maximum_fusion), channel_id=1, source_target_pairs={{0,2},{2,4},{4,6},{6,0},{1,3},{3,5},{5,7},{7,1},{8,10},{10,12},{12... | collective-permute-start | bytes 393224 | tf_op jit(solution)/shard_map/ppermute | solution.py:585
  47.3 7.1 %collective-permute-start.14 = (f32[2,2,4,16,128]{4,3,2,1,0:T(8,128)}, f32[2,2,4,16,128]{4,3,2,1,0:T(8,128)}, u32[]{:S(2)}, u32[]{:S(2)}) collective-permute-start(f32[2,2,4,16,128]{4,3,2,1,0:T(8,128)} %pad_maximum_fusion.1), channel_id=1, source_target_pairs={{0,6},{2,0},{4,2},{6,4},{1,7},{3,1},{5,3},{7,5},{8,14},{10,8},{12,... | collective-permute-start | bytes 393224 | tf_op jit(solution)/shard_map/ppermute | solution.py:585
  49.0 40.6 %collective-permute-start.8 = (f32[4,160,128]{2,1,0:T(8,128)}, f32[4,160,128]{2,1,0:T(8,128)}, u32[]{:S(2)}, u32[]{:S(2)}) collective-permute-start(f32[4,160,128]{2,1,0:T(8,128)} %get-tuple-element.75), channel_id=1, source_target_pairs={{0,8},{8,16},{16,24},{24,0},{1,9},{9,17},{17,25},{25,1},{2,10},{10... | collective-permute-start | bytes 983048 | tf_op jit(solution)/shard_map/ppermute | solution.py:585
  51.4 38.2 %collective-permute-start.9 = (f32[4,160,128]{2,1,0:T(8,128)}, f32[4,160,128]{2,1,0:T(8,128)}, u32[]{:S(2)}, u32[]{:S(2)}) collective-permute-start(f32[4,160,128]{2,1,0:T(8,128)} %get-tuple-element.76), channel_id=1, source_target_pairs={{0,16},{8,24},{16,0},{24,8},{1,17},{9,25},{17,1},{25,9},{2,18},{10... | collective-permute-start | bytes 983048 | tf_op jit(solution)/shard_map/ppermute | solution.py:585
  53.2 36.5 %collective-permute-start.10 = (f32[4,160,128]{2,1,0:T(8,128)}, f32[4,160,128]{2,1,0:T(8,128)}, u32[]{:S(2)}, u32[]{:S(2)}) collective-permute-start(f32[4,160,128]{2,1,0:T(8,128)} %get-tuple-element.77), channel_id=1, source_target_pairs={{0,24},{8,0},{16,8},{24,16},{1,25},{9,1},{17,9},{25,17},{2,26},{10... | collective-permute-start | bytes 983048 | tf_op jit(solution)/shard_map/ppermute | solution.py:585
  84.5 34.2 %collective-permute-start.18 = (f32[544,128]{1,0:T(8,128)S(1)}, f32[544,128]{1,0:T(8,128)S(1)}, u32[]{:S(2)}, u32[]{:S(2)}) collective-permute-start(f32[544,128]{1,0:T(8,128)S(1)} %get-tuple-element.92), channel_id=1, source_target_pairs={{0,8},{8,16},{16,24},{24,0},{1,9},{9,17},{17,25},{25,1},{2,10},{10... | collective-permute-start | bytes 835592 | tf_op jit(solution)/shard_map/ppermute | solution.py:585
  86.0 32.7 %collective-permute-start.19 = (f32[544,128]{1,0:T(8,128)S(1)}, f32[544,128]{1,0:T(8,128)S(1)}, u32[]{:S(2)}, u32[]{:S(2)}) collective-permute-start(f32[544,128]{1,0:T(8,128)S(1)} %get-tuple-element.93), channel_id=1, source_target_pairs={{0,16},{8,24},{16,0},{24,8},{1,17},{9,25},{17,1},{25,9},{2,18},{10... | collective-permute-start | bytes 835592 | tf_op jit(solution)/shard_map/ppermute | solution.py:585
  89.6 29.1 %collective-permute-start.20 = (f32[544,128]{1,0:T(8,128)S(1)}, f32[544,128]{1,0:T(8,128)S(1)}, u32[]{:S(2)}, u32[]{:S(2)}) collective-permute-start(f32[544,128]{1,0:T(8,128)S(1)} %get-tuple-element.94), channel_id=1, source_target_pairs={{0,24},{8,0},{16,8},{24,16},{1,25},{9,1},{17,9},{25,17},{2,26},{10... | collective-permute-start | bytes 835592 | tf_op jit(solution)/shard_map/ppermute | solution.py:585
  89.6 29.1 %copy-start.1 = (f32[8,128,128]{2,1,0:T(8,128)S(1)}, f32[8,128,128]{2,1,0:T(8,128)}, u32[]{:S(2)}) copy-start(f32[8,128,128]{2,1,0:T(8,128)} %cond.1) | copy-start | bytes 1572868
  89.6 29.1 %copy-start.3 = (f32[8,128,128]{2,1,0:T(8,128)S(1)}, f32[8,128,128]{2,1,0:T(8,128)}, u32[]{:S(2)}) copy-start(f32[8,128,128]{2,1,0:T(8,128)} %cot.1) | copy-start | bytes 1572868
  114.8 15.7 %collective-permute-start.15 = (f32[400,128]{1,0:T(8,128)S(1)}, f32[400,128]{1,0:T(8,128)S(1)}, u32[]{:S(2)}, u32[]{:S(2)}) collective-permute-start(f32[400,128]{1,0:T(8,128)S(1)} %get-tuple-element.88), channel_id=1, source_target_pairs={{0,8},{8,16},{16,24},{24,0},{1,9},{9,17},{17,25},{25,1},{2,10},{10... | collective-permute-start | bytes 614408 | tf_op jit(solution)/shard_map/ppermute | solution.py:585
  116.9 15.9 %collective-permute-start.16 = (f32[400,128]{1,0:T(8,128)S(1)}, f32[400,128]{1,0:T(8,128)S(1)}, u32[]{:S(2)}, u32[]{:S(2)}) collective-permute-start(f32[400,128]{1,0:T(8,128)S(1)} %get-tuple-element.89), channel_id=1, source_target_pairs={{0,16},{8,24},{16,0},{24,8},{1,17},{9,25},{17,1},{25,9},{2,18},{10... | collective-permute-start | bytes 614408 | tf_op jit(solution)/shard_map/ppermute | solution.py:585
  118.7 16.0 %collective-permute-start.17 = (f32[400,128]{1,0:T(8,128)S(1)}, f32[400,128]{1,0:T(8,128)S(1)}, u32[]{:S(2)}, u32[]{:S(2)}) collective-permute-start(f32[400,128]{1,0:T(8,128)S(1)} %get-tuple-element.90), channel_id=1, source_target_pairs={{0,24},{8,0},{16,8},{24,16},{1,25},{9,1},{17,9},{25,17},{2,26},{10... | collective-permute-start | bytes 614408 | tf_op jit(solution)/shard_map/ppermute | solution.py:585
  (5 other events, 4.2 us)

commit v10 on v9

--- a/solution.py
+++ b/solution.py
@@ -155,7 +155,24 @@
                 outs[d][n, a] = pick(groups[d], parts)
 
 
-def pack_previous_kernel(strips, both, above, below, *outs):
+def chebyshev_steps(upper, steps):
+    bound = jnp.full((TILE, LANES), upper[0])
+    theta = 0.5 * (bound + 1.0)
+    delta = 0.5 * (bound - 1.0)
+    sigma = theta / delta
+    rho = 1.0 / sigma
+    steps[0, 0] = 1.0 / theta
+    steps[0, 1] = jnp.zeros_like(theta)
+    for k in range(1, CHEB):
+        rho_next = 1.0 / (2.0 * sigma - rho)
+        steps[k, 0] = rho_next * rho
+        steps[k, 1] = 2.0 * rho_next / delta
+        rho = rho_next
+
+
+def pack_previous_kernel(strips, upper, both, above, below, *outs):
+    *outs, steps = outs
+    chebyshev_steps(upper, steps)
     src = lax.broadcasted_iota(jnp.int32, (2 * LANES, 2 * LANES), 0)
     dst = lax.broadcasted_iota(jnp.int32, (2 * LANES, 2 * LANES), 1)
     place = LANES * lax.rem(src, 2) + 64 * (src // LANES) + lax.rem(src, LANES) // 2
@@ -185,17 +202,24 @@
 
 
 def edge_kernel(places, *refs):
-    msgs, (to_left, to_right, head, tail) = refs[:G], refs[G:]
+    msgs, (to_left, to_right) = refs[:G], refs[G:]
     lane = lax.broadcasted_iota(jnp.int32, (BY, LANES), 1)
     low = lax.rem(lane, 16) < 8
-    for n in range(msgs[0].shape[0]):
+    for n in range(2):
         for d in range(G):
             first, second = msgs[d][n, 0], msgs[d][n, 1]
             to_left[n, places[0, d]] = jnp.where(low, first, roll(second, 8))
             to_right[n, places[1, d]] = jnp.where(low, roll(second, -8), first)
-            for a in range(2):
-                head[n, d, a] = msgs[d][n, a, :HALO]
-                tail[n, d, a] = msgs[d][n, a, BY - HALO :]
+
+
+def rows_kernel(*refs):
+    msgs, sides, (head, tail) = refs[:G], refs[G : G + 2], refs[G + 2 :]
+    for n in range(2):
+        for d in range(G):
+            for out, rows in ((head, slice(0, HALO)), (tail, slice(BY - HALO, BY))):
+                for a in range(2):
+                    out[n, d, a] = msgs[d][n, a, rows]
+                    out[n, d, 2 + a] = sides[a][n, d, rows]
 
 
 def unpack(get_brick, get_edge, group, within, put):
@@ -227,27 +251,17 @@
             put(2 * m + k // 2, k % 2, roll(whole, -32 * k - 8))
 
 
-def solve_kernel(adjoint, strip, upper, *refs):
+def solve_kernel(adjoint, strip, steps, *refs):
     if adjoint:
-        bricks, (from_left, from_right, above, below, above_edge, below_edge) = refs[:G], refs[G : G + 6]
-        outs, coefficients, (kap, *scratch) = refs[G + 6 : 2 * G + 6], refs[2 * G + 6 : 2 * G + 11], refs[2 * G + 11 :]
+        bricks, (from_left, from_right, above, below) = refs[:G], refs[G : G + 4]
+        outs, coefficients, (kap, *scratch) = refs[G + 4 : 2 * G + 4], refs[2 * G + 4 : 2 * G + 9], refs[2 * G + 9 :]
     else:
         strips_here, coefficients = refs[:G], refs[G : G + 5]
         outs, scratch = refs[G + 5 : 2 * G + 5], refs[2 * G + 5 :]
     kx, ky, kin, kout, diag = coefficients
-    rhs, xa, xb, xc, turned, steps = scratch
+    rhs, xa, xb, xc, turned, turned_first = scratch
     zero = jnp.zeros((TILE, LANES), F32)
-
-    theta = 0.5 * (jnp.full((TILE, LANES), upper[0]) + 1.0)
-    delta = 0.5 * (jnp.full((TILE, LANES), upper[0]) - 1.0)
-    sigma = theta / delta
-    rho = 1.0 / sigma
-    for k in range(1, CHEB):
-        rho_next = 1.0 / (2.0 * sigma - rho)
-        steps[k, 0] = rho_next * rho
-        steps[k, 1] = 2.0 * rho_next / delta
-        rho = rho_next
-    theta_inv = 1.0 / (0.5 * (jnp.full((2 * TILE, LANES), upper[0]) + 1.0))
+    theta_inv = jnp.concatenate([steps[0, 0]] * 2, axis=0)
 
     def put_at(dst, to, rows):
         def put(i, e, val):
@@ -265,7 +279,7 @@
             dst[i, ROWS - TILE : ROWS] = zero
 
     if adjoint:
-        sides, corners = (from_left, from_right), (above_edge, below_edge)
+        sides = (from_left, from_right)
 
         @pl.loop(0, BY // CHUNK)
         def _(t):
@@ -282,10 +296,10 @@
 
         group_halo, within_halo = lanes_of(HALO, strip[0])
         for n, dst in enumerate((kap, rhs)):
-            for brick, edge, start in ((above, above_edge, TOP - HALO), (below, below_edge, TOP + BY)):
+            for rows, start in ((above, TOP - HALO), (below, TOP + BY)):
                 unpack(
-                    lambda d, a: brick[n, d, a],
-                    lambda side, d: edge[side, n, d],
+                    lambda d, a: rows[n, d, a],
+                    lambda side, d: rows[n, d, 2 + side],
                     group_halo,
                     within_halo,
                     put_at(dst, start, HALO),
@@ -334,7 +348,7 @@
                 before[e] = fx
             now = after
 
-    def turn_lanes(cur, r):
+    def turn_lanes(cur, r, turned):
         at = pl.ds(r, TILE)
         for i in range(PLANES):
             turned[i, 0] = roll(kout[i, at] * cur[i, 1, at], 1)
@@ -343,7 +357,7 @@
             turned[PLANES, e] = roll(kx[PLANES - 1, e, at] * cur[PLANES - 1, e, at], 32)
             turned[PLANES + 1, e] = roll(cur[0, e, at], -32)
 
-    def advance(alpha, beta, old, cur, new, r):
+    def advance(alpha, beta, old, cur, new, r, turned):
         at = pl.ds(r, TILE)
         now = [cur[0, e, at] for e in range(2)]
         before = fbefore = None
@@ -366,34 +380,42 @@
                 new[i, e, at] = centre * now[e] - alpha * old[i, e, at] + beta * near
             before, now, fbefore = now, after, fx
 
-    def sweep(k, old, cur, new, span):
+    def sweep(k, old, cur, new, span, following):
         alpha, beta = steps[k, 0], steps[k, 1]
-        turn_lanes(cur, span[0])
-
-        @pl.loop(0, span[1] // span[2])
+        first, count, unroll = span
+        for u in range(unroll):
+            r = first + TILE * u
+            advance(alpha, beta, old, cur, new, r, turned if u else turned_first)
+            turn_lanes(cur, r + TILE, turned)
+            if u == 2:
+                turn_lanes(new, following, turned_first)
+
+        @pl.loop(1, count // unroll)
         def _(t):
-            for u in range(span[2]):
-                r = pl.multiple_of(span[0] + TILE * (span[2] * t + u), TILE)
-                advance(alpha, beta, old, cur, new, r)
-                turn_lanes(cur, r + TILE)
-
-    def three(k, spans):
-        sweep(k, xa, xb, xc, spans[0])
-        sweep(k + 1, xb, xc, xa, spans[1])
-        sweep(k + 2, xc, xa, xb, spans[2])
+            for u in range(unroll):
+                r = pl.multiple_of(first + TILE * (unroll * t + u), TILE)
+                advance(alpha, beta, old, cur, new, r, turned)
+                turn_lanes(cur, r + TILE, turned)
 
     wide = (TILE, ROWS // TILE - 2, 4)
     narrow = (2 * TILE, ROWS // TILE - 4, 3)
 
+    def three(k, spans, following):
+        sweep(k, xa, xb, xc, spans[0], spans[1][0])
+        sweep(k + 1, xb, xc, xa, spans[1], spans[2][0])
+        sweep(k + 2, xc, xa, xb, spans[2], following[0])
+
+    turn_lanes(xb, wide[0], turned_first)
+
     @pl.loop(0, 2)
     def _(m):
-        three(1 + 3 * m, (wide,) * 3)
-
-    three(7, (wide, narrow, narrow))
+        three(1 + 3 * m, (wide,) * 3, wide)
+
+    three(7, (wide, narrow, narrow), narrow)
 
     @pl.loop(0, 2)
     def _(m):
-        three(10 + 3 * m, (narrow,) * 3)
+        three(10 + 3 * m, (narrow,) * 3, narrow)
 
     def mains(whole, group, within):
         parts = [jnp.where(within < 16, even, roll(odd, 16)) for even, odd in whole]
@@ -615,26 +637,26 @@
     below_rows = shifted(both[:, :, :HALO], "gy", -1)
     parts, above_rows, below_rows = lax.optimization_barrier((parts, above_rows, below_rows))
     edge = (2, G, BY, LANES)
-    rim = (2, G, 2, HALO, LANES)
-    to_left, to_right, head, tail = call(edge_kernel, [edge, edge, rim, rim], [places], parts)
+    rim = (2, G, 4, HALO, LANES)
+    to_left, to_right = call(edge_kernel, [edge, edge], [places], parts)
     to_left, below_rows = lax.optimization_barrier((to_left, below_rows))
-    messages = call(
+    *messages, steps_here = call(
         pack_previous_kernel,
-        [(4, EXTENDED, LANES)] * G,
-        [strip_of(ahead)],
+        [(4, EXTENDED, LANES)] * G + [(CHEB, 2, TILE, LANES)],
+        [strip_of(ahead), upper_bound],
         [both, above_rows, below_rows],
     )
     from_left, from_right = around(to_right, 1), around(to_left, -1)
     from_left, from_right, own = lax.optimization_barrier((from_left, from_right, messages[0]))
-    above, below = shifted(tail, "gy", 1), shifted(head, "gy", -1)
-    edges = [jnp.stack((from_left[:, :, at], from_right[:, :, at])) for at in (slice(BY - HALO, BY), slice(0, HALO))]
-    halos = [from_left, from_right, above, below, shifted(edges[0], "gy", 1), shifted(edges[1], "gy", -1)]
+    head, tail = call(rows_kernel, [rim, rim], [], [*parts, from_left, from_right])
+    halos = [from_left, from_right, shifted(tail, "gy", 1), shifted(head, "gy", -1)]
+
     second = [own] + [shifted(messages[d], "gx", d) for d in range(1, G)]
 
     line = (PLANES, 2, ROWS, LANES)
     half = (PLANES, ROWS, LANES)
-    lines = [line] * 4 + [(PLANES + 2, 2, TILE, LANES), (CHEB, 2, TILE, LANES)]
-    setup = [strip[None], upper_bound]
+    lines = [line] * 4 + [(PLANES + 2, 2, TILE, LANES)] * 2
+    setup = [strip[None]]
 
     def home(solved):
         return [solved[0]] + [shifted(solved[d], "gx", d) for d in range(1, G)]
@@ -643,7 +665,7 @@
         functools.partial(solve_kernel, True),
         [(BOTH, LANES)] * G + [line, line, half, half, line],
         setup,
-        [*parts, *halos],
+        [steps_here, *parts, *halos],
         [line] + lines,
         micros=25,
         mebibytes=24,
@@ -654,7 +676,7 @@
             functools.partial(solve_kernel, False),
             [(FIELD, LANES)] * G,
             setup,
-            [*second, kx, ky, kin, kout, diag],
+            [steps_here, *second, kx, ky, kin, kout, diag],
             lines,
             micros=25,
             mebibytes=24,

time: 140 us -> 136 us (0.971)
  waiting for transfers between devices: 34.9 us -> 39.5 us
  Pallas kernels: 70.7 us -> 68.3 us
  local copies, waits for them, and re-layouts: 5.24 us -> 2.84 us
  starting transfers between devices: 24.7 us -> 22.5 us
    ppermute x19 -> x17, waiting for transfers between devices: 29 us -> 33.3 us  [shifted(): return lax.ppermute(x, axis, [(i, (i + by) % count) for i in range(count)])]
    pallas_call x7 -> x8, Pallas kernels: 70.7 us -> 68.3 us  [call(): pl.pallas_call(kernel, out_shape=[jax.ShapeDtypeStruct(shape, F32) for sh...]
    unnamed x16 -> x12, local copies, waits for them, and re-layouts: 5.2 us -> 2.82 us
    ppermute x19 -> x17, starting transfers between devices: 22.6 us -> 20.5 us  [shifted(): return lax.ppermute(x, axis, [(i, (i + by) % count) for i in range(count)])]
  transfers between devices with their start and end apart: 21 -> 19, of which waited for: 9 -> 10; matrix products, arithmetic and copies ran while one was open for 2% -> 1% of each run, Pallas kernels for 46% -> 45%
where the time goes in v10:
time: 136 us
  Pallas kernels  68.3 us (50%)
  waiting for transfers between devices  39.5 us (29%)
  starting transfers between devices  22.5 us (17%)
  local copies, waits for them, and re-layouts  2.84 us (2%)
  between operations  1.43 us (1%)
    pallas_call x8, Pallas kernels, call(): pl.pallas_call(kernel, out_shape=[jax.ShapeDtypeStruct(shape, F32) for sh...  68.3 us
    ppermute x17, waiting for transfers between devices, shifted(): return lax.ppermute(x, axis, [(i, (i + by) % count) for i in range(count)])  33.3 us
    ppermute x17, starting transfers between devices, shifted(): return lax.ppermute(x, axis, [(i, (i + by) % count) for i in range(count)])  20.5 us
    ppermute x2, waiting for transfers between devices, around(): lax.ppermute(x, ('gx', 'pa'), [(at, order[(i + by) % len(order)]) for i,...  6.13 us
    unnamed x12, local copies, waits for them, and re-layouts  2.82 us
  transfers between devices with their start and end apart: 19, of which 10 were waited for; matrix products, arithmetic and copies ran while one was open for 1% of the time, Pallas kernels for 45%

profile of v10, /device:TPU:8, one launch (start us, length us, event | category | flops | bytes accessed | tf_op | source)
XLA Modules:
  0.0 135.8 jit_solution(11339400225998484572)
XLA Ops:
  2.7 1.2 shard_map.84
  4.0 1.6 %collective-permute-start = (bf16[8,128,128]{2,1,0:T(8,128)(2,1)}, bf16[8,128,128]{2,1,0:T(8,128)(2,1)S(1)}, u32[]{:S(2)}, u32[]{:S(2)}) collective-permute-start(bf16[8,128,128]{2,1,0:T(8,128)(2,1)} %param.6), channel_id=1, source_target_pairs={{0,1},{1,0},{2,3},{3,2},{4,5},{5,4},{6,7},{7,6},{8,9},{9,8},{10,11... | collective-permute-start | bytes 786440 | tf_op jit(solution)/shard_map/ppermute | solution.py:607
  5.6 1.6 %collective-permute-start.1 = (f32[2,2,128,128]{3,2,1,0:T(8,128)S(1)}, f32[2,2,128,128]{3,2,1,0:T(8,128)S(1)}, u32[]{:S(2)}, u32[]{:S(2)}) collective-permute-start(f32[2,2,128,128]{3,2,1,0:T(8,128)S(1)} %get-tuple-element.61), channel_id=1, source_target_pairs={{0,8},{8,16},{16,24},{24,0},{1,9},{9,17},{17,25},{25,1},{2,10},{10... | collective-permute-start | bytes 786440 | tf_op jit(solution)/shard_map/ppermute | solution.py:607
  7.1 1.2 collective-permute-start.2
  8.4 1.8 %collective-permute-start.3 = (f32[2,2,128,128]{3,2,1,0:T(8,128)S(1)}, f32[2,2,128,128]{3,2,1,0:T(8,128)S(1)}, u32[]{:S(2)}, u32[]{:S(2)}) collective-permute-start(f32[2,2,128,128]{3,2,1,0:T(8,128)S(1)} %get-tuple-element.63), channel_id=1, source_target_pairs={{0,24},{8,0},{16,8},{24,16},{1,25},{9,1},{17,9},{25,17},{2,26},{10... | collective-permute-start | bytes 786440 | tf_op jit(solution)/shard_map/ppermute | solution.py:607
  10.2 2.1 %collective-permute-done = bf16[8,128,128]{2,1,0:T(8,128)(2,1)S(1)} collective-permute-done((bf16[8,128,128]{2,1,0:T(8,128)(2,1)}, bf16[8,128,128]{2,1,0:T(8,128)(2,1)S(1)}, u32[]{:S(2)}, u32[]{:S(2)}) %collective-permute-start) | collective-permute-done | bytes 262176 | tf_op jit(solution)/shard_map/ppermute | solution.py:607
  14.1 11.0 %collective-permute-done.1.refs_1_ = f32[2,2,128,128]{3,2,1,0:T(8,128)S(1)} collective-permute-done((f32[2,2,128,128]{3,2,1,0:T(8,128)S(1)}, f32[2,2,128,128]{3,2,1,0:T(8,128)S(1)}, u32[]{:S(2)}, u32[]{:S(2)}) %collective-permute-start.1) | collective-permute-done | bytes 262176 | tf_op jit(solution)/shard_map/ppermute | solution.py:607
  25.1 4.2 %collective-permute-done.2.refs_2_ = f32[2,2,128,128]{3,2,1,0:T(8,128)S(1)} collective-permute-done((f32[2,2,128,128]{3,2,1,0:T(8,128)S(1)}, f32[2,2,128,128]{3,2,1,0:T(8,128)S(1)}, u32[]{:S(2)}, u32[]{:S(2)}) %collective-permute-start.2) | collective-permute-done | bytes 262176 | tf_op jit(solution)/shard_map/ppermute | solution.py:607
  29.3 1.8 %collective-permute-done.3.refs_3_ = f32[2,2,128,128]{3,2,1,0:T(8,128)S(1)} collective-permute-done((f32[2,2,128,128]{3,2,1,0:T(8,128)S(1)}, f32[2,2,128,128]{3,2,1,0:T(8,128)S(1)}, u32[]{:S(2)}, u32[]{:S(2)}) %collective-permute-start.3) | collective-permute-done | bytes 262176 | tf_op jit(solution)/shard_map/ppermute | solution.py:607
  32.0 2.0 %collective-permute-start.6 = (f32[2,4,128,128]{3,2,1,0:T(8,128)S(1)}, f32[2,4,128,128]{3,2,1,0:T(8,128)S(1)}, u32[]{:S(2)}, u32[]{:S(2)}) collective-permute-start(f32[2,4,128,128]{3,2,1,0:T(8,128)S(1)} %get-tuple-element.73), channel_id=1, source_target_pairs={{0,8},{8,16},{16,24},{24,25},{25,17},{17,9},{9,1},{1,0},{2,10},{10... | collective-permute-start | bytes 1572872 | tf_op jit(solution)/shard_map/ppermute | solution.py:612
  34.7 4.4 %shard_map.86 = (f32[4,160,128]{2,1,0:T(8,128)S(1)}, f32[4,160,128]{2,1,0:T(8,128)}, f32[4,160,128]{2,1,0:T(8,128)}, f32[4,160,128]{2,1,0:T(8,128)}, f32[16,2,8,128]{3,2,1,0:T(8,128)S(1)}) custom-call(s32[4]{0:T(128)S(1)} %broadcast_select_fusion.strips, f32[1]{0:T(128)S(6)} %copy.9.upper, f32[2,8,128,128]{3,2,1,0:T(8,128)S(1)} %convert_multiply_fusion.both.previous, ...), custom_call_target="tpu_custom_call" | custom-call | bytes 6000000 | tf_op jit(solution)/shard_map/pallas_call | solution.py:594
  39.8 6.1 %collective-permute-done.7.refs_5_ = f32[2,4,128,128]{3,2,1,0:T(8,128)S(1)} collective-permute-done((f32[2,4,128,128]{3,2,1,0:T(8,128)S(1)}, f32[2,4,128,128]{3,2,1,0:T(8,128)S(1)}, u32[]{:S(2)}, u32[]{:S(2)}) %collective-permute-start.7) | collective-permute-done | bytes 524320 | tf_op jit(solution)/shard_map/ppermute | solution.py:612
  46.8 1.7 %collective-permute-start.12 = (f32[2,4,4,16,128]{4,3,2,1,0:T(8,128)}, f32[2,4,4,16,128]{4,3,2,1,0:T(8,128)}, u32[]{:S(2)}, u32[]{:S(2)}) collective-permute-start(f32[2,4,4,16,128]{4,3,2,1,0:T(8,128)} %get-tuple-element.83), channel_id=1, source_target_pairs={{0,6},{2,0},{4,2},{6,4},{1,7},{3,1},{5,3},{7,5},{8,14},{10,8},{12,... | collective-permute-start | bytes 786440 | tf_op jit(solution)/shard_map/ppermute | solution.py:607
  48.5 1.7 %collective-permute-start.8 = (f32[4,160,128]{2,1,0:T(8,128)}, f32[4,160,128]{2,1,0:T(8,128)}, u32[]{:S(2)}, u32[]{:S(2)}) collective-permute-start(f32[4,160,128]{2,1,0:T(8,128)} %get-tuple-element.77), channel_id=1, source_target_pairs={{0,8},{8,16},{16,24},{24,0},{1,9},{9,17},{17,25},{25,1},{2,10},{10... | collective-permute-start | bytes 983048 | tf_op jit(solution)/shard_map/ppermute | solution.py:607
  52.0 1.8 %collective-permute-done.11.refs_6_ = f32[2,4,4,16,128]{4,3,2,1,0:T(8,128)S(1)} collective-permute-done((f32[2,4,4,16,128]{4,3,2,1,0:T(8,128)}, f32[2,4,4,16,128]{4,3,2,1,0:T(8,128)S(1)}, u32[]{:S(2)}, u32[]{:S(2)}) %collective-permute-start.11) | collective-permute-done | bytes 262176 | tf_op jit(solution)/shard_map/ppermute | solution.py:607
  54.7 26.5 %shard_map.88 = (f32[544,128]{1,0:T(8,128)S(1)}, f32[544,128]{1,0:T(8,128)S(1)}, f32[544,128]{1,0:T(8,128)S(1)}, f32[544,128]{1,0:T(8,128)S(1)}, f32[8,2,176,128...) custom-call(s32[1]{0:T(128)} %bitcast.strip, ...), custom_call_target="tpu_custom_call" | custom-call | bytes 75000000 | tf_op jit(solution)/shard_map/pallas_call | solution.py:594
  81.2 1.7 %collective-permute-start.16 = (f32[544,128]{1,0:T(8,128)S(1)}, f32[544,128]{1,0:T(8,128)S(1)}, u32[]{:S(2)}, u32[]{:S(2)}) collective-permute-start(f32[544,128]{1,0:T(8,128)S(1)} %get-tuple-element.94), channel_id=1, source_target_pairs={{0,8},{8,16},{16,24},{24,0},{1,9},{9,17},{17,25},{25,1},{2,10},{10... | collective-permute-start | bytes 835592 | tf_op jit(solution)/shard_map/ppermute | solution.py:607
  84.8 23.6 %shard_map.89 = (f32[400,128]{1,0:T(8,128)S(1)}, f32[400,128]{1,0:T(8,128)S(1)}, f32[400,128]{1,0:T(8,128)S(1)}, f32[400,128]{1,0:T(8,128)S(1)}) custom-call(s32[1]{0:T(128)} %bitcast.strip, f32[16,2,8,128]{3,2,1,0:T(8,128)S(1)} %get-tuple-element.72.steps, f32[4,160,128]{2,1,0:T(8,128)S(1)} %copy-done.5, f32[4,160,128]{2,1,0:T(8,128)} %collective-permute-done.8.refs_1_, ...), custom_call_target="tpu_custom_call" | custom-call | bytes 75000000 | tf_op jit(solution)/shard_map/pallas_call | solution.py:594
  108.4 1.5 %collective-permute-start.13 = (f32[400,128]{1,0:T(8,128)S(1)}, f32[400,128]{1,0:T(8,128)S(1)}, u32[]{:S(2)}, u32[]{:S(2)}) collective-permute-start(f32[400,128]{1,0:T(8,128)S(1)} %get-tuple-element.90), channel_id=1, source_target_pairs={{0,8},{8,16},{16,24},{24,0},{1,9},{9,17},{17,25},{25,1},{2,10},{10... | collective-permute-start | bytes 614408 | tf_op jit(solution)/shard_map/ppermute | solution.py:607
  109.8 3.6 %collective-permute-start.14 = (f32[400,128]{1,0:T(8,128)S(1)}, f32[400,128]{1,0:T(8,128)S(1)}, u32[]{:S(2)}, u32[]{:S(2)}) collective-permute-start(f32[400,128]{1,0:T(8,128)S(1)} %get-tuple-element.91), channel_id=1, source_target_pairs={{0,16},{8,24},{16,0},{24,8},{1,17},{9,25},{17,1},{25,9},{2,18},{10... | collective-permute-start | bytes 614408 | tf_op jit(solution)/shard_map/ppermute | solution.py:607
  113.5 6.1 %shard_map.90 = (f32[8,128,128]{2,1,0:T(8,128)}, f32[8,128,128]{2,1,0:T(8,128)S(1)}, f32[10,144,128]{2,1,0:T(8,128)S(1)}, f32[10,144,128]{2,1,0:T(8,128)S(1)}, f...) custom-call(s32[4]{0:T(128)S(1)} %broadcast_select_fusion.1.strips, f32[544,128]{1,0:T(8,128)S(1)} %get-tuple-element.93.m0, ...), custom_call_target="tpu_custom_call" | custom-call | bytes 6000000 | tf_op jit(solution)/shard_map/pallas_call | solution.py:594
  119.6 8.2 %collective-permute-done.14.m2 = f32[400,128]{1,0:T(8,128)S(1)} collective-permute-done((f32[400,128]{1,0:T(8,128)S(1)}, f32[400,128]{1,0:T(8,128)S(1)}, u32[]{:S(2)}, u32[]{:S(2)}) %collective-permute-start.14) | collective-permute-done | bytes 204832 | tf_op jit(solution)/shard_map/ppermute | solution.py:607
  127.8 3.3 %collective-permute-done.15.m3 = f32[400,128]{1,0:T(8,128)S(1)} collective-permute-done((f32[400,128]{1,0:T(8,128)S(1)}, f32[400,128]{1,0:T(8,128)S(1)}, u32[]{:S(2)}, u32[]{:S(2)}) %collective-permute-start.15) | collective-permute-done | bytes 204832 | tf_op jit(solution)/shard_map/ppermute | solution.py:607
  131.0 4.8 %shard_map.91 = (f32[8,128,128]{2,1,0:T(8,128)}, f32[8,128,128]{2,1,0:T(8,128)}, f32[2,8,128,128]{3,2,1,0:T(8,128)}) custom-call(s32[4]{0:T(128)S(1)} %broadcast_select_fusion.1.strips, f32[400,128]{1,0:T(8,128)S(1)} %get-tuple-element.89.m0, f32[400,128]{1,0:T(8,128)S(1)} %collective-permute-done.13.m1, f32[400,128]{1,0:T(8,128)S(1)} %collective-permute-done.14.m2, ...), custom_call_target="tpu_custom_call" | custom-call | bytes 6000000 | tf_op jit(solution)/shard_map/pallas_call | solution.py:594
  (40 shorter events, 11.0 us)
Async XLA Ops:
  0.7 1.0 copy-start
  1.7 1.0 copy-start.2
  4.0 8.3 %collective-permute-start = (bf16[8,128,128]{2,1,0:T(8,128)(2,1)}, bf16[8,128,128]{2,1,0:T(8,128)(2,1)S(1)}, u32[]{:S(2)}, u32[]{:S(2)}) collective-permute-start(bf16[8,128,128]{2,1,0:T(8,128)(2,1)} %param.6), channel_id=1, source_target_pairs={{0,1},{1,0},{2,3},{3,2},{4,5},{5,4},{6,7},{7,6},{8,9},{9,8},{10,11... | collective-permute-start | bytes 786440 | tf_op jit(solution)/shard_map/ppermute | solution.py:607
  5.6 19.6 %collective-permute-start.1 = (f32[2,2,128,128]{3,2,1,0:T(8,128)S(1)}, f32[2,2,128,128]{3,2,1,0:T(8,128)S(1)}, u32[]{:S(2)}, u32[]{:S(2)}) collective-permute-start(f32[2,2,128,128]{3,2,1,0:T(8,128)S(1)} %get-tuple-element.61), channel_id=1, source_target_pairs={{0,8},{8,16},{16,24},{24,0},{1,9},{9,17},{17,25},{25,1},{2,10},{10... | collective-permute-start | bytes 786440 | tf_op jit(solution)/shard_map/ppermute | solution.py:607
  7.1 22.1 %collective-permute-start.2 = (f32[2,2,128,128]{3,2,1,0:T(8,128)S(1)}, f32[2,2,128,128]{3,2,1,0:T(8,128)S(1)}, u32[]{:S(2)}, u32[]{:S(2)}) collective-permute-start(f32[2,2,128,128]{3,2,1,0:T(8,128)S(1)} %get-tuple-element.62), channel_id=1, source_target_pairs={{0,16},{8,24},{16,0},{24,8},{1,17},{9,25},{17,1},{25,9},{2,18},{10... | collective-permute-start | bytes 786440 | tf_op jit(solution)/shard_map/ppermute | solution.py:607
  8.4 22.7 %collective-permute-start.3 = (f32[2,2,128,128]{3,2,1,0:T(8,128)S(1)}, f32[2,2,128,128]{3,2,1,0:T(8,128)S(1)}, u32[]{:S(2)}, u32[]{:S(2)}) collective-permute-start(f32[2,2,128,128]{3,2,1,0:T(8,128)S(1)} %get-tuple-element.63), channel_id=1, source_target_pairs={{0,24},{8,0},{16,8},{24,16},{1,25},{9,1},{17,9},{25,17},{2,26},{10... | collective-permute-start | bytes 786440 | tf_op jit(solution)/shard_map/ppermute | solution.py:607
  13.5 17.6 %collective-permute-start.5 = (f32[2,8,16,128]{3,2,1,0:T(8,128)S(1)}, f32[2,8,16,128]{3,2,1,0:T(8,128)S(1)}, u32[]{:S(2)}, u32[]{:S(2)}) collective-permute-start(f32[2,8,16,128]{3,2,1,0:T(8,128)S(1)} %get-tuple-element.106), channel_id=1, source_target_pairs={{0,6},{2,0},{4,2},{6,4},{1,7},{3,1},{5,3},{7,5},{8,14},{10,8},{12,... | collective-permute-start | bytes 393224 | tf_op jit(solution)/shard_map/ppermute | solution.py:607
  13.6 17.5 %collective-permute-start.4 = (f32[2,8,16,128]{3,2,1,0:T(8,128)S(1)}, f32[2,8,16,128]{3,2,1,0:T(8,128)S(1)}, u32[]{:S(2)}, u32[]{:S(2)}) collective-permute-start(f32[2,8,16,128]{3,2,1,0:T(8,128)S(1)} %get-tuple-element.107), channel_id=1, source_target_pairs={{0,2},{2,4},{4,6},{6,0},{1,3},{3,5},{5,7},{7,1},{8,10},{10,12},{12... | collective-permute-start | bytes 393224 | tf_op jit(solution)/shard_map/ppermute | solution.py:607
  32.0 13.9 %collective-permute-start.7 = (f32[2,4,128,128]{3,2,1,0:T(8,128)S(1)}, f32[2,4,128,128]{3,2,1,0:T(8,128)S(1)}, u32[]{:S(2)}, u32[]{:S(2)}) collective-permute-start(f32[2,4,128,128]{3,2,1,0:T(8,128)S(1)} %get-tuple-element.74), channel_id=1, source_target_pairs={{0,1},{8,0},{16,8},{24,16},{25,24},{17,25},{9,17},{1,9},{2,3},{10,... | collective-permute-start | bytes 1572872 | tf_op jit(solution)/shard_map/ppermute | solution.py:612
  32.0 13.9 %collective-permute-start.6 = (f32[2,4,128,128]{3,2,1,0:T(8,128)S(1)}, f32[2,4,128,128]{3,2,1,0:T(8,128)S(1)}, u32[]{:S(2)}, u32[]{:S(2)}) collective-permute-start(f32[2,4,128,128]{3,2,1,0:T(8,128)S(1)} %get-tuple-element.73), channel_id=1, source_target_pairs={{0,8},{8,16},{16,24},{24,25},{25,17},{17,9},{9,1},{1,0},{2,10},{10... | collective-permute-start | bytes 1572872 | tf_op jit(solution)/shard_map/ppermute | solution.py:612
  46.8 7.0 %collective-permute-start.11 = (f32[2,4,4,16,128]{4,3,2,1,0:T(8,128)}, f32[2,4,4,16,128]{4,3,2,1,0:T(8,128)S(1)}, u32[]{:S(2)}, u32[]{:S(2)}) collective-permute-start(f32[2,4,4,16,128]{4,3,2,1,0:T(8,128)} %get-tuple-element.82), channel_id=1, source_target_pairs={{0,2},{2,4},{4,6},{6,0},{1,3},{3,5},{5,7},{7,1},{8,10},{10,12},{12... | collective-permute-start | bytes 786440 | tf_op jit(solution)/shard_map/ppermute | solution.py:607
  46.8 7.9 %collective-permute-start.12 = (f32[2,4,4,16,128]{4,3,2,1,0:T(8,128)}, f32[2,4,4,16,128]{4,3,2,1,0:T(8,128)}, u32[]{:S(2)}, u32[]{:S(2)}) collective-permute-start(f32[2,4,4,16,128]{4,3,2,1,0:T(8,128)} %get-tuple-element.83), channel_id=1, source_target_pairs={{0,6},{2,0},{4,2},{6,4},{1,7},{3,1},{5,3},{7,5},{8,14},{10,8},{12,... | collective-permute-start | bytes 786440 | tf_op jit(solution)/shard_map/ppermute | solution.py:607
  48.5 35.6 %collective-permute-start.8 = (f32[4,160,128]{2,1,0:T(8,128)}, f32[4,160,128]{2,1,0:T(8,128)}, u32[]{:S(2)}, u32[]{:S(2)}) collective-permute-start(f32[4,160,128]{2,1,0:T(8,128)} %get-tuple-element.77), channel_id=1, source_target_pairs={{0,8},{8,16},{16,24},{24,0},{1,9},{9,17},{17,25},{25,1},{2,10},{10... | collective-permute-start | bytes 983048 | tf_op jit(solution)/shard_map/ppermute | solution.py:607
  50.2 34.5 %collective-permute-start.9 = (f32[4,160,128]{2,1,0:T(8,128)}, f32[4,160,128]{2,1,0:T(8,128)}, u32[]{:S(2)}, u32[]{:S(2)}) collective-permute-start(f32[4,160,128]{2,1,0:T(8,128)} %get-tuple-element.78), channel_id=1, source_target_pairs={{0,16},{8,24},{16,0},{24,8},{1,17},{9,25},{17,1},{25,9},{2,18},{10... | collective-permute-start | bytes 983048 | tf_op jit(solution)/shard_map/ppermute | solution.py:607
  51.4 33.4 %collective-permute-start.10 = (f32[4,160,128]{2,1,0:T(8,128)}, f32[4,160,128]{2,1,0:T(8,128)}, u32[]{:S(2)}, u32[]{:S(2)}) collective-permute-start(f32[4,160,128]{2,1,0:T(8,128)} %get-tuple-element.79), channel_id=1, source_target_pairs={{0,24},{8,0},{16,8},{24,16},{1,25},{9,1},{17,9},{25,17},{2,26},{10... | collective-permute-start | bytes 983048 | tf_op jit(solution)/shard_map/ppermute | solution.py:607
  52.0 32.8 %copy-start.5 = (f32[4,160,128]{2,1,0:T(8,128)S(1)}, f32[4,160,128]{2,1,0:T(8,128)}, u32[]{:S(2)}) copy-start(f32[4,160,128]{2,1,0:T(8,128)} %copy-done.4) | copy-start | bytes 983044
  81.2 32.2 %collective-permute-start.16 = (f32[544,128]{1,0:T(8,128)S(1)}, f32[544,128]{1,0:T(8,128)S(1)}, u32[]{:S(2)}, u32[]{:S(2)}) collective-permute-start(f32[544,128]{1,0:T(8,128)S(1)} %get-tuple-element.94), channel_id=1, source_target_pairs={{0,8},{8,16},{16,24},{24,0},{1,9},{9,17},{17,25},{25,1},{2,10},{10... | collective-permute-start | bytes 835592 | tf_op jit(solution)/shard_map/ppermute | solution.py:607
  83.0 30.5 %collective-permute-start.17 = (f32[544,128]{1,0:T(8,128)S(1)}, f32[544,128]{1,0:T(8,128)S(1)}, u32[]{:S(2)}, u32[]{:S(2)}) collective-permute-start(f32[544,128]{1,0:T(8,128)S(1)} %get-tuple-element.95), channel_id=1, source_target_pairs={{0,16},{8,24},{16,0},{24,8},{1,17},{9,25},{17,1},{25,9},{2,18},{10... | collective-permute-start | bytes 835592 | tf_op jit(solution)/shard_map/ppermute | solution.py:607
  84.1 29.4 %collective-permute-start.18 = (f32[544,128]{1,0:T(8,128)S(1)}, f32[544,128]{1,0:T(8,128)S(1)}, u32[]{:S(2)}, u32[]{:S(2)}) collective-permute-start(f32[544,128]{1,0:T(8,128)S(1)} %get-tuple-element.96), channel_id=1, source_target_pairs={{0,24},{8,0},{16,8},{24,16},{1,25},{9,1},{17,9},{25,17},{2,26},{10... | collective-permute-start | bytes 835592 | tf_op jit(solution)/shard_map/ppermute | solution.py:607
  84.7 28.7 %copy-start.1 = (f32[8,128,128]{2,1,0:T(8,128)S(1)}, f32[8,128,128]{2,1,0:T(8,128)}, u32[]{:S(2)}) copy-start(f32[8,128,128]{2,1,0:T(8,128)} %cond.1) | copy-start | bytes 1572868
  84.8 28.7 %copy-start.3 = (f32[8,128,128]{2,1,0:T(8,128)S(1)}, f32[8,128,128]{2,1,0:T(8,128)}, u32[]{:S(2)}) copy-start(f32[8,128,128]{2,1,0:T(8,128)} %cot.1) | copy-start | bytes 1572868
  108.4 11.2 %collective-permute-start.13 = (f32[400,128]{1,0:T(8,128)S(1)}, f32[400,128]{1,0:T(8,128)S(1)}, u32[]{:S(2)}, u32[]{:S(2)}) collective-permute-start(f32[400,128]{1,0:T(8,128)S(1)} %get-tuple-element.90), channel_id=1, source_target_pairs={{0,8},{8,16},{16,24},{24,0},{1,9},{9,17},{17,25},{25,1},{2,10},{10... | collective-permute-start | bytes 614408 | tf_op jit(solution)/shard_map/ppermute | solution.py:607
  109.8 17.9 %collective-permute-start.14 = (f32[400,128]{1,0:T(8,128)S(1)}, f32[400,128]{1,0:T(8,128)S(1)}, u32[]{:S(2)}, u32[]{:S(2)}) collective-permute-start(f32[400,128]{1,0:T(8,128)S(1)} %get-tuple-element.91), channel_id=1, source_target_pairs={{0,16},{8,24},{16,0},{24,8},{1,17},{9,25},{17,1},{25,9},{2,18},{10... | collective-permute-start | bytes 614408 | tf_op jit(solution)/shard_map/ppermute | solution.py:607
  113.4 17.6 %collective-permute-start.15 = (f32[400,128]{1,0:T(8,128)S(1)}, f32[400,128]{1,0:T(8,128)S(1)}, u32[]{:S(2)}, u32[]{:S(2)}) collective-permute-start(f32[400,128]{1,0:T(8,128)S(1)} %get-tuple-element.92), channel_id=1, source_target_pairs={{0,24},{8,0},{16,8},{24,16},{1,25},{9,1},{17,9},{25,17},{2,26},{10... | collective-permute-start | bytes 614408 | tf_op jit(solution)/shard_map/ppermute | solution.py:607
  (1 other events, 0.7 us)

commit v11 on v10

--- a/solution.py
+++ b/solution.py
@@ -91,11 +91,12 @@
 TOP = 8 + HALO
 ROWS = BY + 2 * TOP
 EXTENDED = BY + 2 * HALO
-GROUP = BY + 8
-SIDES = 2 * GROUP
-FIELD = SIDES + BY
-KAP = FIELD + BY
-BOTH = KAP + 16
+TILES = 2 * BY
+SIDES = TILES + 8
+ENDS = SIDES + BY // 2
+FIELD = ENDS + 16
+OWN = FIELD - TILES
+BOTH = FIELD + OWN
 TILE = 8
 CHUNK = 32
 WIDE = 16
@@ -202,7 +203,7 @@
 
 
 def edge_kernel(places, *refs):
-    msgs, (to_left, to_right) = refs[:G], refs[G:]
+    msgs, (to_left, to_right, head, tail) = refs[:G], refs[G:]
     lane = lax.broadcasted_iota(jnp.int32, (BY, LANES), 1)
     low = lax.rem(lane, 16) < 8
     for n in range(2):
@@ -210,16 +211,19 @@
             first, second = msgs[d][n, 0], msgs[d][n, 1]
             to_left[n, places[0, d]] = jnp.where(low, first, roll(second, 8))
             to_right[n, places[1, d]] = jnp.where(low, roll(second, -8), first)
-
-
-def rows_kernel(*refs):
-    msgs, sides, (head, tail) = refs[:G], refs[G : G + 2], refs[G + 2 :]
+            for a in range(2):
+                head[n, d, a] = msgs[d][n, a, :HALO]
+                tail[n, d, a] = msgs[d][n, a, BY - HALO :]
+
+
+def rows_kernel(from_left, from_right, above, below, head, tail, above_out, below_out):
     for n in range(2):
         for d in range(G):
             for out, rows in ((head, slice(0, HALO)), (tail, slice(BY - HALO, BY))):
-                for a in range(2):
-                    out[n, d, a] = msgs[d][n, a, rows]
-                    out[n, d, 2 + a] = sides[a][n, d, rows]
+                for a, side in enumerate((from_left, from_right)):
+                    out[n, d, a] = side[n, d, rows]
+            above_out[n, d] = above[n, d]
+            below_out[n, d] = below[n, d]
 
 
 def unpack(get_brick, get_edge, group, within, put):
@@ -253,8 +257,8 @@
 
 def solve_kernel(adjoint, strip, steps, *refs):
     if adjoint:
-        bricks, (from_left, from_right, above, below) = refs[:G], refs[G : G + 4]
-        outs, coefficients, (kap, *scratch) = refs[G + 4 : 2 * G + 4], refs[2 * G + 4 : 2 * G + 9], refs[2 * G + 9 :]
+        bricks, (from_left, from_right, above, below, above_edge, below_edge) = refs[:G], refs[G : G + 6]
+        outs, coefficients, (kap, *scratch) = refs[G + 6 : 2 * G + 6], refs[2 * G + 6 : 2 * G + 11], refs[2 * G + 11 :]
     else:
         strips_here, coefficients = refs[:G], refs[G : G + 5]
         outs, scratch = refs[G + 5 : 2 * G + 5], refs[2 * G + 5 :]
@@ -296,10 +300,10 @@
 
         group_halo, within_halo = lanes_of(HALO, strip[0])
         for n, dst in enumerate((kap, rhs)):
-            for rows, start in ((above, TOP - HALO), (below, TOP + BY)):
+            for brick, edge, start in ((above, above_edge, TOP - HALO), (below, below_edge, TOP + BY)):
                 unpack(
-                    lambda d, a: rows[n, d, a],
-                    lambda side, d: rows[n, d, 2 + side],
+                    lambda d, a: brick[n, d, a],
+                    lambda side, d: edge[n, d, side],
                     group_halo,
                     within_halo,
                     put_at(dst, start, HALO),
@@ -424,51 +428,57 @@
             [pick(group, [turned[4 * a + (q - d) % G] for q in range(G)]) for a in range(2)] for d in range(G)
         ]
 
-    def beside(whole, parts, group, within):
+    def ends_of(whole, within):
         tree = [jnp.where(within == 31, odd, even) for even, odd in whole]
         for level in range(3):
             width = 1 << level
             keep = (lax.rem(within + 1, STRIP) < width) | ((within >= 16) & (within < 16 + width))
             tree = [jnp.where(keep, tree[j], roll(tree[j + 1], width)) for j in range(0, len(tree), 2)]
-        ends = roll(tree[0], 1)
-        groups = (ends, ends, roll(parts[PLANES - 1], 96), roll(parts[0], 64))
-        return [pick(group, [groups[(q - d) % G] for q in range(G)]) for d in range(G)]
+        return jnp.where(within < 8, roll(tree[0], 1), roll(tree[0], -8))
 
     def load(field, row, rows):
         return [[field[i, e, pl.ds(row, rows)] for e in range(2)] for i in range(PLANES)]
 
-    @pl.loop(0, BY // CHUNK)
+    fields = ((xb, 0),) + (((kap, FIELD - TILES),) if adjoint else ())
+
+    @pl.loop(0, BY // 2 // CHUNK)
     def _(t):
-        row = pl.multiple_of(TOP + CHUNK * t, TILE)
         group, within = lanes_of(CHUNK, strip[0])
-
-        def to(start):
-            return pl.ds(pl.multiple_of(start + CHUNK * t, TILE), CHUNK)
-
-        for field, start in ((xb, SIDES),) + (((kap, FIELD),) if adjoint else ()):
-            whole = load(field, row, CHUNK)
-            parts, main = mains(whole, group, within)
-            sides = beside(whole, parts, group, within)
+        for field, base in fields:
+            beside = []
+            for upper_rows in range(2):
+                start = BY // 2 * upper_rows
+                parts, main = mains(load(field, pl.multiple_of(TOP + start + CHUNK * t, TILE), CHUNK), group, within)
+                if field is xb:
+                    for d in range(G):
+                        for a in range(2):
+                            outs[d][pl.ds(pl.multiple_of(BY * a + start + CHUNK * t, TILE), CHUNK)] = main[d][a]
+                beside += [roll(parts[PLANES - 1], 32 + 64 * upper_rows), roll(parts[0], 64 * upper_rows)]
+            at = pl.ds(pl.multiple_of(base + SIDES + CHUNK * t, TILE), CHUNK)
             for d in range(G):
-                outs[d][to(start)] = sides[d]
-                if field is xb:
-                    for a in range(2):
-                        outs[d][to(GROUP * a)] = main[d][a]
+                outs[d][at] = pick(group, [beside[(q - d) % G] for q in range(G)])
 
     sub = lax.broadcasted_iota(jnp.int32, (TILE, LANES), 0)
     group, within = lanes_of(TILE, strip[0])
-    for field in (xb, kap) if adjoint else (xb,):
+    group_run, within_run = lanes_of(16, strip[0])
+    half_run = within_run // 16
+    for field, base in fields:
         over = mains(load(field, TOP - TILE, TILE), group, within)[1]
         under = mains(load(field, TOP + BY, TILE), group, within)[1]
         for d in range(G):
-            for a in range(2):
-                to = GROUP * a + BY if field is xb else KAP + TILE * a
-                outs[d][to : to + TILE] = jnp.where(
-                    sub == 0, pltpu.roll(over[d][a], 1, 0), pltpu.roll(under[d][a], 1, 0)
-                )
-
-
-def collect(strips, msgs, padded, ends, base, own):
+            rows = [pltpu.roll(v, by, 0) for a, by in ((0, 1), (1, 3)) for v in (over[d][a], under[d][a])]
+            tile = rows[3]
+            for j in range(3):
+                tile = jnp.where(sub == j, rows[j], tile)
+            outs[d][base + TILES : base + TILES + TILE] = tile
+        runs = [roll(ends_of(load(field, TOP + 16 * run, 16), within_run), 16 * run) for run in range(8)]
+        evens = [pick(group_run, [runs[2 * ((q - d) % G)] for q in range(G)]) for d in range(G)]
+        odds = [pick(group_run, [runs[2 * ((q - d) % G) + 1] for q in range(G)]) for d in range(G)]
+        for d in range(G):
+            outs[d][base + ENDS : base + ENDS + 16] = jnp.where(half_run == 0, evens[d], odds[d])
+
+
+def collect(strips, msgs, padded, ends, own):
     order = parity_order(True)
 
     def owners(rows):
@@ -483,41 +493,45 @@
     def bricks(row, rows):
         return [roll(msgs[d][pl.ds(row, rows)], -32 * d) for d in range(G)]
 
-    sides_at, tiles_at = (SIDES, (BY, GROUP + BY)) if own is None else (FIELD, (KAP, KAP + TILE))
+    base = 0 if own is None else FIELD - TILES
 
     @pl.loop(0, BY // CHUNK)
     def _(t):
         to = pl.ds(pl.multiple_of(TILE + CHUNK * t, TILE), CHUNK)
-        owner = owners(CHUNK)
-        whole, places = [], []
-        if own is None:
-            for a in range(2):
-                parts = bricks(pl.multiple_of(GROUP * a + CHUNK * t, TILE), CHUNK)
-                whole += [choose(owner, parts, b) for b in range(4)]
-                places += [1 + 4 * a + b for b in range(4)]
-        else:
+        if own is not None:
             for c in range(BX):
                 padded[1 + c, to] = own[c, pl.ds(pl.multiple_of(CHUNK * t, CHUNK), CHUNK)]
-        parts = bricks(pl.multiple_of(sides_at + CHUNK * t, TILE), CHUNK)
-        for side, end in enumerate((0, G - 1)):
-            val = parts[0]
-            for d in range(1, G):
-                val = jnp.where(strips[d] == end, parts[d], val)
-            ends[side, pl.ds(pl.multiple_of(CHUNK * t, CHUNK), CHUNK)] = val
-        whole += [choose(owner, parts, b) for b in (2, 3)]
-        places += [0, 1 + BX]
+            return
+        owner = owners(CHUNK)
+        whole = []
+        for a in range(2):
+            parts = bricks(pl.multiple_of(BY * a + CHUNK * t, TILE), CHUNK)
+            whole += [choose(owner, parts, b) for b in range(4)]
         ordered = reorder(jnp.concatenate(whole, axis=0), order)
-        for j, at in enumerate(places):
+        for c in range(BX):
+            padded[1 + c, to] = ordered[CHUNK * c : CHUNK * (c + 1)]
+
+    @pl.loop(0, BY // 2 // CHUNK)
+    def _(t):
+        owner = owners(CHUNK)
+        parts = bricks(pl.multiple_of(base + SIDES + CHUNK * t, TILE), CHUNK)
+        ordered = reorder(jnp.concatenate([choose(owner, parts, b) for b in range(4)], axis=0), order)
+        for j, (at, start) in enumerate(((0, 0), (1 + BX, 0), (0, BY // 2), (1 + BX, BY // 2))):
+            to = pl.ds(pl.multiple_of(TILE + start + CHUNK * t, TILE), CHUNK)
             padded[at, to] = ordered[CHUNK * j : CHUNK * (j + 1)]
 
+    parts = bricks(base + ENDS, 16)
+    for side, end in enumerate((0, G - 1)):
+        val = parts[0]
+        for d in range(1, G):
+            val = jnp.where(strips[d] == end, parts[d], val)
+        ends[side] = val
+
     owner = owners(TILE)
-    whole = []
-    for a in range(2):
-        parts = bricks(tiles_at[a], TILE)
-        whole += [choose(owner, parts, b) for b in range(4)]
-    ordered = reorder(jnp.concatenate(whole, axis=0), order)
+    parts = bricks(base + TILES, TILE)
+    ordered = reorder(jnp.concatenate([choose(owner, parts, b) for b in range(4)], axis=0), order)
     for c in range(BX):
-        val = pltpu.roll(ordered[TILE * c : TILE * (c + 1)], 7, 0)
+        val = pltpu.roll(ordered[TILE * (c % 4) : TILE * (c % 4 + 1)], 5 if c >= 4 else 7, 0)
         padded[1 + c, 0:TILE] = val
         padded[1 + c, TILE + BY : 2 * TILE + BY] = val
 
@@ -534,16 +548,17 @@
 
 def along(cell, ends, c, t):
     lane = lax.broadcasted_iota(jnp.int32, (WIDE, LANES), 1)
-    low, high = (ends[side, pl.ds(pl.multiple_of(WIDE * t, WIDE), WIDE)] for side in range(2))
+    low = pltpu.roll(ends[0], lax.rem(LANES - 16 * t - c + LANES, LANES), 1)
+    high = pltpu.roll(ends[1], lax.rem(23 - 16 * t - c + 2 * LANES, LANES), 1)
     return [
-        jnp.where(lane == 0, roll(low, -c), roll(cell, 1)),
-        jnp.where(lane == LANES - 1, roll(high, 14 - c), roll(cell, -1)),
+        jnp.where(lane == 0, low, roll(cell, 1)),
+        jnp.where(lane == LANES - 1, high, roll(cell, -1)),
     ]
 
 
 def adjoint_kernel(strips, m0, m1, m2, m3, cond, cot, adjoint, residual, padded, kap, faces, differences, ends, kends):
-    collect(strips, (m0, m1, m2, m3), padded, ends, 0, None)
-    collect(strips, (m0, m1, m2, m3), kap, kends, 0, cond)
+    collect(strips, (m0, m1, m2, m3), padded, ends, None)
+    collect(strips, (m0, m1, m2, m3), kap, kends, cond)
 
     @pl.loop(0, BY // WIDE)
     def _(t):
@@ -564,7 +579,7 @@
 
 
 def state_kernel(strips, m0, m1, m2, m3, previous, adj, kap, faces, differences, adj_residual, grad, state, residuals, padded, ends):
-    collect(strips, (m0, m1, m2, m3), padded, ends, 0, None)
+    collect(strips, (m0, m1, m2, m3), padded, ends, None)
 
     @pl.loop(0, BY // WIDE)
     def _(t):
@@ -637,8 +652,8 @@
     below_rows = shifted(both[:, :, :HALO], "gy", -1)
     parts, above_rows, below_rows = lax.optimization_barrier((parts, above_rows, below_rows))
     edge = (2, G, BY, LANES)
-    rim = (2, G, 4, HALO, LANES)
-    to_left, to_right = call(edge_kernel, [edge, edge], [places], parts)
+    rim = (2, G, 2, HALO, LANES)
+    to_left, to_right, head, tail = call(edge_kernel, [edge, edge, rim, rim], [places], parts)
     to_left, below_rows = lax.optimization_barrier((to_left, below_rows))
     *messages, steps_here = call(
         pack_previous_kernel,
@@ -647,9 +662,10 @@
         [both, above_rows, below_rows],
     )
     from_left, from_right = around(to_right, 1), around(to_left, -1)
+    above, below = shifted(tail, "gy", 1), shifted(head, "gy", -1)
     from_left, from_right, own = lax.optimization_barrier((from_left, from_right, messages[0]))
-    head, tail = call(rows_kernel, [rim, rim], [], [*parts, from_left, from_right])
-    halos = [from_left, from_right, shifted(tail, "gy", 1), shifted(head, "gy", -1)]
+    head, tail, above, below = call(rows_kernel, [rim] * 4, [], [from_left, from_right, above, below])
+    halos = [from_left, from_right, above, below, shifted(tail, "gy", 1), shifted(head, "gy", -1)]
 
     second = [own] + [shifted(messages[d], "gx", d) for d in range(1, G)]
 
@@ -685,7 +701,7 @@
 
     out = (BX, BY, LANES)
     padded = (BX + 2, BY + 16, LANES)
-    ends = (2, BY, LANES)
+    ends = (2, 16, LANES)
     here = strip_of(behind)
     adjoint, adj_residual, adj, kap, faces, differences = call(
         adjoint_kernel,

time: 136 us -> 138 us (1.015)
  waiting for transfers between devices: 39.5 us -> 41.5 us
  starting transfers between devices: 22.5 us -> 20.9 us
    ppermute x2, waiting for transfers between devices: 6.13 us -> 11.1 us  [around(): lax.ppermute(x, ('gx', 'pa'), [(at, order[(i + by) % len(order)]) for i,...]
    ppermute x17 -> x19, waiting for transfers between devices: 33.3 us -> 30.4 us  [shifted(): return lax.ppermute(x, axis, [(i, (i + by) % count) for i in range(count)])]
    ppermute x17 -> x19, starting transfers between devices: 20.5 us -> 18.8 us  [shifted(): return lax.ppermute(x, axis, [(i, (i + by) % count) for i in range(count)])]
  transfers between devices with their start and end apart: 19 -> 21, of which waited for: 10 -> 10; matrix products, arithmetic and copies ran while one was open for 1% -> 1% of each run, Pallas kernels for 45% -> 45%
where the time goes in v11:
time: 138 us; the launch traced here: 137 us
  Pallas kernels  68.9 us (50%)
  waiting for transfers between devices  41.5 us (30%)
  starting transfers between devices  20.9 us (15%)
  local copies, waits for them, and re-layouts  2.84 us (2%)
  between operations  1.46 us (1%)
    pallas_call x8, Pallas kernels, call(): pl.pallas_call(kernel, out_shape=[jax.ShapeDtypeStruct(shape, F32) for sh...  68.9 us
    ppermute x19, waiting for transfers between devices, shifted(): return lax.ppermute(x, axis, [(i, (i + by) % count) for i in range(count)])  30.4 us
    ppermute x19, starting transfers between devices, shifted(): return lax.ppermute(x, axis, [(i, (i + by) % count) for i in range(count)])  18.8 us
    ppermute x2, waiting for transfers between devices, around(): lax.ppermute(x, ('gx', 'pa'), [(at, order[(i + by) % len(order)]) for i,...  11.1 us
    unnamed x12, local copies, waits for them, and re-layouts  2.82 us
  transfers between devices with their start and end apart: 21, of which 10 were waited for; matrix products, arithmetic and copies ran while one was open for 1% of the time, Pallas kernels for 45%

profile of v11, /device:TPU:8, one launch (start us, length us, event | category | flops | bytes accessed | tf_op | source)
XLA Modules:
  0.0 136.8 jit_solution(5537300400182567359)
XLA Ops:
  4.0 1.6 %collective-permute-start = (bf16[8,128,128]{2,1,0:T(8,128)(2,1)}, bf16[8,128,128]{2,1,0:T(8,128)(2,1)S(1)}, u32[]{:S(2)}, u32[]{:S(2)}) collective-permute-start(bf16[8,128,128]{2,1,0:T(8,128)(2,1)} %param.6), channel_id=1, source_target_pairs={{0,1},{1,0},{2,3},{3,2},{4,5},{5,4},{6,7},{7,6},{8,9},{9,8},{10,11... | collective-permute-start | bytes 786440 | tf_op jit(solution)/shard_map/ppermute | solution.py:622
  5.6 1.6 %collective-permute-start.1 = (f32[2,2,128,128]{3,2,1,0:T(8,128)S(1)}, f32[2,2,128,128]{3,2,1,0:T(8,128)S(1)}, u32[]{:S(2)}, u32[]{:S(2)}) collective-permute-start(f32[2,2,128,128]{3,2,1,0:T(8,128)S(1)} %get-tuple-element.65), channel_id=1, source_target_pairs={{0,8},{8,16},{16,24},{24,0},{1,9},{9,17},{17,25},{25,1},{2,10},{10... | collective-permute-start | bytes 786440 | tf_op jit(solution)/shard_map/ppermute | solution.py:622
  7.1 1.2 collective-permute-start.2
  8.4 1.8 %collective-permute-start.3 = (f32[2,2,128,128]{3,2,1,0:T(8,128)S(1)}, f32[2,2,128,128]{3,2,1,0:T(8,128)S(1)}, u32[]{:S(2)}, u32[]{:S(2)}) collective-permute-start(f32[2,2,128,128]{3,2,1,0:T(8,128)S(1)} %get-tuple-element.67), channel_id=1, source_target_pairs={{0,24},{8,0},{16,8},{24,16},{1,25},{9,1},{17,9},{25,17},{2,26},{10... | collective-permute-start | bytes 786440 | tf_op jit(solution)/shard_map/ppermute | solution.py:622
  10.2 2.1 %collective-permute-done = bf16[8,128,128]{2,1,0:T(8,128)(2,1)S(1)} collective-permute-done((bf16[8,128,128]{2,1,0:T(8,128)(2,1)}, bf16[8,128,128]{2,1,0:T(8,128)(2,1)S(1)}, u32[]{:S(2)}, u32[]{:S(2)}) %collective-permute-start) | collective-permute-done | bytes 262176 | tf_op jit(solution)/shard_map/ppermute | solution.py:622
  14.1 11.0 %collective-permute-done.1.refs_1_ = f32[2,2,128,128]{3,2,1,0:T(8,128)S(1)} collective-permute-done((f32[2,2,128,128]{3,2,1,0:T(8,128)S(1)}, f32[2,2,128,128]{3,2,1,0:T(8,128)S(1)}, u32[]{:S(2)}, u32[]{:S(2)}) %collective-permute-start.1) | collective-permute-done | bytes 262176 | tf_op jit(solution)/shard_map/ppermute | solution.py:622
  25.1 4.2 %collective-permute-done.2.refs_2_ = f32[2,2,128,128]{3,2,1,0:T(8,128)S(1)} collective-permute-done((f32[2,2,128,128]{3,2,1,0:T(8,128)S(1)}, f32[2,2,128,128]{3,2,1,0:T(8,128)S(1)}, u32[]{:S(2)}, u32[]{:S(2)}) %collective-permute-start.2) | collective-permute-done | bytes 262176 | tf_op jit(solution)/shard_map/ppermute | solution.py:622
  29.3 1.8 %collective-permute-done.3.refs_3_ = f32[2,2,128,128]{3,2,1,0:T(8,128)S(1)} collective-permute-done((f32[2,2,128,128]{3,2,1,0:T(8,128)S(1)}, f32[2,2,128,128]{3,2,1,0:T(8,128)S(1)}, u32[]{:S(2)}, u32[]{:S(2)}) %collective-permute-start.3) | collective-permute-done | bytes 262176 | tf_op jit(solution)/shard_map/ppermute | solution.py:622
  32.0 2.0 %collective-permute-start.6 = (f32[2,4,128,128]{3,2,1,0:T(8,128)S(1)}, f32[2,4,128,128]{3,2,1,0:T(8,128)S(1)}, u32[]{:S(2)}, u32[]{:S(2)}) collective-permute-start(f32[2,4,128,128]{3,2,1,0:T(8,128)S(1)} %get-tuple-element.77), channel_id=1, source_target_pairs={{0,8},{8,16},{16,24},{24,25},{25,17},{17,9},{9,1},{1,0},{2,10},{10... | collective-permute-start | bytes 1572872 | tf_op jit(solution)/shard_map/ppermute | solution.py:627
  34.1 1.7 %collective-permute-start.12 = (f32[2,4,2,16,128]{4,3,2,1,0:T(8,128)S(1)}, f32[2,4,2,16,128]{4,3,2,1,0:T(8,128)S(1)}, u32[]{:S(2)}, u32[]{:S(2)}) collective-permute-start(f32[2,4,2,16,128]{4,3,2,1,0:T(8,128)S(1)} %get-tuple-element.87), channel_id=1, source_target_pairs={{0,6},{2,0},{4,2},{6,4},{1,7},{3,1},{5,3},{7,5},{8,14},{10,8},{12,... | collective-permute-start | bytes 393224 | tf_op jit(solution)/shard_map/ppermute | solution.py:622
  36.4 4.4 %shard_map.86 = (f32[4,160,128]{2,1,0:T(8,128)S(1)}, f32[4,160,128]{2,1,0:T(8,128)}, f32[4,160,128]{2,1,0:T(8,128)}, f32[4,160,128]{2,1,0:T(8,128)}, f32[16,2,8,128]{3,2,1,0:T(8,128)S(1)}) custom-call(s32[4]{0:T(128)S(1)} %broadcast_select_fusion.strips, f32[1]{0:T(128)S(6)} %copy.9.upper, f32[2,8,128,128]{3,2,1,0:T(8,128)S(1)} %convert_multiply_fusion.both.previous, ...), custom_call_target="tpu_custom_call" | custom-call | bytes 6000000 | tf_op jit(solution)/shard_map/pallas_call | solution.py:609
  41.8 11.1 %collective-permute-done.7.from_right.refs_5_ = f32[2,4,128,128]{3,2,1,0:T(8,128)S(1)} collective-permute-done((f32[2,4,128,128]{3,2,1,0:T(8,128)S(1)}, f32[2,4,128,128]{3,2,1,0:T(8,128)S(1)}, u32[]{:S(2)}, u32[]{:S(2)}) %collective-permute-start.7) | collective-permute-done | bytes 524320 | tf_op jit(solution)/shard_map/ppermute | solution.py:627
  53.6 1.7 %collective-permute-start.14 = (f32[2,4,2,16,128]{4,3,2,1,0:T(8,128)}, f32[2,4,2,16,128]{4,3,2,1,0:T(8,128)}, u32[]{:S(2)}, u32[]{:S(2)}) collective-permute-start(f32[2,4,2,16,128]{4,3,2,1,0:T(8,128)} %get-tuple-element.91), channel_id=1, source_target_pairs={{0,6},{2,0},{4,2},{6,4},{1,7},{3,1},{5,3},{7,5},{8,14},{10,8},{12,... | collective-permute-start | bytes 393224 | tf_op jit(solution)/shard_map/ppermute | solution.py:622
  56.4 2.0 %collective-permute-done.13.refs_8_ = f32[2,4,2,16,128]{4,3,2,1,0:T(8,128)} collective-permute-done((f32[2,4,2,16,128]{4,3,2,1,0:T(8,128)}, f32[2,4,2,16,128]{4,3,2,1,0:T(8,128)}, u32[]{:S(2)}, u32[]{:S(2)}) %collective-permute-start.13) | collective-permute-done | bytes 131104 | tf_op jit(solution)/shard_map/ppermute | solution.py:622
  58.8 27.0 %shard_map.88 = (f32[432,128]{1,0:T(8,128)S(1)}, f32[432,128]{1,0:T(8,128)S(1)}, f32[432,128]{1,0:T(8,128)S(1)}, f32[432,128]{1,0:T(8,128)S(1)}, f32[8,2,176,128...) custom-call(s32[1]{0:T(128)} %bitcast.strip, ...), custom_call_target="tpu_custom_call" | custom-call | bytes 75000000 | tf_op jit(solution)/shard_map/pallas_call | solution.py:609
  85.8 3.4 %collective-permute-start.19 = (f32[432,128]{1,0:T(8,128)S(1)}, f32[432,128]{1,0:T(8,128)S(1)}, u32[]{:S(2)}, u32[]{:S(2)}) collective-permute-start(f32[432,128]{1,0:T(8,128)S(1)} %get-tuple-element.103), channel_id=1, source_target_pairs={{0,16},{8,24},{16,0},{24,8},{1,17},{9,25},{17,1},{25,9},{2,18},{10... | collective-permute-start | bytes 663560 | tf_op jit(solution)/shard_map/ppermute | solution.py:622
  89.3 23.3 %shard_map.89 = (f32[344,128]{1,0:T(8,128)S(1)}, f32[344,128]{1,0:T(8,128)S(1)}, f32[344,128]{1,0:T(8,128)S(1)}, f32[344,128]{1,0:T(8,128)S(1)}) custom-call(s32[1]{0:T(128)} %bitcast.strip, f32[16,2,8,128]{3,2,1,0:T(8,128)S(1)} %get-tuple-element.76.steps, f32[4,160,128]{2,1,0:T(8,128)S(1)} %copy-done.5, f32[4,160,128]{2,1,0:T(8,128)} %collective-permute-done.8.refs_1_, ...), custom_call_target="tpu_custom_call" | custom-call | bytes 75000000 | tf_op jit(solution)/shard_map/pallas_call | solution.py:609
  112.6 2.1 %collective-permute-start.15 = (f32[344,128]{1,0:T(8,128)S(1)}, f32[344,128]{1,0:T(8,128)S(1)}, u32[]{:S(2)}, u32[]{:S(2)}) collective-permute-start(f32[344,128]{1,0:T(8,128)S(1)} %get-tuple-element.98), channel_id=1, source_target_pairs={{0,8},{8,16},{16,24},{24,0},{1,9},{9,17},{17,25},{25,1},{2,10},{10... | collective-permute-start | bytes 528392 | tf_op jit(solution)/shard_map/ppermute | solution.py:622
  114.6 1.8 %collective-permute-start.16 = (f32[344,128]{1,0:T(8,128)S(1)}, f32[344,128]{1,0:T(8,128)S(1)}, u32[]{:S(2)}, u32[]{:S(2)}) collective-permute-start(f32[344,128]{1,0:T(8,128)S(1)} %get-tuple-element.99), channel_id=1, source_target_pairs={{0,16},{8,24},{16,0},{24,8},{1,17},{9,25},{17,1},{25,9},{2,18},{10... | collective-permute-start | bytes 528392 | tf_op jit(solution)/shard_map/ppermute | solution.py:622
  116.5 6.1 %shard_map.90 = (f32[8,128,128]{2,1,0:T(8,128)}, f32[8,128,128]{2,1,0:T(8,128)S(1)}, f32[10,144,128]{2,1,0:T(8,128)S(1)}, f32[10,144,128]{2,1,0:T(8,128)S(1)}, f...) custom-call(s32[4]{0:T(128)S(1)} %broadcast_select_fusion.1.strips, f32[432,128]{1,0:T(8,128)S(1)} %get-tuple-element.101.m0, ...), custom_call_target="tpu_custom_call" | custom-call | bytes 6000000 | tf_op jit(solution)/shard_map/pallas_call | solution.py:609
  122.6 3.7 %collective-permute-done.15.m1 = f32[344,128]{1,0:T(8,128)S(1)} collective-permute-done((f32[344,128]{1,0:T(8,128)S(1)}, f32[344,128]{1,0:T(8,128)S(1)}, u32[]{:S(2)}, u32[]{:S(2)}) %collective-permute-start.15) | collective-permute-done | bytes 176160 | tf_op jit(solution)/shard_map/ppermute | solution.py:622
  126.3 2.6 %collective-permute-done.16.m2 = f32[344,128]{1,0:T(8,128)S(1)} collective-permute-done((f32[344,128]{1,0:T(8,128)S(1)}, f32[344,128]{1,0:T(8,128)S(1)}, u32[]{:S(2)}, u32[]{:S(2)}) %collective-permute-start.16) | collective-permute-done | bytes 176160 | tf_op jit(solution)/shard_map/ppermute | solution.py:622
  128.9 2.6 %collective-permute-done.17.m3 = f32[344,128]{1,0:T(8,128)S(1)} collective-permute-done((f32[344,128]{1,0:T(8,128)S(1)}, f32[344,128]{1,0:T(8,128)S(1)}, u32[]{:S(2)}, u32[]{:S(2)}) %collective-permute-start.17) | collective-permute-done | bytes 176160 | tf_op jit(solution)/shard_map/ppermute | solution.py:622
  131.5 5.3 %shard_map.91 = (f32[8,128,128]{2,1,0:T(8,128)}, f32[8,128,128]{2,1,0:T(8,128)}, f32[2,8,128,128]{3,2,1,0:T(8,128)}) custom-call(s32[4]{0:T(128)S(1)} %broadcast_select_fusion.1.strips, f32[344,128]{1,0:T(8,128)S(1)} %get-tuple-element.97.m0, f32[344,128]{1,0:T(8,128)S(1)} %collective-permute-done.15.m1, f32[344,128]{1,0:T(8,128)S(1)} %collective-permute-done.16.m2, ...), custom_call_target="tpu_custom_call" | custom-call | bytes 6000000 | tf_op jit(solution)/shard_map/pallas_call | solution.py:609
  (44 shorter events, 9.2 us)
Async XLA Ops:
  4.0 8.3 %collective-permute-start = (bf16[8,128,128]{2,1,0:T(8,128)(2,1)}, bf16[8,128,128]{2,1,0:T(8,128)(2,1)S(1)}, u32[]{:S(2)}, u32[]{:S(2)}) collective-permute-start(bf16[8,128,128]{2,1,0:T(8,128)(2,1)} %param.6), channel_id=1, source_target_pairs={{0,1},{1,0},{2,3},{3,2},{4,5},{5,4},{6,7},{7,6},{8,9},{9,8},{10,11... | collective-permute-start | bytes 786440 | tf_op jit(solution)/shard_map/ppermute | solution.py:622
  5.6 19.6 %collective-permute-start.1 = (f32[2,2,128,128]{3,2,1,0:T(8,128)S(1)}, f32[2,2,128,128]{3,2,1,0:T(8,128)S(1)}, u32[]{:S(2)}, u32[]{:S(2)}) collective-permute-start(f32[2,2,128,128]{3,2,1,0:T(8,128)S(1)} %get-tuple-element.65), channel_id=1, source_target_pairs={{0,8},{8,16},{16,24},{24,0},{1,9},{9,17},{17,25},{25,1},{2,10},{10... | collective-permute-start | bytes 786440 | tf_op jit(solution)/shard_map/ppermute | solution.py:622
  7.1 22.1 %collective-permute-start.2 = (f32[2,2,128,128]{3,2,1,0:T(8,128)S(1)}, f32[2,2,128,128]{3,2,1,0:T(8,128)S(1)}, u32[]{:S(2)}, u32[]{:S(2)}) collective-permute-start(f32[2,2,128,128]{3,2,1,0:T(8,128)S(1)} %get-tuple-element.66), channel_id=1, source_target_pairs={{0,16},{8,24},{16,0},{24,8},{1,17},{9,25},{17,1},{25,9},{2,18},{10... | collective-permute-start | bytes 786440 | tf_op jit(solution)/shard_map/ppermute | solution.py:622
  8.4 22.7 %collective-permute-start.3 = (f32[2,2,128,128]{3,2,1,0:T(8,128)S(1)}, f32[2,2,128,128]{3,2,1,0:T(8,128)S(1)}, u32[]{:S(2)}, u32[]{:S(2)}) collective-permute-start(f32[2,2,128,128]{3,2,1,0:T(8,128)S(1)} %get-tuple-element.67), channel_id=1, source_target_pairs={{0,24},{8,0},{16,8},{24,16},{1,25},{9,1},{17,9},{25,17},{2,26},{10... | collective-permute-start | bytes 786440 | tf_op jit(solution)/shard_map/ppermute | solution.py:622
  13.5 17.6 %collective-permute-start.5 = (f32[2,8,16,128]{3,2,1,0:T(8,128)S(1)}, f32[2,8,16,128]{3,2,1,0:T(8,128)S(1)}, u32[]{:S(2)}, u32[]{:S(2)}) collective-permute-start(f32[2,8,16,128]{3,2,1,0:T(8,128)S(1)} %get-tuple-element.114), channel_id=1, source_target_pairs={{0,6},{2,0},{4,2},{6,4},{1,7},{3,1},{5,3},{7,5},{8,14},{10,8},{12,... | collective-permute-start | bytes 393224 | tf_op jit(solution)/shard_map/ppermute | solution.py:622
  13.6 17.5 %collective-permute-start.4 = (f32[2,8,16,128]{3,2,1,0:T(8,128)S(1)}, f32[2,8,16,128]{3,2,1,0:T(8,128)S(1)}, u32[]{:S(2)}, u32[]{:S(2)}) collective-permute-start(f32[2,8,16,128]{3,2,1,0:T(8,128)S(1)} %get-tuple-element.115), channel_id=1, source_target_pairs={{0,2},{2,4},{4,6},{6,0},{1,3},{3,5},{5,7},{7,1},{8,10},{10,12},{12... | collective-permute-start | bytes 393224 | tf_op jit(solution)/shard_map/ppermute | solution.py:622
  32.0 20.9 %collective-permute-start.7 = (f32[2,4,128,128]{3,2,1,0:T(8,128)S(1)}, f32[2,4,128,128]{3,2,1,0:T(8,128)S(1)}, u32[]{:S(2)}, u32[]{:S(2)}) collective-permute-start(f32[2,4,128,128]{3,2,1,0:T(8,128)S(1)} %get-tuple-element.78), channel_id=1, source_target_pairs={{0,1},{8,0},{16,8},{24,16},{25,24},{17,25},{9,17},{1,9},{2,3},{10,... | collective-permute-start | bytes 1572872 | tf_op jit(solution)/shard_map/ppermute | solution.py:627
  32.0 20.9 %collective-permute-start.6 = (f32[2,4,128,128]{3,2,1,0:T(8,128)S(1)}, f32[2,4,128,128]{3,2,1,0:T(8,128)S(1)}, u32[]{:S(2)}, u32[]{:S(2)}) collective-permute-start(f32[2,4,128,128]{3,2,1,0:T(8,128)S(1)} %get-tuple-element.77), channel_id=1, source_target_pairs={{0,8},{8,16},{16,24},{24,25},{25,17},{17,9},{9,1},{1,0},{2,10},{10... | collective-permute-start | bytes 1572872 | tf_op jit(solution)/shard_map/ppermute | solution.py:627
  34.1 18.8 %collective-permute-start.11 = (f32[2,4,2,16,128]{4,3,2,1,0:T(8,128)S(1)}, f32[2,4,2,16,128]{4,3,2,1,0:T(8,128)S(1)}, u32[]{:S(2)}, u32[]{:S(2)}) collective-permute-start(f32[2,4,2,16,128]{4,3,2,1,0:T(8,128)S(1)} %get-tuple-element.86), channel_id=1, source_target_pairs={{0,2},{2,4},{4,6},{6,0},{1,3},{3,5},{5,7},{7,1},{8,10},{10,12},{12... | collective-permute-start | bytes 393224 | tf_op jit(solution)/shard_map/ppermute | solution.py:622
  34.1 18.8 %collective-permute-start.12 = (f32[2,4,2,16,128]{4,3,2,1,0:T(8,128)S(1)}, f32[2,4,2,16,128]{4,3,2,1,0:T(8,128)S(1)}, u32[]{:S(2)}, u32[]{:S(2)}) collective-permute-start(f32[2,4,2,16,128]{4,3,2,1,0:T(8,128)S(1)} %get-tuple-element.87), channel_id=1, source_target_pairs={{0,6},{2,0},{4,2},{6,4},{1,7},{3,1},{5,3},{7,5},{8,14},{10,8},{12,... | collective-permute-start | bytes 393224 | tf_op jit(solution)/shard_map/ppermute | solution.py:622
  41.6 47.7 %collective-permute-start.8 = (f32[4,160,128]{2,1,0:T(8,128)}, f32[4,160,128]{2,1,0:T(8,128)}, u32[]{:S(2)}, u32[]{:S(2)}) collective-permute-start(f32[4,160,128]{2,1,0:T(8,128)} %get-tuple-element.81), channel_id=1, source_target_pairs={{0,8},{8,16},{16,24},{24,0},{1,9},{9,17},{17,25},{25,1},{2,10},{10... | collective-permute-start | bytes 983048 | tf_op jit(solution)/shard_map/ppermute | solution.py:622
  53.6 4.7 %collective-permute-start.13 = (f32[2,4,2,16,128]{4,3,2,1,0:T(8,128)}, f32[2,4,2,16,128]{4,3,2,1,0:T(8,128)}, u32[]{:S(2)}, u32[]{:S(2)}) collective-permute-start(f32[2,4,2,16,128]{4,3,2,1,0:T(8,128)} %get-tuple-element.90), channel_id=1, source_target_pairs={{0,2},{2,4},{4,6},{6,0},{1,3},{3,5},{5,7},{7,1},{8,10},{10,12},{12... | collective-permute-start | bytes 393224 | tf_op jit(solution)/shard_map/ppermute | solution.py:622
  53.6 5.1 %collective-permute-start.14 = (f32[2,4,2,16,128]{4,3,2,1,0:T(8,128)}, f32[2,4,2,16,128]{4,3,2,1,0:T(8,128)}, u32[]{:S(2)}, u32[]{:S(2)}) collective-permute-start(f32[2,4,2,16,128]{4,3,2,1,0:T(8,128)} %get-tuple-element.91), channel_id=1, source_target_pairs={{0,6},{2,0},{4,2},{6,4},{1,7},{3,1},{5,3},{7,5},{8,14},{10,8},{12,... | collective-permute-start | bytes 393224 | tf_op jit(solution)/shard_map/ppermute | solution.py:622
  55.4 33.9 %collective-permute-start.9 = (f32[4,160,128]{2,1,0:T(8,128)}, f32[4,160,128]{2,1,0:T(8,128)}, u32[]{:S(2)}, u32[]{:S(2)}) collective-permute-start(f32[4,160,128]{2,1,0:T(8,128)} %get-tuple-element.82), channel_id=1, source_target_pairs={{0,16},{8,24},{16,0},{24,8},{1,17},{9,25},{17,1},{25,9},{2,18},{10... | collective-permute-start | bytes 983048 | tf_op jit(solution)/shard_map/ppermute | solution.py:622
  55.4 33.9 %collective-permute-start.10 = (f32[4,160,128]{2,1,0:T(8,128)}, f32[4,160,128]{2,1,0:T(8,128)}, u32[]{:S(2)}, u32[]{:S(2)}) collective-permute-start(f32[4,160,128]{2,1,0:T(8,128)} %get-tuple-element.83), channel_id=1, source_target_pairs={{0,24},{8,0},{16,8},{24,16},{1,25},{9,1},{17,9},{25,17},{2,26},{10... | collective-permute-start | bytes 983048 | tf_op jit(solution)/shard_map/ppermute | solution.py:622
  56.4 32.9 %copy-start.5 = (f32[4,160,128]{2,1,0:T(8,128)S(1)}, f32[4,160,128]{2,1,0:T(8,128)}, u32[]{:S(2)}) copy-start(f32[4,160,128]{2,1,0:T(8,128)} %copy-done.4) | copy-start | bytes 983044
  85.8 30.7 %collective-permute-start.18 = (f32[432,128]{1,0:T(8,128)S(1)}, f32[432,128]{1,0:T(8,128)S(1)}, u32[]{:S(2)}, u32[]{:S(2)}) collective-permute-start(f32[432,128]{1,0:T(8,128)S(1)} %get-tuple-element.102), channel_id=1, source_target_pairs={{0,8},{8,16},{16,24},{24,0},{1,9},{9,17},{17,25},{25,1},{2,10},{10... | collective-permute-start | bytes 663560 | tf_op jit(solution)/shard_map/ppermute | solution.py:622
  85.8 30.6 %collective-permute-start.19 = (f32[432,128]{1,0:T(8,128)S(1)}, f32[432,128]{1,0:T(8,128)S(1)}, u32[]{:S(2)}, u32[]{:S(2)}) collective-permute-start(f32[432,128]{1,0:T(8,128)S(1)} %get-tuple-element.103), channel_id=1, source_target_pairs={{0,16},{8,24},{16,0},{24,8},{1,17},{9,25},{17,1},{25,9},{2,18},{10... | collective-permute-start | bytes 663560 | tf_op jit(solution)/shard_map/ppermute | solution.py:622
  89.2 27.2 %collective-permute-start.20 = (f32[432,128]{1,0:T(8,128)S(1)}, f32[432,128]{1,0:T(8,128)S(1)}, u32[]{:S(2)}, u32[]{:S(2)}) collective-permute-start(f32[432,128]{1,0:T(8,128)S(1)} %get-tuple-element.104), channel_id=1, source_target_pairs={{0,24},{8,0},{16,8},{24,16},{1,25},{9,1},{17,9},{25,17},{2,26},{10... | collective-permute-start | bytes 663560 | tf_op jit(solution)/shard_map/ppermute | solution.py:622
  89.3 27.2 %copy-start.1 = (f32[8,128,128]{2,1,0:T(8,128)S(1)}, f32[8,128,128]{2,1,0:T(8,128)}, u32[]{:S(2)}) copy-start(f32[8,128,128]{2,1,0:T(8,128)} %cond.1) | copy-start | bytes 1572868
  89.3 27.2 %copy-start.3 = (f32[8,128,128]{2,1,0:T(8,128)S(1)}, f32[8,128,128]{2,1,0:T(8,128)}, u32[]{:S(2)}) copy-start(f32[8,128,128]{2,1,0:T(8,128)} %cot.1) | copy-start | bytes 1572868
  112.6 13.8 %collective-permute-start.15 = (f32[344,128]{1,0:T(8,128)S(1)}, f32[344,128]{1,0:T(8,128)S(1)}, u32[]{:S(2)}, u32[]{:S(2)}) collective-permute-start(f32[344,128]{1,0:T(8,128)S(1)} %get-tuple-element.98), channel_id=1, source_target_pairs={{0,8},{8,16},{16,24},{24,0},{1,9},{9,17},{17,25},{25,1},{2,10},{10... | collective-permute-start | bytes 528392 | tf_op jit(solution)/shard_map/ppermute | solution.py:622
  114.6 14.3 %collective-permute-start.16 = (f32[344,128]{1,0:T(8,128)S(1)}, f32[344,128]{1,0:T(8,128)S(1)}, u32[]{:S(2)}, u32[]{:S(2)}) collective-permute-start(f32[344,128]{1,0:T(8,128)S(1)} %get-tuple-element.99), channel_id=1, source_target_pairs={{0,16},{8,24},{16,0},{24,8},{1,17},{9,25},{17,1},{25,9},{2,18},{10... | collective-permute-start | bytes 528392 | tf_op jit(solution)/shard_map/ppermute | solution.py:622
  116.4 15.1 %collective-permute-start.17 = (f32[344,128]{1,0:T(8,128)S(1)}, f32[344,128]{1,0:T(8,128)S(1)}, u32[]{:S(2)}, u32[]{:S(2)}) collective-permute-start(f32[344,128]{1,0:T(8,128)S(1)} %get-tuple-element.100), channel_id=1, source_target_pairs={{0,24},{8,0},{16,8},{24,16},{1,25},{9,1},{17,9},{25,17},{2,26},{10... | collective-permute-start | bytes 528392 | tf_op jit(solution)/shard_map/ppermute | solution.py:622
  (3 other events, 2.8 us)

commit v12 on v11

--- a/solution.py
+++ b/solution.py
@@ -203,7 +203,7 @@
 
 
 def edge_kernel(places, *refs):
-    msgs, (to_left, to_right, head, tail) = refs[:G], refs[G:]
+    msgs, (to_left, to_right) = refs[:G], refs[G:]
     lane = lax.broadcasted_iota(jnp.int32, (BY, LANES), 1)
     low = lax.rem(lane, 16) < 8
     for n in range(2):
@@ -211,19 +211,16 @@
             first, second = msgs[d][n, 0], msgs[d][n, 1]
             to_left[n, places[0, d]] = jnp.where(low, first, roll(second, 8))
             to_right[n, places[1, d]] = jnp.where(low, roll(second, -8), first)
-            for a in range(2):
-                head[n, d, a] = msgs[d][n, a, :HALO]
-                tail[n, d, a] = msgs[d][n, a, BY - HALO :]
-
-
-def rows_kernel(from_left, from_right, above, below, head, tail, above_out, below_out):
+
+
+def rows_kernel(*refs):
+    msgs, sides, (head, tail) = refs[:G], refs[G : G + 2], refs[G + 2 :]
     for n in range(2):
         for d in range(G):
             for out, rows in ((head, slice(0, HALO)), (tail, slice(BY - HALO, BY))):
-                for a, side in enumerate((from_left, from_right)):
-                    out[n, d, a] = side[n, d, rows]
-            above_out[n, d] = above[n, d]
-            below_out[n, d] = below[n, d]
+                for a in range(2):
+                    out[n, d, a] = msgs[d][n, a, rows]
+                    out[n, d, 2 + a] = sides[a][n, d, rows]
 
 
 def unpack(get_brick, get_edge, group, within, put):
@@ -257,8 +254,8 @@
 
 def solve_kernel(adjoint, strip, steps, *refs):
     if adjoint:
-        bricks, (from_left, from_right, above, below, above_edge, below_edge) = refs[:G], refs[G : G + 6]
-        outs, coefficients, (kap, *scratch) = refs[G + 6 : 2 * G + 6], refs[2 * G + 6 : 2 * G + 11], refs[2 * G + 11 :]
+        bricks, (from_left, from_right, above, below) = refs[:G], refs[G : G + 4]
+        outs, coefficients, (kap, *scratch) = refs[G + 4 : 2 * G + 4], refs[2 * G + 4 : 2 * G + 9], refs[2 * G + 9 :]
     else:
         strips_here, coefficients = refs[:G], refs[G : G + 5]
         outs, scratch = refs[G + 5 : 2 * G + 5], refs[2 * G + 5 :]
@@ -300,10 +297,10 @@
 
         group_halo, within_halo = lanes_of(HALO, strip[0])
         for n, dst in enumerate((kap, rhs)):
-            for brick, edge, start in ((above, above_edge, TOP - HALO), (below, below_edge, TOP + BY)):
+            for rows, start in ((above, TOP - HALO), (below, TOP + BY)):
                 unpack(
-                    lambda d, a: brick[n, d, a],
-                    lambda side, d: edge[n, d, side],
+                    lambda d, a: rows[n, d, a],
+                    lambda side, d: rows[n, d, 2 + side],
                     group_halo,
                     within_halo,
                     put_at(dst, start, HALO),
@@ -652,8 +649,8 @@
     below_rows = shifted(both[:, :, :HALO], "gy", -1)
     parts, above_rows, below_rows = lax.optimization_barrier((parts, above_rows, below_rows))
     edge = (2, G, BY, LANES)
-    rim = (2, G, 2, HALO, LANES)
-    to_left, to_right, head, tail = call(edge_kernel, [edge, edge, rim, rim], [places], parts)
+    rim = (2, G, 4, HALO, LANES)
+    to_left, to_right = call(edge_kernel, [edge, edge], [places], parts)
     to_left, below_rows = lax.optimization_barrier((to_left, below_rows))
     *messages, steps_here = call(
         pack_previous_kernel,
@@ -662,10 +659,9 @@
         [both, above_rows, below_rows],
     )
     from_left, from_right = around(to_right, 1), around(to_left, -1)
-    above, below = shifted(tail, "gy", 1), shifted(head, "gy", -1)
     from_left, from_right, own = lax.optimization_barrier((from_left, from_right, messages[0]))
-    head, tail, above, below = call(rows_kernel, [rim] * 4, [], [from_left, from_right, above, below])
-    halos = [from_left, from_right, above, below, shifted(tail, "gy", 1), shifted(head, "gy", -1)]
+    head, tail = call(rows_kernel, [rim, rim], [], [*parts, from_left, from_right])
+    halos = [from_left, from_right, shifted(tail, "gy", 1), shifted(head, "gy", -1)]
 
     second = [own] + [shifted(messages[d], "gx", d) for d in range(1, G)]
 

time: 138 us -> 134 us (0.971)
  waiting for transfers between devices: 41.5 us -> 37 us
  starting transfers between devices: 20.9 us -> 22.5 us
    ppermute x2, waiting for transfers between devices: 11.1 us -> 6.13 us  [around(): lax.ppermute(x, ('gx', 'pa'), [(at, order[(i + by) % len(order)]) for i,...]
    ppermute x19 -> x17, starting transfers between devices: 18.8 us -> 20.5 us  [shifted(): return lax.ppermute(x, axis, [(i, (i + by) % count) for i in range(count)])]
    ppermute x19 -> x17, waiting for transfers between devices: 30.4 us -> 30.8 us  [shifted(): return lax.ppermute(x, axis, [(i, (i + by) % count) for i in range(count)])]
  transfers between devices with their start and end apart: 21 -> 19, of which waited for: 10 -> 10; matrix products, arithmetic and copies ran while one was open for 1% -> 1% of each run, Pallas kernels for 45% -> 45%
where the time goes in v12:
time: 134 us
  Pallas kernels  69 us (51%)
  waiting for transfers between devices  37 us (28%)
  starting transfers between devices  22.5 us (17%)
  local copies, waits for them, and re-layouts  2.84 us (2%)
  between operations  1.43 us (1%)
    pallas_call x8, Pallas kernels, call(): pl.pallas_call(kernel, out_shape=[jax.ShapeDtypeStruct(shape, F32) for sh...  69 us
    ppermute x17, waiting for transfers between devices, shifted(): return lax.ppermute(x, axis, [(i, (i + by) % count) for i in range(count)])  30.8 us
    ppermute x17, starting transfers between devices, shifted(): return lax.ppermute(x, axis, [(i, (i + by) % count) for i in range(count)])  20.5 us
    ppermute x2, waiting for transfers between devices, around(): lax.ppermute(x, ('gx', 'pa'), [(at, order[(i + by) % len(order)]) for i,...  6.13 us
    unnamed x12, local copies, waits for them, and re-layouts  2.82 us
  transfers between devices with their start and end apart: 19, of which 10 were waited for; matrix products, arithmetic and copies ran while one was open for 1% of the time, Pallas kernels for 45%

profile of v12, /device:TPU:8, one launch (start us, length us, event | category | flops | bytes accessed | tf_op | source)
XLA Modules:
  0.0 134.0 jit_solution(2902051610194317661)
XLA Ops:
  2.7 1.2 shard_map.84
  4.0 1.6 %collective-permute-start = (bf16[8,128,128]{2,1,0:T(8,128)(2,1)}, bf16[8,128,128]{2,1,0:T(8,128)(2,1)S(1)}, u32[]{:S(2)}, u32[]{:S(2)}) collective-permute-start(bf16[8,128,128]{2,1,0:T(8,128)(2,1)} %param.6), channel_id=1, source_target_pairs={{0,1},{1,0},{2,3},{3,2},{4,5},{5,4},{6,7},{7,6},{8,9},{9,8},{10,11... | collective-permute-start | bytes 786440 | tf_op jit(solution)/shard_map/ppermute | solution.py:619
  5.6 1.6 %collective-permute-start.1 = (f32[2,2,128,128]{3,2,1,0:T(8,128)S(1)}, f32[2,2,128,128]{3,2,1,0:T(8,128)S(1)}, u32[]{:S(2)}, u32[]{:S(2)}) collective-permute-start(f32[2,2,128,128]{3,2,1,0:T(8,128)S(1)} %get-tuple-element.61), channel_id=1, source_target_pairs={{0,8},{8,16},{16,24},{24,0},{1,9},{9,17},{17,25},{25,1},{2,10},{10... | collective-permute-start | bytes 786440 | tf_op jit(solution)/shard_map/ppermute | solution.py:619
  7.1 1.2 collective-permute-start.2
  8.4 1.8 %collective-permute-start.3 = (f32[2,2,128,128]{3,2,1,0:T(8,128)S(1)}, f32[2,2,128,128]{3,2,1,0:T(8,128)S(1)}, u32[]{:S(2)}, u32[]{:S(2)}) collective-permute-start(f32[2,2,128,128]{3,2,1,0:T(8,128)S(1)} %get-tuple-element.63), channel_id=1, source_target_pairs={{0,24},{8,0},{16,8},{24,16},{1,25},{9,1},{17,9},{25,17},{2,26},{10... | collective-permute-start | bytes 786440 | tf_op jit(solution)/shard_map/ppermute | solution.py:619
  10.2 2.1 %collective-permute-done = bf16[8,128,128]{2,1,0:T(8,128)(2,1)S(1)} collective-permute-done((bf16[8,128,128]{2,1,0:T(8,128)(2,1)}, bf16[8,128,128]{2,1,0:T(8,128)(2,1)S(1)}, u32[]{:S(2)}, u32[]{:S(2)}) %collective-permute-start) | collective-permute-done | bytes 262176 | tf_op jit(solution)/shard_map/ppermute | solution.py:619
  14.1 11.0 %collective-permute-done.1.refs_1_ = f32[2,2,128,128]{3,2,1,0:T(8,128)S(1)} collective-permute-done((f32[2,2,128,128]{3,2,1,0:T(8,128)S(1)}, f32[2,2,128,128]{3,2,1,0:T(8,128)S(1)}, u32[]{:S(2)}, u32[]{:S(2)}) %collective-permute-start.1) | collective-permute-done | bytes 262176 | tf_op jit(solution)/shard_map/ppermute | solution.py:619
  25.1 4.2 %collective-permute-done.2.refs_2_ = f32[2,2,128,128]{3,2,1,0:T(8,128)S(1)} collective-permute-done((f32[2,2,128,128]{3,2,1,0:T(8,128)S(1)}, f32[2,2,128,128]{3,2,1,0:T(8,128)S(1)}, u32[]{:S(2)}, u32[]{:S(2)}) %collective-permute-start.2) | collective-permute-done | bytes 262176 | tf_op jit(solution)/shard_map/ppermute | solution.py:619
  29.3 1.8 %collective-permute-done.3.refs_3_ = f32[2,2,128,128]{3,2,1,0:T(8,128)S(1)} collective-permute-done((f32[2,2,128,128]{3,2,1,0:T(8,128)S(1)}, f32[2,2,128,128]{3,2,1,0:T(8,128)S(1)}, u32[]{:S(2)}, u32[]{:S(2)}) %collective-permute-start.3) | collective-permute-done | bytes 262176 | tf_op jit(solution)/shard_map/ppermute | solution.py:619
  32.0 2.0 %collective-permute-start.6 = (f32[2,4,128,128]{3,2,1,0:T(8,128)S(1)}, f32[2,4,128,128]{3,2,1,0:T(8,128)S(1)}, u32[]{:S(2)}, u32[]{:S(2)}) collective-permute-start(f32[2,4,128,128]{3,2,1,0:T(8,128)S(1)} %get-tuple-element.73), channel_id=1, source_target_pairs={{0,8},{8,16},{16,24},{24,25},{25,17},{17,9},{9,1},{1,0},{2,10},{10... | collective-permute-start | bytes 1572872 | tf_op jit(solution)/shard_map/ppermute | solution.py:624
  34.7 4.4 %shard_map.86 = (f32[4,160,128]{2,1,0:T(8,128)S(1)}, f32[4,160,128]{2,1,0:T(8,128)}, f32[4,160,128]{2,1,0:T(8,128)}, f32[4,160,128]{2,1,0:T(8,128)}, f32[16,2,8,128]{3,2,1,0:T(8,128)S(1)}) custom-call(s32[4]{0:T(128)S(1)} %broadcast_select_fusion.strips, f32[1]{0:T(128)S(6)} %copy.9.upper, f32[2,8,128,128]{3,2,1,0:T(8,128)S(1)} %convert_multiply_fusion.both.previous, ...), custom_call_target="tpu_custom_call" | custom-call | bytes 6000000 | tf_op jit(solution)/shard_map/pallas_call | solution.py:606
  39.8 6.1 %collective-permute-done.7.refs_5_ = f32[2,4,128,128]{3,2,1,0:T(8,128)S(1)} collective-permute-done((f32[2,4,128,128]{3,2,1,0:T(8,128)S(1)}, f32[2,4,128,128]{3,2,1,0:T(8,128)S(1)}, u32[]{:S(2)}, u32[]{:S(2)}) %collective-permute-start.7) | collective-permute-done | bytes 524320 | tf_op jit(solution)/shard_map/ppermute | solution.py:624
  46.8 1.7 %collective-permute-start.12 = (f32[2,4,4,16,128]{4,3,2,1,0:T(8,128)}, f32[2,4,4,16,128]{4,3,2,1,0:T(8,128)}, u32[]{:S(2)}, u32[]{:S(2)}) collective-permute-start(f32[2,4,4,16,128]{4,3,2,1,0:T(8,128)} %get-tuple-element.83), channel_id=1, source_target_pairs={{0,6},{2,0},{4,2},{6,4},{1,7},{3,1},{5,3},{7,5},{8,14},{10,8},{12,... | collective-permute-start | bytes 786440 | tf_op jit(solution)/shard_map/ppermute | solution.py:619
  48.5 1.7 %collective-permute-start.8 = (f32[4,160,128]{2,1,0:T(8,128)}, f32[4,160,128]{2,1,0:T(8,128)}, u32[]{:S(2)}, u32[]{:S(2)}) collective-permute-start(f32[4,160,128]{2,1,0:T(8,128)} %get-tuple-element.77), channel_id=1, source_target_pairs={{0,8},{8,16},{16,24},{24,0},{1,9},{9,17},{17,25},{25,1},{2,10},{10... | collective-permute-start | bytes 983048 | tf_op jit(solution)/shard_map/ppermute | solution.py:619
  52.0 1.8 %collective-permute-done.11.refs_6_ = f32[2,4,4,16,128]{4,3,2,1,0:T(8,128)S(1)} collective-permute-done((f32[2,4,4,16,128]{4,3,2,1,0:T(8,128)}, f32[2,4,4,16,128]{4,3,2,1,0:T(8,128)S(1)}, u32[]{:S(2)}, u32[]{:S(2)}) %collective-permute-start.11) | collective-permute-done | bytes 262176 | tf_op jit(solution)/shard_map/ppermute | solution.py:619
  54.7 27.0 %shard_map.88 = (f32[432,128]{1,0:T(8,128)S(1)}, f32[432,128]{1,0:T(8,128)S(1)}, f32[432,128]{1,0:T(8,128)S(1)}, f32[432,128]{1,0:T(8,128)S(1)}, f32[8,2,176,128...) custom-call(s32[1]{0:T(128)} %bitcast.strip, ...), custom_call_target="tpu_custom_call" | custom-call | bytes 75000000 | tf_op jit(solution)/shard_map/pallas_call | solution.py:606
  81.7 1.7 %collective-permute-start.16 = (f32[432,128]{1,0:T(8,128)S(1)}, f32[432,128]{1,0:T(8,128)S(1)}, u32[]{:S(2)}, u32[]{:S(2)}) collective-permute-start(f32[432,128]{1,0:T(8,128)S(1)} %get-tuple-element.94), channel_id=1, source_target_pairs={{0,8},{8,16},{16,24},{24,0},{1,9},{9,17},{17,25},{25,1},{2,10},{10... | collective-permute-start | bytes 663560 | tf_op jit(solution)/shard_map/ppermute | solution.py:619
  85.2 23.3 %shard_map.89 = (f32[344,128]{1,0:T(8,128)S(1)}, f32[344,128]{1,0:T(8,128)S(1)}, f32[344,128]{1,0:T(8,128)S(1)}, f32[344,128]{1,0:T(8,128)S(1)}) custom-call(s32[1]{0:T(128)} %bitcast.strip, f32[16,2,8,128]{3,2,1,0:T(8,128)S(1)} %get-tuple-element.72.steps, f32[4,160,128]{2,1,0:T(8,128)S(1)} %copy-done.5, f32[4,160,128]{2,1,0:T(8,128)} %collective-permute-done.8.refs_1_, ...), custom_call_target="tpu_custom_call" | custom-call | bytes 75000000 | tf_op jit(solution)/shard_map/pallas_call | solution.py:606
  108.5 1.5 %collective-permute-start.13 = (f32[344,128]{1,0:T(8,128)S(1)}, f32[344,128]{1,0:T(8,128)S(1)}, u32[]{:S(2)}, u32[]{:S(2)}) collective-permute-start(f32[344,128]{1,0:T(8,128)S(1)} %get-tuple-element.90), channel_id=1, source_target_pairs={{0,8},{8,16},{16,24},{24,0},{1,9},{9,17},{17,25},{25,1},{2,10},{10... | collective-permute-start | bytes 528392 | tf_op jit(solution)/shard_map/ppermute | solution.py:619
  109.9 3.6 %collective-permute-start.14 = (f32[344,128]{1,0:T(8,128)S(1)}, f32[344,128]{1,0:T(8,128)S(1)}, u32[]{:S(2)}, u32[]{:S(2)}) collective-permute-start(f32[344,128]{1,0:T(8,128)S(1)} %get-tuple-element.91), channel_id=1, source_target_pairs={{0,16},{8,24},{16,0},{24,8},{1,17},{9,25},{17,1},{25,9},{2,18},{10... | collective-permute-start | bytes 528392 | tf_op jit(solution)/shard_map/ppermute | solution.py:619
  113.6 6.1 %shard_map.90 = (f32[8,128,128]{2,1,0:T(8,128)}, f32[8,128,128]{2,1,0:T(8,128)S(1)}, f32[10,144,128]{2,1,0:T(8,128)S(1)}, f32[10,144,128]{2,1,0:T(8,128)S(1)}, f...) custom-call(s32[4]{0:T(128)S(1)} %broadcast_select_fusion.1.strips, f32[432,128]{1,0:T(8,128)S(1)} %get-tuple-element.93.m0, ...), custom_call_target="tpu_custom_call" | custom-call | bytes 6000000 | tf_op jit(solution)/shard_map/pallas_call | solution.py:606
  119.7 5.7 %collective-permute-done.14.m2 = f32[344,128]{1,0:T(8,128)S(1)} collective-permute-done((f32[344,128]{1,0:T(8,128)S(1)}, f32[344,128]{1,0:T(8,128)S(1)}, u32[]{:S(2)}, u32[]{:S(2)}) %collective-permute-start.14) | collective-permute-done | bytes 176160 | tf_op jit(solution)/shard_map/ppermute | solution.py:619
  125.4 3.3 %collective-permute-done.15.m3 = f32[344,128]{1,0:T(8,128)S(1)} collective-permute-done((f32[344,128]{1,0:T(8,128)S(1)}, f32[344,128]{1,0:T(8,128)S(1)}, u32[]{:S(2)}, u32[]{:S(2)}) %collective-permute-start.15) | collective-permute-done | bytes 176160 | tf_op jit(solution)/shard_map/ppermute | solution.py:619
  128.7 5.3 %shard_map.91 = (f32[8,128,128]{2,1,0:T(8,128)}, f32[8,128,128]{2,1,0:T(8,128)}, f32[2,8,128,128]{3,2,1,0:T(8,128)}) custom-call(s32[4]{0:T(128)S(1)} %broadcast_select_fusion.1.strips, f32[344,128]{1,0:T(8,128)S(1)} %get-tuple-element.89.m0, f32[344,128]{1,0:T(8,128)S(1)} %collective-permute-done.13.m1, f32[344,128]{1,0:T(8,128)S(1)} %collective-permute-done.14.m2, ...), custom_call_target="tpu_custom_call" | custom-call | bytes 6000000 | tf_op jit(solution)/shard_map/pallas_call | solution.py:606
  (40 shorter events, 11.0 us)
Async XLA Ops:
  0.7 1.0 copy-start
  1.7 1.0 copy-start.2
  4.0 8.3 %collective-permute-start = (bf16[8,128,128]{2,1,0:T(8,128)(2,1)}, bf16[8,128,128]{2,1,0:T(8,128)(2,1)S(1)}, u32[]{:S(2)}, u32[]{:S(2)}) collective-permute-start(bf16[8,128,128]{2,1,0:T(8,128)(2,1)} %param.6), channel_id=1, source_target_pairs={{0,1},{1,0},{2,3},{3,2},{4,5},{5,4},{6,7},{7,6},{8,9},{9,8},{10,11... | collective-permute-start | bytes 786440 | tf_op jit(solution)/shard_map/ppermute | solution.py:619
  5.6 19.6 %collective-permute-start.1 = (f32[2,2,128,128]{3,2,1,0:T(8,128)S(1)}, f32[2,2,128,128]{3,2,1,0:T(8,128)S(1)}, u32[]{:S(2)}, u32[]{:S(2)}) collective-permute-start(f32[2,2,128,128]{3,2,1,0:T(8,128)S(1)} %get-tuple-element.61), channel_id=1, source_target_pairs={{0,8},{8,16},{16,24},{24,0},{1,9},{9,17},{17,25},{25,1},{2,10},{10... | collective-permute-start | bytes 786440 | tf_op jit(solution)/shard_map/ppermute | solution.py:619
  7.1 22.1 %collective-permute-start.2 = (f32[2,2,128,128]{3,2,1,0:T(8,128)S(1)}, f32[2,2,128,128]{3,2,1,0:T(8,128)S(1)}, u32[]{:S(2)}, u32[]{:S(2)}) collective-permute-start(f32[2,2,128,128]{3,2,1,0:T(8,128)S(1)} %get-tuple-element.62), channel_id=1, source_target_pairs={{0,16},{8,24},{16,0},{24,8},{1,17},{9,25},{17,1},{25,9},{2,18},{10... | collective-permute-start | bytes 786440 | tf_op jit(solution)/shard_map/ppermute | solution.py:619
  8.4 22.7 %collective-permute-start.3 = (f32[2,2,128,128]{3,2,1,0:T(8,128)S(1)}, f32[2,2,128,128]{3,2,1,0:T(8,128)S(1)}, u32[]{:S(2)}, u32[]{:S(2)}) collective-permute-start(f32[2,2,128,128]{3,2,1,0:T(8,128)S(1)} %get-tuple-element.63), channel_id=1, source_target_pairs={{0,24},{8,0},{16,8},{24,16},{1,25},{9,1},{17,9},{25,17},{2,26},{10... | collective-permute-start | bytes 786440 | tf_op jit(solution)/shard_map/ppermute | solution.py:619
  13.5 17.6 %collective-permute-start.5 = (f32[2,8,16,128]{3,2,1,0:T(8,128)S(1)}, f32[2,8,16,128]{3,2,1,0:T(8,128)S(1)}, u32[]{:S(2)}, u32[]{:S(2)}) collective-permute-start(f32[2,8,16,128]{3,2,1,0:T(8,128)S(1)} %get-tuple-element.106), channel_id=1, source_target_pairs={{0,6},{2,0},{4,2},{6,4},{1,7},{3,1},{5,3},{7,5},{8,14},{10,8},{12,... | collective-permute-start | bytes 393224 | tf_op jit(solution)/shard_map/ppermute | solution.py:619
  13.6 17.5 %collective-permute-start.4 = (f32[2,8,16,128]{3,2,1,0:T(8,128)S(1)}, f32[2,8,16,128]{3,2,1,0:T(8,128)S(1)}, u32[]{:S(2)}, u32[]{:S(2)}) collective-permute-start(f32[2,8,16,128]{3,2,1,0:T(8,128)S(1)} %get-tuple-element.107), channel_id=1, source_target_pairs={{0,2},{2,4},{4,6},{6,0},{1,3},{3,5},{5,7},{7,1},{8,10},{10,12},{12... | collective-permute-start | bytes 393224 | tf_op jit(solution)/shard_map/ppermute | solution.py:619
  32.0 13.9 %collective-permute-start.7 = (f32[2,4,128,128]{3,2,1,0:T(8,128)S(1)}, f32[2,4,128,128]{3,2,1,0:T(8,128)S(1)}, u32[]{:S(2)}, u32[]{:S(2)}) collective-permute-start(f32[2,4,128,128]{3,2,1,0:T(8,128)S(1)} %get-tuple-element.74), channel_id=1, source_target_pairs={{0,1},{8,0},{16,8},{24,16},{25,24},{17,25},{9,17},{1,9},{2,3},{10,... | collective-permute-start | bytes 1572872 | tf_op jit(solution)/shard_map/ppermute | solution.py:624
  32.0 13.9 %collective-permute-start.6 = (f32[2,4,128,128]{3,2,1,0:T(8,128)S(1)}, f32[2,4,128,128]{3,2,1,0:T(8,128)S(1)}, u32[]{:S(2)}, u32[]{:S(2)}) collective-permute-start(f32[2,4,128,128]{3,2,1,0:T(8,128)S(1)} %get-tuple-element.73), channel_id=1, source_target_pairs={{0,8},{8,16},{16,24},{24,25},{25,17},{17,9},{9,1},{1,0},{2,10},{10... | collective-permute-start | bytes 1572872 | tf_op jit(solution)/shard_map/ppermute | solution.py:624
  46.8 7.0 %collective-permute-start.11 = (f32[2,4,4,16,128]{4,3,2,1,0:T(8,128)}, f32[2,4,4,16,128]{4,3,2,1,0:T(8,128)S(1)}, u32[]{:S(2)}, u32[]{:S(2)}) collective-permute-start(f32[2,4,4,16,128]{4,3,2,1,0:T(8,128)} %get-tuple-element.82), channel_id=1, source_target_pairs={{0,2},{2,4},{4,6},{6,0},{1,3},{3,5},{5,7},{7,1},{8,10},{10,12},{12... | collective-permute-start | bytes 786440 | tf_op jit(solution)/shard_map/ppermute | solution.py:619
  46.8 7.9 %collective-permute-start.12 = (f32[2,4,4,16,128]{4,3,2,1,0:T(8,128)}, f32[2,4,4,16,128]{4,3,2,1,0:T(8,128)}, u32[]{:S(2)}, u32[]{:S(2)}) collective-permute-start(f32[2,4,4,16,128]{4,3,2,1,0:T(8,128)} %get-tuple-element.83), channel_id=1, source_target_pairs={{0,6},{2,0},{4,2},{6,4},{1,7},{3,1},{5,3},{7,5},{8,14},{10,8},{12,... | collective-permute-start | bytes 786440 | tf_op jit(solution)/shard_map/ppermute | solution.py:619
  48.5 36.0 %collective-permute-start.8 = (f32[4,160,128]{2,1,0:T(8,128)}, f32[4,160,128]{2,1,0:T(8,128)}, u32[]{:S(2)}, u32[]{:S(2)}) collective-permute-start(f32[4,160,128]{2,1,0:T(8,128)} %get-tuple-element.77), channel_id=1, source_target_pairs={{0,8},{8,16},{16,24},{24,0},{1,9},{9,17},{17,25},{25,1},{2,10},{10... | collective-permute-start | bytes 983048 | tf_op jit(solution)/shard_map/ppermute | solution.py:619
  50.2 35.0 %collective-permute-start.9 = (f32[4,160,128]{2,1,0:T(8,128)}, f32[4,160,128]{2,1,0:T(8,128)}, u32[]{:S(2)}, u32[]{:S(2)}) collective-permute-start(f32[4,160,128]{2,1,0:T(8,128)} %get-tuple-element.78), channel_id=1, source_target_pairs={{0,16},{8,24},{16,0},{24,8},{1,17},{9,25},{17,1},{25,9},{2,18},{10... | collective-permute-start | bytes 983048 | tf_op jit(solution)/shard_map/ppermute | solution.py:619
  51.4 33.8 %collective-permute-start.10 = (f32[4,160,128]{2,1,0:T(8,128)}, f32[4,160,128]{2,1,0:T(8,128)}, u32[]{:S(2)}, u32[]{:S(2)}) collective-permute-start(f32[4,160,128]{2,1,0:T(8,128)} %get-tuple-element.79), channel_id=1, source_target_pairs={{0,24},{8,0},{16,8},{24,16},{1,25},{9,1},{17,9},{25,17},{2,26},{10... | collective-permute-start | bytes 983048 | tf_op jit(solution)/shard_map/ppermute | solution.py:619
  52.0 33.2 %copy-start.5 = (f32[4,160,128]{2,1,0:T(8,128)S(1)}, f32[4,160,128]{2,1,0:T(8,128)}, u32[]{:S(2)}) copy-start(f32[4,160,128]{2,1,0:T(8,128)} %copy-done.4) | copy-start | bytes 983044
  81.7 31.9 %collective-permute-start.16 = (f32[432,128]{1,0:T(8,128)S(1)}, f32[432,128]{1,0:T(8,128)S(1)}, u32[]{:S(2)}, u32[]{:S(2)}) collective-permute-start(f32[432,128]{1,0:T(8,128)S(1)} %get-tuple-element.94), channel_id=1, source_target_pairs={{0,8},{8,16},{16,24},{24,0},{1,9},{9,17},{17,25},{25,1},{2,10},{10... | collective-permute-start | bytes 663560 | tf_op jit(solution)/shard_map/ppermute | solution.py:619
  83.4 30.1 %collective-permute-start.17 = (f32[432,128]{1,0:T(8,128)S(1)}, f32[432,128]{1,0:T(8,128)S(1)}, u32[]{:S(2)}, u32[]{:S(2)}) collective-permute-start(f32[432,128]{1,0:T(8,128)S(1)} %get-tuple-element.95), channel_id=1, source_target_pairs={{0,16},{8,24},{16,0},{24,8},{1,17},{9,25},{17,1},{25,9},{2,18},{10... | collective-permute-start | bytes 663560 | tf_op jit(solution)/shard_map/ppermute | solution.py:619
  84.5 29.0 %collective-permute-start.18 = (f32[432,128]{1,0:T(8,128)S(1)}, f32[432,128]{1,0:T(8,128)S(1)}, u32[]{:S(2)}, u32[]{:S(2)}) collective-permute-start(f32[432,128]{1,0:T(8,128)S(1)} %get-tuple-element.96), channel_id=1, source_target_pairs={{0,24},{8,0},{16,8},{24,16},{1,25},{9,1},{17,9},{25,17},{2,26},{10... | collective-permute-start | bytes 663560 | tf_op jit(solution)/shard_map/ppermute | solution.py:619
  85.2 28.4 %copy-start.1 = (f32[8,128,128]{2,1,0:T(8,128)S(1)}, f32[8,128,128]{2,1,0:T(8,128)}, u32[]{:S(2)}) copy-start(f32[8,128,128]{2,1,0:T(8,128)} %cond.1) | copy-start | bytes 1572868
  85.2 28.4 %copy-start.3 = (f32[8,128,128]{2,1,0:T(8,128)S(1)}, f32[8,128,128]{2,1,0:T(8,128)}, u32[]{:S(2)}) copy-start(f32[8,128,128]{2,1,0:T(8,128)} %cot.1) | copy-start | bytes 1572868
  108.5 11.3 %collective-permute-start.13 = (f32[344,128]{1,0:T(8,128)S(1)}, f32[344,128]{1,0:T(8,128)S(1)}, u32[]{:S(2)}, u32[]{:S(2)}) collective-permute-start(f32[344,128]{1,0:T(8,128)S(1)} %get-tuple-element.90), channel_id=1, source_target_pairs={{0,8},{8,16},{16,24},{24,0},{1,9},{9,17},{17,25},{25,1},{2,10},{10... | collective-permute-start | bytes 528392 | tf_op jit(solution)/shard_map/ppermute | solution.py:619
  109.9 15.5 %collective-permute-start.14 = (f32[344,128]{1,0:T(8,128)S(1)}, f32[344,128]{1,0:T(8,128)S(1)}, u32[]{:S(2)}, u32[]{:S(2)}) collective-permute-start(f32[344,128]{1,0:T(8,128)S(1)} %get-tuple-element.91), channel_id=1, source_target_pairs={{0,16},{8,24},{16,0},{24,8},{1,17},{9,25},{17,1},{25,9},{2,18},{10... | collective-permute-start | bytes 528392 | tf_op jit(solution)/shard_map/ppermute | solution.py:619
  113.5 15.2 %collective-permute-start.15 = (f32[344,128]{1,0:T(8,128)S(1)}, f32[344,128]{1,0:T(8,128)S(1)}, u32[]{:S(2)}, u32[]{:S(2)}) collective-permute-start(f32[344,128]{1,0:T(8,128)S(1)} %get-tuple-element.92), channel_id=1, source_target_pairs={{0,24},{8,0},{16,8},{24,16},{1,25},{9,1},{17,9},{25,17},{2,26},{10... | collective-permute-start | bytes 528392 | tf_op jit(solution)/shard_map/ppermute | solution.py:619
  (1 other events, 0.7 us)

commit v13 on v12

--- a/solution.py
+++ b/solution.py
@@ -99,6 +99,7 @@
 BOTH = FIELD + OWN
 TILE = 8
 CHUNK = 32
+SPAN = 64
 WIDE = 16
 
 BLOCK = (0, 3, 2, 1)
@@ -492,30 +493,30 @@
 
     base = 0 if own is None else FIELD - TILES
 
-    @pl.loop(0, BY // CHUNK)
+    @pl.loop(0, BY // SPAN)
     def _(t):
-        to = pl.ds(pl.multiple_of(TILE + CHUNK * t, TILE), CHUNK)
+        to = pl.ds(pl.multiple_of(TILE + SPAN * t, TILE), SPAN)
         if own is not None:
             for c in range(BX):
-                padded[1 + c, to] = own[c, pl.ds(pl.multiple_of(CHUNK * t, CHUNK), CHUNK)]
+                padded[1 + c, to] = own[c, pl.ds(pl.multiple_of(SPAN * t, SPAN), SPAN)]
             return
-        owner = owners(CHUNK)
+        owner = owners(SPAN)
         whole = []
         for a in range(2):
-            parts = bricks(pl.multiple_of(BY * a + CHUNK * t, TILE), CHUNK)
+            parts = bricks(pl.multiple_of(BY * a + SPAN * t, TILE), SPAN)
             whole += [choose(owner, parts, b) for b in range(4)]
         ordered = reorder(jnp.concatenate(whole, axis=0), order)
         for c in range(BX):
-            padded[1 + c, to] = ordered[CHUNK * c : CHUNK * (c + 1)]
-
-    @pl.loop(0, BY // 2 // CHUNK)
+            padded[1 + c, to] = ordered[SPAN * c : SPAN * (c + 1)]
+
+    @pl.loop(0, BY // 2 // SPAN)
     def _(t):
-        owner = owners(CHUNK)
-        parts = bricks(pl.multiple_of(base + SIDES + CHUNK * t, TILE), CHUNK)
+        owner = owners(SPAN)
+        parts = bricks(pl.multiple_of(base + SIDES + SPAN * t, TILE), SPAN)
         ordered = reorder(jnp.concatenate([choose(owner, parts, b) for b in range(4)], axis=0), order)
         for j, (at, start) in enumerate(((0, 0), (1 + BX, 0), (0, BY // 2), (1 + BX, BY // 2))):
-            to = pl.ds(pl.multiple_of(TILE + start + CHUNK * t, TILE), CHUNK)
-            padded[at, to] = ordered[CHUNK * j : CHUNK * (j + 1)]
+            to = pl.ds(pl.multiple_of(TILE + start + SPAN * t, TILE), SPAN)
+            padded[at, to] = ordered[SPAN * j : SPAN * (j + 1)]
 
     parts = bricks(base + ENDS, 16)
     for side, end in enumerate((0, G - 1)):

time: 134 us -> 133 us (level)
  Pallas kernels: 69 us -> 66.3 us
  waiting for transfers between devices: 37 us -> 38.5 us
    pallas_call x8, Pallas kernels: 69 us -> 66.3 us  [call(): pl.pallas_call(kernel, out_shape=[jax.ShapeDtypeStruct(shape, F32) for sh...]
    ppermute x17, waiting for transfers between devices: 30.8 us -> 32.4 us  [shifted(): return lax.ppermute(x, axis, [(i, (i + by) % count) for i in range(count)])]
where the time goes in v13:
time: 133 us
  Pallas kernels  66.3 us (50%)
  waiting for transfers between devices  38.5 us (29%)
  starting transfers between devices  22.5 us (17%)
  local copies, waits for them, and re-layouts  2.84 us (2%)
  between operations  1.43 us (1%)
    pallas_call x8, Pallas kernels, call(): pl.pallas_call(kernel, out_shape=[jax.ShapeDtypeStruct(shape, F32) for sh...  66.3 us
    ppermute x17, waiting for transfers between devices, shifted(): return lax.ppermute(x, axis, [(i, (i + by) % count) for i in range(count)])  32.4 us
    ppermute x17, starting transfers between devices, shifted(): return lax.ppermute(x, axis, [(i, (i + by) % count) for i in range(count)])  20.5 us
    ppermute x2, waiting for transfers between devices, around(): lax.ppermute(x, ('gx', 'pa'), [(at, order[(i + by) % len(order)]) for i,...  6.13 us
    unnamed x12, local copies, waits for them, and re-layouts  2.82 us
  transfers between devices with their start and end apart: 19, of which 10 were waited for; matrix products, arithmetic and copies ran while one was open for 1% of the time, Pallas kernels for 45%

profile of v13, /device:TPU:8, one launch (start us, length us, event | category | flops | bytes accessed | tf_op | source)
XLA Modules:
  0.0 132.9 jit_solution(16400766374405317494)
XLA Ops:
  2.7 1.2 shard_map.84
  4.0 1.6 %collective-permute-start = (bf16[8,128,128]{2,1,0:T(8,128)(2,1)}, bf16[8,128,128]{2,1,0:T(8,128)(2,1)S(1)}, u32[]{:S(2)}, u32[]{:S(2)}) collective-permute-start(bf16[8,128,128]{2,1,0:T(8,128)(2,1)} %param.6), channel_id=1, source_target_pairs={{0,1},{1,0},{2,3},{3,2},{4,5},{5,4},{6,7},{7,6},{8,9},{9,8},{10,11... | collective-permute-start | bytes 786440 | tf_op jit(solution)/shard_map/ppermute | solution.py:620
  5.6 1.6 %collective-permute-start.1 = (f32[2,2,128,128]{3,2,1,0:T(8,128)S(1)}, f32[2,2,128,128]{3,2,1,0:T(8,128)S(1)}, u32[]{:S(2)}, u32[]{:S(2)}) collective-permute-start(f32[2,2,128,128]{3,2,1,0:T(8,128)S(1)} %get-tuple-element.61), channel_id=1, source_target_pairs={{0,8},{8,16},{16,24},{24,0},{1,9},{9,17},{17,25},{25,1},{2,10},{10... | collective-permute-start | bytes 786440 | tf_op jit(solution)/shard_map/ppermute | solution.py:620
  7.1 1.2 collective-permute-start.2
  8.4 1.8 %collective-permute-start.3 = (f32[2,2,128,128]{3,2,1,0:T(8,128)S(1)}, f32[2,2,128,128]{3,2,1,0:T(8,128)S(1)}, u32[]{:S(2)}, u32[]{:S(2)}) collective-permute-start(f32[2,2,128,128]{3,2,1,0:T(8,128)S(1)} %get-tuple-element.63), channel_id=1, source_target_pairs={{0,24},{8,0},{16,8},{24,16},{1,25},{9,1},{17,9},{25,17},{2,26},{10... | collective-permute-start | bytes 786440 | tf_op jit(solution)/shard_map/ppermute | solution.py:620
  10.2 2.1 %collective-permute-done = bf16[8,128,128]{2,1,0:T(8,128)(2,1)S(1)} collective-permute-done((bf16[8,128,128]{2,1,0:T(8,128)(2,1)}, bf16[8,128,128]{2,1,0:T(8,128)(2,1)S(1)}, u32[]{:S(2)}, u32[]{:S(2)}) %collective-permute-start) | collective-permute-done | bytes 262176 | tf_op jit(solution)/shard_map/ppermute | solution.py:620
  14.1 11.0 %collective-permute-done.1.refs_1_ = f32[2,2,128,128]{3,2,1,0:T(8,128)S(1)} collective-permute-done((f32[2,2,128,128]{3,2,1,0:T(8,128)S(1)}, f32[2,2,128,128]{3,2,1,0:T(8,128)S(1)}, u32[]{:S(2)}, u32[]{:S(2)}) %collective-permute-start.1) | collective-permute-done | bytes 262176 | tf_op jit(solution)/shard_map/ppermute | solution.py:620
  25.1 4.2 %collective-permute-done.2.refs_2_ = f32[2,2,128,128]{3,2,1,0:T(8,128)S(1)} collective-permute-done((f32[2,2,128,128]{3,2,1,0:T(8,128)S(1)}, f32[2,2,128,128]{3,2,1,0:T(8,128)S(1)}, u32[]{:S(2)}, u32[]{:S(2)}) %collective-permute-start.2) | collective-permute-done | bytes 262176 | tf_op jit(solution)/shard_map/ppermute | solution.py:620
  29.3 1.8 %collective-permute-done.3.refs_3_ = f32[2,2,128,128]{3,2,1,0:T(8,128)S(1)} collective-permute-done((f32[2,2,128,128]{3,2,1,0:T(8,128)S(1)}, f32[2,2,128,128]{3,2,1,0:T(8,128)S(1)}, u32[]{:S(2)}, u32[]{:S(2)}) %collective-permute-start.3) | collective-permute-done | bytes 262176 | tf_op jit(solution)/shard_map/ppermute | solution.py:620
  32.0 2.0 %collective-permute-start.6 = (f32[2,4,128,128]{3,2,1,0:T(8,128)S(1)}, f32[2,4,128,128]{3,2,1,0:T(8,128)S(1)}, u32[]{:S(2)}, u32[]{:S(2)}) collective-permute-start(f32[2,4,128,128]{3,2,1,0:T(8,128)S(1)} %get-tuple-element.73), channel_id=1, source_target_pairs={{0,8},{8,16},{16,24},{24,25},{25,17},{17,9},{9,1},{1,0},{2,10},{10... | collective-permute-start | bytes 1572872 | tf_op jit(solution)/shard_map/ppermute | solution.py:625
  34.7 4.4 %shard_map.86 = (f32[4,160,128]{2,1,0:T(8,128)S(1)}, f32[4,160,128]{2,1,0:T(8,128)}, f32[4,160,128]{2,1,0:T(8,128)}, f32[4,160,128]{2,1,0:T(8,128)}, f32[16,2,8,128]{3,2,1,0:T(8,128)S(1)}) custom-call(s32[4]{0:T(128)S(1)} %broadcast_select_fusion.strips, f32[1]{0:T(128)S(6)} %copy.9.upper, f32[2,8,128,128]{3,2,1,0:T(8,128)S(1)} %convert_multiply_fusion.both.previous, ...), custom_call_target="tpu_custom_call" | custom-call | bytes 6000000 | tf_op jit(solution)/shard_map/pallas_call | solution.py:607
  39.8 6.1 %collective-permute-done.7.refs_5_ = f32[2,4,128,128]{3,2,1,0:T(8,128)S(1)} collective-permute-done((f32[2,4,128,128]{3,2,1,0:T(8,128)S(1)}, f32[2,4,128,128]{3,2,1,0:T(8,128)S(1)}, u32[]{:S(2)}, u32[]{:S(2)}) %collective-permute-start.7) | collective-permute-done | bytes 524320 | tf_op jit(solution)/shard_map/ppermute | solution.py:625
  46.8 1.7 %collective-permute-start.12 = (f32[2,4,4,16,128]{4,3,2,1,0:T(8,128)}, f32[2,4,4,16,128]{4,3,2,1,0:T(8,128)}, u32[]{:S(2)}, u32[]{:S(2)}) collective-permute-start(f32[2,4,4,16,128]{4,3,2,1,0:T(8,128)} %get-tuple-element.83), channel_id=1, source_target_pairs={{0,6},{2,0},{4,2},{6,4},{1,7},{3,1},{5,3},{7,5},{8,14},{10,8},{12,... | collective-permute-start | bytes 786440 | tf_op jit(solution)/shard_map/ppermute | solution.py:620
  48.5 1.7 %collective-permute-start.8 = (f32[4,160,128]{2,1,0:T(8,128)}, f32[4,160,128]{2,1,0:T(8,128)}, u32[]{:S(2)}, u32[]{:S(2)}) collective-permute-start(f32[4,160,128]{2,1,0:T(8,128)} %get-tuple-element.77), channel_id=1, source_target_pairs={{0,8},{8,16},{16,24},{24,0},{1,9},{9,17},{17,25},{25,1},{2,10},{10... | collective-permute-start | bytes 983048 | tf_op jit(solution)/shard_map/ppermute | solution.py:620
  52.0 1.8 %collective-permute-done.11.refs_6_ = f32[2,4,4,16,128]{4,3,2,1,0:T(8,128)S(1)} collective-permute-done((f32[2,4,4,16,128]{4,3,2,1,0:T(8,128)}, f32[2,4,4,16,128]{4,3,2,1,0:T(8,128)S(1)}, u32[]{:S(2)}, u32[]{:S(2)}) %collective-permute-start.11) | collective-permute-done | bytes 262176 | tf_op jit(solution)/shard_map/ppermute | solution.py:620
  54.7 27.0 %shard_map.88 = (f32[432,128]{1,0:T(8,128)S(1)}, f32[432,128]{1,0:T(8,128)S(1)}, f32[432,128]{1,0:T(8,128)S(1)}, f32[432,128]{1,0:T(8,128)S(1)}, f32[8,2,176,128...) custom-call(s32[1]{0:T(128)} %bitcast.strip, ...), custom_call_target="tpu_custom_call" | custom-call | bytes 75000000 | tf_op jit(solution)/shard_map/pallas_call | solution.py:607
  81.7 1.7 %collective-permute-start.16 = (f32[432,128]{1,0:T(8,128)S(1)}, f32[432,128]{1,0:T(8,128)S(1)}, u32[]{:S(2)}, u32[]{:S(2)}) collective-permute-start(f32[432,128]{1,0:T(8,128)S(1)} %get-tuple-element.94), channel_id=1, source_target_pairs={{0,8},{8,16},{16,24},{24,0},{1,9},{9,17},{17,25},{25,1},{2,10},{10... | collective-permute-start | bytes 663560 | tf_op jit(solution)/shard_map/ppermute | solution.py:620
  85.2 23.3 %shard_map.89 = (f32[344,128]{1,0:T(8,128)S(1)}, f32[344,128]{1,0:T(8,128)S(1)}, f32[344,128]{1,0:T(8,128)S(1)}, f32[344,128]{1,0:T(8,128)S(1)}) custom-call(s32[1]{0:T(128)} %bitcast.strip, f32[16,2,8,128]{3,2,1,0:T(8,128)S(1)} %get-tuple-element.72.steps, f32[4,160,128]{2,1,0:T(8,128)S(1)} %copy-done.5, f32[4,160,128]{2,1,0:T(8,128)} %collective-permute-done.8.refs_1_, ...), custom_call_target="tpu_custom_call" | custom-call | bytes 75000000 | tf_op jit(solution)/shard_map/pallas_call | solution.py:607
  108.5 1.5 %collective-permute-start.13 = (f32[344,128]{1,0:T(8,128)S(1)}, f32[344,128]{1,0:T(8,128)S(1)}, u32[]{:S(2)}, u32[]{:S(2)}) collective-permute-start(f32[344,128]{1,0:T(8,128)S(1)} %get-tuple-element.90), channel_id=1, source_target_pairs={{0,8},{8,16},{16,24},{24,0},{1,9},{9,17},{17,25},{25,1},{2,10},{10... | collective-permute-start | bytes 528392 | tf_op jit(solution)/shard_map/ppermute | solution.py:620
  109.9 3.6 %collective-permute-start.14 = (f32[344,128]{1,0:T(8,128)S(1)}, f32[344,128]{1,0:T(8,128)S(1)}, u32[]{:S(2)}, u32[]{:S(2)}) collective-permute-start(f32[344,128]{1,0:T(8,128)S(1)} %get-tuple-element.91), channel_id=1, source_target_pairs={{0,16},{8,24},{16,0},{24,8},{1,17},{9,25},{17,1},{25,9},{2,18},{10... | collective-permute-start | bytes 528392 | tf_op jit(solution)/shard_map/ppermute | solution.py:620
  113.6 4.6 %shard_map.90 = (f32[8,128,128]{2,1,0:T(8,128)}, f32[8,128,128]{2,1,0:T(8,128)S(1)}, f32[10,144,128]{2,1,0:T(8,128)S(1)}, f32[10,144,128]{2,1,0:T(8,128)S(1)}, f...) custom-call(s32[4]{0:T(128)S(1)} %broadcast_select_fusion.1.strips, f32[432,128]{1,0:T(8,128)S(1)} %get-tuple-element.93.m0, ...), custom_call_target="tpu_custom_call" | custom-call | bytes 6000000 | tf_op jit(solution)/shard_map/pallas_call | solution.py:607
  118.2 7.2 %collective-permute-done.14.m2 = f32[344,128]{1,0:T(8,128)S(1)} collective-permute-done((f32[344,128]{1,0:T(8,128)S(1)}, f32[344,128]{1,0:T(8,128)S(1)}, u32[]{:S(2)}, u32[]{:S(2)}) %collective-permute-start.14) | collective-permute-done | bytes 176160 | tf_op jit(solution)/shard_map/ppermute | solution.py:620
  125.4 3.3 %collective-permute-done.15.m3 = f32[344,128]{1,0:T(8,128)S(1)} collective-permute-done((f32[344,128]{1,0:T(8,128)S(1)}, f32[344,128]{1,0:T(8,128)S(1)}, u32[]{:S(2)}, u32[]{:S(2)}) %collective-permute-start.15) | collective-permute-done | bytes 176160 | tf_op jit(solution)/shard_map/ppermute | solution.py:620
  128.7 4.2 %shard_map.91 = (f32[8,128,128]{2,1,0:T(8,128)}, f32[8,128,128]{2,1,0:T(8,128)}, f32[2,8,128,128]{3,2,1,0:T(8,128)}) custom-call(s32[4]{0:T(128)S(1)} %broadcast_select_fusion.1.strips, f32[344,128]{1,0:T(8,128)S(1)} %get-tuple-element.89.m0, f32[344,128]{1,0:T(8,128)S(1)} %collective-permute-done.13.m1, f32[344,128]{1,0:T(8,128)S(1)} %collective-permute-done.14.m2, ...), custom_call_target="tpu_custom_call" | custom-call | bytes 6000000 | tf_op jit(solution)/shard_map/pallas_call | solution.py:607
  (40 shorter events, 11.0 us)
Async XLA Ops:
  0.7 1.0 copy-start
  1.7 1.0 copy-start.2
  4.0 8.3 %collective-permute-start = (bf16[8,128,128]{2,1,0:T(8,128)(2,1)}, bf16[8,128,128]{2,1,0:T(8,128)(2,1)S(1)}, u32[]{:S(2)}, u32[]{:S(2)}) collective-permute-start(bf16[8,128,128]{2,1,0:T(8,128)(2,1)} %param.6), channel_id=1, source_target_pairs={{0,1},{1,0},{2,3},{3,2},{4,5},{5,4},{6,7},{7,6},{8,9},{9,8},{10,11... | collective-permute-start | bytes 786440 | tf_op jit(solution)/shard_map/ppermute | solution.py:620
  5.6 19.6 %collective-permute-start.1 = (f32[2,2,128,128]{3,2,1,0:T(8,128)S(1)}, f32[2,2,128,128]{3,2,1,0:T(8,128)S(1)}, u32[]{:S(2)}, u32[]{:S(2)}) collective-permute-start(f32[2,2,128,128]{3,2,1,0:T(8,128)S(1)} %get-tuple-element.61), channel_id=1, source_target_pairs={{0,8},{8,16},{16,24},{24,0},{1,9},{9,17},{17,25},{25,1},{2,10},{10... | collective-permute-start | bytes 786440 | tf_op jit(solution)/shard_map/ppermute | solution.py:620
  7.1 22.1 %collective-permute-start.2 = (f32[2,2,128,128]{3,2,1,0:T(8,128)S(1)}, f32[2,2,128,128]{3,2,1,0:T(8,128)S(1)}, u32[]{:S(2)}, u32[]{:S(2)}) collective-permute-start(f32[2,2,128,128]{3,2,1,0:T(8,128)S(1)} %get-tuple-element.62), channel_id=1, source_target_pairs={{0,16},{8,24},{16,0},{24,8},{1,17},{9,25},{17,1},{25,9},{2,18},{10... | collective-permute-start | bytes 786440 | tf_op jit(solution)/shard_map/ppermute | solution.py:620
  8.4 22.7 %collective-permute-start.3 = (f32[2,2,128,128]{3,2,1,0:T(8,128)S(1)}, f32[2,2,128,128]{3,2,1,0:T(8,128)S(1)}, u32[]{:S(2)}, u32[]{:S(2)}) collective-permute-start(f32[2,2,128,128]{3,2,1,0:T(8,128)S(1)} %get-tuple-element.63), channel_id=1, source_target_pairs={{0,24},{8,0},{16,8},{24,16},{1,25},{9,1},{17,9},{25,17},{2,26},{10... | collective-permute-start | bytes 786440 | tf_op jit(solution)/shard_map/ppermute | solution.py:620
  13.5 17.6 %collective-permute-start.5 = (f32[2,8,16,128]{3,2,1,0:T(8,128)S(1)}, f32[2,8,16,128]{3,2,1,0:T(8,128)S(1)}, u32[]{:S(2)}, u32[]{:S(2)}) collective-permute-start(f32[2,8,16,128]{3,2,1,0:T(8,128)S(1)} %get-tuple-element.106), channel_id=1, source_target_pairs={{0,6},{2,0},{4,2},{6,4},{1,7},{3,1},{5,3},{7,5},{8,14},{10,8},{12,... | collective-permute-start | bytes 393224 | tf_op jit(solution)/shard_map/ppermute | solution.py:620
  13.6 17.5 %collective-permute-start.4 = (f32[2,8,16,128]{3,2,1,0:T(8,128)S(1)}, f32[2,8,16,128]{3,2,1,0:T(8,128)S(1)}, u32[]{:S(2)}, u32[]{:S(2)}) collective-permute-start(f32[2,8,16,128]{3,2,1,0:T(8,128)S(1)} %get-tuple-element.107), channel_id=1, source_target_pairs={{0,2},{2,4},{4,6},{6,0},{1,3},{3,5},{5,7},{7,1},{8,10},{10,12},{12... | collective-permute-start | bytes 393224 | tf_op jit(solution)/shard_map/ppermute | solution.py:620
  32.0 13.9 %collective-permute-start.7 = (f32[2,4,128,128]{3,2,1,0:T(8,128)S(1)}, f32[2,4,128,128]{3,2,1,0:T(8,128)S(1)}, u32[]{:S(2)}, u32[]{:S(2)}) collective-permute-start(f32[2,4,128,128]{3,2,1,0:T(8,128)S(1)} %get-tuple-element.74), channel_id=1, source_target_pairs={{0,1},{8,0},{16,8},{24,16},{25,24},{17,25},{9,17},{1,9},{2,3},{10,... | collective-permute-start | bytes 1572872 | tf_op jit(solution)/shard_map/ppermute | solution.py:625
  32.0 13.9 %collective-permute-start.6 = (f32[2,4,128,128]{3,2,1,0:T(8,128)S(1)}, f32[2,4,128,128]{3,2,1,0:T(8,128)S(1)}, u32[]{:S(2)}, u32[]{:S(2)}) collective-permute-start(f32[2,4,128,128]{3,2,1,0:T(8,128)S(1)} %get-tuple-element.73), channel_id=1, source_target_pairs={{0,8},{8,16},{16,24},{24,25},{25,17},{17,9},{9,1},{1,0},{2,10},{10... | collective-permute-start | bytes 1572872 | tf_op jit(solution)/shard_map/ppermute | solution.py:625
  46.8 7.0 %collective-permute-start.11 = (f32[2,4,4,16,128]{4,3,2,1,0:T(8,128)}, f32[2,4,4,16,128]{4,3,2,1,0:T(8,128)S(1)}, u32[]{:S(2)}, u32[]{:S(2)}) collective-permute-start(f32[2,4,4,16,128]{4,3,2,1,0:T(8,128)} %get-tuple-element.82), channel_id=1, source_target_pairs={{0,2},{2,4},{4,6},{6,0},{1,3},{3,5},{5,7},{7,1},{8,10},{10,12},{12... | collective-permute-start | bytes 786440 | tf_op jit(solution)/shard_map/ppermute | solution.py:620
  46.8 7.9 %collective-permute-start.12 = (f32[2,4,4,16,128]{4,3,2,1,0:T(8,128)}, f32[2,4,4,16,128]{4,3,2,1,0:T(8,128)}, u32[]{:S(2)}, u32[]{:S(2)}) collective-permute-start(f32[2,4,4,16,128]{4,3,2,1,0:T(8,128)} %get-tuple-element.83), channel_id=1, source_target_pairs={{0,6},{2,0},{4,2},{6,4},{1,7},{3,1},{5,3},{7,5},{8,14},{10,8},{12,... | collective-permute-start | bytes 786440 | tf_op jit(solution)/shard_map/ppermute | solution.py:620
  48.5 36.0 %collective-permute-start.8 = (f32[4,160,128]{2,1,0:T(8,128)}, f32[4,160,128]{2,1,0:T(8,128)}, u32[]{:S(2)}, u32[]{:S(2)}) collective-permute-start(f32[4,160,128]{2,1,0:T(8,128)} %get-tuple-element.77), channel_id=1, source_target_pairs={{0,8},{8,16},{16,24},{24,0},{1,9},{9,17},{17,25},{25,1},{2,10},{10... | collective-permute-start | bytes 983048 | tf_op jit(solution)/shard_map/ppermute | solution.py:620
  50.2 35.0 %collective-permute-start.9 = (f32[4,160,128]{2,1,0:T(8,128)}, f32[4,160,128]{2,1,0:T(8,128)}, u32[]{:S(2)}, u32[]{:S(2)}) collective-permute-start(f32[4,160,128]{2,1,0:T(8,128)} %get-tuple-element.78), channel_id=1, source_target_pairs={{0,16},{8,24},{16,0},{24,8},{1,17},{9,25},{17,1},{25,9},{2,18},{10... | collective-permute-start | bytes 983048 | tf_op jit(solution)/shard_map/ppermute | solution.py:620
  51.4 33.8 %collective-permute-start.10 = (f32[4,160,128]{2,1,0:T(8,128)}, f32[4,160,128]{2,1,0:T(8,128)}, u32[]{:S(2)}, u32[]{:S(2)}) collective-permute-start(f32[4,160,128]{2,1,0:T(8,128)} %get-tuple-element.79), channel_id=1, source_target_pairs={{0,24},{8,0},{16,8},{24,16},{1,25},{9,1},{17,9},{25,17},{2,26},{10... | collective-permute-start | bytes 983048 | tf_op jit(solution)/shard_map/ppermute | solution.py:620
  52.0 33.2 %copy-start.5 = (f32[4,160,128]{2,1,0:T(8,128)S(1)}, f32[4,160,128]{2,1,0:T(8,128)}, u32[]{:S(2)}) copy-start(f32[4,160,128]{2,1,0:T(8,128)} %copy-done.4) | copy-start | bytes 983044
  81.7 31.9 %collective-permute-start.16 = (f32[432,128]{1,0:T(8,128)S(1)}, f32[432,128]{1,0:T(8,128)S(1)}, u32[]{:S(2)}, u32[]{:S(2)}) collective-permute-start(f32[432,128]{1,0:T(8,128)S(1)} %get-tuple-element.94), channel_id=1, source_target_pairs={{0,8},{8,16},{16,24},{24,0},{1,9},{9,17},{17,25},{25,1},{2,10},{10... | collective-permute-start | bytes 663560 | tf_op jit(solution)/shard_map/ppermute | solution.py:620
  83.4 30.1 %collective-permute-start.17 = (f32[432,128]{1,0:T(8,128)S(1)}, f32[432,128]{1,0:T(8,128)S(1)}, u32[]{:S(2)}, u32[]{:S(2)}) collective-permute-start(f32[432,128]{1,0:T(8,128)S(1)} %get-tuple-element.95), channel_id=1, source_target_pairs={{0,16},{8,24},{16,0},{24,8},{1,17},{9,25},{17,1},{25,9},{2,18},{10... | collective-permute-start | bytes 663560 | tf_op jit(solution)/shard_map/ppermute | solution.py:620
  84.5 29.0 %collective-permute-start.18 = (f32[432,128]{1,0:T(8,128)S(1)}, f32[432,128]{1,0:T(8,128)S(1)}, u32[]{:S(2)}, u32[]{:S(2)}) collective-permute-start(f32[432,128]{1,0:T(8,128)S(1)} %get-tuple-element.96), channel_id=1, source_target_pairs={{0,24},{8,0},{16,8},{24,16},{1,25},{9,1},{17,9},{25,17},{2,26},{10... | collective-permute-start | bytes 663560 | tf_op jit(solution)/shard_map/ppermute | solution.py:620
  85.2 28.4 %copy-start.1 = (f32[8,128,128]{2,1,0:T(8,128)S(1)}, f32[8,128,128]{2,1,0:T(8,128)}, u32[]{:S(2)}) copy-start(f32[8,128,128]{2,1,0:T(8,128)} %cond.1) | copy-start | bytes 1572868
  85.2 28.4 %copy-start.3 = (f32[8,128,128]{2,1,0:T(8,128)S(1)}, f32[8,128,128]{2,1,0:T(8,128)}, u32[]{:S(2)}) copy-start(f32[8,128,128]{2,1,0:T(8,128)} %cot.1) | copy-start | bytes 1572868
  108.5 9.7 %collective-permute-start.13 = (f32[344,128]{1,0:T(8,128)S(1)}, f32[344,128]{1,0:T(8,128)S(1)}, u32[]{:S(2)}, u32[]{:S(2)}) collective-permute-start(f32[344,128]{1,0:T(8,128)S(1)} %get-tuple-element.90), channel_id=1, source_target_pairs={{0,8},{8,16},{16,24},{24,0},{1,9},{9,17},{17,25},{25,1},{2,10},{10... | collective-permute-start | bytes 528392 | tf_op jit(solution)/shard_map/ppermute | solution.py:620
  109.9 15.5 %collective-permute-start.14 = (f32[344,128]{1,0:T(8,128)S(1)}, f32[344,128]{1,0:T(8,128)S(1)}, u32[]{:S(2)}, u32[]{:S(2)}) collective-permute-start(f32[344,128]{1,0:T(8,128)S(1)} %get-tuple-element.91), channel_id=1, source_target_pairs={{0,16},{8,24},{16,0},{24,8},{1,17},{9,25},{17,1},{25,9},{2,18},{10... | collective-permute-start | bytes 528392 | tf_op jit(solution)/shard_map/ppermute | solution.py:620
  113.5 15.2 %collective-permute-start.15 = (f32[344,128]{1,0:T(8,128)S(1)}, f32[344,128]{1,0:T(8,128)S(1)}, u32[]{:S(2)}, u32[]{:S(2)}) collective-permute-start(f32[344,128]{1,0:T(8,128)S(1)} %get-tuple-element.92), channel_id=1, source_target_pairs={{0,24},{8,0},{16,8},{24,16},{1,25},{9,1},{17,9},{25,17},{2,26},{10... | collective-permute-start | bytes 528392 | tf_op jit(solution)/shard_map/ppermute | solution.py:620
  (1 other events, 0.7 us)
